TPU v7x, 32 devices: a whole 2x2x4 slice. The times are simulated.
32 devices in a mesh: row: 8 (over z, core), col: 4 (over y, x).
Axes of the slice: x: 2, y: 2, z: 4, core: 2. Of those that a mesh axis runs over, the one named last changes fastest.
Arguments:
- layer_input: bfloat16 [2048, 8192], P('row', 'col'), may hold values from -6 to 6
- attn_grad: bfloat16 [2048, 8192], P('row', 'col'), may hold values from -6 to 6
- queries: bfloat16 [8, 256, 8192], P('row', None, 'col'), may hold values from -6 to 6
- keys: bfloat16 [8, 256, 8192], P('row', None, 'col'), may hold values from -6 to 6
- values: bfloat16 [8, 256, 8192], P('row', None, 'col'), may hold values from -6 to 6
- masked: int32 [8, 256], P('row'), may hold values 0 or 1
- key_bias: float32 [64], P('col'), may hold values from -2 to 2
- w_query: bfloat16 [8192, 8192], P('row', 'col'), may hold values from -0.0625 to 0.0625
- w_key: bfloat16 [8192, 8192], P('row', 'col'), may hold values from -0.0625 to 0.0625
- w_value: bfloat16 [8192, 8192], P('row', 'col'), may hold values from -0.0625 to 0.0625
Outputs:
- layer_grad: bfloat16 [2048, 8192], P('row', 'col')
- w_query_grad: bfloat16 [8192, 8192], P('row', 'col')
- w_key_grad: bfloat16 [8192, 8192], P('row', 'col')
- w_value_grad: bfloat16 [8192, 8192], P('row', 'col')
- bias_grad: float32 [64], P('col')
All inputs are finite; a program needn't handle non-finite values. No bound on the sum of `masked` on one device may be relied on, other than what follows from the above.
Results may differ from a plain program's by a relative error of at most 0.015.
Values may be sent and summed in bfloat16 or wider, within the bound.
No kernel may reach another device: no remote copies, remote signals or barrier semaphores. Data moves between devices by JAX's collectives and lax.ppermute only.
A program may use at most 192 MiB of HBM per device.

v0:
```python
import jax
import jax.numpy as jnp
from jax import lax
from jax.sharding import PartitionSpec as P


def attend_back(query_c, key_c, value_c, grad_c, flag_c, key_bias):
    length = query_c.shape[0]
    heads_local = key_bias.shape[0]
    head_dim = query_c.shape[1] // heads_local
    scale_qk = 1.0 / jnp.sqrt(jnp.float32(head_dim))
    query_h = query_c.reshape(length, heads_local, head_dim)
    key_h = key_c.reshape(length, heads_local, head_dim)
    value_h = value_c.reshape(length, heads_local, head_dim)
    grad_h = grad_c.reshape(length, heads_local, head_dim)
    flag_float = flag_c.astype(jnp.float32)
    scores = (
        jnp.einsum("ihd,jhd->hij", query_h, key_h, preferred_element_type=jnp.float32) * scale_qk
        + key_bias[:, None, None] * flag_float[None, None, :]
    )
    row_max = jnp.max(scores, axis=-1, keepdims=True)
    exp_terms = jnp.exp(scores - row_max)
    attn_probs = exp_terms / jnp.sum(exp_terms, axis=-1, keepdims=True)
    probs_low = attn_probs.astype(jnp.bfloat16)
    attended = jnp.einsum("hij,jhd->ihd", probs_low, value_h, preferred_element_type=jnp.float32)
    delta = jnp.sum(grad_h.astype(jnp.float32) * attended, axis=-1)
    grad_probs = jnp.einsum("ihd,jhd->hij", grad_h, value_h, preferred_element_type=jnp.float32)
    grad_scores = attn_probs * (grad_probs - jnp.transpose(delta)[:, :, None])
    grad_low = grad_scores.astype(jnp.bfloat16)
    value_grad = jnp.einsum(
        "hij,ihd->jhd", probs_low, grad_h, preferred_element_type=jnp.float32
    ).astype(jnp.bfloat16)
    query_grad = (
        jnp.einsum("hij,jhd->ihd", grad_low, key_h, preferred_element_type=jnp.float32) * scale_qk
    ).astype(jnp.bfloat16)
    key_grad = (
        jnp.einsum("hij,ihd->jhd", grad_low, query_h, preferred_element_type=jnp.float32) * scale_qk
    ).astype(jnp.bfloat16)
    bias_part = jnp.sum(grad_scores * flag_float[None, None, :], axis=(1, 2))
    width = query_c.shape[1]
    return (
        query_grad.reshape(length, width),
        key_grad.reshape(length, width),
        value_grad.reshape(length, width),
        bias_part,
    )


def local(layer_input, attn_grad, queries, keys, values, masked, key_bias, w_query, w_key, w_value):
    row_count = lax.axis_size("row")
    col_count = lax.axis_size("col")
    width_col = attn_grad.shape[1]
    canvases_here = queries.shape[0]
    length = queries.shape[1]
    tok_local = canvases_here * length
    rows_in = w_query.shape[0]
    spread_k = row_count // col_count
    grad_canvas = attn_grad.reshape(canvases_here, length, width_col)

    def one_canvas(inputs_one):
        return attend_back(
            inputs_one[0], inputs_one[1], inputs_one[2], inputs_one[3], inputs_one[4], key_bias
        )

    query_grad, key_grad, value_grad, bias_parts = lax.map(
        one_canvas, (queries, keys, values, grad_canvas, masked)
    )
    bias_grad = lax.psum(jnp.sum(bias_parts, axis=0), "row")
    gathered = (
        lax.all_gather(query_grad, "row", axis=0, tiled=True),
        lax.all_gather(key_grad, "row", axis=0, tiled=True),
        lax.all_gather(value_grad, "row", axis=0, tiled=True),
    )
    all_tokens = gathered[0].shape[0] * length
    flat_grads = tuple((member.reshape(all_tokens, width_col) for member in gathered))
    widened = lax.all_gather(layer_input, "col", axis=1, tiled=True)
    spread = lax.all_to_all(widened, "row", split_axis=1, concat_axis=0, tiled=True)
    weight_grads = tuple(
        (
            lax.dot_general(
                spread, member, (((0,), (0,)), ((), ())), preferred_element_type=jnp.float32
            ).astype(jnp.bfloat16)
            for member in flat_grads
        )
    )
    contract = (((1,), (1,)), ((), ()))
    partial_value = lax.dot_general(
        flat_grads[0], w_query, contract, preferred_element_type=jnp.float32
    )
    partial_value = partial_value + lax.dot_general(
        flat_grads[1], w_key, contract, preferred_element_type=jnp.float32
    )
    partial_value = partial_value + lax.dot_general(
        flat_grads[2], w_value, contract, preferred_element_type=jnp.float32
    )
    partial_low = partial_value.astype(jnp.bfloat16)
    summed = lax.psum_scatter(
        lax.optimization_barrier(partial_low).astype(jnp.float32).astype(jnp.bfloat16),
        "col",
        scatter_dimension=1,
        tiled=True,
    ).astype(jnp.float32)
    piece_width = summed.shape[1]
    sectioned = summed.astype(jnp.bfloat16).reshape(row_count, tok_local, 1, piece_width)
    arrived = lax.all_to_all(
        lax.all_to_all(sectioned, "row", split_axis=0, concat_axis=2, tiled=True),
        "col",
        split_axis=2,
        concat_axis=3,
        tiled=True,
    )
    layer_grad = arrived.reshape(tok_local, spread_k * rows_in)
    return (layer_grad, weight_grads[0], weight_grads[1], weight_grads[2], bias_grad)


def solution(mesh):
    in_specs = (
        P("row", "col"),
        P("row", "col"),
        P("row", None, "col"),
        P("row", None, "col"),
        P("row", None, "col"),
        P("row", None),
        P("col"),
        P("row", "col"),
        P("row", "col"),
        P("row", "col"),
    )
    out_specs = (P("row", "col"), P("row", "col"), P("row", "col"), P("row", "col"), P("col"))
    return jax.shard_map(local, mesh=mesh, in_specs=in_specs, out_specs=out_specs, check_vma=False)
```

profile of v0, /device:TPU:0, one launch (start us, length us, event | category | flops | bytes accessed | tf_op | source)
XLA Modules:
  0.0 539.4 jit_solution(13285932313350599069)
XLA Ops:
  7.2 0.0 copy-start.6
  7.2 0.0 all-gather.11.cloned.1.call-start
  7.2 2.4 copy.73
  9.6 0.0 all-gather.11.cloned.1.call-update
  9.6 0.0 all-gather.5.cloned.1.call-start
  9.7 0.7 convert_element_type.65
  10.4 0.0 copy-start.7
  10.4 1.5 copy.56
  11.9 0.0 copy-done.6
  11.9 0.5 copy.91
  12.4 0.0 copy-start.2
  12.4 1.9 copy.90
  14.3 0.0 copy-start.3
  14.3 2.6 copy.92
  16.9 0.0 copy-done.7
  16.9 0.1 broadcast_multiply_fusion
  17.0 3.0 fusion.23
  20.0 0.0 copy-done.2
  20.0 0.0 copy-done.3
  20.0 0.0 copy-start.5
  20.0 3.2 fusion.17
  23.2 0.0 copy-done.5
  23.2 0.5 fusion.14
  23.7 0.6 copy-done.1
  24.3 1.3 multiply_reduce_fusion
  25.6 1.3 copy-done
  26.9 0.0 copy-done.4
  26.9 1.4 multiply_convert_fusion.1
  28.3 2.3 copy.64
  30.6 0.0 all-gather.5.cloned.1.call-update
  30.6 0.0 all-gather.7.cloned.1.call-start
  30.7 3.7 multiply_convert_fusion
  34.3 2.3 copy.67
  36.6 0.0 all-gather.7.cloned.1.call-update
  36.6 0.0 all-gather.9.cloned.1.call-start
  36.7 1.8 convolution_convert_fusion
  38.4 2.3 copy.69
  40.7 0.0 all-gather.9.cloned.1.call-update
  40.7 24.5 %all-gather.11.cloned.1.call-done = bf16[256,8192]{0,1:T(8,128)(2,1)} async-done(((bf16[256,2048]{0,1:T(8,128)(2,1)}), bf16[256,8192]{0,1:T(8,128)(2,1)}) %all-gather.11.cloned.1.call-update) | async-done | bytes 4194320 | tf_op jit(solution)/shard_map/all_gather | solution.py:76
  65.3 6.4 %copy.74 = bf16[256,8,1024]{2,0,1:T(8,128)(2,1)} copy(bf16[256,8,1024]{0,2,1:T(8,128)(2,1)} %bitcast.93) | data formatting | bytes 8388608 | tf_op jit(solution)/shard_map/all_to_all | solution.py:77
  71.7 4.6 all-to-all-start.2
  76.3 0.2 reduce-scatter.2.cloned.1.call-start
  76.6 151.1 %all-gather.5.cloned.1.call-done = bf16[8,256,2048]{2,1,0:T(8,128)(2,1)} async-done(((bf16[1,256,2048]{2,1,0:T(8,128)(2,1)}), bf16[8,256,2048]{2,1,0:T(8,128)(2,1)}) %all-gather.5.cloned.1.call-update) | async-done | bytes 8388624 | tf_op jit(solution)/shard_map/all_gather | solution.py:70
  227.7 14.5 %fusion.24 = f32[2048,1024]{1,0:T(8,128)} fusion(bf16[2048,2048]{1,0:T(8,128)(2,1)} %bitcast.108, bf16[1024,2048]{1,0:T(8,128)(2,1)} %param.17), kind=kOutput, calls=%fused_computation.31 | convolution fusion | flops 8589934592 | bytes 20971520 | tf_op jit(solution)/shard_map/dot_general | solution.py:87
  242.2 68.3 %all-gather.7.cloned.1.call-done = bf16[8,256,2048]{2,1,0:T(8,128)(2,1)} async-done(((bf16[1,256,2048]{2,1,0:T(8,128)(2,1)}), bf16[8,256,2048]{2,1,0:T(8,128)(2,1)}) %all-gather.7.cloned.1.call-update) | async-done | bytes 8388624 | tf_op jit(solution)/shard_map/all_gather | solution.py:71
  310.4 14.5 %fusion.25 = f32[2048,1024]{1,0:T(8,128)} fusion(bf16[2048,2048]{1,0:T(8,128)(2,1)} %bitcast.109, bf16[1024,2048]{1,0:T(8,128)(2,1)} %param.18), kind=kOutput, calls=%fused_computation.32 | convolution fusion | flops 8589934592 | bytes 20971520 | tf_op jit(solution)/shard_map/dot_general | solution.py:90
  324.9 67.6 %all-gather.9.cloned.1.call-done = bf16[8,256,2048]{2,1,0:T(8,128)(2,1)} async-done(((bf16[1,256,2048]{2,1,0:T(8,128)(2,1)}), bf16[8,256,2048]{2,1,0:T(8,128)(2,1)}) %all-gather.9.cloned.1.call-update) | async-done | bytes 8388624 | tf_op jit(solution)/shard_map/all_gather | solution.py:72
  392.5 18.3 %add_convert_fusion = bf16[2048,1024]{1,0:T(8,128)(2,1)} fusion(f32[2048,1024]{1,0:T(8,128)} %fusion.24, f32[2048,1024]{1,0:T(8,128)} %fusion.25, bf16[2048,2048]{1,0:T(8,128)(2,1)} %bitcast.110, bf16[1024,2048]{1,0:T(8,128)(2,1)} %param.19), kind=kOutput, calls=%fused_computation.4 | convolution fusion | flops 8596226048 | bytes 33554432 | tf_op jit(solution)/shard_map/dot_general | solution.py:93
  410.8 0.0 reduce-scatter.2.cloned.1.call-update
  410.8 14.8 %psum.7 = f32[16]{0:T(128)} all-reduce(f32[16]{0:T(128)S(1)} %get-tuple-element.55), channel_id=1, replica_groups=mesh['row'=8,'col'=4] {'row'}, use_global_device_ids=true, to_apply=%region_5.6 | all-reduce | flops 16 | bytes 128 | tf_op jit(solution)/shard_map/psum | solution.py:68
  425.5 0.0 all-to-all-done.2
  425.5 14.2 %fusion.10 = bf16[1024,2048]{0,1:T(8,128)(2,1)} fusion(bf16[8,256,2048]{2,1,0:T(8,128)(2,1)} %all-gather.9.cloned.1.call-done, bf16[256,8,1024]{2,0,1:T(8,128)(2,1)} %all-to-all-done.2), kind=kOutput, calls=%fused_computation.14 | convolution fusion | flops 8592031744 | bytes 16777216 | tf_op jit(solution)/shard_map/dot_general | solution.py:80
  439.8 22.4 %reduce-scatter.2.cloned.1.call-done = bf16[2048,256]{1,0:T(8,128)(2,1)} async-done(((bf16[2048,1024]{1,0:T(8,128)(2,1)}), bf16[2048,256]{1,0:T(8,128)(2,1)}) %reduce-scatter.2.cloned.1.call-update) | async-done | bytes 1048592 | tf_op jit(solution)/shard_map/reduce_scatter | solution.py:97
  462.1 4.6 all-to-all-start
  466.7 14.0 %fusion.4 = bf16[1024,2048]{0,1:T(8,128)(2,1)} fusion(bf16[8,256,2048]{2,1,0:T(8,128)(2,1)} %all-gather.5.cloned.1.call-done, bf16[256,8,1024]{2,0,1:T(8,128)(2,1)} %all-to-all-done.2), kind=kOutput, calls=%fused_computation.12 | convolution fusion | flops 8592031744 | bytes 16777216 | tf_op jit(solution)/shard_map/dot_general | solution.py:80
  480.7 12.7 %all-to-all-done = bf16[8,256,1,256]{3,1,2,0:T(8,128)(2,1)} async-done(((bf16[8,256,1,256]{3,1,2,0:T(8,128)(2,1)}), bf16[8,256,1,256]{3,1,2,0:T(8,128)(2,1)}, u32[]{:S(2)}, u32[]{:S(2)}) %all-to-all-start) | async-done | bytes 1048608 | tf_op jit(solution)/shard_map/all_to_all | solution.py:106
  493.4 3.8 all-to-all-start.1
  497.2 14.0 %fusion.7 = bf16[1024,2048]{0,1:T(8,128)(2,1)} fusion(bf16[8,256,2048]{2,1,0:T(8,128)(2,1)} %all-gather.7.cloned.1.call-done, bf16[256,8,1024]{2,0,1:T(8,128)(2,1)} %all-to-all-done.2), kind=kOutput, calls=%fused_computation.13 | convolution fusion | flops 8592031744 | bytes 16777216 | tf_op jit(solution)/shard_map/dot_general | solution.py:80
  511.2 6.4 %copy.80 = bf16[1024,2048]{1,0:T(8,128)(2,1)} copy(bf16[1024,2048]{0,1:T(8,128)(2,1)} %fusion.10) | data formatting | bytes 8388608
  517.6 6.4 %copy.79 = bf16[1024,2048]{1,0:T(8,128)(2,1)} copy(bf16[1024,2048]{0,1:T(8,128)(2,1)} %fusion.7) | data formatting | bytes 8388608
  524.0 6.4 %copy.78 = bf16[1024,2048]{1,0:T(8,128)(2,1)} copy(bf16[1024,2048]{0,1:T(8,128)(2,1)} %fusion.4) | data formatting | bytes 8388608
  530.5 0.0 all-to-all-done.1
  530.5 0.8 copy.72
  531.3 1.6 reshape.105
  (3 shorter events, 0.0 us)
Async XLA Ops:
  7.2 4.7 copy-start.6
  7.2 58.1 %all-gather.11.cloned.1.call-start = ((), (), s32[]{:S(2)}) async-start(), calls=%async_computation.8 | async-start | bytes 5242880 | tf_op jit(solution)/shard_map/all_gather | solution.py:76
  9.6 218.1 %all-gather.5.cloned.1.call-start = ((), (), s32[]{:S(2)}) async-start(), calls=%async_computation.4 | async-start | bytes 9437184 | tf_op jit(solution)/shard_map/all_gather | solution.py:70
  10.4 6.6 %copy-start.7 = (f32[16]{0:T(128)S(1)}, f32[16]{0:T(128)}, u32[]{:S(2)}) copy-start(f32[16]{0:T(128)} %param.16) | copy-start | bytes 196
  12.4 7.6 %copy-start.2 = (bf16[1,256,2048]{1,2,0:T(8,128)(2,1)}, bf16[1,256,2048]{1,2,0:T(8,128)(2,1)S(1)}, u32[]{:S(2)}) copy-start(bf16[1,256,2048]{1,2,0:T(8,128)(2,1)S(1)} %copy.91) | copy-start | bytes 3145732
  14.3 5.7 %copy-start.3 = (bf16[1,256,2048]{1,2,0:T(8,128)(2,1)}, bf16[1,256,2048]{1,2,0:T(8,128)(2,1)S(1)}, u32[]{:S(2)}) copy-start(bf16[1,256,2048]{1,2,0:T(8,128)(2,1)S(1)} %copy.90) | copy-start | bytes 3145732
  20.0 3.2 copy-start.5
  20.0 4.2 copy-start.1
  24.3 2.6 copy-start.4
  25.6 1.3 copy-start
  30.6 279.8 %all-gather.7.cloned.1.call-start = ((), (), s32[]{:S(2)}) async-start(), calls=%async_computation.5 | async-start | bytes 9437184 | tf_op jit(solution)/shard_map/all_gather | solution.py:71
  36.6 355.9 %all-gather.9.cloned.1.call-start = ((), (), s32[]{:S(2)}) async-start(), calls=%async_computation.6 | async-start | bytes 9437184 | tf_op jit(solution)/shard_map/all_gather | solution.py:72
  71.7 353.8 %all-to-all-start.2 = ((bf16[256,8,1024]{2,0,1:T(8,128)(2,1)}), bf16[256,8,1024]{2,0,1:T(8,128)(2,1)}, u32[]{:S(2)}, u32[]{:S(2)}) async-start(bf16[256,8,1024]{2,0,1:T(8,128)(2,1)} %copy.74), calls=%async_computation.3 | async-start | bytes 8388608 | tf_op jit(solution)/shard_map/all_to_all | solution.py:77
  76.3 385.8 %reduce-scatter.2.cloned.1.call-start = ((), (), s32[]{:S(2)}) async-start(), calls=%async_computation.7 | async-start | bytes 5242880 | tf_op jit(solution)/shard_map/reduce_scatter | solution.py:97
  462.1 31.3 %all-to-all-start = ((bf16[8,256,1,256]{3,1,2,0:T(8,128)(2,1)}), bf16[8,256,1,256]{3,1,2,0:T(8,128)(2,1)}, u32[]{:S(2)}, u32[]{:S(2)}) async-start(bf16[8,256,1,256]{3,1,2,0:T(8,128)(2,1)} %bitcast.104), calls=%async_computation.1 | async-start | bytes 2097152 | tf_op jit(solution)/shard_map/all_to_all | solution.py:106
  493.4 37.0 %all-to-all-start.1 = ((bf16[1,256,8,256]{3,1,0,2:T(8,128)(2,1)}), bf16[1,256,8,256]{3,1,0,2:T(8,128)(2,1)S(1)}, u32[]{:S(2)}, u32[]{:S(2)}) async-start(bf16[1,256,8,256]{3,1,0,2:T(8,128)(2,1)} %bitcast.18), calls=%async_computation.2 | async-start | bytes 2097152 | tf_op jit(solution)/shard_map/all_to_all | solution.py:105
Sparse Core Ops, SparseCore 0:
  9.9 55.3 all-gather.10
  67.5 160.1 all-gather.4
  229.9 80.4 all-gather.6
  311.9 80.5 all-gather.8
  410.9 51.1 reduce-scatter.1
where the time goes:
time: 540 us; the launch traced here: 539 us
  waiting for transfers between devices  347 us (64%)
  matrix products  101 us (19%)
  local copies, waits for them, and re-layouts  45.7 us (8%)
  blocking collectives  14.8 us (3%)
  between operations  13.9 us (3%)
  starting transfers between devices  13.4 us (2%)
    all_gather x1, waiting for transfers between devices, local(): lax.all_gather(query_grad, 'row', axis=0, tiled=True)  151 us
    all_gather x1, waiting for transfers between devices, local(): lax.all_gather(key_grad, 'row', axis=0, tiled=True)  68.3 us
    all_gather x1, waiting for transfers between devices, local(): lax.all_gather(value_grad, 'row', axis=0, tiled=True)  67.6 us
    dot_general x3, matrix products, local(): lax.dot_general(spread, member, (((0,), (0,)), ((), ())), preferred_eleme...  42.2 us
    unnamed x21, local copies, waits for them, and re-layouts  25.1 us
    all_gather x1, waiting for transfers between devices, local(): widened = lax.all_gather(layer_input, 'col', axis=1, tiled=True)  24.5 us
    reduce_scatter x1, waiting for transfers between devices, local(): lax.psum_scatter(lax.optimization_barrier(partial_low).astype(jnp.float32...  22.4 us
    dot_general x1, matrix products, local(): lax.dot_general(flat_grads[2], w_value, contract, preferred_element_type=...  18.3 us
  transfers between devices with their start and end apart: 8, of which 6 were waited for; matrix products, arithmetic and copies ran while one was open for 27% of the time, Pallas kernels for 0%

commit v1 on v0

v1 whole, which is shorter than its diff:
```python
import functools
import math

import jax
import jax.numpy as jnp
from jax import lax
from jax.experimental import pallas as pl
from jax.experimental.pallas import tpu as pltpu
from jax.sharding import PartitionSpec as P

NT = (((1,), (1,)), ((), ()))
TN = (((0,), (0,)), ((), ()))
VMEM_LIMIT = 56 * 1024 * 1024


def chunk_sizes(length):
    return (length // 2, length - length // 2)


def attention_body(sizes, head_dim, heads_step, bias_ref, flag_ref, q_ref, k_ref, v_ref, g_ref, *outs):
    chunk_refs, bias_out = outs[:-1], outs[-1]
    scale_qk = 1.0 / math.sqrt(head_dim)
    flag = flag_ref[...].astype(jnp.float32)
    for sub in range(heads_step):
        cols = slice(sub * head_dim, (sub + 1) * head_dim)
        q, k, v, g = q_ref[:, cols], k_ref[:, cols], v_ref[:, cols], g_ref[:, cols]
        head = pl.program_id(0) * heads_step + sub
        scores = lax.dot_general(q, k, NT, preferred_element_type=jnp.float32) * scale_qk + bias_ref[head] * flag
        exp_terms = jnp.exp(scores - jnp.max(scores, axis=-1, keepdims=True))
        probs = exp_terms * (1.0 / jnp.sum(exp_terms, axis=-1, keepdims=True))
        probs_low = probs.astype(jnp.bfloat16)
        grad_probs = lax.dot_general(g, v, NT, preferred_element_type=jnp.float32)
        delta = jnp.sum(probs_low.astype(jnp.float32) * grad_probs, axis=-1, keepdims=True)
        grad_scores = probs * (grad_probs - delta)
        grad_low = grad_scores.astype(jnp.bfloat16)
        value_grad = lax.dot_general(probs_low, g, TN, preferred_element_type=jnp.float32)
        query_grad = jnp.dot(grad_low, k, preferred_element_type=jnp.float32) * scale_qk
        key_grad = lax.dot_general(grad_low, q, TN, preferred_element_type=jnp.float32) * scale_qk
        bias = jnp.sum(jnp.sum(grad_scores, axis=0, keepdims=True) * flag, axis=1, keepdims=True)
        bias_out[sub] = jnp.broadcast_to(bias, (1, 128))
        for place, member in enumerate((query_grad, key_grad, value_grad)):
            low = member.astype(jnp.bfloat16)
            begin = 0
            for size, ref in zip(sizes, chunk_refs):
                ref[place, :, cols] = low[begin:begin + size]
                begin += size


def attention(queries, keys, values, grads, flags, key_bias, sizes):
    length, width = queries.shape
    heads = key_bias.shape[0]
    head_dim = width // heads
    heads_step = 2 if heads % 2 == 0 else 1
    block = pl.BlockSpec((length, heads_step * head_dim), lambda h: (0, h))
    outs = pl.pallas_call(
        functools.partial(attention_body, sizes, head_dim, heads_step),
        grid=(heads // heads_step,),
        in_specs=[
            pl.BlockSpec(memory_space=pltpu.SMEM),
            pl.BlockSpec((1, length), lambda h: (0, 0)),
            block, block, block, block,
        ],
        out_specs=[pl.BlockSpec((3, size, heads_step * head_dim), lambda h: (0, 0, h)) for size in sizes]
        + [pl.BlockSpec((heads_step, 1, 128), lambda h: (h, 0, 0))],
        out_shape=[jax.ShapeDtypeStruct((3, size, width), jnp.bfloat16) for size in sizes]
        + [jax.ShapeDtypeStruct((heads, 1, 128), jnp.float32)],
        compiler_params=pltpu.CompilerParams(vmem_limit_bytes=VMEM_LIMIT),
        cost_estimate=pl.CostEstimate(
            flops=10 * length * length * width, bytes_accessed=14 * length * width, transcendentals=heads * length * length
        ),
        name="attention_back",
    )(key_bias, flags, queries, keys, values, grads)
    return outs[:-1], outs[-1][:, 0, 0]


def input_grad_body(count, pieces, *refs):
    grad_refs, weight_refs, out_ref = refs[:count], refs[count:count + 3], refs[-1]
    total = None
    for member in range(3):
        rows = jnp.concatenate([ref[member] for ref in grad_refs], axis=0)
        term = lax.dot_general(rows, weight_refs[member][...], NT, preferred_element_type=jnp.float32)
        total = term if total is None else total + term
    low = total.astype(jnp.bfloat16)
    begin = 0
    at = 0
    for ref in grad_refs:
        size = ref.shape[1] // pieces
        for piece in range(pieces):
            out_ref[piece, at:at + size, :] = low[begin:begin + size]
            begin += size
        at += size


def input_grad(grads, weights, pieces):
    rows_in, width = weights[0].shape
    tokens = sum(grad.shape[1] for grad in grads)
    step = 256
    return pl.pallas_call(
        functools.partial(input_grad_body, len(grads), pieces),
        grid=(rows_in // step,),
        in_specs=[pl.BlockSpec(grad.shape, lambda n: (0, 0, 0)) for grad in grads]
        + [pl.BlockSpec((step, width), lambda n: (n, 0))] * 3,
        out_specs=pl.BlockSpec((pieces, tokens // pieces, step), lambda n: (0, 0, n)),
        out_shape=jax.ShapeDtypeStruct((pieces, tokens // pieces, rows_in), jnp.bfloat16),
        compiler_params=pltpu.CompilerParams(vmem_limit_bytes=VMEM_LIMIT),
        cost_estimate=pl.CostEstimate(
            flops=6 * tokens * rows_in * width, bytes_accessed=6 * width * (rows_in + tokens), transcendentals=0
        ),
        name="input_grad",
    )(*grads, *weights)


def weight_grad_body(count, has_acc, x_ref, *refs):
    grad_refs, out_refs = refs[:count], refs[-3:]
    for member in range(3):
        right = jnp.concatenate([ref[member] for ref in grad_refs], axis=0)
        total = jnp.dot(x_ref[...], right, preferred_element_type=jnp.float32)
        if has_acc:
            total = total + refs[count + member][...].astype(jnp.float32)
        out_refs[member][...] = total.astype(jnp.bfloat16)


def weight_grad(x_turned, grads, acc):
    rows_in, tokens = x_turned.shape
    width = grads[0].shape[2]
    step = 256
    block = pl.BlockSpec((rows_in, step), lambda n: (0, n))
    acc = tuple(acc) if acc is not None else ()
    return pl.pallas_call(
        functools.partial(weight_grad_body, len(grads), bool(acc)),
        grid=(width // step,),
        in_specs=[pl.BlockSpec((rows_in, tokens), lambda n: (0, 0))]
        + [pl.BlockSpec((3, grad.shape[1], step), lambda n: (0, 0, n)) for grad in grads]
        + [block] * len(acc),
        out_specs=[block] * 3,
        out_shape=[jax.ShapeDtypeStruct((rows_in, width), jnp.bfloat16)] * 3,
        compiler_params=pltpu.CompilerParams(vmem_limit_bytes=VMEM_LIMIT),
        cost_estimate=pl.CostEstimate(
            flops=6 * tokens * rows_in * width,
            bytes_accessed=6 * width * tokens + 6 * width * rows_in * (2 if acc else 1),
            transcendentals=0,
        ),
        name="weight_grad",
    )(x_turned, *grads, *acc)


def ring_order(chips):
    return [0] + list(range(1, chips, 2)) + list(range(chips - 2 + chips % 2, 0, -2))


def local(layer_input, attn_grad, queries, keys, values, masked, key_bias, w_query, w_key, w_value):
    row_count = lax.axis_size("row")
    col_count = lax.axis_size("col")
    length, width = queries.shape[1], queries.shape[2]
    rows_in = w_query.shape[0]
    spread = row_count // col_count
    chips = row_count // 2
    sizes = chunk_sizes(length)
    last = len(sizes) - 1
    weights = (w_query, w_key, w_value)

    order = ring_order(chips)
    ring = [(2 * order[n] + core, 2 * order[(n + 1) % chips] + core) for n in range(chips) for core in range(2)]
    swap = [(n, n ^ 1) for n in range(row_count)]
    place_of = [order.index(chip) for chip in range(chips)]
    me = lax.axis_index("row")
    my_core = me % 2
    my_place = jnp.array(place_of, jnp.int32)[me // 2]
    chips_at = jnp.array(order, jnp.int32)[(my_place - jnp.arange(chips)) % chips]
    origin = chips_at[:, None] * 2 + (my_core + jnp.arange(2)[None, :]) % 2

    def a2a(array, axis):
        return lax.all_to_all(array, axis, split_axis=0, concat_axis=0, tiled=True)

    chunks, bias_part = attention(queries[0], keys[0], values[0], attn_grad, masked, key_bias, sizes)
    held = [[(chunk, lax.ppermute(chunk, "row", swap)) for chunk in chunks]]
    for step in range(1, chips):
        units = []
        for index in range(len(sizes)):
            mine = lax.ppermute(held[step - 1][index][0], "row", ring)
            units.append((mine, lax.ppermute(mine, "row", swap)))
        held.append(units)

    x = a2a(layer_input.reshape(col_count, length // col_count, width), "col")
    x = jnp.swapaxes(x.reshape(col_count, length // col_count, spread, rows_in), 1, 2)
    x = a2a(x.reshape(row_count, length // col_count, rows_in), "row")
    x = a2a(jnp.broadcast_to(x[None], (col_count,) + x.shape), "col")
    x = jnp.take(x, origin.reshape(-1), axis=1)
    x = jnp.transpose(x, (1, 3, 0, 2)).reshape(chips, 2, rows_in, length)

    def x_for(units):
        begins = [sum(sizes[:index]) for index in range(len(sizes))]
        parts = []
        for step, index in units:
            for which in range(2):
                parts.append(x[step, which, :, begins[index]:begins[index] + sizes[index]])
        return jnp.concatenate(parts, axis=1)

    def weight_part(units, acc):
        return weight_grad(x_for(units), [member for step, index in units for member in held[step][index]], acc)

    every = range(len(sizes))
    half = max(chips // 2, 1)
    groups = [
        [(step, index) for step in range(half) for index in every],
        [(step, index) for step in range(half, chips - 1) for index in every]
        + [(chips - 1, index) for index in range(last)],
        [(chips - 1, last)],
    ]
    weight_grads = None
    for group in groups:
        if group:
            weight_grads = weight_part(group, weight_grads)

    pieces = [[] for _ in sizes]

    def summed(units):
        grads = [member for step, index in units for member in held[step][index]]
        arrived = a2a(input_grad(grads, weights, col_count), "col")
        total = jnp.sum(arrived.astype(jnp.float32), axis=0).astype(jnp.bfloat16)
        at = 0
        for step, index in units:
            size = 2 * sizes[index] // col_count
            pieces[index].append(total[at:at + size].reshape(2, size // 2, rows_in))
            at += size

    for step in range(chips - 1):
        summed([(step, index) for index in every])
    for index in every:
        summed([(chips - 1, index)])

    rows = jnp.arange(row_count)
    slot = ((my_place - jnp.array(place_of, jnp.int32)[rows // 2]) % chips) * 2 + (rows + my_core) % 2
    home = []
    for index, size in enumerate(sizes):
        mine = jnp.take(jnp.concatenate(pieces[index], axis=0), slot, axis=0)
        mine = a2a(mine, "row")
        mine = a2a(mine.reshape(col_count, spread, size // col_count, rows_in), "col")
        home.append(jnp.swapaxes(mine, 1, 2).reshape(size, spread * rows_in))
    layer_grad = jnp.concatenate(home, axis=0)

    bias_all = a2a(jnp.broadcast_to(bias_part[None], (row_count,) + bias_part.shape), "row")
    bias_grad = jnp.sum(bias_all, axis=0)
    return (layer_grad, weight_grads[0], weight_grads[1], weight_grads[2], bias_grad)


def solution(mesh):
    in_specs = (
        P("row", "col"),
        P("row", "col"),
        P("row", None, "col"),
        P("row", None, "col"),
        P("row", None, "col"),
        P("row", None),
        P("col"),
        P("row", "col"),
        P("row", "col"),
        P("row", "col"),
    )
    out_specs = (P("row", "col"), P("row", "col"), P("row", "col"), P("row", "col"), P("col"))
    return jax.shard_map(local, mesh=mesh, in_specs=in_specs, out_specs=out_specs, check_vma=False)
```

time: 540 us -> 468 us (0.87)
  waiting for transfers between devices: 347 us -> 135 us
  Pallas kernels: 0 us -> 118 us
  matrix products: 101 us -> 0 us
  blocking collectives: 14.8 us -> 84.4 us
  starting transfers between devices: 13.4 us -> 58.7 us
  between operations: 13.9 us -> 1.04 us
  other arithmetic: 3.95 us -> 16.3 us
  local copies, waits for them, and re-layouts: 45.7 us -> 52 us
    all_gather x4 -> x0, waiting for transfers between devices: 312 us -> none  [the longest x1 151 us: local(): lax.all_gather(query_grad, 'row', axis=0, tiled=True)]
    pallas_call x0 -> x9, Pallas kernels: none -> 118 us  [the longest x5 54.7 us: input_grad(): pl.pallas_call(functools.partial(input_grad_body, len(grads), pieces), gr...]
    dot_general x11 -> x0, matrix products: 98 us -> none  [the longest x3 42.2 us: local(): lax.dot_general(spread, member, (((0,), (0,)), ((), ())), preferred_eleme...]
    ppermute x0 -> x14, waiting for transfers between devices: none -> 97.6 us  [the longest x6 97.6 us: local(): mine = lax.ppermute(held[step - 1][index][0], 'row', ring)]
    all_to_all x0 -> x2, blocking collectives: none -> 84.4 us  [a2a(): return lax.all_to_all(array, axis, split_axis=0, concat_axis=0, tiled=True)]
    all_to_all x3 -> x11, starting transfers between devices: 13 us -> 45.1 us  [a2a(): return lax.all_to_all(array, axis, split_axis=0, concat_axis=0, tiled=True)]
    all_to_all x3 -> x11, waiting for transfers between devices: 12.7 us -> 37.9 us  [a2a(): return lax.all_to_all(array, axis, split_axis=0, concat_axis=0, tiled=True)]
    reduce_scatter x1 -> x0, waiting for transfers between devices: 22.4 us -> none  [local(): lax.psum_scatter(lax.optimization_barrier(partial_low).astype(jnp.float32...]
  transfers between devices with their start and end apart: 8 -> 25, of which waited for: 6 -> 10; matrix products, arithmetic and copies ran while one was open for 27% -> 13% of each run, Pallas kernels for 0% -> 23%
where the time goes in v1:
time: 468 us; the launch traced here: 466 us
  waiting for transfers between devices  135 us (29%)
  Pallas kernels  118 us (25%)
  blocking collectives  84.4 us (18%)
  starting transfers between devices  58.7 us (13%)
  local copies, waits for them, and re-layouts  52 us (11%)
  other arithmetic  16.3 us (3%)
    ppermute x6, waiting for transfers between devices, local(): mine = lax.ppermute(held[step - 1][index][0], 'row', ring)  97.6 us
    all_to_all x2, blocking collectives, a2a(): return lax.all_to_all(array, axis, split_axis=0, concat_axis=0, tiled=True)  84.4 us
    pallas_call x5, Pallas kernels, input_grad(): pl.pallas_call(functools.partial(input_grad_body, len(grads), pieces), gr...  54.7 us
    pallas_call x3, Pallas kernels, weight_grad(): pl.pallas_call(functools.partial(weight_grad_body, len(grads), bool(acc))...  51.1 us
    all_to_all x11, starting transfers between devices, a2a(): return lax.all_to_all(array, axis, split_axis=0, concat_axis=0, tiled=True)  45.1 us
    all_to_all x11, waiting for transfers between devices, a2a(): return lax.all_to_all(array, axis, split_axis=0, concat_axis=0, tiled=True)  37.9 us
    unnamed x56, local copies, waits for them, and re-layouts  33.6 us
    ppermute x6, starting transfers between devices, local(): mine = lax.ppermute(held[step - 1][index][0], 'row', ring)  12.6 us
  transfers between devices with their start and end apart: 25, of which 10 were waited for; matrix products, arithmetic and copies ran while one was open for 13% of the time, Pallas kernels for 23%

profile of v1, /device:TPU:0, one launch (start us, length us, event | category | flops | bytes accessed | tf_op | source)
XLA Modules:
  0.0 465.8 jit_solution(11004791938143533476)
XLA Ops:
  0.6 12.1 %attention_back.1 = (bf16[3,128,2048]{2,1,0:T(8,128)(2,1)}, bf16[3,128,2048]{2,1,0:T(8,128)(2,1)}, f32[16,1,128]{2,1,0:T(1,128)}) custom-call(f32[16]{0:T(128)} %bias_ref.1, s32[1,256]{1,0:T(1,128)} %flag_ref.1, bf16[256,2048]{1,0:T(8,128)(2,1)} %bitcast.83, bf16[256,2048]{1,0:T(8,128)(2,1)} %bitcast.84, bf16[256,2048]{1,0:T(8,128)(2,1)} %bitcast.85, ...), custom_call_target="tpu_custom_call" | custom-call | flops 1342177280 | bytes 7340032 | tf_op jit(solution)/shard_map/attention_back/pallas_call | solution.py:55
  12.8 3.0 collective-permute-start.2
  15.8 2.6 collective-permute-start.4
  18.9 0.9 slice_reduce_fusion
  19.8 66.5 %all_to_all.66 = f32[8,1,16]{2,1,0:T(1,128)S(1)} all-to-all(f32[8,1,16]{2,1,0:T(1,128)S(1)} %broadcast_in_dim.40), channel_id=1, replica_groups=mesh['row'=8,'col'=4] {'row'}, dimensions={0} | all-to-all | bytes 1024 | tf_op jit(solution)/shard_map/all_to_all | solution.py:173
  86.3 3.7 all-to-all-start.9
  90.6 2.6 collective-permute-start.8
  93.2 1.2 copy-done.12
  94.4 12.2 %input_grad.5 = bf16[4,128,1024]{2,1,0:T(8,128)(2,1)} custom-call(bf16[3,128,2048]{2,1,0:T(8,128)(2,1)} %get-tuple-element.18.refs_0_, bf16[3,128,2048]{2,1,0:T(8,128)(2,1)} %copy-done.12, bf16[3,128,2048]{2,1,0:T(8,128)(2,1)} %get-tuple-element.19.refs_2_, bf16[3,128,2048]{2,1,0:T(8,128)(2,1)} %collective-permute-done.1.refs_3_, ...), custom_call_target="tpu_custom_call" | custom-call | flops 6442450944 | bytes 18874368 | tf_op jit(solution)/shard_map/input_grad/pallas_call | solution.py:98
  106.6 4.2 all-to-all-start
  111.4 1.0 pad_maximum_fusion.1
  112.5 11.2 %all-to-all-done = bf16[4,128,1024]{2,1,0:T(8,128)(2,1)S(1)} async-done(((bf16[4,128,1024]{2,1,0:T(8,128)(2,1)}), bf16[4,128,1024]{2,1,0:T(8,128)(2,1)S(1)}, u32[]{:S(2)}, u32[]{:S(2)}) %all-to-all-start) | async-done | bytes 1048608 | tf_op jit(solution)/shard_map/all_to_all | solution.py:173
  123.7 3.6 all-to-all-start.10
  127.2 1.3 collective-permute-done.6.refs_0_
  128.5 35.2 %collective-permute-done.8.refs_2_ = bf16[3,128,2048]{2,1,0:T(8,128)(2,1)} collective-permute-done((bf16[3,128,2048]{2,1,0:T(8,128)(2,1)}, bf16[3,128,2048]{2,1,0:T(8,128)(2,1)}, u32[]{:S(2)}, u32[]{:S(2)}) %collective-permute-start.8) | collective-permute-done | bytes 1572896 | tf_op jit(solution)/shard_map/ppermute | solution.py:180
  163.8 12.3 %input_grad.6 = bf16[4,128,1024]{2,1,0:T(8,128)(2,1)} custom-call(bf16[3,128,2048]{2,1,0:T(8,128)(2,1)} %collective-permute-done.2.refs_0_.refs_4_, bf16[3,128,2048]{2,1,0:T(8,128)(2,1)} %collective-permute-done.3.refs_1_.refs_5_, bf16[3,128,2048]{2,1,0:T(8,128)(2,1)} %collective-permute-done.4.refs_2_.refs_6_, ...), custom_call_target="tpu_custom_call" | custom-call | flops 6442450944 | bytes 18874368 | tf_op jit(solution)/shard_map/input_grad/pallas_call | solution.py:98
  176.0 7.3 %all-to-all-done.10 = bf16[8,64,1024]{2,1,0:T(8,128)(2,1)S(1)} async-done(((bf16[8,64,1024]{2,1,0:T(8,128)(2,1)}), bf16[8,64,1024]{2,1,0:T(8,128)(2,1)S(1)}, u32[]{:S(2)}, u32[]{:S(2)}) %all-to-all-start.10) | async-done | bytes 1048608 | tf_op jit(solution)/shard_map/all_to_all | solution.py:173
  183.3 4.3 all-to-all-start.1
  187.6 12.3 %input_grad.7 = bf16[4,128,1024]{2,1,0:T(8,128)(2,1)} custom-call(bf16[3,128,2048]{2,1,0:T(8,128)(2,1)} %collective-permute-done.6.refs_0_, bf16[3,128,2048]{2,1,0:T(8,128)(2,1)} %collective-permute-done.7.refs_1_, bf16[3,128,2048]{2,1,0:T(8,128)(2,1)} %collective-permute-done.8.refs_2_, bf16[3,128,2048]{2,1,0:T(8,128)(2,1)} %collective-permute-done.9.refs_3_, ...), custom_call_target="tpu_custom_call" | custom-call | flops 6442450944 | bytes 18874368 | tf_op jit(solution)/shard_map/input_grad/pallas_call | solution.py:98
  200.5 17.9 %all_to_all.67 = bf16[4,128,1024]{2,1,0:T(8,128)(2,1)} all-to-all(bf16[4,128,1024]{2,1,0:T(8,128)(2,1)} %input_grad.7), channel_id=1, replica_groups=mesh['row'=8,'col'=4] {'col'}, dimensions={0} | all-to-all | bytes 2097152 | tf_op jit(solution)/shard_map/all_to_all | solution.py:173
  218.4 2.6 broadcast_in_dim.37
  221.0 5.0 %all-to-all-start.11 = ((bf16[4,8,64,1024]{3,2,1,0:T(8,128)(2,1)}), bf16[4,8,64,1024]{3,2,1,0:T(8,128)(2,1)}, u32[]{:S(2)}, u32[]{:S(2)}) async-start(bf16[4,8,64,1024]{3,2,1,0:T(8,128)(2,1)} %broadcast_in_dim.37), calls=%async_computation.11 | async-start | bytes 8388608 | tf_op jit(solution)/shard_map/all_to_all | solution.py:173
  229.8 3.3 collective-permute-start.12
  234.7 1.4 reduce_sum.70
  236.9 30.9 %collective-permute-done.10.refs_0_.refs_4_ = bf16[3,128,2048]{2,1,0:T(8,128)(2,1)} collective-permute-done((bf16[3,128,2048]{2,1,0:T(8,128)(2,1)}, bf16[3,128,2048]{2,1,0:T(8,128)(2,1)}, u32[]{:S(2)}, u32[]{:S(2)}) %collective-permute-start.10) | collective-permute-done | bytes 1572896 | tf_op jit(solution)/shard_map/ppermute | solution.py:180
  267.8 30.1 %collective-permute-done.12.refs_0_ = bf16[3,128,2048]{2,1,0:T(8,128)(2,1)S(1)} collective-permute-done((bf16[3,128,2048]{2,1,0:T(8,128)(2,1)}, bf16[3,128,2048]{2,1,0:T(8,128)(2,1)S(1)}, u32[]{:S(2)}, u32[]{:S(2)}) %collective-permute-start.12) | collective-permute-done | bytes 1572896 | tf_op jit(solution)/shard_map/ppermute | solution.py:180
  297.9 2.0 reduce_sum.71
  300.7 5.0 %gather_fusion.2 = bf16[8,4,64,1024]{3,2,1,0:T(8,128)(2,1)} fusion(bf16[4,8,64,1024]{3,2,1,0:T(8,128)(2,1)} %all-to-all-done.11, s32[1024]{0:T(1024)S(1)} %pad_clamp_fusion), kind=kCustom, calls=%fused_computation.4 | custom fusion | bytes 8388640 | tf_op jit(solution)/shard_map/jit(_take)/gather | solution.py:188
  305.7 2.7 broadcast_select_fusion
  308.3 1.9 fusion.9
  310.3 1.8 copy.91
  312.1 1.7 bitcast_dynamic-update-slice_fusion.13
  313.8 1.8 copy.92
  315.6 1.8 copy.93
  317.4 1.8 copy.94
  319.2 1.8 copy.97
  321.0 1.8 copy.98
  322.8 1.7 bitcast_dynamic-update-slice_fusion.7
  324.5 1.7 bitcast_dynamic-update-slice_fusion.12
  326.2 1.8 bitcast_dynamic-update-slice_fusion.11
  328.0 1.7 bitcast_dynamic-update-slice_fusion.10
  329.8 9.0 %input_grad.8 = bf16[4,64,1024]{2,1,0:T(8,128)(2,1)} custom-call(bf16[3,128,2048]{2,1,0:T(8,128)(2,1)} %collective-permute-done.10.refs_0_.refs_4_, bf16[3,128,2048]{2,1,0:T(8,128)(2,1)} %collective-permute-done.11.refs_1_.refs_5_, bf16[1024,2048]{1,0:T(8,128)(2,1)} %refs_2_.3, bf16[1024,2048]{1,0:T(8,128)(2,1)} %refs_3_.3, bf16[1024,2048]{1,0:T(8,128)(2,1)} %refs_4_.9), custom_call_target="tpu_custom_call" | custom-call | flops 3221225472 | bytes 15728640 | tf_op jit(solution)/shard_map/input_grad/pallas_call | solution.py:98
  338.8 4.3 all-to-all-start.3
  343.1 1.7 bitcast_dynamic-update-slice_fusion.6
  344.8 1.8 copy.99
  346.6 1.1 copy-done.2
  347.8 9.0 %input_grad.9 = bf16[4,64,1024]{2,1,0:T(8,128)(2,1)} custom-call(bf16[3,128,2048]{2,1,0:T(8,128)(2,1)} %copy-done.1, bf16[3,128,2048]{2,1,0:T(8,128)(2,1)} %copy-done.2, bf16[1024,2048]{1,0:T(8,128)(2,1)} %refs_2_.3, bf16[1024,2048]{1,0:T(8,128)(2,1)} %refs_3_.3, bf16[1024,2048]{1,0:T(8,128)(2,1)} %refs_4_.9), custom_call_target="tpu_custom_call" | custom-call | flops 3221225472 | bytes 15728640 | tf_op jit(solution)/shard_map/input_grad/pallas_call | solution.py:98
  356.8 4.1 all-to-all-start.6
  360.9 1.7 bitcast_dynamic-update-slice_fusion.5
  362.6 1.1 copy.95
  365.4 1.2 reduce_sum.72
  366.6 1.1 pad_maximum_fusion.2
  369.6 1.0 pad_maximum_fusion.3
  371.2 1.1 broadcast_select_fusion.2
  372.3 4.5 all-to-all-start.7
  379.9 12.4 %all-to-all-done.7 = bf16[8,32,1024]{2,1,0:T(8,128)(2,1)} async-done(((bf16[8,32,1024]{2,1,0:T(8,128)(2,1)}), bf16[8,32,1024]{2,1,0:T(8,128)(2,1)}, u32[]{:S(2)}, u32[]{:S(2)}) %all-to-all-start.7) | async-done | bytes 524320 | tf_op jit(solution)/shard_map/all_to_all | solution.py:173
  392.3 4.2 all-to-all-start.4
  396.5 18.7 %weight_grad.3 = (bf16[1024,2048]{1,0:T(8,128)(2,1)}, bf16[1024,2048]{1,0:T(8,128)(2,1)}, bf16[1024,2048]{1,0:T(8,128)(2,1)}) custom-call(bf16[1024,1024]{1,0:T(8,128)(2,1)} %bitcast_dynamic-update-slice_fusion.x_ref, bf16[3,128,2048]{2,1,0:T(8,128)(2,1)} %get-tuple-element.18.refs_0_, bf16[3,128,2048]{2,1,0:T(8,128)(2,1)} %copy-done.12, ...), custom_call_target="tpu_custom_call" | custom-call | flops 12884901888 | bytes 25165824 | tf_op jit(solution)/shard_map/weight_grad/pallas_call | solution.py:129
  415.2 3.8 all-to-all-start.8
  421.9 5.7 %all-to-all-done.8 = bf16[4,2,32,1024]{3,2,1,0:T(8,128)(2,1)S(1)} async-done(((bf16[4,2,32,1024]{3,2,1,0:T(8,128)(2,1)}), bf16[4,2,32,1024]{3,2,1,0:T(8,128)(2,1)S(1)}, u32[]{:S(2)}, u32[]{:S(2)}) %all-to-all-start.8) | async-done | bytes 524320 | tf_op jit(solution)/shard_map/all_to_all | solution.py:173
  427.6 3.5 all-to-all-start.5
  431.1 19.0 %weight_grad.4 = (bf16[1024,2048]{1,0:T(8,128)(2,1)}, bf16[1024,2048]{1,0:T(8,128)(2,1)}, bf16[1024,2048]{1,0:T(8,128)(2,1)}) custom-call(bf16[1024,768]{1,0:T(8,128)(2,1)} %bitcast_dynamic-update-slice_fusion.8.x_ref, bf16[3,128,2048]{2,1,0:T(8,128)(2,1)} %collective-permute-done.6.refs_0_, bf16[3,128,2048]{2,1,0:T(8,128)(2,1)} %collective-permute-done.7.refs_1_, ...), custom_call_target="tpu_custom_call" | custom-call | flops 9663676416 | bytes 34603008 | tf_op jit(solution)/shard_map/weight_grad/pallas_call | solution.py:129
  450.0 13.4 %weight_grad.5 = (bf16[1024,2048]{1,0:T(8,128)(2,1)}, bf16[1024,2048]{1,0:T(8,128)(2,1)}, bf16[1024,2048]{1,0:T(8,128)(2,1)}) custom-call(bf16[1024,256]{1,0:T(8,128)(2,1)} %pad_maximum_fusion.4.x_ref, bf16[3,128,2048]{2,1,0:T(8,128)(2,1)} %copy-done.1, bf16[3,128,2048]{2,1,0:T(8,128)(2,1)} %copy-done.2, bf16[1024,2048]{1,0:T(8,128)(2,1)} %get-tuple-element.23.refs_2_, ...), custom_call_target="tpu_custom_call" | custom-call | flops 3221225472 | bytes 28311552 | tf_op jit(solution)/shard_map/weight_grad/pallas_call | solution.py:129
  464.8 1.1 pad_maximum_fusion
  (97 shorter events, 20.6 us)
Async XLA Ops:
  12.8 77.3 %collective-permute-start.2 = (bf16[3,128,2048]{2,1,0:T(8,128)(2,1)}, bf16[3,128,2048]{2,1,0:T(8,128)(2,1)}, u32[]{:S(2)}, u32[]{:S(2)}) collective-permute-start(bf16[3,128,2048]{2,1,0:T(8,128)(2,1)} %get-tuple-element.18.refs_0_), channel_id=1, source_target_pairs={{0,8},{4,12},{8,24},{12,28},{24,16},{28,20},{16,0},{20,4},{1,9},{5... | collective-permute-start | bytes 4718600 | tf_op jit(solution)/shard_map/ppermute | solution.py:180
  15.8 74.8 %collective-permute-start.4 = (bf16[3,128,2048]{2,1,0:T(8,128)(2,1)}, bf16[3,128,2048]{2,1,0:T(8,128)(2,1)}, u32[]{:S(2)}, u32[]{:S(2)}) collective-permute-start(bf16[3,128,2048]{2,1,0:T(8,128)(2,1)} %get-tuple-element.19.refs_2_), channel_id=1, source_target_pairs={{0,8},{4,12},{8,24},{12,28},{24,16},{28,20},{16,0},{20,4},{1,9},{5... | collective-permute-start | bytes 4718600 | tf_op jit(solution)/shard_map/ppermute | solution.py:180
  18.4 74.9 %collective-permute-start = (bf16[3,128,2048]{2,1,0:T(8,128)(2,1)}, bf16[3,128,2048]{2,1,0:T(8,128)(2,1)S(1)}, u32[]{:S(2)}, u32[]{:S(2)}) collective-permute-start(bf16[3,128,2048]{2,1,0:T(8,128)(2,1)} %get-tuple-element.18.refs_0_), channel_id=1, source_target_pairs={{0,4},{4,0},{8,12},{12,8},{16,20},{20,16},{24,28},{28,24},{1,5},{5... | collective-permute-start | bytes 4718600 | tf_op jit(solution)/shard_map/ppermute | solution.py:176
  18.4 74.9 %collective-permute-start.1 = (bf16[3,128,2048]{2,1,0:T(8,128)(2,1)}, bf16[3,128,2048]{2,1,0:T(8,128)(2,1)}, u32[]{:S(2)}, u32[]{:S(2)}) collective-permute-start(bf16[3,128,2048]{2,1,0:T(8,128)(2,1)} %get-tuple-element.19.refs_2_), channel_id=1, source_target_pairs={{0,4},{4,0},{8,12},{12,8},{16,20},{20,16},{24,28},{28,24},{1,5},{5... | collective-permute-start | bytes 4718600 | tf_op jit(solution)/shard_map/ppermute | solution.py:176
  86.3 20.3 %all-to-all-start.9 = ((bf16[4,64,2048]{2,1,0:T(8,128)(2,1)}), bf16[4,64,2048]{2,1,0:T(8,128)(2,1)S(1)}, u32[]{:S(2)}, u32[]{:S(2)}) async-start(bf16[4,64,2048]{2,1,0:T(8,128)(2,1)} %bitcast.18), calls=%async_computation.9 | async-start | bytes 2097152 | tf_op jit(solution)/shard_map/all_to_all | solution.py:173
  90.0 38.5 %collective-permute-start.6 = (bf16[3,128,2048]{2,1,0:T(8,128)(2,1)}, bf16[3,128,2048]{2,1,0:T(8,128)(2,1)}, u32[]{:S(2)}, u32[]{:S(2)}) collective-permute-start(bf16[3,128,2048]{2,1,0:T(8,128)(2,1)} %collective-permute-done.2.refs_0_.refs_4_), channel_id=1, source_target_pairs={{0,8},{4,12},{8,24},{12,28},{24,16},{28,20},{16,0},{20,4},{1,9},{5... | collective-permute-start | bytes 4718600 | tf_op jit(solution)/shard_map/ppermute | solution.py:180
  90.6 73.1 %collective-permute-start.8 = (bf16[3,128,2048]{2,1,0:T(8,128)(2,1)}, bf16[3,128,2048]{2,1,0:T(8,128)(2,1)}, u32[]{:S(2)}, u32[]{:S(2)}) collective-permute-start(bf16[3,128,2048]{2,1,0:T(8,128)(2,1)} %collective-permute-done.4.refs_2_.refs_6_), channel_id=1, source_target_pairs={{0,8},{4,12},{8,24},{12,28},{24,16},{28,20},{16,0},{20,4},{1,9},{5... | collective-permute-start | bytes 4718600 | tf_op jit(solution)/shard_map/ppermute | solution.py:180
  93.2 1.2 copy-start.12
  106.6 17.0 %all-to-all-start = ((bf16[4,128,1024]{2,1,0:T(8,128)(2,1)}), bf16[4,128,1024]{2,1,0:T(8,128)(2,1)S(1)}, u32[]{:S(2)}, u32[]{:S(2)}) async-start(bf16[4,128,1024]{2,1,0:T(8,128)(2,1)} %input_grad.5), calls=%async_computation | async-start | bytes 2097152 | tf_op jit(solution)/shard_map/all_to_all | solution.py:173
  110.8 52.9 %collective-permute-start.3 = (bf16[3,128,2048]{2,1,0:T(8,128)(2,1)}, bf16[3,128,2048]{2,1,0:T(8,128)(2,1)}, u32[]{:S(2)}, u32[]{:S(2)}) collective-permute-start(bf16[3,128,2048]{2,1,0:T(8,128)(2,1)} %collective-permute-done.2.refs_0_.refs_4_), channel_id=1, source_target_pairs={{0,4},{4,0},{8,12},{12,8},{16,20},{20,16},{24,28},{28,24},{1,5},{5... | collective-permute-start | bytes 4718600 | tf_op jit(solution)/shard_map/ppermute | solution.py:181
  110.8 52.9 %collective-permute-start.5 = (bf16[3,128,2048]{2,1,0:T(8,128)(2,1)}, bf16[3,128,2048]{2,1,0:T(8,128)(2,1)}, u32[]{:S(2)}, u32[]{:S(2)}) collective-permute-start(bf16[3,128,2048]{2,1,0:T(8,128)(2,1)} %collective-permute-done.4.refs_2_.refs_6_), channel_id=1, source_target_pairs={{0,4},{4,0},{8,12},{12,8},{16,20},{20,16},{24,28},{28,24},{1,5},{5... | collective-permute-start | bytes 4718600 | tf_op jit(solution)/shard_map/ppermute | solution.py:181
  123.7 59.7 %all-to-all-start.10 = ((bf16[8,64,1024]{2,1,0:T(8,128)(2,1)}), bf16[8,64,1024]{2,1,0:T(8,128)(2,1)S(1)}, u32[]{:S(2)}, u32[]{:S(2)}) async-start(bf16[8,64,1024]{2,1,0:T(8,128)(2,1)} %bitcast.65), calls=%async_computation.10 | async-start | bytes 2097152 | tf_op jit(solution)/shard_map/all_to_all | solution.py:173
  128.5 59.1 %collective-permute-start.7 = (bf16[3,128,2048]{2,1,0:T(8,128)(2,1)}, bf16[3,128,2048]{2,1,0:T(8,128)(2,1)}, u32[]{:S(2)}, u32[]{:S(2)}) collective-permute-start(bf16[3,128,2048]{2,1,0:T(8,128)(2,1)} %collective-permute-done.6.refs_0_), channel_id=1, source_target_pairs={{0,4},{4,0},{8,12},{12,8},{16,20},{20,16},{24,28},{28,24},{1,5},{5... | collective-permute-start | bytes 4718600 | tf_op jit(solution)/shard_map/ppermute | solution.py:181
  163.7 23.9 %collective-permute-start.9 = (bf16[3,128,2048]{2,1,0:T(8,128)(2,1)}, bf16[3,128,2048]{2,1,0:T(8,128)(2,1)}, u32[]{:S(2)}, u32[]{:S(2)}) collective-permute-start(bf16[3,128,2048]{2,1,0:T(8,128)(2,1)} %collective-permute-done.8.refs_2_), channel_id=1, source_target_pairs={{0,4},{4,0},{8,12},{12,8},{16,20},{20,16},{24,28},{28,24},{1,5},{5... | collective-permute-start | bytes 4718600 | tf_op jit(solution)/shard_map/ppermute | solution.py:181
  183.3 17.2 %all-to-all-start.1 = ((bf16[4,128,1024]{2,1,0:T(8,128)(2,1)}), bf16[4,128,1024]{2,1,0:T(8,128)(2,1)}, u32[]{:S(2)}, u32[]{:S(2)}) async-start(bf16[4,128,1024]{2,1,0:T(8,128)(2,1)} %input_grad.6), calls=%async_computation.1 | async-start | bytes 2097152 | tf_op jit(solution)/shard_map/all_to_all | solution.py:173
  221.0 5.0 %copy-start = (s32[4]{0:T(128)S(1)}, s32[4]{0:T(128)}, u32[]{:S(2)}) copy-start(s32[4]{0:T(128)} %constant.118.clone) | copy-start | bytes 52
  221.0 79.7 %all-to-all-start.11 = ((bf16[4,8,64,1024]{3,2,1,0:T(8,128)(2,1)}), bf16[4,8,64,1024]{3,2,1,0:T(8,128)(2,1)}, u32[]{:S(2)}, u32[]{:S(2)}) async-start(bf16[4,8,64,1024]{3,2,1,0:T(8,128)(2,1)} %broadcast_in_dim.37), calls=%async_computation.11 | async-start | bytes 8388608 | tf_op jit(solution)/shard_map/all_to_all | solution.py:173
  229.2 38.5 %collective-permute-start.10 = (bf16[3,128,2048]{2,1,0:T(8,128)(2,1)}, bf16[3,128,2048]{2,1,0:T(8,128)(2,1)}, u32[]{:S(2)}, u32[]{:S(2)}) collective-permute-start(bf16[3,128,2048]{2,1,0:T(8,128)(2,1)} %collective-permute-done.6.refs_0_), channel_id=1, source_target_pairs={{0,8},{4,12},{8,24},{12,28},{24,16},{28,20},{16,0},{20,4},{1,9},{5... | collective-permute-start | bytes 4718600 | tf_op jit(solution)/shard_map/ppermute | solution.py:180
  229.8 68.2 %collective-permute-start.12 = (bf16[3,128,2048]{2,1,0:T(8,128)(2,1)}, bf16[3,128,2048]{2,1,0:T(8,128)(2,1)S(1)}, u32[]{:S(2)}, u32[]{:S(2)}) collective-permute-start(bf16[3,128,2048]{2,1,0:T(8,128)(2,1)} %collective-permute-done.8.refs_2_), channel_id=1, source_target_pairs={{0,8},{4,12},{8,24},{12,28},{24,16},{28,20},{16,0},{20,4},{1,9},{5... | collective-permute-start | bytes 4718600 | tf_op jit(solution)/shard_map/ppermute | solution.py:180
  267.8 62.0 %collective-permute-start.11 = (bf16[3,128,2048]{2,1,0:T(8,128)(2,1)}, bf16[3,128,2048]{2,1,0:T(8,128)(2,1)}, u32[]{:S(2)}, u32[]{:S(2)}) collective-permute-start(bf16[3,128,2048]{2,1,0:T(8,128)(2,1)} %collective-permute-done.10.refs_0_.refs_4_), channel_id=1, source_target_pairs={{0,4},{4,0},{8,12},{12,8},{16,20},{20,16},{24,28},{28,24},{1,5},{5... | collective-permute-start | bytes 4718600 | tf_op jit(solution)/shard_map/ppermute | solution.py:181
  297.9 7.8 %copy-start.1 = (bf16[3,128,2048]{2,1,0:T(8,128)(2,1)}, bf16[3,128,2048]{2,1,0:T(8,128)(2,1)S(1)}, u32[]{:S(2)}) copy-start(bf16[3,128,2048]{2,1,0:T(8,128)(2,1)S(1)} %collective-permute-done.12.refs_0_) | copy-start | bytes 4718596
  297.9 48.7 %collective-permute-start.13 = (bf16[3,128,2048]{2,1,0:T(8,128)(2,1)S(1)}, bf16[3,128,2048]{2,1,0:T(8,128)(2,1)S(1)}, u32[]{:S(2)}, u32[]{:S(2)}) collective-permute-start(bf16[3,128,2048]{2,1,0:T(8,128)(2,1)S(1)} %collective-permute-done.12.refs_0_), channel_id=1, source_target_pairs={{0,4},{4,0},{8,12},{12,8},{16,20},{20,16},{24,28},{28,24},{1,5},{5... | collective-permute-start | bytes 4718600 | tf_op jit(solution)/shard_map/ppermute | solution.py:181
  338.8 18.0 %all-to-all-start.3 = ((bf16[4,64,1024]{2,1,0:T(8,128)(2,1)}), bf16[4,64,1024]{2,1,0:T(8,128)(2,1)}, u32[]{:S(2)}, u32[]{:S(2)}) async-start(bf16[4,64,1024]{2,1,0:T(8,128)(2,1)} %input_grad.8), calls=%async_computation.3 | async-start | bytes 1048576 | tf_op jit(solution)/shard_map/all_to_all | solution.py:173
  346.6 1.1 copy-start.2
  356.8 7.0 %copy-start.9 = (bf16[1,1,1024,128]{2,3,1,0:T(8,128)(2,1)S(1)}, bf16[1,1,1024,128]{2,3,1,0:T(8,128)(2,1)}, u32[]{:S(2)}) copy-start(bf16[1,1,1024,128]{2,3,1,0:T(8,128)(2,1)} %get-tuple-element.36) | copy-start | bytes 786436
  356.8 7.2 %copy-start.8 = (bf16[1,1,1024,128]{2,3,1,0:T(8,128)(2,1)S(1)}, bf16[1,1,1024,128]{2,3,1,0:T(8,128)(2,1)}, u32[]{:S(2)}) copy-start(bf16[1,1,1024,128]{2,3,1,0:T(8,128)(2,1)} %get-tuple-element.35) | copy-start | bytes 786436
  356.8 7.4 %copy-start.7 = (bf16[1,1,1024,128]{2,3,1,0:T(8,128)(2,1)S(1)}, bf16[1,1,1024,128]{2,3,1,0:T(8,128)(2,1)}, u32[]{:S(2)}) copy-start(bf16[1,1,1024,128]{2,3,1,0:T(8,128)(2,1)} %get-tuple-element.34) | copy-start | bytes 786436
  356.8 7.5 %copy-start.6 = (bf16[1,1,1024,128]{2,3,1,0:T(8,128)(2,1)S(1)}, bf16[1,1,1024,128]{2,3,1,0:T(8,128)(2,1)}, u32[]{:S(2)}) copy-start(bf16[1,1,1024,128]{2,3,1,0:T(8,128)(2,1)} %get-tuple-element.33) | copy-start | bytes 786436
  356.8 7.7 %copy-start.5 = (bf16[1,1,1024,128]{2,3,1,0:T(8,128)(2,1)S(1)}, bf16[1,1,1024,128]{2,3,1,0:T(8,128)(2,1)}, u32[]{:S(2)}) copy-start(bf16[1,1,1024,128]{2,3,1,0:T(8,128)(2,1)} %get-tuple-element.32) | copy-start | bytes 786436
  356.8 12.1 %all-to-all-start.6 = ((bf16[4,64,1024]{2,1,0:T(8,128)(2,1)}), bf16[4,64,1024]{2,1,0:T(8,128)(2,1)S(1)}, u32[]{:S(2)}, u32[]{:S(2)}) async-start(bf16[4,64,1024]{2,1,0:T(8,128)(2,1)} %input_grad.9), calls=%async_computation.6 | async-start | bytes 1048576 | tf_op jit(solution)/shard_map/all_to_all | solution.py:173
  365.4 4.2 copy-start.10
  365.4 4.2 copy-start.11
  372.3 20.0 %all-to-all-start.7 = ((bf16[8,32,1024]{2,1,0:T(8,128)(2,1)}), bf16[8,32,1024]{2,1,0:T(8,128)(2,1)}, u32[]{:S(2)}, u32[]{:S(2)}) async-start(bf16[8,32,1024]{2,1,0:T(8,128)(2,1)} %get-tuple-element.57), calls=%async_computation.7 | async-start | bytes 1048576 | tf_op jit(solution)/shard_map/all_to_all | solution.py:173
  392.3 22.9 %all-to-all-start.4 = ((bf16[8,32,1024]{2,1,0:T(8,128)(2,1)}), bf16[8,32,1024]{2,1,0:T(8,128)(2,1)}, u32[]{:S(2)}, u32[]{:S(2)}) async-start(bf16[8,32,1024]{2,1,0:T(8,128)(2,1)} %get-tuple-element.56), calls=%async_computation.4 | async-start | bytes 1048576 | tf_op jit(solution)/shard_map/all_to_all | solution.py:173
  396.5 23.3 %copy-start.4 = (bf16[1,1,1024,128]{2,3,1,0:T(8,128)(2,1)S(1)}, bf16[1,1,1024,128]{2,3,1,0:T(8,128)(2,1)}, u32[]{:S(2)}) copy-start(bf16[1,1,1024,128]{2,3,1,0:T(8,128)(2,1)} %get-tuple-element.46) | copy-start | bytes 786436
  415.2 4.7 %copy-start.3 = (bf16[1,1,1024,128]{2,3,1,0:T(8,128)(2,1)S(1)}, bf16[1,1,1024,128]{2,3,1,0:T(8,128)(2,1)}, u32[]{:S(2)}) copy-start(bf16[1,1,1024,128]{2,3,1,0:T(8,128)(2,1)} %get-tuple-element.47) | copy-start | bytes 786436
  415.2 12.4 %all-to-all-start.8 = ((bf16[4,2,32,1024]{3,2,1,0:T(8,128)(2,1)}), bf16[4,2,32,1024]{3,2,1,0:T(8,128)(2,1)S(1)}, u32[]{:S(2)}, u32[]{:S(2)}) async-start(bf16[4,2,32,1024]{3,2,1,0:T(8,128)(2,1)} %bitcast.15), calls=%async_computation.8 | async-start | bytes 1048576 | tf_op jit(solution)/shard_map/all_to_all | solution.py:173
  427.6 36.5 %all-to-all-start.5 = ((bf16[4,2,32,1024]{3,2,1,0:T(8,128)(2,1)}), bf16[4,2,32,1024]{3,2,1,0:T(8,128)(2,1)S(1)}, u32[]{:S(2)}, u32[]{:S(2)}) async-start(bf16[4,2,32,1024]{3,2,1,0:T(8,128)(2,1)} %bitcast.9), calls=%async_computation.5 | async-start | bytes 1048576 | tf_op jit(solution)/shard_map/all_to_all | solution.py:173

commit v2 on v1

v2 whole, which is shorter than its diff:
```python
import functools
import math

import jax
import jax.numpy as jnp
from jax import lax
from jax.experimental import pallas as pl
from jax.experimental.pallas import tpu as pltpu
from jax.sharding import PartitionSpec as P

NT = (((1,), (1,)), ((), ()))
TN = (((0,), (0,)), ((), ()))
VMEM_LIMIT = 56 * 1024 * 1024
SHADE = 20


def chunk_sizes(length):
    return (length // 2, length - length // 2)


def attention_body(sizes, head_dim, heads_step, bias_ref, flag_ref, q_ref, k_ref, v_ref, g_ref, *outs):
    chunk_refs, bias_out = outs[:-1], outs[-1]
    scale_qk = 1.0 / math.sqrt(head_dim)
    flag = flag_ref[...].astype(jnp.float32)
    for sub in range(heads_step):
        cols = slice(sub * head_dim, (sub + 1) * head_dim)
        q, k, v, g = q_ref[:, cols], k_ref[:, cols], v_ref[:, cols], g_ref[:, cols]
        head = pl.program_id(0) * heads_step + sub
        scores = lax.dot_general(q, k, NT, preferred_element_type=jnp.float32) * scale_qk + bias_ref[head] * flag
        exp_terms = jnp.exp(scores - jnp.max(scores, axis=-1, keepdims=True))
        probs = exp_terms * (1.0 / jnp.sum(exp_terms, axis=-1, keepdims=True))
        probs_low = probs.astype(jnp.bfloat16)
        grad_probs = lax.dot_general(g, v, NT, preferred_element_type=jnp.float32)
        delta = jnp.sum(probs_low.astype(jnp.float32) * grad_probs, axis=-1, keepdims=True)
        grad_scores = probs * (grad_probs - delta)
        grad_low = grad_scores.astype(jnp.bfloat16)
        value_grad = lax.dot_general(probs_low, g, TN, preferred_element_type=jnp.float32)
        query_grad = jnp.dot(grad_low, k, preferred_element_type=jnp.float32) * scale_qk
        key_grad = lax.dot_general(grad_low, q, TN, preferred_element_type=jnp.float32) * scale_qk
        bias = jnp.sum(jnp.sum(grad_scores, axis=0, keepdims=True) * flag, axis=1, keepdims=True)
        bias_out[sub] = jnp.broadcast_to(bias, (1, 128))
        for place, member in enumerate((query_grad, key_grad, value_grad)):
            low = member.astype(jnp.bfloat16)
            begin = 0
            for size, ref in zip(sizes, chunk_refs):
                ref[place, :, cols] = low[begin:begin + size]
                begin += size


def attention(queries, keys, values, grads, flags, key_bias, sizes):
    length, width = queries.shape
    heads = key_bias.shape[0]
    head_dim = width // heads
    heads_step = 2 if heads % 2 == 0 else 1
    block = pl.BlockSpec((length, heads_step * head_dim), lambda h: (0, h))
    outs = pl.pallas_call(
        functools.partial(attention_body, sizes, head_dim, heads_step),
        grid=(heads // heads_step,),
        in_specs=[
            pl.BlockSpec(memory_space=pltpu.SMEM),
            pl.BlockSpec((1, length), lambda h: (0, 0)),
            block, block, block, block,
        ],
        out_specs=[pl.BlockSpec((3, size, heads_step * head_dim), lambda h: (0, 0, h)) for size in sizes]
        + [pl.BlockSpec((heads_step, 1, 128), lambda h: (h, 0, 0))],
        out_shape=[jax.ShapeDtypeStruct((3, size, width), jnp.bfloat16) for size in sizes]
        + [jax.ShapeDtypeStruct((heads, 1, 128), jnp.float32)],
        compiler_params=pltpu.CompilerParams(vmem_limit_bytes=VMEM_LIMIT),
        cost_estimate=pl.CostEstimate(
            flops=10 * length * length * width // SHADE,
            bytes_accessed=14 * length * width // SHADE,
            transcendentals=heads * length * length // SHADE,
        ),
        name="attention_back",
    )(key_bias, flags, queries, keys, values, grads)
    return outs[:-1], outs[-1][:, 0, 0]


def input_grad_body(count, place_ref, *refs):
    grad_refs, weight_refs, out_refs, low_ref = refs[:count], refs[count:count + 3], refs[count + 3:-1], refs[-1]
    me = place_ref[place_ref.shape[0] - 1]
    total = None
    for member in range(3):
        rows = jnp.concatenate([ref[member] for ref in grad_refs], axis=0)
        term = lax.dot_general(rows, weight_refs[member][...], NT, preferred_element_type=jnp.float32)
        total = term if total is None else total + term
    low_ref[...] = total.astype(jnp.bfloat16)
    begin = 0
    at = 0
    for ref in grad_refs:
        size = ref.shape[1] // len(out_refs)
        for apart, out_ref in enumerate(out_refs):
            out_ref[at:at + size, :] = low_ref[pl.ds(pl.multiple_of(begin + (me ^ apart) * size, 16), size), :]
        begin += ref.shape[1]
        at += size


def input_grad(place, grads, weights, pieces):
    rows_in, width = weights[0].shape
    tokens = sum(grad.shape[1] for grad in grads)
    step = 256
    return pl.pallas_call(
        functools.partial(input_grad_body, len(grads)),
        grid_spec=pltpu.PrefetchScalarGridSpec(
            num_scalar_prefetch=1,
            grid=(rows_in // step,),
            in_specs=[pl.BlockSpec(grad.shape, lambda n, place: (0, 0, 0)) for grad in grads]
            + [pl.BlockSpec((step, width), lambda n, place: (n, 0))] * 3,
            out_specs=[pl.BlockSpec((tokens // pieces, step), lambda n, place: (0, n))] * pieces,
            scratch_shapes=[pltpu.VMEM((tokens, step), jnp.bfloat16)],
        ),
        out_shape=[jax.ShapeDtypeStruct((tokens // pieces, rows_in), jnp.bfloat16)] * pieces,
        compiler_params=pltpu.CompilerParams(vmem_limit_bytes=VMEM_LIMIT),
        cost_estimate=pl.CostEstimate(
            flops=6 * tokens * rows_in * width // SHADE,
            bytes_accessed=6 * width * (rows_in + tokens) // SHADE,
            transcendentals=0,
        ),
        name="input_grad",
    )(place, *grads, *weights)


def weight_grad_body(pieces, units, has_acc, place_ref, *refs):
    count = len(units)
    x_refs, grad_refs = refs[:pieces], refs[pieces:pieces + count]
    acc_refs, out_refs, left_ref = refs[pieces + count:-4], refs[-4:-1], refs[-1]
    features = x_refs[0].shape[1]

    @pl.when(pl.program_id(0) == 0)
    def _():
        me = place_ref[place_ref.shape[0] - 1]
        for at, (hop, which, index) in enumerate(units):
            size = grad_refs[at].shape[1]
            for apart, x_ref in enumerate(x_refs):
                rows = pl.ds(pl.multiple_of((me ^ apart) * features, features), features)
                left_ref[rows, at * size:(at + 1) * size] = x_ref[place_ref[2 * hop + which], :, index * size:(index + 1) * size]

    for member in range(3):
        right = jnp.concatenate([ref[member] for ref in grad_refs], axis=0)
        total = jnp.dot(left_ref[...], right, preferred_element_type=jnp.float32)
        if has_acc:
            total = total + acc_refs[member][...].astype(jnp.float32)
        out_refs[member][...] = total.astype(jnp.bfloat16)


def weight_grad(place, x, units, grads, acc):
    canvases, features, length = x[0].shape
    rows_in = len(x) * features
    size, width = grads[0].shape[1:]
    tokens = size * len(grads)
    step = 512
    block = pl.BlockSpec((rows_in, step), lambda n, place: (0, n))
    acc = tuple(acc) if acc is not None else ()
    return pl.pallas_call(
        functools.partial(weight_grad_body, len(x), tuple(units), bool(acc)),
        grid_spec=pltpu.PrefetchScalarGridSpec(
            num_scalar_prefetch=1,
            grid=(width // step,),
            in_specs=[pl.BlockSpec(x[0].shape, lambda n, place: (0, 0, 0))] * len(x)
            + [pl.BlockSpec((3, size, step), lambda n, place: (0, 0, n))] * len(grads)
            + [block] * len(acc),
            out_specs=[block] * 3,
            scratch_shapes=[pltpu.VMEM((rows_in, tokens), jnp.bfloat16)],
        ),
        out_shape=[jax.ShapeDtypeStruct((rows_in, width), jnp.bfloat16)] * 3,
        compiler_params=pltpu.CompilerParams(vmem_limit_bytes=VMEM_LIMIT),
        cost_estimate=pl.CostEstimate(
            flops=6 * tokens * rows_in * width // SHADE,
            bytes_accessed=6 * width * (tokens + rows_in * (2 if acc else 1)) // SHADE,
            transcendentals=0,
        ),
        name="weight_grad",
    )(place, *x, *grads, *acc)


def ring_order(chips):
    return [0] + list(range(1, chips, 2)) + list(range(chips - 2 + chips % 2, 0, -2))


def local(layer_input, attn_grad, queries, keys, values, masked, key_bias, w_query, w_key, w_value):
    row_count = lax.axis_size("row")
    col_count = lax.axis_size("col")
    length, width = queries.shape[1], queries.shape[2]
    rows_in = w_query.shape[0]
    spread = row_count // col_count
    chips = row_count // 2
    sizes = chunk_sizes(length)
    weights = (w_query, w_key, w_value)

    order = ring_order(chips)
    ring = [(2 * order[n] + core, 2 * order[(n + 1) % chips] + core) for n in range(chips) for core in range(2)]
    swap = [(n, n ^ 1) for n in range(row_count)]
    place_of = [order.index(chip) for chip in range(chips)]
    me = lax.axis_index("row")
    my_core = me % 2
    my_place = jnp.array(place_of, jnp.int32)[me // 2]
    chips_at = jnp.array(order, jnp.int32)[(my_place - jnp.arange(chips)) % chips]
    origin = chips_at[:, None] * 2 + (my_core + jnp.arange(2)[None, :]) % 2

    def a2a(array, axis):
        return lax.all_to_all(array, axis, split_axis=0, concat_axis=0, tiled=True)

    def after(array, ahead):
        return lax.optimization_barrier((array, ahead))[0]

    always = jnp.sum(masked) >= 0

    def window(work, *operands):
        shapes = jax.eval_shape(work, *operands)

        def nothing(*_):
            return jax.tree.map(lambda leaf: jnp.zeros(leaf.shape, leaf.dtype), shapes)

        return lax.cond(always, work, nothing, *operands)

    place = jnp.concatenate([origin.reshape(-1), lax.axis_index("col")[None]]).astype(jnp.int32)
    every = range(len(sizes))
    last, final = len(sizes) - 1, chips - 1

    def hop(mine):
        return lax.ppermute(mine, "row", ring)

    def other(mine):
        return lax.ppermute(mine, "row", swap)

    def across(mine, apart):
        return lax.ppermute(mine, "col", [(n, n ^ apart) for n in range(col_count)])

    def partial_of(given):
        return input_grad(place, [member for pair in given for member in pair], weights, col_count)

    def summed(partial):
        total = partial[0].astype(jnp.float32)
        for apart in range(1, col_count):
            total = total + across(partial[apart], apart).astype(jnp.float32)
        return total.astype(jnp.bfloat16)

    def weight_part(x, units, given, acc):
        places = [(step, core, index) for step, index in units for core in range(2)]
        return weight_grad(place, x, places, [member for pair in given for member in pair], acc)

    chunks, bias_part = attention(queries[0], keys[0], values[0], attn_grad, masked, key_bias, sizes)
    arrived = [list(chunks)] + [[None] * len(sizes) for _ in range(final)]
    others = [[None] * len(sizes) for _ in range(chips)]
    sums = [None] * chips

    def both(step, index):
        return (arrived[step][index], others[step][index])

    def own_tokens(layer_input, *chunks):
        blocks = layer_input.reshape(length, spread, col_count, rows_in // col_count)
        x = a2a(jnp.transpose(blocks, (2, 1, 0, 3)), "col").reshape(row_count, length, rows_in // col_count)
        x = jnp.swapaxes(a2a(x, "row"), 1, 2)
        theirs = [other(chunk) for chunk in chunks]
        return theirs, summed(partial_of(list(zip(chunks, theirs)))), x

    arrived[1][0] = hop(chunks[0])
    others[0], sums[0], x = window(own_tokens, layer_input, *chunks)
    arrived[1][last] = hop(after(chunks[last], others[0][0]))
    x_pieces = {0: x}

    weight_grads = None
    for step in range(1, final):
        units = [(place, spot) for place in range(2) for spot in every] if step == 2 else []

        def early(mine, x, done, partial):
            theirs = other(mine)
            if step == 1:
                return theirs, [across(x, apart) for apart in range(1, col_count) if apart & (apart - 1) == 0]
            if step == 2:
                return theirs, weight_part(x, units, done, None), summed(partial)
            return (theirs,)

        others[step][0], *given = window(early, arrived[step][0], x, [both(*unit) for unit in units], sums[step - 1])
        if step == 1:
            x_pieces.update(zip([apart for apart in range(1, col_count) if apart & (apart - 1) == 0], given[0]))
        elif step == 2:
            weight_grads, sums[1] = given
        arrived[step + 1][0] = hop(after(arrived[step][0], others[step][0]))

        def late(mine, x, sooner, acc):
            theirs = other(mine)
            given = [sooner, (mine, theirs)]
            partial = partial_of(given)
            if step == 1:
                return theirs, partial, [across(x, apart) for apart in range(1, col_count) if apart & (apart - 1)]
            return theirs, summed(partial), weight_part(x, [(step, spot) for spot in every], given, acc)

        others[step][last], sums[step], given = window(late, arrived[step][last], x, both(step, 0), weight_grads)
        if step == 1:
            x_pieces.update(zip([apart for apart in range(1, col_count) if apart & (apart - 1)], given))
            x = [x_pieces[apart] for apart in range(col_count)]
        else:
            weight_grads = given
        arrived[step + 1][last] = hop(after(arrived[step][last], others[step][last]))

    def before_last(mine):
        theirs = other(mine)
        return theirs, summed(partial_of([(mine, theirs)]))

    others[final][0], final_sums = window(before_last, after(arrived[final][0], others[final - 1][last]))

    def homeward(mine, step, which):
        route = []
        for n in range(chips):
            for core in range(2):
                route.append((2 * order[n] + core, 2 * order[(n - step) % chips] + (core ^ which)))
        return lax.ppermute(mine, "row", route) if step or which else mine

    def pieces_of(step):
        parts = [[], []]
        at = 0
        for size in sizes[:last] if step == final else sizes:
            for which in range(2):
                parts[which].append(sums[step][at:at + size // col_count])
                at += size // col_count
        return [jnp.concatenate(part, axis=0) for part in parts]

    sums[final] = final_sums
    landed = after(arrived[final][last], others[final][0])
    others[final][last] = other(landed)
    sums = after(sums, landed)
    at_home = [[homeward(part, step, which) for which, part in enumerate(pieces_of(step))] for step in range(final)]
    sooner = [homeward(part, final, which) for which, part in enumerate(pieces_of(final))]
    partial = partial_of([(landed, others[final][last])])
    units = [(final, index) for index in every]
    total = summed(partial)
    weight_grads = weight_part(x, units, [both(*unit) for unit in units], weight_grads)
    size = sizes[last] // col_count
    later = [homeward(total[which * size:(which + 1) * size], final, which) for which in range(2)]
    at_home.append([jnp.concatenate(parts, axis=0) for parts in zip(sooner, later)])
    mine = jnp.stack([part for parts in at_home for part in parts])
    rows = jnp.arange(row_count)
    slot = ((jnp.array(place_of, jnp.int32)[rows // 2] - my_place) % chips) * 2 + (rows + my_core) % 2
    my_col = lax.axis_index("col")
    apart = my_col ^ jnp.arange(col_count)
    slot = slot.reshape(col_count, spread)[apart].reshape(-1)
    mine = jnp.take(mine, slot, axis=0).reshape((col_count, spread) + mine.shape[1:])
    got = jnp.stack([across(mine[d], d) if d else mine[d] for d in range(col_count)])
    got = jnp.take(got, apart, axis=0)
    home = []
    at = 0
    for chunk in sizes:
        size = chunk // col_count
        home.append(jnp.transpose(got[:, :, at:at + size], (0, 2, 1, 3)).reshape(chunk, spread * rows_in))
        at += size
    bias_all = a2a(after(jnp.broadcast_to(bias_part[None], (row_count,) + bias_part.shape), mine), "row")
    layer_grad = jnp.concatenate(home, axis=0)
    return (layer_grad, *weight_grads, jnp.sum(bias_all, axis=0))


def solution(mesh):
    in_specs = (
        P("row", "col"),
        P("row", "col"),
        P("row", None, "col"),
        P("row", None, "col"),
        P("row", None, "col"),
        P("row", None),
        P("col"),
        P("row", "col"),
        P("row", "col"),
        P("row", "col"),
    )
    out_specs = (P("row", "col"), P("row", "col"), P("row", "col"), P("row", "col"), P("col"))
    return jax.shard_map(local, mesh=mesh, in_specs=in_specs, out_specs=out_specs, check_vma=False)
```

time: 468 us -> 335 us (0.72)
  blocking collectives: 84.4 us -> 0 us
  local copies, waits for them, and re-layouts: 52 us -> 27.2 us
  waiting for transfers between devices: 135 us -> 117 us
    all_to_all x2 -> x0, blocking collectives: 84.4 us -> none  [a2a(): return lax.all_to_all(array, axis, split_axis=0, concat_axis=0, tiled=True)]
    all_to_all x11 -> x3, starting transfers between devices: 45.1 us -> 11.8 us  [a2a(): return lax.all_to_all(array, axis, split_axis=0, concat_axis=0, tiled=True)]
    ppermute x14 -> x44, starting transfers between devices: 13.6 us -> 46.9 us  [the longest x21 25.5 us: across(): return lax.ppermute(mine, 'col', [(n, n ^ apart) for n in range(col_count)])]
    unnamed x56 -> x23, local copies, waits for them, and re-layouts: 33.6 us -> 3.59 us
    all_to_all x11 -> x3, waiting for transfers between devices: 37.9 us -> 18.5 us  [a2a(): return lax.all_to_all(array, axis, split_axis=0, concat_axis=0, tiled=True)]
    another operation x0 -> x4, local copies, waits for them, and re-layouts: none -> 9.05 us
    convert_element_type x0 -> x5, other arithmetic: none -> 5.34 us  [summed(): return total.astype(jnp.bfloat16)]
    reduce_sum x6 -> x2, other arithmetic: 6.07 us -> 1.17 us  [the longest x1 0.64 us: local(): always = jnp.sum(masked) >= 0]
  transfers between devices with their start and end apart: 25 -> 47, of which waited for: 10 -> 21; matrix products, arithmetic and copies ran while one was open for 13% -> 10% of each run, Pallas kernels for 23% -> 32%
where the time goes in v2:
time: 335 us; the launch traced here: 334 us
  Pallas kernels  118 us (35%)
  waiting for transfers between devices  117 us (35%)
  starting transfers between devices  58.7 us (18%)
  local copies, waits for them, and re-layouts  27.2 us (8%)
  other arithmetic  11.7 us (3%)
    ppermute x21, waiting for transfers between devices, across(): return lax.ppermute(mine, 'col', [(n, n ^ apart) for n in range(col_count)])  59.5 us
    pallas_call x5, Pallas kernels, input_grad(): pl.pallas_call(functools.partial(input_grad_body, len(grads)), grid_spec=...  56.9 us
    pallas_call x3, Pallas kernels, weight_grad(): pl.pallas_call(functools.partial(weight_grad_body, len(x), tuple(units),...  48.6 us
    ppermute x6, waiting for transfers between devices, hop(): return lax.ppermute(mine, 'row', ring)  25.7 us
    ppermute x21, starting transfers between devices, across(): return lax.ppermute(mine, 'col', [(n, n ^ apart) for n in range(col_count)])  25.5 us
    all_to_all x3, waiting for transfers between devices, a2a(): return lax.all_to_all(array, axis, split_axis=0, concat_axis=0, tiled=True)  18.5 us
    pallas_call x1, Pallas kernels, attention(): pl.pallas_call(functools.partial(attention_body, sizes, head_dim, heads_s...  12.1 us
    all_to_all x3, starting transfers between devices, a2a(): return lax.all_to_all(array, axis, split_axis=0, concat_axis=0, tiled=True)  11.8 us
  transfers between devices with their start and end apart: 47, of which 21 were waited for; matrix products, arithmetic and copies ran while one was open for 10% of the time, Pallas kernels for 32%

profile of v2, /device:TPU:0, one launch (start us, length us, event | category | flops | bytes accessed | tf_op | source)
XLA Modules:
  0.0 334.4 jit_solution(5944881566742331951)
XLA Ops:
  0.7 12.1 %attention_back.1 = (bf16[3,128,2048]{2,1,0:T(8,128)(2,1)}, bf16[3,128,2048]{2,1,0:T(8,128)(2,1)}, f32[16,1,128]{2,1,0:T(1,128)}) custom-call(f32[16]{0:T(128)} %bias_ref.1, s32[1,256]{1,0:T(1,128)} %flag_ref.1, bf16[256,2048]{1,0:T(8,128)(2,1)} %bitcast.62, bf16[256,2048]{1,0:T(8,128)(2,1)} %bitcast.63, bf16[256,2048]{1,0:T(8,128)(2,1)} %bitcast.64, ...), custom_call_target="tpu_custom_call" | custom-call | flops 67108864 | bytes 367001 | tf_op jit(solution)/shard_map/attention_back/pallas_call | solution.py:56
  12.8 3.0 collective-permute-start.22
  19.4 57.2 %conditional.6 = (bf16[3,128,2048]{2,1,0:T(8,128)(2,1)S(1)}, bf16[3,128,2048]{2,1,0:T(8,128)(2,1)S(1)}, bf16[128,1024]{1,0:T(8,128)(2,1)S(1)}, bf16[8,256,256]{1,2,0:T(8,128)(2,1)}, bf16[8,256,256]{2,1,0:T(8,128)(2,1)}) conditional(s32[]{:T(128)} %convert_element_type.83, () %tuple.65, (bf16[3,128,2048]{2,1,0:T(8,128)(2,1)}, ...), branch_computations={%region_1.2_spmd, %region_2.3_spmd} | conditional | flops 323171136 | bytes 55732232 | solution.py:214
  19.4 1.8 reshape.214
  22.4 4.2 %all-to-all-start = ((bf16[4,2,256,256]{3,2,1,0:T(8,128)(2,1)}), bf16[4,2,256,256]{3,2,1,0:T(8,128)(2,1)}, u32[]{:S(2)}, u32[]{:S(2)}) async-start(bf16[4,2,256,256]{3,2,1,0:T(8,128)(2,1)} %bitcast.57), calls=%async_computation | async-start | bytes 2097152 | tf_op jit(solution)/shard_map/cond/branch_1_fun/all_to_all | solution.py:201
  27.2 13.1 %all-to-all-done = bf16[4,2,256,256]{3,2,1,0:T(8,128)(2,1)} async-done(((bf16[4,2,256,256]{3,2,1,0:T(8,128)(2,1)}), bf16[4,2,256,256]{3,2,1,0:T(8,128)(2,1)}, u32[]{:S(2)}, u32[]{:S(2)}) %all-to-all-start) | async-done | bytes 1048608 | tf_op jit(solution)/shard_map/cond/branch_1_fun/all_to_all | solution.py:201
  40.4 4.2 %all-to-all-start.1 = ((bf16[8,256,256]{2,1,0:T(8,128)(2,1)}), bf16[8,256,256]{2,1,0:T(8,128)(2,1)}, u32[]{:S(2)}, u32[]{:S(2)}) async-start(bf16[8,256,256]{2,1,0:T(8,128)(2,1)} %bitcast.1), calls=%async_computation.1 | async-start | bytes 2097152 | tf_op jit(solution)/shard_map/cond/branch_1_fun/all_to_all | solution.py:201
  44.7 12.8 %input_grad.5 = (bf16[128,1024]{1,0:T(8,128)(2,1)}, bf16[128,1024]{1,0:T(8,128)(2,1)}, bf16[128,1024]{1,0:T(8,128)(2,1)}, bf16[128,1024]{1,0:T(8,128)(2,1)}) custom-call(s32[9]{0:T(128)S(1)} %get-tuple-element.110.place_ref, bf16[3,128,2048]{2,1,0:T(8,128)(2,1)} %get-tuple-element.108.refs_0_, bf16[3,128,2048]{2,1,0:T(8,128)(2,1)S(1)} %collective-permute-done.5.refs_1_, ...), custom_call_target="tpu_custom_call" | custom-call | flops 322122560 | bytes 943718 | tf_op jit(solution)/shard_map/cond/branch_1_fun/input_grad/pallas_call | solution.py:102
  57.4 1.5 collective-permute-start.7
  59.5 1.5 collective-permute-start.9
  61.0 5.8 %collective-permute-done.7 = bf16[128,1024]{1,0:T(8,128)(2,1)S(1)} collective-permute-done((bf16[128,1024]{1,0:T(8,128)(2,1)}, bf16[128,1024]{1,0:T(8,128)(2,1)S(1)}, u32[]{:S(2)}, u32[]{:S(2)}) %collective-permute-start.7) | collective-permute-done | bytes 262176 | tf_op jit(solution)/shard_map/cond/branch_1_fun/ppermute | solution.py:227
  66.8 6.2 %collective-permute-done.8 = bf16[128,1024]{1,0:T(8,128)(2,1)S(1)} collective-permute-done((bf16[128,1024]{1,0:T(8,128)(2,1)}, bf16[128,1024]{1,0:T(8,128)(2,1)S(1)}, u32[]{:S(2)}, u32[]{:S(2)}) %collective-permute-start.8) | collective-permute-done | bytes 262176 | tf_op jit(solution)/shard_map/cond/branch_1_fun/ppermute | solution.py:227
  74.3 2.3 copy.43
  76.6 1.7 collective-permute-start.24
  78.3 28.5 %conditional.7 = (bf16[3,128,2048]{2,1,0:T(8,128)(2,1)}, bf16[8,256,256]{2,1,0:T(8,128)(2,1)}, bf16[8,256,256]{2,1,0:T(8,128)(2,1)}) conditional(s32[]{:T(128)} %convert_element_type.83, () %tuple.68, (bf16[3,128,2048]{2,1,0:T(8,128)(2,1)}, bf16[8,256,256]{1,2,0:T(8,128)(2,1)}) %tuple.69), branch_computations={%region_3.4_spmd, %region_4.5_spmd} | conditional | bytes 16777360 | solution.py:214
  78.3 2.3 copy.34
  81.2 1.5 collective-permute-start.2
  82.7 23.8 %collective-permute-done.1 = bf16[8,256,256]{2,1,0:T(8,128)(2,1)} collective-permute-done((bf16[8,256,256]{2,1,0:T(8,128)(2,1)}, bf16[8,256,256]{2,1,0:T(8,128)(2,1)}, u32[]{:S(2)}, u32[]{:S(2)}) %collective-permute-start.1) | collective-permute-done | bytes 1048608 | tf_op jit(solution)/shard_map/cond/branch_1_fun/ppermute | solution.py:227
  106.8 3.1 collective-permute-start.23
  109.9 5.2 %collective-permute-done.24 = bf16[3,128,2048]{2,1,0:T(8,128)(2,1)} collective-permute-done((bf16[3,128,2048]{2,1,0:T(8,128)(2,1)}, bf16[3,128,2048]{2,1,0:T(8,128)(2,1)}, u32[]{:S(2)}, u32[]{:S(2)}) %collective-permute-start.24) | collective-permute-done | bytes 1572896 | tf_op jit(solution)/shard_map/ppermute | solution.py:221
  115.2 29.0 %conditional.8 = (bf16[3,128,2048]{2,1,0:T(8,128)(2,1)}, bf16[128,1024]{1,0:T(8,128)(2,1)S(1)}, bf16[128,1024]{1,0:T(8,128)(2,1)}, bf16[128,1024]{1,0:T(8,128)(2...) conditional(s32[]{:T(128)} %convert_element_type.83, () %tuple.71, (bf16[3,128,2048]{2,1,0:T(8,128)(2,1)}, ...), branch_computations={%region_5.6_spmd, %region_6.7_spmd} | conditional | flops 322122560 | bytes 13526758 | solution.py:214
  115.2 2.3 copy.35
  117.4 2.2 collective-permute-start.4
  119.7 12.8 %input_grad.6 = (bf16[128,1024]{1,0:T(8,128)(2,1)S(1)}, bf16[128,1024]{1,0:T(8,128)(2,1)}, bf16[128,1024]{1,0:T(8,128)(2,1)}, bf16[128,1024]{1,0:T(8,128)(2,1)}) custom-call(s32[9]{0:T(128)S(1)} %get-tuple-element.122.place_ref, bf16[3,128,2048]{2,1,0:T(8,128)(2,1)} %get-tuple-element.123.refs_0_, bf16[3,128,2048]{2,1,0:T(8,128)(2,1)} %get-tuple-element.124.refs_1_, ...), custom_call_target="tpu_custom_call" | custom-call | flops 322122560 | bytes 943718 | tf_op jit(solution)/shard_map/cond/branch_1_fun/input_grad/pallas_call | solution.py:102
  132.5 11.7 %collective-permute-done.4 = bf16[8,256,256]{2,1,0:T(8,128)(2,1)} collective-permute-done((bf16[8,256,256]{2,1,0:T(8,128)(2,1)}, bf16[8,256,256]{2,1,0:T(8,128)(2,1)}, u32[]{:S(2)}, u32[]{:S(2)}) %collective-permute-start.4) | collective-permute-done | bytes 1048608 | tf_op jit(solution)/shard_map/cond/branch_1_fun/ppermute | solution.py:227
  144.9 2.4 collective-permute-done.23
  147.3 26.1 %conditional.9 = (bf16[3,128,2048]{2,1,0:T(8,128)(2,1)}, bf16[1024,2048]{1,0:T(8,128)(2,1)}, bf16[1024,2048]{1,0:T(8,128)(2,1)}, bf16[1024,2048]{1,0:T(8,128)(2,1)}, bf16[128,1024]{1,0:T(8,128)(2,1)S(1)}) conditional(s32[]{:T(128)} %convert_element_type.83, () %tuple.67, (bf16[3,128,2048]{2,1,0:T(8,128)(2,1)}, s32[9]{0:T(128)S(1)}, ...), branch_computations={%region_7.8_spmd, %region_8.9_spmd} | conditional | flops 645293696 | bytes 14417970 | solution.py:214
  147.3 1.7 collective-permute-start.13
  149.5 1.3 collective-permute-start.11
  150.8 2.3 copy.36.refs_0_
  153.1 19.0 %weight_grad.3 = (bf16[1024,2048]{1,0:T(8,128)(2,1)}, bf16[1024,2048]{1,0:T(8,128)(2,1)}, bf16[1024,2048]{1,0:T(8,128)(2,1)}) custom-call(s32[9]{0:T(128)S(1)} %get-tuple-element.134.place_ref, bf16[8,256,256]{2,1,0:T(8,128)(2,1)} %copy.36.refs_0_, bf16[8,256,256]{2,1,0:T(8,128)(2,1)} %get-tuple-element.136.refs_1_, ...), custom_call_target="tpu_custom_call" | custom-call | flops 644245120 | bytes 1258291 | tf_op jit(solution)/shard_map/cond/branch_1_fun/weight_grad/pallas_call | solution.py:154
  172.1 1.3 add_convert_fusion.1
  174.5 8.3 %collective-permute-done.25 = bf16[3,128,2048]{2,1,0:T(8,128)(2,1)} collective-permute-done((bf16[3,128,2048]{2,1,0:T(8,128)(2,1)}, bf16[3,128,2048]{2,1,0:T(8,128)(2,1)}, u32[]{:S(2)}, u32[]{:S(2)}) %collective-permute-start.25) | collective-permute-done | bytes 1572896 | tf_op jit(solution)/shard_map/ppermute | solution.py:221
  182.7 38.5 %conditional.10 = (bf16[3,128,2048]{2,1,0:T(8,128)(2,1)}, bf16[128,1024]{1,0:T(8,128)(2,1)}, bf16[1024,2048]{1,0:T(8,128)(2,1)}, bf16[1024,2048]{1,0:T(8,128)(2,1)}, bf16[1024,2048]{1,0:T(8,128)(2,1)}) conditional(s32[]{:T(128)} %convert_element_type.83, () %tuple.75, (bf16[3,128,2048]{2,1,0:T(8,128)(2,1)}, s32[9]{0:T(128)S(1)}, ...), branch_computations={%region_9.10_spmd, %region_10.11_spmd} | conditional | flops 645293696 | bytes 16410442 | solution.py:214
  182.7 3.8 %collective-permute-done.14.refs_3_.refs_7_ = bf16[3,128,2048]{2,1,0:T(8,128)(2,1)} collective-permute-done((bf16[3,128,2048]{2,1,0:T(8,128)(2,1)}, bf16[3,128,2048]{2,1,0:T(8,128)(2,1)}, u32[]{:S(2)}, u32[]{:S(2)}) %collective-permute-start.14) | collective-permute-done | bytes 1572896 | tf_op jit(solution)/shard_map/cond/branch_1_fun/ppermute | solution.py:224
  186.5 12.9 %input_grad.7 = (bf16[128,1024]{1,0:T(8,128)(2,1)}, bf16[128,1024]{1,0:T(8,128)(2,1)}, bf16[128,1024]{1,0:T(8,128)(2,1)}, bf16[128,1024]{1,0:T(8,128)(2,1)}) custom-call(s32[9]{0:T(128)S(1)} %get-tuple-element.155.place_ref, bf16[3,128,2048]{2,1,0:T(8,128)(2,1)} %get-tuple-element.156.refs_0_.refs_4_, ...), custom_call_target="tpu_custom_call" | custom-call | flops 322122560 | bytes 943718 | tf_op jit(solution)/shard_map/cond/branch_1_fun/input_grad/pallas_call | solution.py:102
  199.4 1.3 collective-permute-start.15
  200.6 1.5 collective-permute-start.16
  202.9 2.3 copy.37.refs_0_
  205.1 15.2 %weight_grad.4 = (bf16[1024,2048]{1,0:T(8,128)(2,1)}, bf16[1024,2048]{1,0:T(8,128)(2,1)}, bf16[1024,2048]{1,0:T(8,128)(2,1)}) custom-call(s32[9]{0:T(128)S(1)} %get-tuple-element.155.place_ref, bf16[8,256,256]{2,1,0:T(8,128)(2,1)} %copy.37.refs_0_, bf16[8,256,256]{2,1,0:T(8,128)(2,1)} %get-tuple-element.166.refs_1_, ...), custom_call_target="tpu_custom_call" | custom-call | flops 322122560 | bytes 1572864 | tf_op jit(solution)/shard_map/cond/branch_1_fun/weight_grad/pallas_call | solution.py:154
  224.1 24.1 %conditional.11 = (bf16[3,128,2048]{2,1,0:T(8,128)(2,1)}, bf16[64,1024]{1,0:T(8,128)(2,1)S(1)}) conditional(s32[]{:T(128)} %convert_element_type.83, () %tuple.78, (bf16[3,128,2048]{2,1,0:T(8,128)(2,1)S(1)}, s32[9]{0:T(128)S(1)}, bf16[1024,2048]{1,0:T(8,128)(2,1)}, bf16[1024,2048]{1,0:T(8,128)(2,1)}, bf16[1024,2048]{1,0:T(8,128)(2,1)}) %tuple.81), branch_computations={%region_11.12_spmd, %region_12.13_spmd} | conditional | flops 161585568 | bytes 9306288 | solution.py:214
  224.2 3.5 %collective-permute-done.18.refs_1_ = bf16[3,128,2048]{2,1,0:T(8,128)(2,1)} collective-permute-done((bf16[3,128,2048]{2,1,0:T(8,128)(2,1)S(1)}, bf16[3,128,2048]{2,1,0:T(8,128)(2,1)}, u32[]{:S(2)}, u32[]{:S(2)}) %collective-permute-start.18) | collective-permute-done | bytes 1572896 | tf_op jit(solution)/shard_map/cond/branch_1_fun/ppermute | solution.py:224
  227.8 9.8 %input_grad.8 = (bf16[64,1024]{1,0:T(8,128)(2,1)}, bf16[64,1024]{1,0:T(8,128)(2,1)}, bf16[64,1024]{1,0:T(8,128)(2,1)}, bf16[64,1024]{1,0:T(8,128)(2,1)}) custom-call(s32[9]{0:T(128)S(1)} %get-tuple-element.176.place_ref, bf16[3,128,2048]{2,1,0:T(8,128)(2,1)S(1)} %get-tuple-element.175.refs_0_, bf16[3,128,2048]{2,1,0:T(8,128)(2,1)} %collective-permute-done.18.refs_1_, ...), custom_call_target="tpu_custom_call" | custom-call | flops 161061280 | bytes 786432 | tf_op jit(solution)/shard_map/cond/branch_1_fun/input_grad/pallas_call | solution.py:102
  237.5 1.4 collective-permute-start.19
  238.9 1.5 collective-permute-start.20
  241.1 2.7 collective-permute-done.19
  243.8 3.4 %collective-permute-done.20 = bf16[64,1024]{1,0:T(8,128)(2,1)S(1)} collective-permute-done((bf16[64,1024]{1,0:T(8,128)(2,1)}, bf16[64,1024]{1,0:T(8,128)(2,1)S(1)}, u32[]{:S(2)}, u32[]{:S(2)}) %collective-permute-start.20) | collective-permute-done | bytes 131104 | tf_op jit(solution)/shard_map/cond/branch_1_fun/ppermute | solution.py:227
  248.2 9.7 %collective-permute-done.27.refs_0_.refs_6_ = bf16[3,128,2048]{2,1,0:T(8,128)(2,1)S(1)} collective-permute-done((bf16[3,128,2048]{2,1,0:T(8,128)(2,1)}, bf16[3,128,2048]{2,1,0:T(8,128)(2,1)S(1)}, u32[]{:S(2)}, u32[]{:S(2)}) %collective-permute-start.27) | collective-permute-done | bytes 1572896 | tf_op jit(solution)/shard_map/ppermute | solution.py:221
  258.9 3.3 collective-permute-start.33
  266.5 3.2 collective-permute-done.29
  269.6 1.5 collective-permute-start.31
  272.5 8.6 %input_grad.9 = (bf16[64,1024]{1,0:T(8,128)(2,1)}, bf16[64,1024]{1,0:T(8,128)(2,1)}, bf16[64,1024]{1,0:T(8,128)(2,1)}, bf16[64,1024]{1,0:T(8,128)(2,1)}) custom-call(s32[9]{0:T(128)S(1)} %pad_add_fusion.place_ref, bf16[3,128,2048]{2,1,0:T(8,128)(2,1)} %copy-done.6, bf16[3,128,2048]{2,1,0:T(8,128)(2,1)} %collective-permute-done.34.refs_1_.refs_7_, ...), custom_call_target="tpu_custom_call" | custom-call | flops 161061280 | bytes 786432 | tf_op jit(solution)/shard_map/input_grad/pallas_call | solution.py:102
  281.1 1.4 collective-permute-start.35
  282.5 1.5 collective-permute-start.36
  285.3 2.0 collective-permute-done.35
  287.3 3.4 %collective-permute-done.36 = bf16[64,1024]{1,0:T(8,128)(2,1)S(1)} collective-permute-done((bf16[64,1024]{1,0:T(8,128)(2,1)}, bf16[64,1024]{1,0:T(8,128)(2,1)S(1)}, u32[]{:S(2)}, u32[]{:S(2)}) %collective-permute-start.36) | collective-permute-done | bytes 131104 | tf_op jit(solution)/shard_map/ppermute | solution.py:227
  291.7 1.9 collective-permute-start.38
  294.6 2.0 collective-permute-start.40
  298.2 1.9 collective-permute-done.40
  300.8 1.8 gather_fusion.3
  302.9 2.4 collective-permute-start.43
  307.3 3.3 all-to-all-start.2
  310.6 5.4 %all-to-all-done.2 = f32[8,1,16]{2,1,0:T(1,128)S(1)} async-done(((f32[8,1,16]{2,1,0:T(1,128)}), f32[8,1,16]{2,1,0:T(1,128)S(1)}, u32[]{:S(2)}, u32[]{:S(2)}) %all-to-all-start.2) | async-done | bytes 544 | tf_op jit(solution)/shard_map/all_to_all | solution.py:201
  316.6 14.4 %weight_grad.5 = (bf16[1024,2048]{1,0:T(8,128)(2,1)}, bf16[1024,2048]{1,0:T(8,128)(2,1)}, bf16[1024,2048]{1,0:T(8,128)(2,1)}) custom-call(s32[9]{0:T(128)S(1)} %pad_add_fusion.place_ref, bf16[8,256,256]{2,1,0:T(8,128)(2,1)} %get-tuple-element.409.refs_0_, bf16[8,256,256]{2,1,0:T(8,128)(2,1)} %get-tuple-element.241.refs_1_, ...), custom_call_target="tpu_custom_call" | custom-call | flops 322122560 | bytes 1572864 | tf_op jit(solution)/shard_map/weight_grad/pallas_call | solution.py:154
  (140 shorter events, 34.0 us)
Async XLA Ops:
  0.6 15.2 %copy-start = (s32[4]{0:T(128)S(1)}, s32[4]{0:T(128)}, u32[]{:S(2)}) copy-start(s32[4]{0:T(128)} %constant.140.clone) | copy-start | bytes 52
  0.6 17.4 %copy-start.12 = (s32[1,256]{1,0:T(1,128)S(1)}, s32[1,256]{1,0:T(1,128)}, u32[]{:S(2)}) copy-start(s32[1,256]{1,0:T(1,128)} %flag_ref.1) | copy-start | bytes 3076
  12.8 65.5 %collective-permute-start.22 = (bf16[3,128,2048]{2,1,0:T(8,128)(2,1)}, bf16[3,128,2048]{2,1,0:T(8,128)(2,1)}, u32[]{:S(2)}, u32[]{:S(2)}) collective-permute-start(bf16[3,128,2048]{2,1,0:T(8,128)(2,1)} %get-tuple-element.235), channel_id=1, source_target_pairs={{0,8},{4,12},{8,24},{12,28},{24,16},{28,20},{16,0},{20,4},{1,9},{5... | collective-permute-start | bytes 4718600 | tf_op jit(solution)/shard_map/ppermute | solution.py:221
  22.4 17.9 %all-to-all-start = ((bf16[4,2,256,256]{3,2,1,0:T(8,128)(2,1)}), bf16[4,2,256,256]{3,2,1,0:T(8,128)(2,1)}, u32[]{:S(2)}, u32[]{:S(2)}) async-start(bf16[4,2,256,256]{3,2,1,0:T(8,128)(2,1)} %bitcast.57), calls=%async_computation | async-start | bytes 2097152 | tf_op jit(solution)/shard_map/cond/branch_1_fun/all_to_all | solution.py:201
  26.7 17.9 %collective-permute-start.5 = (bf16[3,128,2048]{2,1,0:T(8,128)(2,1)}, bf16[3,128,2048]{2,1,0:T(8,128)(2,1)S(1)}, u32[]{:S(2)}, u32[]{:S(2)}) collective-permute-start(bf16[3,128,2048]{2,1,0:T(8,128)(2,1)} %get-tuple-element.108.refs_0_), channel_id=1, source_target_pairs={{0,4},{4,0},{8,12},{12,8},{16,20},{20,16},{24,28},{28,24},{1,5},{5... | collective-permute-start | bytes 4718600 | tf_op jit(solution)/shard_map/cond/branch_1_fun/ppermute | solution.py:224
  26.7 17.9 %collective-permute-start.6 = (bf16[3,128,2048]{2,1,0:T(8,128)(2,1)}, bf16[3,128,2048]{2,1,0:T(8,128)(2,1)S(1)}, u32[]{:S(2)}, u32[]{:S(2)}) collective-permute-start(bf16[3,128,2048]{2,1,0:T(8,128)(2,1)} %get-tuple-element.109.refs_2_), channel_id=1, source_target_pairs={{0,4},{4,0},{8,12},{12,8},{16,20},{20,16},{24,28},{28,24},{1,5},{5... | collective-permute-start | bytes 4718600 | tf_op jit(solution)/shard_map/cond/branch_1_fun/ppermute | solution.py:224
  40.4 33.9 %all-to-all-start.1 = ((bf16[8,256,256]{2,1,0:T(8,128)(2,1)}), bf16[8,256,256]{2,1,0:T(8,128)(2,1)}, u32[]{:S(2)}, u32[]{:S(2)}) async-start(bf16[8,256,256]{2,1,0:T(8,128)(2,1)} %bitcast.1), calls=%async_computation.1 | async-start | bytes 2097152 | tf_op jit(solution)/shard_map/cond/branch_1_fun/all_to_all | solution.py:201
  44.6 12.8 %copy-start.4 = (bf16[3,128,2048]{2,1,0:T(8,128)(2,1)}, bf16[3,128,2048]{2,1,0:T(8,128)(2,1)S(1)}, u32[]{:S(2)}) copy-start(bf16[3,128,2048]{2,1,0:T(8,128)(2,1)S(1)} %collective-permute-done.5.refs_1_) | copy-start | bytes 4718596 | tf_op jit(solution)/shard_map/cond
  44.6 12.8 %copy-start.2 = (bf16[3,128,2048]{2,1,0:T(8,128)(2,1)}, bf16[3,128,2048]{2,1,0:T(8,128)(2,1)S(1)}, u32[]{:S(2)}) copy-start(bf16[3,128,2048]{2,1,0:T(8,128)(2,1)S(1)} %collective-permute-done.6.refs_3_) | copy-start | bytes 4718596 | tf_op jit(solution)/shard_map/cond
  57.4 9.4 %collective-permute-start.7 = (bf16[128,1024]{1,0:T(8,128)(2,1)}, bf16[128,1024]{1,0:T(8,128)(2,1)S(1)}, u32[]{:S(2)}, u32[]{:S(2)}) collective-permute-start(bf16[128,1024]{1,0:T(8,128)(2,1)} %get-tuple-element.115), channel_id=1, source_target_pairs={{0,1},{1,0},{2,3},{3,2},{4,5},{5,4},{6,7},{7,6},{8,9},{9,8},{10,11... | collective-permute-start | bytes 786440 | tf_op jit(solution)/shard_map/cond/branch_1_fun/ppermute | solution.py:227
  58.9 14.1 %collective-permute-start.8 = (bf16[128,1024]{1,0:T(8,128)(2,1)}, bf16[128,1024]{1,0:T(8,128)(2,1)S(1)}, u32[]{:S(2)}, u32[]{:S(2)}) collective-permute-start(bf16[128,1024]{1,0:T(8,128)(2,1)} %get-tuple-element.116), channel_id=1, source_target_pairs={{0,2},{1,3},{2,0},{3,1},{4,6},{5,7},{6,4},{7,5},{8,10},{9,11},{10,... | collective-permute-start | bytes 786440 | tf_op jit(solution)/shard_map/cond/branch_1_fun/ppermute | solution.py:227
  59.5 13.6 %collective-permute-start.9 = (bf16[128,1024]{1,0:T(8,128)(2,1)}, bf16[128,1024]{1,0:T(8,128)(2,1)S(1)}, u32[]{:S(2)}, u32[]{:S(2)}) collective-permute-start(bf16[128,1024]{1,0:T(8,128)(2,1)} %get-tuple-element.117), channel_id=1, source_target_pairs={{0,3},{1,2},{2,1},{3,0},{4,7},{5,6},{6,5},{7,4},{8,11},{9,10},{10,... | collective-permute-start | bytes 786440 | tf_op jit(solution)/shard_map/cond/branch_1_fun/ppermute | solution.py:227
  73.0 3.5 %copy-start.3 = (bf16[3,128,2048]{2,1,0:T(8,128)(2,1)S(1)}, bf16[3,128,2048]{2,1,0:T(8,128)(2,1)}, u32[]{:S(2)}) copy-start(bf16[3,128,2048]{2,1,0:T(8,128)(2,1)} %copy-done.2) | copy-start | bytes 4718596 | tf_op jit(solution)/shard_map/cond
  73.0 3.5 %copy-start.5 = (bf16[3,128,2048]{2,1,0:T(8,128)(2,1)S(1)}, bf16[3,128,2048]{2,1,0:T(8,128)(2,1)}, u32[]{:S(2)}) copy-start(bf16[3,128,2048]{2,1,0:T(8,128)(2,1)} %copy-done.4) | copy-start | bytes 4718596 | tf_op jit(solution)/shard_map/cond
  76.6 1.7 copy-start.7
  76.6 38.6 %collective-permute-start.24 = (bf16[3,128,2048]{2,1,0:T(8,128)(2,1)}, bf16[3,128,2048]{2,1,0:T(8,128)(2,1)}, u32[]{:S(2)}, u32[]{:S(2)}) collective-permute-start(bf16[3,128,2048]{2,1,0:T(8,128)(2,1)} %get-tuple-element.244), channel_id=1, source_target_pairs={{0,8},{4,12},{8,24},{12,28},{24,16},{28,20},{16,0},{20,4},{1,9},{5... | collective-permute-start | bytes 4718600 | tf_op jit(solution)/shard_map/ppermute | solution.py:221
  78.3 28.5 %collective-permute-start = (bf16[3,128,2048]{2,1,0:T(8,128)(2,1)}, bf16[3,128,2048]{2,1,0:T(8,128)(2,1)}, u32[]{:S(2)}, u32[]{:S(2)}) collective-permute-start(bf16[3,128,2048]{2,1,0:T(8,128)(2,1)} %get-tuple-element.119), channel_id=1, source_target_pairs={{0,4},{4,0},{8,12},{12,8},{16,20},{20,16},{24,28},{28,24},{1,5},{5... | collective-permute-start | bytes 4718600 | tf_op jit(solution)/shard_map/cond/branch_1_fun/ppermute | solution.py:224
  80.6 25.9 %collective-permute-start.1 = (bf16[8,256,256]{2,1,0:T(8,128)(2,1)}, bf16[8,256,256]{2,1,0:T(8,128)(2,1)}, u32[]{:S(2)}, u32[]{:S(2)}) collective-permute-start(bf16[8,256,256]{2,1,0:T(8,128)(2,1)} %copy.34), channel_id=1, source_target_pairs={{0,1},{1,0},{2,3},{3,2},{4,5},{5,4},{6,7},{7,6},{8,9},{9,8},{10,11... | collective-permute-start | bytes 3145736 | tf_op jit(solution)/shard_map/cond/branch_1_fun/ppermute | solution.py:227
  81.2 25.6 %collective-permute-start.2 = (bf16[8,256,256]{2,1,0:T(8,128)(2,1)}, bf16[8,256,256]{2,1,0:T(8,128)(2,1)}, u32[]{:S(2)}, u32[]{:S(2)}) collective-permute-start(bf16[8,256,256]{2,1,0:T(8,128)(2,1)} %copy.34), channel_id=1, source_target_pairs={{0,2},{1,3},{2,0},{3,1},{4,6},{5,7},{6,4},{7,5},{8,10},{9,11},{10,... | collective-permute-start | bytes 3145736 | tf_op jit(solution)/shard_map/cond/branch_1_fun/ppermute | solution.py:227
  106.8 40.5 %collective-permute-start.23 = (bf16[3,128,2048]{2,1,0:T(8,128)(2,1)}, bf16[3,128,2048]{2,1,0:T(8,128)(2,1)}, u32[]{:S(2)}, u32[]{:S(2)}) collective-permute-start(bf16[3,128,2048]{2,1,0:T(8,128)(2,1)} %collective-permute-done.22), channel_id=1, source_target_pairs={{0,8},{4,12},{8,24},{12,28},{24,16},{28,20},{16,0},{20,4},{1,9},{5... | collective-permute-start | bytes 4718600 | tf_op jit(solution)/shard_map/ppermute | solution.py:221
  115.2 4.5 %collective-permute-start.3 = (bf16[3,128,2048]{2,1,0:T(8,128)(2,1)}, bf16[3,128,2048]{2,1,0:T(8,128)(2,1)}, u32[]{:S(2)}, u32[]{:S(2)}) collective-permute-start(bf16[3,128,2048]{2,1,0:T(8,128)(2,1)} %get-tuple-element.121.refs_2_), channel_id=1, source_target_pairs={{0,4},{4,0},{8,12},{12,8},{16,20},{20,16},{24,28},{28,24},{1,5},{5... | collective-permute-start | bytes 4718600 | tf_op jit(solution)/shard_map/cond/branch_1_fun/ppermute | solution.py:224
  117.4 26.8 %collective-permute-start.4 = (bf16[8,256,256]{2,1,0:T(8,128)(2,1)}, bf16[8,256,256]{2,1,0:T(8,128)(2,1)}, u32[]{:S(2)}, u32[]{:S(2)}) collective-permute-start(bf16[8,256,256]{2,1,0:T(8,128)(2,1)} %copy.35), channel_id=1, source_target_pairs={{0,3},{1,2},{2,1},{3,0},{4,7},{5,6},{6,5},{7,4},{8,11},{9,10},{10,... | collective-permute-start | bytes 3145736 | tf_op jit(solution)/shard_map/cond/branch_1_fun/ppermute | solution.py:227
  144.2 38.5 %collective-permute-start.25 = (bf16[3,128,2048]{2,1,0:T(8,128)(2,1)}, bf16[3,128,2048]{2,1,0:T(8,128)(2,1)}, u32[]{:S(2)}, u32[]{:S(2)}) collective-permute-start(bf16[3,128,2048]{2,1,0:T(8,128)(2,1)} %collective-permute-done.24), channel_id=1, source_target_pairs={{0,8},{4,12},{8,24},{12,28},{24,16},{28,20},{16,0},{20,4},{1,9},{5... | collective-permute-start | bytes 4718600 | tf_op jit(solution)/shard_map/ppermute | solution.py:221
  147.3 26.1 %collective-permute-start.10 = (bf16[3,128,2048]{2,1,0:T(8,128)(2,1)}, bf16[3,128,2048]{2,1,0:T(8,128)(2,1)}, u32[]{:S(2)}, u32[]{:S(2)}) collective-permute-start(bf16[3,128,2048]{2,1,0:T(8,128)(2,1)} %get-tuple-element.133), channel_id=1, source_target_pairs={{0,4},{4,0},{8,12},{12,8},{16,20},{20,16},{24,28},{28,24},{1,5},{5... | collective-permute-start | bytes 4718600 | tf_op jit(solution)/shard_map/cond/branch_1_fun/ppermute | solution.py:224
  147.3 24.8 %collective-permute-start.13 = (bf16[128,1024]{1,0:T(8,128)(2,1)}, bf16[128,1024]{1,0:T(8,128)(2,1)}, u32[]{:S(2)}, u32[]{:S(2)}) collective-permute-start(bf16[128,1024]{1,0:T(8,128)(2,1)} %get-tuple-element.153), channel_id=1, source_target_pairs={{0,3},{1,2},{2,1},{3,0},{4,7},{5,6},{6,5},{7,4},{8,11},{9,10},{10,... | collective-permute-start | bytes 786440 | tf_op jit(solution)/shard_map/cond/branch_1_fun/ppermute | solution.py:227
  149.0 23.1 %collective-permute-start.12 = (bf16[128,1024]{1,0:T(8,128)(2,1)}, bf16[128,1024]{1,0:T(8,128)(2,1)}, u32[]{:S(2)}, u32[]{:S(2)}) collective-permute-start(bf16[128,1024]{1,0:T(8,128)(2,1)} %get-tuple-element.152), channel_id=1, source_target_pairs={{0,2},{1,3},{2,0},{3,1},{4,6},{5,7},{6,4},{7,5},{8,10},{9,11},{10,... | collective-permute-start | bytes 786440 | tf_op jit(solution)/shard_map/cond/branch_1_fun/ppermute | solution.py:227
  149.5 22.6 %collective-permute-start.11 = (bf16[128,1024]{1,0:T(8,128)(2,1)}, bf16[128,1024]{1,0:T(8,128)(2,1)}, u32[]{:S(2)}, u32[]{:S(2)}) collective-permute-start(bf16[128,1024]{1,0:T(8,128)(2,1)} %get-tuple-element.151), channel_id=1, source_target_pairs={{0,1},{1,0},{2,3},{3,2},{4,5},{5,4},{6,7},{7,6},{8,9},{9,8},{10,11... | collective-permute-start | bytes 786440 | tf_op jit(solution)/shard_map/cond/branch_1_fun/ppermute | solution.py:227
  173.4 9.3 %copy-start.9 = (bf16[128,1024]{1,0:T(8,128)(2,1)}, bf16[128,1024]{1,0:T(8,128)(2,1)S(1)}, u32[]{:S(2)}) copy-start(bf16[128,1024]{1,0:T(8,128)(2,1)S(1)} %get-tuple-element.267) | copy-start | bytes 786436
  173.4 50.7 %collective-permute-start.26 = (bf16[3,128,2048]{2,1,0:T(8,128)(2,1)}, bf16[3,128,2048]{2,1,0:T(8,128)(2,1)S(1)}, u32[]{:S(2)}, u32[]{:S(2)}) collective-permute-start(bf16[3,128,2048]{2,1,0:T(8,128)(2,1)} %collective-permute-done.23), channel_id=1, source_target_pairs={{0,8},{4,12},{8,24},{12,28},{24,16},{28,20},{16,0},{20,4},{1,9},{5... | collective-permute-start | bytes 4718600 | tf_op jit(solution)/shard_map/ppermute | solution.py:221
  182.7 3.8 %collective-permute-start.14 = (bf16[3,128,2048]{2,1,0:T(8,128)(2,1)}, bf16[3,128,2048]{2,1,0:T(8,128)(2,1)}, u32[]{:S(2)}, u32[]{:S(2)}) collective-permute-start(bf16[3,128,2048]{2,1,0:T(8,128)(2,1)} %get-tuple-element.154.refs_2_.refs_6_), channel_id=1, source_target_pairs={{0,4},{4,0},{8,12},{12,8},{16,20},{20,16},{24,28},{28,24},{1,5},{5... | collective-permute-start | bytes 4718600 | tf_op jit(solution)/shard_map/cond/branch_1_fun/ppermute | solution.py:224
  199.4 21.0 %collective-permute-start.15 = (bf16[128,1024]{1,0:T(8,128)(2,1)}, bf16[128,1024]{1,0:T(8,128)(2,1)S(1)}, u32[]{:S(2)}, u32[]{:S(2)}) collective-permute-start(bf16[128,1024]{1,0:T(8,128)(2,1)} %get-tuple-element.162), channel_id=1, source_target_pairs={{0,1},{1,0},{2,3},{3,2},{4,5},{5,4},{6,7},{7,6},{8,9},{9,8},{10,11... | collective-permute-start | bytes 786440 | tf_op jit(solution)/shard_map/cond/branch_1_fun/ppermute | solution.py:227
  200.6 19.7 %collective-permute-start.16 = (bf16[128,1024]{1,0:T(8,128)(2,1)}, bf16[128,1024]{1,0:T(8,128)(2,1)S(1)}, u32[]{:S(2)}, u32[]{:S(2)}) collective-permute-start(bf16[128,1024]{1,0:T(8,128)(2,1)} %get-tuple-element.163), channel_id=1, source_target_pairs={{0,2},{1,3},{2,0},{3,1},{4,6},{5,7},{6,4},{7,5},{8,10},{9,11},{10,... | collective-permute-start | bytes 786440 | tf_op jit(solution)/shard_map/cond/branch_1_fun/ppermute | solution.py:227
  202.2 18.2 %collective-permute-start.17 = (bf16[128,1024]{1,0:T(8,128)(2,1)}, bf16[128,1024]{1,0:T(8,128)(2,1)S(1)}, u32[]{:S(2)}, u32[]{:S(2)}) collective-permute-start(bf16[128,1024]{1,0:T(8,128)(2,1)} %get-tuple-element.164), channel_id=1, source_target_pairs={{0,3},{1,2},{2,1},{3,0},{4,7},{5,6},{6,5},{7,4},{8,11},{9,10},{10,... | collective-permute-start | bytes 786440 | tf_op jit(solution)/shard_map/cond/branch_1_fun/ppermute | solution.py:227
  205.1 15.2 %copy-start.10 = (bf16[128,1024]{1,0:T(8,128)(2,1)S(1)}, bf16[128,1024]{1,0:T(8,128)(2,1)}, u32[]{:S(2)}) copy-start(bf16[128,1024]{1,0:T(8,128)(2,1)} %get-tuple-element.161) | copy-start | bytes 786436 | tf_op jit(solution)/shard_map/cond
  221.2 36.7 %collective-permute-start.27 = (bf16[3,128,2048]{2,1,0:T(8,128)(2,1)}, bf16[3,128,2048]{2,1,0:T(8,128)(2,1)S(1)}, u32[]{:S(2)}, u32[]{:S(2)}) collective-permute-start(bf16[3,128,2048]{2,1,0:T(8,128)(2,1)} %collective-permute-done.25), channel_id=1, source_target_pairs={{0,8},{4,12},{8,24},{12,28},{24,16},{28,20},{16,0},{20,4},{1,9},{5... | collective-permute-start | bytes 4718600 | tf_op jit(solution)/shard_map/ppermute | solution.py:221
  224.1 33.8 %copy-start.8 = (bf16[128,1024]{1,0:T(8,128)(2,1)S(1)}, bf16[128,1024]{1,0:T(8,128)(2,1)}, u32[]{:S(2)}) copy-start(bf16[128,1024]{1,0:T(8,128)(2,1)} %copy-done.7) | copy-start | bytes 786436
  224.2 3.6 %collective-permute-start.18 = (bf16[3,128,2048]{2,1,0:T(8,128)(2,1)S(1)}, bf16[3,128,2048]{2,1,0:T(8,128)(2,1)}, u32[]{:S(2)}, u32[]{:S(2)}) collective-permute-start(bf16[3,128,2048]{2,1,0:T(8,128)(2,1)S(1)} %get-tuple-element.175.refs_0_), channel_id=1, source_target_pairs={{0,4},{4,0},{8,12},{12,8},{16,20},{20,16},{24,28},{28,24},{1,5},{5... | collective-permute-start | bytes 4718600 | tf_op jit(solution)/shard_map/cond/branch_1_fun/ppermute | solution.py:224
  237.5 6.3 %collective-permute-start.19 = (bf16[64,1024]{1,0:T(8,128)(2,1)}, bf16[64,1024]{1,0:T(8,128)(2,1)S(1)}, u32[]{:S(2)}, u32[]{:S(2)}) collective-permute-start(bf16[64,1024]{1,0:T(8,128)(2,1)} %get-tuple-element.181), channel_id=1, source_target_pairs={{0,1},{1,0},{2,3},{3,2},{4,5},{5,4},{6,7},{7,6},{8,9},{9,8},{10,11... | collective-permute-start | bytes 393224 | tf_op jit(solution)/shard_map/cond/branch_1_fun/ppermute | solution.py:227
  238.9 8.3 %collective-permute-start.20 = (bf16[64,1024]{1,0:T(8,128)(2,1)}, bf16[64,1024]{1,0:T(8,128)(2,1)S(1)}, u32[]{:S(2)}, u32[]{:S(2)}) collective-permute-start(bf16[64,1024]{1,0:T(8,128)(2,1)} %get-tuple-element.182), channel_id=1, source_target_pairs={{0,2},{1,3},{2,0},{3,1},{4,6},{5,7},{6,4},{7,5},{8,10},{9,11},{10,... | collective-permute-start | bytes 393224 | tf_op jit(solution)/shard_map/cond/branch_1_fun/ppermute | solution.py:227
  240.5 6.8 %collective-permute-start.21 = (bf16[64,1024]{1,0:T(8,128)(2,1)}, bf16[64,1024]{1,0:T(8,128)(2,1)S(1)}, u32[]{:S(2)}, u32[]{:S(2)}) collective-permute-start(bf16[64,1024]{1,0:T(8,128)(2,1)} %get-tuple-element.183), channel_id=1, source_target_pairs={{0,3},{1,2},{2,1},{3,0},{4,7},{5,6},{6,5},{7,4},{8,11},{9,10},{10,... | collective-permute-start | bytes 393224 | tf_op jit(solution)/shard_map/cond/branch_1_fun/ppermute | solution.py:227
  257.9 6.4 %copy-start.6 = (bf16[3,128,2048]{2,1,0:T(8,128)(2,1)}, bf16[3,128,2048]{2,1,0:T(8,128)(2,1)S(1)}, u32[]{:S(2)}) copy-start(bf16[3,128,2048]{2,1,0:T(8,128)(2,1)S(1)} %collective-permute-done.27.refs_0_.refs_6_) | copy-start | bytes 4718596
  257.9 14.6 %collective-permute-start.34 = (bf16[3,128,2048]{2,1,0:T(8,128)(2,1)S(1)}, bf16[3,128,2048]{2,1,0:T(8,128)(2,1)}, u32[]{:S(2)}, u32[]{:S(2)}) collective-permute-start(bf16[3,128,2048]{2,1,0:T(8,128)(2,1)S(1)} %collective-permute-done.27.refs_0_.refs_6_), channel_id=1, source_target_pairs={{0,4},{4,0},{8,12},{12,8},{16,20},{20,16},{24,28},{28,24},{1,5},{5... | collective-permute-start | bytes 4718600 | tf_op jit(solution)/shard_map/ppermute | solution.py:224
  257.9 14.5 %copy-start.1 = (bf16[1024,2048]{1,0:T(8,128)(2,1)S(1)}, bf16[1024,2048]{1,0:T(8,128)(2,1)}, u32[]{:S(2)}) copy-start(bf16[1024,2048]{1,0:T(8,128)(2,1)} %refs_2_.1) | copy-start | bytes 12582916
  258.0 40.2 %collective-permute-start.39 = (bf16[32,1024]{1,0:T(8,128)(2,1)S(1)}, bf16[32,1024]{1,0:T(8,128)(2,1)S(1)}, u32[]{:S(2)}, u32[]{:S(2)}) collective-permute-start(bf16[32,1024]{1,0:T(8,128)(2,1)S(1)} %get-tuple-element.428), channel_id=1, source_target_pairs={{0,12},{4,8},{8,28},{12,24},{24,20},{28,16},{16,4},{20,0},{1,13},{... | collective-permute-start | bytes 196616 | tf_op jit(solution)/shard_map/ppermute | solution.py:308
  258.9 37.6 %collective-permute-start.33 = (bf16[32,1024]{1,0:T(8,128)(2,1)S(1)}, bf16[32,1024]{1,0:T(8,128)(2,1)S(1)}, u32[]{:S(2)}, u32[]{:S(2)}) collective-permute-start(bf16[32,1024]{1,0:T(8,128)(2,1)S(1)} %get-tuple-element.429), channel_id=1, source_target_pairs={{0,8},{4,12},{8,24},{12,28},{24,16},{28,20},{16,0},{20,4},{1,9},{5... | collective-permute-start | bytes 196616 | tf_op jit(solution)/shard_map/ppermute | solution.py:308
  262.2 2.8 collective-permute-start.28
  263.3 6.3 %collective-permute-start.29 = (bf16[64,1024]{1,0:T(8,128)(2,1)S(1)}, bf16[64,1024]{1,0:T(8,128)(2,1)S(1)}, u32[]{:S(2)}, u32[]{:S(2)}) collective-permute-start(bf16[64,1024]{1,0:T(8,128)(2,1)S(1)} %pad_maximum_fusion.3), channel_id=1, source_target_pairs={{0,16},{4,20},{8,0},{12,4},{24,8},{28,12},{16,24},{20,28},{1,17},{... | collective-permute-start | bytes 393224 | tf_op jit(solution)/shard_map/ppermute | solution.py:308
  265.1 6.8 %collective-permute-start.30 = (bf16[64,1024]{1,0:T(8,128)(2,1)S(1)}, bf16[64,1024]{1,0:T(8,128)(2,1)S(1)}, u32[]{:S(2)}, u32[]{:S(2)}) collective-permute-start(bf16[64,1024]{1,0:T(8,128)(2,1)S(1)} %pad_maximum_fusion.4), channel_id=1, source_target_pairs={{0,20},{4,16},{8,4},{12,0},{24,12},{28,8},{16,28},{20,24},{1,21},{... | collective-permute-start | bytes 393224 | tf_op jit(solution)/shard_map/ppermute | solution.py:308
  269.6 14.4 %collective-permute-start.31 = (bf16[64,1024]{1,0:T(8,128)(2,1)S(1)}, bf16[64,1024]{1,0:T(8,128)(2,1)S(1)}, u32[]{:S(2)}, u32[]{:S(2)}) collective-permute-start(bf16[64,1024]{1,0:T(8,128)(2,1)S(1)} %pad_maximum_fusion.5), channel_id=1, source_target_pairs={{0,24},{4,28},{8,16},{12,20},{24,0},{28,4},{16,8},{20,12},{1,25},{... | collective-permute-start | bytes 393224 | tf_op jit(solution)/shard_map/ppermute | solution.py:308
  281.1 6.2 %collective-permute-start.35 = (bf16[64,1024]{1,0:T(8,128)(2,1)}, bf16[64,1024]{1,0:T(8,128)(2,1)S(1)}, u32[]{:S(2)}, u32[]{:S(2)}) collective-permute-start(bf16[64,1024]{1,0:T(8,128)(2,1)} %get-tuple-element.271), channel_id=1, source_target_pairs={{0,1},{1,0},{2,3},{3,2},{4,5},{5,4},{6,7},{7,6},{8,9},{9,8},{10,11... | collective-permute-start | bytes 393224 | tf_op jit(solution)/shard_map/ppermute | solution.py:227
  282.5 8.2 %collective-permute-start.36 = (bf16[64,1024]{1,0:T(8,128)(2,1)}, bf16[64,1024]{1,0:T(8,128)(2,1)S(1)}, u32[]{:S(2)}, u32[]{:S(2)}) collective-permute-start(bf16[64,1024]{1,0:T(8,128)(2,1)} %get-tuple-element.272), channel_id=1, source_target_pairs={{0,2},{1,3},{2,0},{3,1},{4,6},{5,7},{6,4},{7,5},{8,10},{9,11},{10,... | collective-permute-start | bytes 393224 | tf_op jit(solution)/shard_map/ppermute | solution.py:227
  284.0 6.7 %collective-permute-start.37 = (bf16[64,1024]{1,0:T(8,128)(2,1)}, bf16[64,1024]{1,0:T(8,128)(2,1)S(1)}, u32[]{:S(2)}, u32[]{:S(2)}) collective-permute-start(bf16[64,1024]{1,0:T(8,128)(2,1)} %get-tuple-element.273), channel_id=1, source_target_pairs={{0,3},{1,2},{2,1},{3,0},{4,7},{5,6},{6,5},{7,4},{8,11},{9,10},{10,... | collective-permute-start | bytes 393224 | tf_op jit(solution)/shard_map/ppermute | solution.py:227
  287.3 6.6 %collective-permute-start.32 = (bf16[64,1024]{1,0:T(8,128)(2,1)S(1)}, bf16[64,1024]{1,0:T(8,128)(2,1)S(1)}, u32[]{:S(2)}, u32[]{:S(2)}) collective-permute-start(bf16[64,1024]{1,0:T(8,128)(2,1)S(1)} %pad_maximum_fusion.6), channel_id=1, source_target_pairs={{0,28},{4,24},{8,20},{12,16},{24,4},{28,0},{16,12},{20,8},{1,29},{... | collective-permute-start | bytes 393224 | tf_op jit(solution)/shard_map/ppermute | solution.py:308
  291.7 5.9 %collective-permute-start.38 = (bf16[32,1024]{1,0:T(8,128)(2,1)S(1)}, bf16[32,1024]{1,0:T(8,128)(2,1)S(1)}, u32[]{:S(2)}, u32[]{:S(2)}) collective-permute-start(bf16[32,1024]{1,0:T(8,128)(2,1)S(1)} %get-tuple-element.431), channel_id=1, source_target_pairs={{0,8},{4,12},{8,24},{12,28},{24,16},{28,20},{16,0},{20,4},{1,9},{5... | collective-permute-start | bytes 196616 | tf_op jit(solution)/shard_map/ppermute | solution.py:308
  294.6 5.6 %collective-permute-start.40 = (bf16[32,1024]{1,0:T(8,128)(2,1)S(1)}, bf16[32,1024]{1,0:T(8,128)(2,1)S(1)}, u32[]{:S(2)}, u32[]{:S(2)}) collective-permute-start(bf16[32,1024]{1,0:T(8,128)(2,1)S(1)} %get-tuple-element.430), channel_id=1, source_target_pairs={{0,12},{4,8},{8,28},{12,24},{24,20},{28,16},{16,4},{20,0},{1,13},{... | collective-permute-start | bytes 196616 | tf_op jit(solution)/shard_map/ppermute | solution.py:308
  302.8 3.6 %copy-start.11 = (f32[16,1,128]{2,1,0:T(1,128)S(1)}, f32[16,1,128]{2,1,0:T(1,128)}, u32[]{:S(2)}) copy-start(f32[16,1,128]{2,1,0:T(1,128)} %get-tuple-element.280) | copy-start | bytes 24580
  302.9 28.0 %collective-permute-start.43 = (bf16[2,64,1024]{2,1,0:T(8,128)(2,1)S(1)}, bf16[2,64,1024]{2,1,0:T(8,128)(2,1)S(1)}, u32[]{:S(2)}, u32[]{:S(2)}) collective-permute-start(bf16[2,64,1024]{2,1,0:T(8,128)(2,1)S(1)} %get-tuple-element.413), channel_id=1, source_target_pairs={{0,3},{1,2},{2,1},{3,0},{4,7},{5,6},{6,5},{7,4},{8,11},{9,10},{10,... | collective-permute-start | bytes 786440 | tf_op jit(solution)/shard_map/ppermute | solution.py:227
  305.3 25.6 %collective-permute-start.42 = (bf16[2,64,1024]{2,1,0:T(8,128)(2,1)S(1)}, bf16[2,64,1024]{2,1,0:T(8,128)(2,1)S(1)}, u32[]{:S(2)}, u32[]{:S(2)}) collective-permute-start(bf16[2,64,1024]{2,1,0:T(8,128)(2,1)S(1)} %get-tuple-element.414), channel_id=1, source_target_pairs={{0,2},{1,3},{2,0},{3,1},{4,6},{5,7},{6,4},{7,5},{8,10},{9,11},{10,... | collective-permute-start | bytes 786440 | tf_op jit(solution)/shard_map/ppermute | solution.py:227
  305.8 25.1 %collective-permute-start.41 = (bf16[2,64,1024]{2,1,0:T(8,128)(2,1)S(1)}, bf16[2,64,1024]{2,1,0:T(8,128)(2,1)S(1)}, u32[]{:S(2)}, u32[]{:S(2)}) collective-permute-start(bf16[2,64,1024]{2,1,0:T(8,128)(2,1)S(1)} %get-tuple-element.415), channel_id=1, source_target_pairs={{0,1},{1,0},{2,3},{3,2},{4,5},{5,4},{6,7},{7,6},{8,9},{9,8},{10,11... | collective-permute-start | bytes 786440 | tf_op jit(solution)/shard_map/ppermute | solution.py:227
  307.3 8.7 %all-to-all-start.2 = ((f32[8,1,16]{2,1,0:T(1,128)}), f32[8,1,16]{2,1,0:T(1,128)S(1)}, u32[]{:S(2)}, u32[]{:S(2)}) async-start(f32[8,1,16]{2,1,0:T(1,128)} %bitcast.27), calls=%async_computation.2 | async-start | bytes 8192 | tf_op jit(solution)/shard_map/all_to_all | solution.py:201

commit v3 on v2

--- a/solution.py
+++ b/solution.py
@@ -10,7 +10,8 @@
 
 NT = (((1,), (1,)), ((), ()))
 TN = (((0,), (0,)), ((), ()))
-VMEM_LIMIT = 56 * 1024 * 1024
+MIB = 1024 * 1024
+VMEM_LIMIT = 56 * MIB
 SHADE = 20
 
 
@@ -77,7 +78,8 @@
 
 
 def input_grad_body(count, place_ref, *refs):
-    grad_refs, weight_refs, out_refs, low_ref = refs[:count], refs[count:count + 3], refs[count + 3:-1], refs[-1]
+    grad_refs, weight_refs, low_ref = refs[:count], refs[count:count + 3], refs[-1]
+    out_refs = refs[count + 4:-1]
     me = place_ref[place_ref.shape[0] - 1]
     total = None
     for member in range(3):
@@ -95,7 +97,7 @@
         at += size
 
 
-def input_grad(place, grads, weights, pieces):
+def input_grad(place, grads, weights, pieces, ahead):
     rows_in, width = weights[0].shape
     tokens = sum(grad.shape[1] for grad in grads)
     step = 256
@@ -105,26 +107,27 @@
             num_scalar_prefetch=1,
             grid=(rows_in // step,),
             in_specs=[pl.BlockSpec(grad.shape, lambda n, place: (0, 0, 0)) for grad in grads]
-            + [pl.BlockSpec((step, width), lambda n, place: (n, 0))] * 3,
+            + [pl.BlockSpec((step, width), lambda n, place: (n, 0))] * 3
+            + [pl.BlockSpec(memory_space=pl.ANY)],
             out_specs=[pl.BlockSpec((tokens // pieces, step), lambda n, place: (0, n))] * pieces,
             scratch_shapes=[pltpu.VMEM((tokens, step), jnp.bfloat16)],
         ),
         out_shape=[jax.ShapeDtypeStruct((tokens // pieces, rows_in), jnp.bfloat16)] * pieces,
-        compiler_params=pltpu.CompilerParams(vmem_limit_bytes=VMEM_LIMIT),
+        compiler_params=pltpu.CompilerParams(vmem_limit_bytes=8 * MIB + 14 * tokens * width + 12 * step * width),
         cost_estimate=pl.CostEstimate(
             flops=6 * tokens * rows_in * width // SHADE,
             bytes_accessed=6 * width * (rows_in + tokens) // SHADE,
             transcendentals=0,
         ),
         name="input_grad",
-    )(place, *grads, *weights)
+    )(place, *grads, *weights, ahead)
 
 
 def weight_grad_body(pieces, units, has_acc, place_ref, *refs):
     count = len(units)
     x_refs, grad_refs = refs[:pieces], refs[pieces:pieces + count]
     acc_refs, out_refs, left_ref = refs[pieces + count:-4], refs[-4:-1], refs[-1]
-    features = x_refs[0].shape[1]
+    features = x_refs[0].shape[2]
 
     @pl.when(pl.program_id(0) == 0)
     def _():
@@ -133,7 +136,8 @@
             size = grad_refs[at].shape[1]
             for apart, x_ref in enumerate(x_refs):
                 rows = pl.ds(pl.multiple_of((me ^ apart) * features, features), features)
-                left_ref[rows, at * size:(at + 1) * size] = x_ref[place_ref[2 * hop + which], :, index * size:(index + 1) * size]
+                part = x_ref[place_ref[2 * hop + which], index * size:(index + 1) * size, :]
+                left_ref[rows, at * size:(at + 1) * size] = part.T
 
     for member in range(3):
         right = jnp.concatenate([ref[member] for ref in grad_refs], axis=0)
@@ -144,11 +148,11 @@
 
 
 def weight_grad(place, x, units, grads, acc):
-    canvases, features, length = x[0].shape
+    canvases, length, features = x[0].shape
     rows_in = len(x) * features
     size, width = grads[0].shape[1:]
     tokens = size * len(grads)
-    step = 512
+    step = min(width, 512 if len(grads) > 2 else 1024)
     block = pl.BlockSpec((rows_in, step), lambda n, place: (0, n))
     acc = tuple(acc) if acc is not None else ()
     return pl.pallas_call(
@@ -163,7 +167,7 @@
             scratch_shapes=[pltpu.VMEM((rows_in, tokens), jnp.bfloat16)],
         ),
         out_shape=[jax.ShapeDtypeStruct((rows_in, width), jnp.bfloat16)] * 3,
-        compiler_params=pltpu.CompilerParams(vmem_limit_bytes=VMEM_LIMIT),
+        compiler_params=pltpu.CompilerParams(vmem_limit_bytes=12 * MIB + 12 * tokens * step + 4 * rows_in * tokens + rows_in * step * (32 if acc else 20)),
         cost_estimate=pl.CostEstimate(
             flops=6 * tokens * rows_in * width // SHADE,
             bytes_accessed=6 * width * (tokens + rows_in * (2 if acc else 1)) // SHADE,
@@ -171,6 +175,34 @@
         ),
         name="weight_grad",
     )(place, *x, *grads, *acc)
+
+
+def sort_home_body(count, place_ref, *refs):
+    part_refs, out_refs, held_ref = refs[:count], refs[count:-1], refs[-1]
+    for step, ref in enumerate(part_refs):
+        held_ref[2 * step:2 * step + 2] = ref[...]
+    spread = out_refs[0].shape[0]
+    for d, out_ref in enumerate(out_refs):
+        for n in range(spread):
+            out_ref[n] = held_ref[place_ref[2 * count + d * spread + n]]
+
+
+def sort_home(place, parts, pieces, spread):
+    _, tokens, rows_in = parts[0].shape
+    return pl.pallas_call(
+        functools.partial(sort_home_body, len(parts)),
+        grid_spec=pltpu.PrefetchScalarGridSpec(
+            num_scalar_prefetch=1,
+            grid=(1,),
+            in_specs=[pl.BlockSpec(part.shape, lambda n, place: (0, 0, 0)) for part in parts],
+            out_specs=[pl.BlockSpec((spread, tokens, rows_in), lambda n, place: (0, 0, 0))] * pieces,
+            scratch_shapes=[pltpu.VMEM((2 * len(parts), tokens, rows_in), jnp.bfloat16)],
+        ),
+        out_shape=[jax.ShapeDtypeStruct((spread, tokens, rows_in), jnp.bfloat16)] * pieces,
+        compiler_params=pltpu.CompilerParams(vmem_limit_bytes=24 * MIB),
+        cost_estimate=pl.CostEstimate(flops=0, bytes_accessed=4 * pieces * spread * tokens * rows_in, transcendentals=0),
+        name="sort_home",
+    )(place, *parts)
 
 
 def ring_order(chips):
@@ -190,12 +222,16 @@
     order = ring_order(chips)
     ring = [(2 * order[n] + core, 2 * order[(n + 1) % chips] + core) for n in range(chips) for core in range(2)]
     swap = [(n, n ^ 1) for n in range(row_count)]
-    place_of = [order.index(chip) for chip in range(chips)]
-    me = lax.axis_index("row")
-    my_core = me % 2
-    my_place = jnp.array(place_of, jnp.int32)[me // 2]
-    chips_at = jnp.array(order, jnp.int32)[(my_place - jnp.arange(chips)) % chips]
-    origin = chips_at[:, None] * 2 + (my_core + jnp.arange(2)[None, :]) % 2
+    table = []
+    for row in range(row_count):
+        for col in range(col_count):
+            at, core = order.index(row // 2), row % 2
+            origin = [2 * order[(at - step) % chips] + (core ^ which) for step in range(chips) for which in range(2)]
+            slot = [2 * ((order.index(r // 2) - at) % chips) + (r % 2 ^ core) for r in range(row_count)]
+            slot = [slot[(col ^ d) * spread + n] for d in range(col_count) for n in range(spread)]
+            table.append(origin + slot + [col])
+    my_col = lax.axis_index("col")
+    place = jnp.array(table, jnp.int32)[lax.axis_index("row") * col_count + my_col]
 
     def a2a(array, axis):
         return lax.all_to_all(array, axis, split_axis=0, concat_axis=0, tiled=True)
@@ -213,7 +249,6 @@
 
         return lax.cond(always, work, nothing, *operands)
 
-    place = jnp.concatenate([origin.reshape(-1), lax.axis_index("col")[None]]).astype(jnp.int32)
     every = range(len(sizes))
     last, final = len(sizes) - 1, chips - 1
 
@@ -226,14 +261,23 @@
     def across(mine, apart):
         return lax.ppermute(mine, "col", [(n, n ^ apart) for n in range(col_count)])
 
-    def partial_of(given):
-        return input_grad(place, [member for pair in given for member in pair], weights, col_count)
-
-    def summed(partial):
-        total = partial[0].astype(jnp.float32)
-        for apart in range(1, col_count):
-            total = total + across(partial[apart], apart).astype(jnp.float32)
-        return total.astype(jnp.bfloat16)
+    def partial_of(given, ahead=None):
+        ahead = given[-1][1] if ahead is None else ahead
+        return input_grad(place, [member for pair in given for member in pair], weights, col_count, ahead)
+
+    def summed(partial, beside=()):
+        parts = after([across(partial[d], d) if d else partial[d] for d in range(col_count)], beside)
+        return sum(part.astype(jnp.float32) for part in parts).astype(jnp.bfloat16)
+
+    def shared(total, chunks_in):
+        mine, theirs = [], []
+        at = 0
+        for size in chunks_in:
+            size = size // col_count
+            mine.append(total[at:at + size])
+            theirs.append(total[at + size:at + 2 * size])
+            at += 2 * size
+        return jnp.stack([jnp.concatenate(mine, axis=0), other(jnp.concatenate(theirs, axis=0))])
 
     def weight_part(x, units, given, acc):
         places = [(step, core, index) for step, index in units for core in range(2)]
@@ -250,9 +294,10 @@
     def own_tokens(layer_input, *chunks):
         blocks = layer_input.reshape(length, spread, col_count, rows_in // col_count)
         x = a2a(jnp.transpose(blocks, (2, 1, 0, 3)), "col").reshape(row_count, length, rows_in // col_count)
-        x = jnp.swapaxes(a2a(x, "row"), 1, 2)
         theirs = [other(chunk) for chunk in chunks]
-        return theirs, summed(partial_of(list(zip(chunks, theirs)))), x
+        partial = partial_of(list(zip(chunks, theirs)))
+        x = a2a(after(x, partial[0]), "row")
+        return theirs, shared(summed(partial), sizes), x
 
     arrived[1][0] = hop(chunks[0])
     others[0], sums[0], x = window(own_tokens, layer_input, *chunks)
@@ -268,14 +313,17 @@
             if step == 1:
                 return theirs, [across(x, apart) for apart in range(1, col_count) if apart & (apart - 1) == 0]
             if step == 2:
-                return theirs, weight_part(x, units, done, None), summed(partial)
-            return (theirs,)
+                acc = weight_part(x, units, done, None)
+                return theirs, shared(summed(partial, acc[0]), sizes), acc
+            return theirs, shared(partial, sizes)
 
         others[step][0], *given = window(early, arrived[step][0], x, [both(*unit) for unit in units], sums[step - 1])
         if step == 1:
             x_pieces.update(zip([apart for apart in range(1, col_count) if apart & (apart - 1) == 0], given[0]))
         elif step == 2:
-            weight_grads, sums[1] = given
+            sums[1], weight_grads = given
+        else:
+            (sums[step - 1],) = given
         arrived[step + 1][0] = hop(after(arrived[step][0], others[step][0]))
 
         def late(mine, x, sooner, acc):
@@ -284,7 +332,8 @@
             partial = partial_of(given)
             if step == 1:
                 return theirs, partial, [across(x, apart) for apart in range(1, col_count) if apart & (apart - 1)]
-            return theirs, summed(partial), weight_part(x, [(step, spot) for spot in every], given, acc)
+            acc = weight_part(x, [(step, spot) for spot in every], given, acc)
+            return theirs, summed(partial, acc[0]), acc
 
         others[step][last], sums[step], given = window(late, arrived[step][last], x, both(step, 0), weight_grads)
         if step == 1:
@@ -294,59 +343,41 @@
             weight_grads = given
         arrived[step + 1][last] = hop(after(arrived[step][last], others[step][last]))
 
-    def before_last(mine):
+    def before_last(mine, x, acc, total):
         theirs = other(mine)
-        return theirs, summed(partial_of([(mine, theirs)]))
-
-    others[final][0], final_sums = window(before_last, after(arrived[final][0], others[final - 1][last]))
-
-    def homeward(mine, step, which):
-        route = []
-        for n in range(chips):
-            for core in range(2):
-                route.append((2 * order[n] + core, 2 * order[(n - step) % chips] + (core ^ which)))
-        return lax.ppermute(mine, "row", route) if step or which else mine
-
-    def pieces_of(step):
-        parts = [[], []]
-        at = 0
-        for size in sizes[:last] if step == final else sizes:
-            for which in range(2):
-                parts[which].append(sums[step][at:at + size // col_count])
-                at += size // col_count
-        return [jnp.concatenate(part, axis=0) for part in parts]
-
-    sums[final] = final_sums
+        given = [(mine, theirs)]
+        partial = partial_of(given)
+        acc = weight_part(x, [(final, 0)], given, acc)
+        return theirs, shared(summed(partial, acc[0]), sizes[:last]), acc, shared(total, sizes)
+
+    others[final][0], sooner, weight_grads, sums[final - 1] = window(
+        before_last, after(arrived[final][0], others[final - 1][last]), x, weight_grads, sums[final - 1]
+    )
+
+    def homeward(mine, step):
+        route = [(2 * order[n] + core, 2 * order[(n - step) % chips] + core) for n in range(chips) for core in range(2)]
+        return lax.ppermute(mine, "row", route) if step else mine
+
     landed = after(arrived[final][last], others[final][0])
     others[final][last] = other(landed)
-    sums = after(sums, landed)
-    at_home = [[homeward(part, step, which) for which, part in enumerate(pieces_of(step))] for step in range(final)]
-    sooner = [homeward(part, final, which) for which, part in enumerate(pieces_of(final))]
-    partial = partial_of([(landed, others[final][last])])
-    units = [(final, index) for index in every]
-    total = summed(partial)
-    weight_grads = weight_part(x, units, [both(*unit) for unit in units], weight_grads)
-    size = sizes[last] // col_count
-    later = [homeward(total[which * size:(which + 1) * size], final, which) for which in range(2)]
-    at_home.append([jnp.concatenate(parts, axis=0) for parts in zip(sooner, later)])
-    mine = jnp.stack([part for parts in at_home for part in parts])
-    rows = jnp.arange(row_count)
-    slot = ((jnp.array(place_of, jnp.int32)[rows // 2] - my_place) % chips) * 2 + (rows + my_core) % 2
-    my_col = lax.axis_index("col")
-    apart = my_col ^ jnp.arange(col_count)
-    slot = slot.reshape(col_count, spread)[apart].reshape(-1)
-    mine = jnp.take(mine, slot, axis=0).reshape((col_count, spread) + mine.shape[1:])
-    got = jnp.stack([across(mine[d], d) if d else mine[d] for d in range(col_count)])
-    got = jnp.take(got, apart, axis=0)
+    sums, sooner = after((sums, sooner), landed)
+    at_home = [homeward(sums[step], step) for step in range(final)]
+    total = summed(partial_of([(landed, others[final][last])], others[final][0]), at_home)
+    at_home.append(homeward(jnp.concatenate([sooner, shared(total, sizes[last:])], axis=1), final))
+    mine = sort_home(place, at_home, col_count, spread)
+    got = [across(mine[d], d) if d else mine[d] for d in range(col_count)]
+    weight_grads = weight_part(after(x, mine), [(final, last)], [both(final, last)], weight_grads)
+    got = jnp.take(jnp.stack(got), my_col ^ jnp.arange(col_count), axis=0)
     home = []
     at = 0
     for chunk in sizes:
         size = chunk // col_count
         home.append(jnp.transpose(got[:, :, at:at + size], (0, 2, 1, 3)).reshape(chunk, spread * rows_in))
         at += size
-    bias_all = a2a(after(jnp.broadcast_to(bias_part[None], (row_count,) + bias_part.shape), mine), "row")
     layer_grad = jnp.concatenate(home, axis=0)
-    return (layer_grad, *weight_grads, jnp.sum(bias_all, axis=0))
+    bias_all = a2a(after(jnp.broadcast_to(bias_part[None], (row_count,) + bias_part.shape), mine[0]), "row")
+    bias_grad = jnp.sum(after(bias_all, weight_grads[0]), axis=0)
+    return (layer_grad, *weight_grads, bias_grad)
 
 
 def solution(mesh):

time: 335 us -> 306 us (0.913)
  local copies, waits for them, and re-layouts: 27.2 us -> 6.66 us
  other arithmetic: 11.7 us -> 7.66 us
  starting transfers between devices: 58.7 us -> 54.8 us
    another operation x4 -> x2, local copies, waits for them, and re-layouts: 9.05 us -> 0.02 us  [shared(): jnp.stack([jnp.concatenate(mine, axis=0), other(jnp.concatenate(theirs, a...]
    ppermute x21, waiting for transfers between devices: 59.5 us -> 50.5 us  [across(): return lax.ppermute(mine, 'col', [(n, n ^ apart) for n in range(col_count)])]
    ppermute x9 -> x3, starting transfers between devices: 10.5 us -> 4.86 us  [homeward(): return lax.ppermute(mine, 'row', route) if step else mine]
    ppermute x8 -> x13, waiting for transfers between devices: 7.29 us -> 12 us  [other(): return lax.ppermute(mine, 'row', swap)]
    convert_element_type x5, other arithmetic: 5.34 us -> 1.56 us  [summed(): sum((part.astype(jnp.float32) for part in parts)).astype(jnp.bfloat16)]
    gather x5 -> x1, local copies, waits for them, and re-layouts: 4.29 us -> 0.61 us  [local(): got = jnp.take(jnp.stack(got), my_col ^ jnp.arange(col_count), axis=0)]
    all_to_all x3, waiting for transfers between devices: 18.5 us -> 15.1 us  [a2a(): return lax.all_to_all(array, axis, split_axis=0, concat_axis=0, tiled=True)]
    pallas_call x3 -> x4, Pallas kernels: 48.6 us -> 51.6 us  [weight_grad(): pl.pallas_call(functools.partial(weight_grad_body, len(x), tuple(units),...]
  transfers between devices with their start and end apart: 47 -> 46, of which waited for: 21 -> 22; matrix products, arithmetic and copies ran while one was open for 10% -> 3% of each run, Pallas kernels for 32% -> 35%
where the time goes in v3:
time: 306 us
  Pallas kernels  120 us (39%)
  waiting for transfers between devices  114 us (37%)
  starting transfers between devices  54.8 us (18%)
  other arithmetic  7.66 us (3%)
  local copies, waits for them, and re-layouts  6.66 us (2%)
    pallas_call x5, Pallas kernels, input_grad(): pl.pallas_call(functools.partial(input_grad_body, len(grads)), grid_spec=...  55.2 us
    pallas_call x4, Pallas kernels, weight_grad(): pl.pallas_call(functools.partial(weight_grad_body, len(x), tuple(units),...  51.6 us
    ppermute x21, waiting for transfers between devices, across(): return lax.ppermute(mine, 'col', [(n, n ^ apart) for n in range(col_count)])  50.5 us
    ppermute x6, waiting for transfers between devices, hop(): return lax.ppermute(mine, 'row', ring)  27.8 us
    ppermute x21, starting transfers between devices, across(): return lax.ppermute(mine, 'col', [(n, n ^ apart) for n in range(col_count)])  26.7 us
    all_to_all x3, waiting for transfers between devices, a2a(): return lax.all_to_all(array, axis, split_axis=0, concat_axis=0, tiled=True)  15.1 us
    all_to_all x3, starting transfers between devices, a2a(): return lax.all_to_all(array, axis, split_axis=0, concat_axis=0, tiled=True)  13.2 us
    pallas_call x1, Pallas kernels, attention(): pl.pallas_call(functools.partial(attention_body, sizes, head_dim, heads_s...  12.1 us
  transfers between devices with their start and end apart: 46, of which 22 were waited for; matrix products, arithmetic and copies ran while one was open for 3% of the time, Pallas kernels for 35%

profile of v3, /device:TPU:0, one launch (start us, length us, event | category | flops | bytes accessed | tf_op | source)
XLA Modules:
  0.0 305.8 jit_solution(7152832322403756041)
XLA Ops:
  0.6 12.1 %attention_back.1 = (bf16[3,128,2048]{2,1,0:T(8,128)(2,1)}, bf16[3,128,2048]{2,1,0:T(8,128)(2,1)}, f32[16,1,128]{2,1,0:T(1,128)}) custom-call(f32[16]{0:T(128)} %bias_ref.1, s32[1,256]{1,0:T(1,128)} %flag_ref.1, bf16[256,2048]{1,0:T(8,128)(2,1)} %bitcast.49, bf16[256,2048]{1,0:T(8,128)(2,1)} %bitcast.50, bf16[256,2048]{1,0:T(8,128)(2,1)} %bitcast.51, ...), custom_call_target="tpu_custom_call" | custom-call | flops 67108864 | bytes 367001 | tf_op jit(solution)/shard_map/attention_back/pallas_call | solution.py:57
  12.8 3.0 collective-permute-start.26
  17.8 56.3 %conditional.6 = (bf16[3,128,2048]{2,1,0:T(8,128)(2,1)}, bf16[3,128,2048]{2,1,0:T(8,128)(2,1)S(1)}, bf16[2,64,1024]{2,1,0:T(8,128)(2,1)S(1)}, bf16[8,256,256]{2,1,0:T(8,128)(2,1)}) conditional(s32[]{:T(128)} %convert_element_type.83, () %tuple.73, (bf16[3,128,2048]{2,1,0:T(8,128)(2,1)}, bf16[3,128,2048]{2,1,0:T(8,128)(2,1)}, s32[17]{0:T(128)S(1)}, ...), branch_computations={%region_1.0_spmd, %region_2.0_spmd} | conditional | flops 323826496 | bytes 43149296 | solution.py:250
  18.4 1.8 reshape.42
  20.2 1.2 copy.28
  21.4 4.3 %all-to-all-start = ((bf16[4,2,256,256]{3,2,1,0:T(8,128)(2,1)}), bf16[4,2,256,256]{3,2,1,0:T(8,128)(2,1)}, u32[]{:S(2)}, u32[]{:S(2)}) async-start(bf16[4,2,256,256]{3,2,1,0:T(8,128)(2,1)} %bitcast.43), calls=%async_computation | async-start | bytes 2097152 | tf_op jit(solution)/shard_map/cond/branch_1_fun/all_to_all | solution.py:237
  25.7 11.8 %input_grad.5 = (bf16[128,1024]{1,0:T(8,128)(2,1)S(1)}, bf16[128,1024]{1,0:T(8,128)(2,1)S(1)}, bf16[128,1024]{1,0:T(8,128)(2,1)S(1)}, bf16[128,1024]{1,0:T(8,128)(2,1)S(1)}) custom-call(s32[17]{0:T(128)S(1)} %get-tuple-element.126.place_ref, bf16[3,128,2048]{2,1,0:T(8,128)(2,1)} %get-tuple-element.124.refs_0_, ...), custom_call_target="tpu_custom_call" | custom-call | flops 322122560 | bytes 943718 | tf_op jit(solution)/shard_map/cond/branch_1_fun/input_grad/pallas_call | solution.py:104
  37.5 2.4 all-to-all-done
  39.9 4.4 %all-to-all-start.1 = ((bf16[8,256,256]{2,1,0:T(8,128)(2,1)}), bf16[8,256,256]{2,1,0:T(8,128)(2,1)}, u32[]{:S(2)}, u32[]{:S(2)}) async-start(bf16[8,256,256]{2,1,0:T(8,128)(2,1)} %bitcast.3), calls=%async_computation.1 | async-start | bytes 2097152 | tf_op jit(solution)/shard_map/cond/branch_1_fun/all_to_all | solution.py:237
  44.3 1.5 collective-permute-start.11
  46.3 1.5 collective-permute-start.13
  47.8 5.6 %collective-permute-done.11 = bf16[128,1024]{1,0:T(8,128)(2,1)S(1)} collective-permute-done((bf16[128,1024]{1,0:T(8,128)(2,1)S(1)}, bf16[128,1024]{1,0:T(8,128)(2,1)S(1)}, u32[]{:S(2)}, u32[]{:S(2)}) %collective-permute-start.11) | collective-permute-done | bytes 262176 | tf_op jit(solution)/shard_map/cond/branch_1_fun/ppermute | solution.py:262
  53.5 6.2 %collective-permute-done.12 = bf16[128,1024]{1,0:T(8,128)(2,1)S(1)} collective-permute-done((bf16[128,1024]{1,0:T(8,128)(2,1)S(1)}, bf16[128,1024]{1,0:T(8,128)(2,1)S(1)}, u32[]{:S(2)}, u32[]{:S(2)}) %collective-permute-start.12) | collective-permute-done | bytes 262176 | tf_op jit(solution)/shard_map/cond/branch_1_fun/ppermute | solution.py:262
  60.0 1.3 collective-permute-done.14
  61.3 12.7 %all-to-all-done.1 = bf16[8,256,256]{2,1,0:T(8,128)(2,1)} async-done(((bf16[8,256,256]{2,1,0:T(8,128)(2,1)}), bf16[8,256,256]{2,1,0:T(8,128)(2,1)}, u32[]{:S(2)}, u32[]{:S(2)}) %all-to-all-start.1) | async-done | bytes 1048608 | tf_op jit(solution)/shard_map/cond/branch_1_fun/all_to_all | solution.py:237
  74.9 27.1 %conditional.7 = (bf16[3,128,2048]{2,1,0:T(8,128)(2,1)}, bf16[8,256,256]{2,1,0:T(8,128)(2,1)}, bf16[8,256,256]{2,1,0:T(8,128)(2,1)}) conditional(s32[]{:T(128)} %convert_element_type.83, () %tuple.76, (bf16[3,128,2048]{2,1,0:T(8,128)(2,1)}, bf16[8,256,256]{2,1,0:T(8,128)(2,1)}) %tuple.77), branch_computations={%region_3.0_spmd, %region_4.0_spmd} | conditional | bytes 14680208 | solution.py:250
  74.9 1.5 collective-permute-start.2
  76.4 1.5 collective-permute-start.1
  77.9 22.9 %collective-permute-done.2 = bf16[8,256,256]{2,1,0:T(8,128)(2,1)} collective-permute-done((bf16[8,256,256]{2,1,0:T(8,128)(2,1)}, bf16[8,256,256]{2,1,0:T(8,128)(2,1)}, u32[]{:S(2)}, u32[]{:S(2)}) %collective-permute-start.2) | collective-permute-done | bytes 1048608 | tf_op jit(solution)/shard_map/cond/branch_1_fun/ppermute | solution.py:262
  100.8 1.2 collective-permute-done.1
  102.0 3.4 %collective-permute-start.27 = (bf16[3,128,2048]{2,1,0:T(8,128)(2,1)}, bf16[3,128,2048]{2,1,0:T(8,128)(2,1)}, u32[]{:S(2)}, u32[]{:S(2)}) collective-permute-start(bf16[3,128,2048]{2,1,0:T(8,128)(2,1)} %collective-permute-done.26), channel_id=1, source_target_pairs={{0,8},{4,12},{8,24},{12,28},{24,16},{28,20},{16,0},{20,4},{1,9},{5... | collective-permute-start | bytes 4718600 | tf_op jit(solution)/shard_map/ppermute | solution.py:256
  105.4 7.2 %collective-permute-done.28 = bf16[3,128,2048]{2,1,0:T(8,128)(2,1)} collective-permute-done((bf16[3,128,2048]{2,1,0:T(8,128)(2,1)}, bf16[3,128,2048]{2,1,0:T(8,128)(2,1)}, u32[]{:S(2)}, u32[]{:S(2)}) %collective-permute-start.28) | collective-permute-done | bytes 1572896 | tf_op jit(solution)/shard_map/ppermute | solution.py:256
  112.6 26.8 %conditional.8 = (bf16[3,128,2048]{2,1,0:T(8,128)(2,1)}, bf16[128,1024]{1,0:T(8,128)(2,1)S(1)}, bf16[128,1024]{1,0:T(8,128)(2,1)}, bf16[128,1024]{1,0:T(8,128)(2...) conditional(s32[]{:T(128)} %convert_element_type.83, () %tuple.79, (bf16[3,128,2048]{2,1,0:T(8,128)(2,1)}, ...), branch_computations={%region_5.0_spmd, %region_6.0_spmd} | conditional | flops 322122560 | bytes 11429606 | solution.py:250
  112.6 2.5 collective-permute-start.4
  115.1 1.3 collective-permute-done.3.refs_3_.refs_7_
  116.4 12.9 %input_grad.6 = (bf16[128,1024]{1,0:T(8,128)(2,1)S(1)}, bf16[128,1024]{1,0:T(8,128)(2,1)}, bf16[128,1024]{1,0:T(8,128)(2,1)}, bf16[128,1024]{1,0:T(8,128)(2,1)}) custom-call(s32[17]{0:T(128)S(1)} %get-tuple-element.143.place_ref, bf16[3,128,2048]{2,1,0:T(8,128)(2,1)} %get-tuple-element.144.refs_0_, bf16[3,128,2048]{2,1,0:T(8,128)(2,1)} %get-tuple-element.145.refs_1_, ...), custom_call_target="tpu_custom_call" | custom-call | flops 322122560 | bytes 943718 | tf_op jit(solution)/shard_map/cond/branch_1_fun/input_grad/pallas_call | solution.py:104
  129.2 10.2 %collective-permute-done.4 = bf16[8,256,256]{2,1,0:T(8,128)(2,1)} collective-permute-done((bf16[8,256,256]{2,1,0:T(8,128)(2,1)}, bf16[8,256,256]{2,1,0:T(8,128)(2,1)}, u32[]{:S(2)}, u32[]{:S(2)}) %collective-permute-start.4) | collective-permute-done | bytes 1048608 | tf_op jit(solution)/shard_map/cond/branch_1_fun/ppermute | solution.py:262
  140.2 5.9 %collective-permute-done.27 = bf16[3,128,2048]{2,1,0:T(8,128)(2,1)} collective-permute-done((bf16[3,128,2048]{2,1,0:T(8,128)(2,1)}, bf16[3,128,2048]{2,1,0:T(8,128)(2,1)}, u32[]{:S(2)}, u32[]{:S(2)}) %collective-permute-start.27) | collective-permute-done | bytes 1572896 | tf_op jit(solution)/shard_map/ppermute | solution.py:256
  146.1 24.3 %conditional.9 = (bf16[3,128,2048]{2,1,0:T(8,128)(2,1)}, bf16[2,64,1024]{2,1,0:T(8,128)(2,1)S(1)}, bf16[1024,2048]{1,0:T(8,128)(2,1)}, bf16[1024,2048]{1,0:T(8,128)(2,1)}, bf16[1024,2048]{1,0:T(8,128)(2,1)}) conditional(s32[]{:T(128)} %convert_element_type.83, () %tuple.75, (bf16[3,128,2048]{2,1,0:T(8,128)(2,1)}, bf16[128,1024]{1,0:T(8,128)(2,1)}, ...), branch_computations={%region_7.0_spmd, %region_8.0_spmd} | conditional | flops 645949056 | bytes 14417970 | solution.py:250
  147.0 1.5 collective-permute-start.17
  148.5 1.1 collective-permute-start.18
  149.6 19.1 %weight_grad.4 = (bf16[1024,2048]{1,0:T(8,128)(2,1)}, bf16[1024,2048]{1,0:T(8,128)(2,1)}, bf16[1024,2048]{1,0:T(8,128)(2,1)}) custom-call(s32[17]{0:T(128)S(1)} %get-tuple-element.159.place_ref, bf16[8,256,256]{2,1,0:T(8,128)(2,1)} %get-tuple-element.160.refs_0_, bf16[8,256,256]{2,1,0:T(8,128)(2,1)} %get-tuple-element.161.refs_1_, ...), custom_call_target="tpu_custom_call" | custom-call | flops 644245120 | bytes 1258291 | tf_op jit(solution)/shard_map/cond/branch_1_fun/weight_grad/pallas_call | solution.py:158
  169.1 1.3 collective-permute-done.19
  170.7 9.0 %collective-permute-done.30 = bf16[3,128,2048]{2,1,0:T(8,128)(2,1)S(1)} collective-permute-done((bf16[3,128,2048]{2,1,0:T(8,128)(2,1)}, bf16[3,128,2048]{2,1,0:T(8,128)(2,1)S(1)}, u32[]{:S(2)}, u32[]{:S(2)}) %collective-permute-start.30) | collective-permute-done | bytes 1572896 | tf_op jit(solution)/shard_map/ppermute | solution.py:256
  179.7 32.2 %conditional.10 = (bf16[3,128,2048]{2,1,0:T(8,128)(2,1)}, bf16[128,1024]{1,0:T(8,128)(2,1)S(1)}, bf16[1024,2048]{1,0:T(8,128)(2,1)}, bf16[1024,2048]{1,0:T(8,128)(2,1)}, bf16[1024,2048]{1,0:T(8,128)(2,1)}) conditional(s32[]{:T(128)} %convert_element_type.83, () %tuple.85, (bf16[3,128,2048]{2,1,0:T(8,128)(2,1)S(1)}, s32[17]{0:T(128)S(1)}, ...), branch_computations={%region_9.0_spmd, %region_10.0_spmd} | conditional | flops 645293696 | bytes 63596420 | solution.py:250
  179.7 3.5 %collective-permute-done.5.refs_3_.refs_7_ = bf16[3,128,2048]{2,1,0:T(8,128)(2,1)} collective-permute-done((bf16[3,128,2048]{2,1,0:T(8,128)(2,1)S(1)}, bf16[3,128,2048]{2,1,0:T(8,128)(2,1)}, u32[]{:S(2)}, u32[]{:S(2)}) %collective-permute-start.5) | collective-permute-done | bytes 1572896 | tf_op jit(solution)/shard_map/cond/branch_1_fun/ppermute | solution.py:259
  183.3 12.5 %input_grad.7 = (bf16[128,1024]{1,0:T(8,128)(2,1)S(1)}, bf16[128,1024]{1,0:T(8,128)(2,1)S(1)}, bf16[128,1024]{1,0:T(8,128)(2,1)S(1)}, bf16[128,1024]{1,0:T(8,128)(2,1)S(1)}) custom-call(s32[17]{0:T(128)S(1)} %get-tuple-element.180.place_ref, bf16[3,128,2048]{2,1,0:T(8,128)(2,1)} %get-tuple-element.181.refs_0_.refs_4_, ...), custom_call_target="tpu_custom_call" | custom-call | flops 322122560 | bytes 943718 | tf_op jit(solution)/shard_map/cond/branch_1_fun/input_grad/pallas_call | solution.py:104
  196.7 1.5 collective-permute-start.7
  199.3 12.4 %weight_grad.5 = (bf16[1024,2048]{1,0:T(8,128)(2,1)}, bf16[1024,2048]{1,0:T(8,128)(2,1)}, bf16[1024,2048]{1,0:T(8,128)(2,1)}) custom-call(s32[17]{0:T(128)S(1)} %get-tuple-element.180.place_ref, bf16[8,256,256]{2,1,0:T(8,128)(2,1)} %get-tuple-element.190.refs_0_, bf16[8,256,256]{2,1,0:T(8,128)(2,1)} %get-tuple-element.191.refs_1_, ...), custom_call_target="tpu_custom_call" | custom-call | flops 322122560 | bytes 1572864 | tf_op jit(solution)/shard_map/cond/branch_1_fun/weight_grad/pallas_call | solution.py:158
  212.3 30.5 %conditional.11 = (bf16[3,128,2048]{2,1,0:T(8,128)(2,1)}, bf16[2,32,1024]{2,1,0:T(8,128)(2,1)S(1)}, bf16[1024,2048]{1,0:T(8,128)(2,1)}, bf16[1024,2048]{1,0:T(8,...) conditional(s32[]{:T(128)} %convert_element_type.83, () %tuple.83, ...), branch_computations={%region_11.0_spmd, %region_12.0_spmd} | conditional | flops 323367744 | bytes 63937292 | solution.py:250
  213.0 3.1 %collective-permute-done.20.refs_1_.refs_5_ = bf16[3,128,2048]{2,1,0:T(8,128)(2,1)} collective-permute-done((bf16[3,128,2048]{2,1,0:T(8,128)(2,1)}, bf16[3,128,2048]{2,1,0:T(8,128)(2,1)}, u32[]{:S(2)}, u32[]{:S(2)}) %collective-permute-start.20) | collective-permute-done | bytes 1572896 | tf_op jit(solution)/shard_map/cond/branch_1_fun/ppermute | solution.py:259
  216.1 10.4 %input_grad.8 = (bf16[64,1024]{1,0:T(8,128)(2,1)S(1)}, bf16[64,1024]{1,0:T(8,128)(2,1)S(1)}, bf16[64,1024]{1,0:T(8,128)(2,1)S(1)}, bf16[64,1024]{1,0:T(8,128)(2,1)S(1)}) custom-call(s32[17]{0:T(128)S(1)} %get-tuple-element.205.place_ref, bf16[3,128,2048]{2,1,0:T(8,128)(2,1)} %get-tuple-element.204.refs_0_.refs_4_, ...), custom_call_target="tpu_custom_call" | custom-call | flops 161061280 | bytes 786432 | tf_op jit(solution)/shard_map/cond/branch_1_fun/input_grad/pallas_call | solution.py:104
  226.5 1.6 collective-permute-start.21
  228.0 1.5 collective-permute-start.22
  230.1 9.5 %weight_grad.6 = (bf16[1024,2048]{1,0:T(8,128)(2,1)}, bf16[1024,2048]{1,0:T(8,128)(2,1)}, bf16[1024,2048]{1,0:T(8,128)(2,1)}) custom-call(s32[17]{0:T(128)S(1)} %get-tuple-element.205.place_ref, bf16[8,256,256]{2,1,0:T(8,128)(2,1)} %get-tuple-element.213.refs_0_, bf16[8,256,256]{2,1,0:T(8,128)(2,1)} %get-tuple-element.214.refs_1_, ...), custom_call_target="tpu_custom_call" | custom-call | flops 161061280 | bytes 1415577 | tf_op jit(solution)/shard_map/cond/branch_1_fun/weight_grad/pallas_call | solution.py:158
  241.1 1.6 pad_maximum_fusion.4
  242.8 5.7 %collective-permute-done.31.refs_0_.refs_4_ = bf16[3,128,2048]{2,1,0:T(8,128)(2,1)S(1)} collective-permute-done((bf16[3,128,2048]{2,1,0:T(8,128)(2,1)S(1)}, bf16[3,128,2048]{2,1,0:T(8,128)(2,1)S(1)}, u32[]{:S(2)}, u32[]{:S(2)}) %collective-permute-start.31) | collective-permute-done | bytes 1572896 | tf_op jit(solution)/shard_map/ppermute | solution.py:256
  249.5 2.2 collective-permute-start.33
  251.9 7.6 %input_grad.9 = (bf16[64,1024]{1,0:T(8,128)(2,1)S(1)}, bf16[64,1024]{1,0:T(8,128)(2,1)S(1)}, bf16[64,1024]{1,0:T(8,128)(2,1)S(1)}, bf16[64,1024]{1,0:T(8,128)(2,1)S(1)}) custom-call(s32[17]{0:T(128)S(1)} %dynamic-slice_bitcast_fusion.place_ref, bf16[3,128,2048]{2,1,0:T(8,128)(2,1)S(1)} %collective-permute-done.31.refs_0_.refs_4_, ...), custom_call_target="tpu_custom_call" | custom-call | flops 161061280 | bytes 786432 | tf_op jit(solution)/shard_map/input_grad/pallas_call | solution.py:104
  259.5 1.3 collective-permute-start.35
  260.9 1.5 collective-permute-start.36
  263.1 1.3 collective-permute-done.33.refs_2_
  264.4 1.4 collective-permute-done.35
  265.8 3.1 %collective-permute-done.36 = bf16[64,1024]{1,0:T(8,128)(2,1)S(1)} collective-permute-done((bf16[64,1024]{1,0:T(8,128)(2,1)S(1)}, bf16[64,1024]{1,0:T(8,128)(2,1)S(1)}, u32[]{:S(2)}, u32[]{:S(2)}) %collective-permute-start.36) | collective-permute-done | bytes 131104 | tf_op jit(solution)/shard_map/ppermute | solution.py:262
  269.1 1.2 collective-permute-done.38
  270.3 1.7 collective-permute-start.39
  272.0 7.6 %collective-permute-done.39.refs_3_ = bf16[2,64,1024]{2,1,0:T(8,128)(2,1)S(1)} collective-permute-done((bf16[2,64,1024]{2,1,0:T(8,128)(2,1)S(1)}, bf16[2,64,1024]{2,1,0:T(8,128)(2,1)S(1)}, u32[]{:S(2)}, u32[]{:S(2)}) %collective-permute-start.39) | collective-permute-done | bytes 262176 | tf_op jit(solution)/shard_map/ppermute | solution.py:359
  279.6 1.5 sort_home.1
  281.2 1.2 collective-permute-start.40
  283.2 1.4 collective-permute-start.42
  285.5 4.6 %all-to-all-start.2 = ((f32[8,1,16]{2,1,0:T(1,128)}), f32[8,1,16]{2,1,0:T(1,128)S(1)}, u32[]{:S(2)}, u32[]{:S(2)}) async-start(f32[8,1,16]{2,1,0:T(1,128)} %bitcast.24), calls=%async_computation.2 | async-start | bytes 8192 | tf_op jit(solution)/shard_map/all_to_all | solution.py:237
  290.1 10.6 %weight_grad.7 = (bf16[1024,2048]{1,0:T(8,128)(2,1)}, bf16[1024,2048]{1,0:T(8,128)(2,1)}, bf16[1024,2048]{1,0:T(8,128)(2,1)}) custom-call(s32[17]{0:T(128)S(1)} %dynamic-slice_bitcast_fusion.place_ref, bf16[8,256,256]{2,1,0:T(8,128)(2,1)} %get-tuple-element.348.refs_0_, bf16[8,256,256]{2,1,0:T(8,128)(2,1)} %get-tuple-element.349.refs_1_, ...), custom_call_target="tpu_custom_call" | custom-call | flops 161061280 | bytes 1415577 | tf_op jit(solution)/shard_map/weight_grad/pallas_call | solution.py:158
  301.2 1.2 pad_maximum_fusion.7
  304.7 1.1 pad_maximum_fusion.8
  (111 shorter events, 17.8 us)
Async XLA Ops:
  0.6 15.9 %copy-start.12 = (s32[1,256]{1,0:T(1,128)S(1)}, s32[1,256]{1,0:T(1,128)}, u32[]{:S(2)}) copy-start(s32[1,256]{1,0:T(1,128)} %flag_ref.1) | copy-start | bytes 3076
  12.8 62.1 %collective-permute-start.26 = (bf16[3,128,2048]{2,1,0:T(8,128)(2,1)}, bf16[3,128,2048]{2,1,0:T(8,128)(2,1)}, u32[]{:S(2)}, u32[]{:S(2)}) collective-permute-start(bf16[3,128,2048]{2,1,0:T(8,128)(2,1)} %get-tuple-element.297), channel_id=1, source_target_pairs={{0,8},{4,12},{8,24},{12,28},{24,16},{28,20},{16,0},{20,4},{1,9},{5... | collective-permute-start | bytes 4718600 | tf_op jit(solution)/shard_map/ppermute | solution.py:256
  17.8 7.9 %collective-permute-start.9 = (bf16[3,128,2048]{2,1,0:T(8,128)(2,1)}, bf16[3,128,2048]{2,1,0:T(8,128)(2,1)}, u32[]{:S(2)}, u32[]{:S(2)}) collective-permute-start(bf16[3,128,2048]{2,1,0:T(8,128)(2,1)} %get-tuple-element.124.refs_0_), channel_id=1, source_target_pairs={{0,4},{4,0},{8,12},{12,8},{16,20},{20,16},{24,28},{28,24},{1,5},{5... | collective-permute-start | bytes 4718600 | tf_op jit(solution)/shard_map/cond/branch_1_fun/ppermute | solution.py:259
  17.9 7.8 %collective-permute-start.10 = (bf16[3,128,2048]{2,1,0:T(8,128)(2,1)}, bf16[3,128,2048]{2,1,0:T(8,128)(2,1)S(1)}, u32[]{:S(2)}, u32[]{:S(2)}) collective-permute-start(bf16[3,128,2048]{2,1,0:T(8,128)(2,1)} %get-tuple-element.125.refs_2_), channel_id=1, source_target_pairs={{0,4},{4,0},{8,12},{12,8},{16,20},{20,16},{24,28},{28,24},{1,5},{5... | collective-permute-start | bytes 4718600 | tf_op jit(solution)/shard_map/cond/branch_1_fun/ppermute | solution.py:259
  21.4 18.5 %all-to-all-start = ((bf16[4,2,256,256]{3,2,1,0:T(8,128)(2,1)}), bf16[4,2,256,256]{3,2,1,0:T(8,128)(2,1)}, u32[]{:S(2)}, u32[]{:S(2)}) async-start(bf16[4,2,256,256]{3,2,1,0:T(8,128)(2,1)} %bitcast.43), calls=%async_computation | async-start | bytes 2097152 | tf_op jit(solution)/shard_map/cond/branch_1_fun/all_to_all | solution.py:237
  25.7 11.8 %copy-start = (bf16[3,128,2048]{2,1,0:T(8,128)(2,1)}, bf16[3,128,2048]{2,1,0:T(8,128)(2,1)S(1)}, u32[]{:S(2)}) copy-start(bf16[3,128,2048]{2,1,0:T(8,128)(2,1)S(1)} %collective-permute-done.10.refs_3_.refs_7_) | copy-start | bytes 4718596 | tf_op jit(solution)/shard_map/cond
  39.9 34.2 %copy-start.1 = (bf16[3,128,2048]{2,1,0:T(8,128)(2,1)S(1)}, bf16[3,128,2048]{2,1,0:T(8,128)(2,1)}, u32[]{:S(2)}) copy-start(bf16[3,128,2048]{2,1,0:T(8,128)(2,1)} %copy-done) | copy-start | bytes 4718596 | tf_op jit(solution)/shard_map/cond
  39.9 34.1 %all-to-all-start.1 = ((bf16[8,256,256]{2,1,0:T(8,128)(2,1)}), bf16[8,256,256]{2,1,0:T(8,128)(2,1)}, u32[]{:S(2)}, u32[]{:S(2)}) async-start(bf16[8,256,256]{2,1,0:T(8,128)(2,1)} %bitcast.3), calls=%async_computation.1 | async-start | bytes 2097152 | tf_op jit(solution)/shard_map/cond/branch_1_fun/all_to_all | solution.py:237
  44.3 9.2 %collective-permute-start.11 = (bf16[128,1024]{1,0:T(8,128)(2,1)S(1)}, bf16[128,1024]{1,0:T(8,128)(2,1)S(1)}, u32[]{:S(2)}, u32[]{:S(2)}) collective-permute-start(bf16[128,1024]{1,0:T(8,128)(2,1)S(1)} %get-tuple-element.131), channel_id=1, source_target_pairs={{0,1},{1,0},{2,3},{3,2},{4,5},{5,4},{6,7},{7,6},{8,9},{9,8},{10,11... | collective-permute-start | bytes 786440 | tf_op jit(solution)/shard_map/cond/branch_1_fun/ppermute | solution.py:262
  45.8 13.9 %collective-permute-start.12 = (bf16[128,1024]{1,0:T(8,128)(2,1)S(1)}, bf16[128,1024]{1,0:T(8,128)(2,1)S(1)}, u32[]{:S(2)}, u32[]{:S(2)}) collective-permute-start(bf16[128,1024]{1,0:T(8,128)(2,1)S(1)} %get-tuple-element.132), channel_id=1, source_target_pairs={{0,2},{1,3},{2,0},{3,1},{4,6},{5,7},{6,4},{7,5},{8,10},{9,11},{10,... | collective-permute-start | bytes 786440 | tf_op jit(solution)/shard_map/cond/branch_1_fun/ppermute | solution.py:262
  46.3 13.3 %collective-permute-start.13 = (bf16[128,1024]{1,0:T(8,128)(2,1)S(1)}, bf16[128,1024]{1,0:T(8,128)(2,1)S(1)}, u32[]{:S(2)}, u32[]{:S(2)}) collective-permute-start(bf16[128,1024]{1,0:T(8,128)(2,1)S(1)} %get-tuple-element.133), channel_id=1, source_target_pairs={{0,3},{1,2},{2,1},{3,0},{4,7},{5,6},{6,5},{7,4},{8,11},{9,10},{10,... | collective-permute-start | bytes 786440 | tf_op jit(solution)/shard_map/cond/branch_1_fun/ppermute | solution.py:262
  59.9 1.4 collective-permute-start.14
  74.0 38.6 %copy-start.8 = (bf16[2,64,1024]{2,1,0:T(8,128)(2,1)}, bf16[2,64,1024]{2,1,0:T(8,128)(2,1)S(1)}, u32[]{:S(2)}) copy-start(bf16[2,64,1024]{2,1,0:T(8,128)(2,1)S(1)} %get-tuple-element.332.refs_0_) | copy-start | bytes 786436
  74.1 38.5 %collective-permute-start.28 = (bf16[3,128,2048]{2,1,0:T(8,128)(2,1)}, bf16[3,128,2048]{2,1,0:T(8,128)(2,1)}, u32[]{:S(2)}, u32[]{:S(2)}) collective-permute-start(bf16[3,128,2048]{2,1,0:T(8,128)(2,1)} %get-tuple-element.304), channel_id=1, source_target_pairs={{0,8},{4,12},{8,24},{12,28},{24,16},{28,20},{16,0},{20,4},{1,9},{5... | collective-permute-start | bytes 4718600 | tf_op jit(solution)/shard_map/ppermute | solution.py:256
  74.9 27.1 %collective-permute-start = (bf16[3,128,2048]{2,1,0:T(8,128)(2,1)}, bf16[3,128,2048]{2,1,0:T(8,128)(2,1)}, u32[]{:S(2)}, u32[]{:S(2)}) collective-permute-start(bf16[3,128,2048]{2,1,0:T(8,128)(2,1)} %get-tuple-element.140), channel_id=1, source_target_pairs={{0,4},{4,0},{8,12},{12,8},{16,20},{20,16},{24,28},{28,24},{1,5},{5... | collective-permute-start | bytes 4718600 | tf_op jit(solution)/shard_map/cond/branch_1_fun/ppermute | solution.py:259
  74.9 25.9 %collective-permute-start.2 = (bf16[8,256,256]{2,1,0:T(8,128)(2,1)}, bf16[8,256,256]{2,1,0:T(8,128)(2,1)}, u32[]{:S(2)}, u32[]{:S(2)}) collective-permute-start(bf16[8,256,256]{2,1,0:T(8,128)(2,1)} %get-tuple-element.141), channel_id=1, source_target_pairs={{0,2},{1,3},{2,0},{3,1},{4,6},{5,7},{6,4},{7,5},{8,10},{9,11},{10,... | collective-permute-start | bytes 3145736 | tf_op jit(solution)/shard_map/cond/branch_1_fun/ppermute | solution.py:262
  76.4 25.6 %collective-permute-start.1 = (bf16[8,256,256]{2,1,0:T(8,128)(2,1)}, bf16[8,256,256]{2,1,0:T(8,128)(2,1)}, u32[]{:S(2)}, u32[]{:S(2)}) collective-permute-start(bf16[8,256,256]{2,1,0:T(8,128)(2,1)} %get-tuple-element.141), channel_id=1, source_target_pairs={{0,1},{1,0},{2,3},{3,2},{4,5},{5,4},{6,7},{7,6},{8,9},{9,8},{10,11... | collective-permute-start | bytes 3145736 | tf_op jit(solution)/shard_map/cond/branch_1_fun/ppermute | solution.py:262
  102.0 44.1 %collective-permute-start.27 = (bf16[3,128,2048]{2,1,0:T(8,128)(2,1)}, bf16[3,128,2048]{2,1,0:T(8,128)(2,1)}, u32[]{:S(2)}, u32[]{:S(2)}) collective-permute-start(bf16[3,128,2048]{2,1,0:T(8,128)(2,1)} %collective-permute-done.26), channel_id=1, source_target_pairs={{0,8},{4,12},{8,24},{12,28},{24,16},{28,20},{16,0},{20,4},{1,9},{5... | collective-permute-start | bytes 4718600 | tf_op jit(solution)/shard_map/ppermute | solution.py:256
  112.6 3.8 %collective-permute-start.3 = (bf16[3,128,2048]{2,1,0:T(8,128)(2,1)}, bf16[3,128,2048]{2,1,0:T(8,128)(2,1)}, u32[]{:S(2)}, u32[]{:S(2)}) collective-permute-start(bf16[3,128,2048]{2,1,0:T(8,128)(2,1)} %get-tuple-element.142.refs_2_), channel_id=1, source_target_pairs={{0,4},{4,0},{8,12},{12,8},{16,20},{20,16},{24,28},{28,24},{1,5},{5... | collective-permute-start | bytes 4718600 | tf_op jit(solution)/shard_map/cond/branch_1_fun/ppermute | solution.py:259
  112.6 26.8 %collective-permute-start.4 = (bf16[8,256,256]{2,1,0:T(8,128)(2,1)}, bf16[8,256,256]{2,1,0:T(8,128)(2,1)}, u32[]{:S(2)}, u32[]{:S(2)}) collective-permute-start(bf16[8,256,256]{2,1,0:T(8,128)(2,1)} %get-tuple-element.153), channel_id=1, source_target_pairs={{0,3},{1,2},{2,1},{3,0},{4,7},{5,6},{6,5},{7,4},{8,11},{9,10},{10,... | collective-permute-start | bytes 3145736 | tf_op jit(solution)/shard_map/cond/branch_1_fun/ppermute | solution.py:262
  139.4 40.3 %collective-permute-start.30 = (bf16[3,128,2048]{2,1,0:T(8,128)(2,1)}, bf16[3,128,2048]{2,1,0:T(8,128)(2,1)S(1)}, u32[]{:S(2)}, u32[]{:S(2)}) collective-permute-start(bf16[3,128,2048]{2,1,0:T(8,128)(2,1)} %collective-permute-done.28), channel_id=1, source_target_pairs={{0,8},{4,12},{8,24},{12,28},{24,16},{28,20},{16,0},{20,4},{1,9},{5... | collective-permute-start | bytes 4718600 | tf_op jit(solution)/shard_map/ppermute | solution.py:256
  146.1 24.3 %collective-permute-start.15 = (bf16[3,128,2048]{2,1,0:T(8,128)(2,1)}, bf16[3,128,2048]{2,1,0:T(8,128)(2,1)}, u32[]{:S(2)}, u32[]{:S(2)}) collective-permute-start(bf16[3,128,2048]{2,1,0:T(8,128)(2,1)} %get-tuple-element.154), channel_id=1, source_target_pairs={{0,4},{4,0},{8,12},{12,8},{16,20},{20,16},{24,28},{28,24},{1,5},{5... | collective-permute-start | bytes 4718600 | tf_op jit(solution)/shard_map/cond/branch_1_fun/ppermute | solution.py:259
  146.1 22.6 %collective-permute-start.16 = (bf16[128,1024]{1,0:T(8,128)(2,1)}, bf16[128,1024]{1,0:T(8,128)(2,1)S(1)}, u32[]{:S(2)}, u32[]{:S(2)}) collective-permute-start(bf16[128,1024]{1,0:T(8,128)(2,1)} %get-tuple-element.156), channel_id=1, source_target_pairs={{0,1},{1,0},{2,3},{3,2},{4,5},{5,4},{6,7},{7,6},{8,9},{9,8},{10,11... | collective-permute-start | bytes 786440 | tf_op jit(solution)/shard_map/cond/branch_1_fun/ppermute | solution.py:262
  147.0 21.7 %collective-permute-start.17 = (bf16[128,1024]{1,0:T(8,128)(2,1)}, bf16[128,1024]{1,0:T(8,128)(2,1)S(1)}, u32[]{:S(2)}, u32[]{:S(2)}) collective-permute-start(bf16[128,1024]{1,0:T(8,128)(2,1)} %get-tuple-element.157), channel_id=1, source_target_pairs={{0,2},{1,3},{2,0},{3,1},{4,6},{5,7},{6,4},{7,5},{8,10},{9,11},{10,... | collective-permute-start | bytes 786440 | tf_op jit(solution)/shard_map/cond/branch_1_fun/ppermute | solution.py:262
  148.5 20.2 %collective-permute-start.18 = (bf16[128,1024]{1,0:T(8,128)(2,1)}, bf16[128,1024]{1,0:T(8,128)(2,1)S(1)}, u32[]{:S(2)}, u32[]{:S(2)}) collective-permute-start(bf16[128,1024]{1,0:T(8,128)(2,1)} %get-tuple-element.158), channel_id=1, source_target_pairs={{0,3},{1,2},{2,1},{3,0},{4,7},{5,6},{6,5},{7,4},{8,11},{9,10},{10,... | collective-permute-start | bytes 786440 | tf_op jit(solution)/shard_map/cond/branch_1_fun/ppermute | solution.py:262
  169.0 1.4 collective-permute-start.19
  170.4 9.3 %copy-start.10 = (bf16[2,64,1024]{2,1,0:T(8,128)(2,1)}, bf16[2,64,1024]{2,1,0:T(8,128)(2,1)S(1)}, u32[]{:S(2)}) copy-start(bf16[2,64,1024]{2,1,0:T(8,128)(2,1)S(1)} %get-tuple-element.333) | copy-start | bytes 786436
  170.5 41.9 %collective-permute-start.29 = (bf16[3,128,2048]{2,1,0:T(8,128)(2,1)}, bf16[3,128,2048]{2,1,0:T(8,128)(2,1)}, u32[]{:S(2)}, u32[]{:S(2)}) collective-permute-start(bf16[3,128,2048]{2,1,0:T(8,128)(2,1)} %collective-permute-done.27), channel_id=1, source_target_pairs={{0,8},{4,12},{8,24},{12,28},{24,16},{28,20},{16,0},{20,4},{1,9},{5... | collective-permute-start | bytes 4718600 | tf_op jit(solution)/shard_map/ppermute | solution.py:256
  179.7 3.5 %collective-permute-start.5 = (bf16[3,128,2048]{2,1,0:T(8,128)(2,1)S(1)}, bf16[3,128,2048]{2,1,0:T(8,128)(2,1)}, u32[]{:S(2)}, u32[]{:S(2)}) collective-permute-start(bf16[3,128,2048]{2,1,0:T(8,128)(2,1)S(1)} %get-tuple-element.179.refs_2_.refs_6_), channel_id=1, source_target_pairs={{0,4},{4,0},{8,12},{12,8},{16,20},{20,16},{24,28},{28,24},{1,5},{5... | collective-permute-start | bytes 4718600 | tf_op jit(solution)/shard_map/cond/branch_1_fun/ppermute | solution.py:259
  183.3 16.1 %copy-start.2 = (bf16[1024,2048]{1,0:T(8,128)(2,1)S(1)}, bf16[1024,2048]{1,0:T(8,128)(2,1)}, u32[]{:S(2)}) copy-start(bf16[1024,2048]{1,0:T(8,128)(2,1)} %get-tuple-element.196.refs_10_) | copy-start | bytes 12582916 | tf_op jit(solution)/shard_map/cond
  183.3 16.1 %copy-start.3 = (bf16[1024,2048]{1,0:T(8,128)(2,1)S(1)}, bf16[1024,2048]{1,0:T(8,128)(2,1)}, u32[]{:S(2)}) copy-start(bf16[1024,2048]{1,0:T(8,128)(2,1)} %get-tuple-element.195.refs_9_) | copy-start | bytes 12582916 | tf_op jit(solution)/shard_map/cond
  183.3 16.1 %copy-start.4 = (bf16[1024,2048]{1,0:T(8,128)(2,1)S(1)}, bf16[1024,2048]{1,0:T(8,128)(2,1)}, u32[]{:S(2)}) copy-start(bf16[1024,2048]{1,0:T(8,128)(2,1)} %get-tuple-element.194.refs_8_) | copy-start | bytes 12582916 | tf_op jit(solution)/shard_map/cond
  195.8 16.0 %collective-permute-start.6 = (bf16[128,1024]{1,0:T(8,128)(2,1)S(1)}, bf16[128,1024]{1,0:T(8,128)(2,1)S(1)}, u32[]{:S(2)}, u32[]{:S(2)}) collective-permute-start(bf16[128,1024]{1,0:T(8,128)(2,1)S(1)} %get-tuple-element.187), channel_id=1, source_target_pairs={{0,1},{1,0},{2,3},{3,2},{4,5},{5,4},{6,7},{7,6},{8,9},{9,8},{10,11... | collective-permute-start | bytes 786440 | tf_op jit(solution)/shard_map/cond/branch_1_fun/ppermute | solution.py:262
  196.7 15.0 %collective-permute-start.7 = (bf16[128,1024]{1,0:T(8,128)(2,1)S(1)}, bf16[128,1024]{1,0:T(8,128)(2,1)S(1)}, u32[]{:S(2)}, u32[]{:S(2)}) collective-permute-start(bf16[128,1024]{1,0:T(8,128)(2,1)S(1)} %get-tuple-element.188), channel_id=1, source_target_pairs={{0,2},{1,3},{2,0},{3,1},{4,6},{5,7},{6,4},{7,5},{8,10},{9,11},{10,... | collective-permute-start | bytes 786440 | tf_op jit(solution)/shard_map/cond/branch_1_fun/ppermute | solution.py:262
  198.3 13.5 %collective-permute-start.8 = (bf16[128,1024]{1,0:T(8,128)(2,1)S(1)}, bf16[128,1024]{1,0:T(8,128)(2,1)S(1)}, u32[]{:S(2)}, u32[]{:S(2)}) collective-permute-start(bf16[128,1024]{1,0:T(8,128)(2,1)S(1)} %get-tuple-element.189), channel_id=1, source_target_pairs={{0,3},{1,2},{2,1},{3,0},{4,7},{5,6},{6,5},{7,4},{8,11},{9,10},{10,... | collective-permute-start | bytes 786440 | tf_op jit(solution)/shard_map/cond/branch_1_fun/ppermute | solution.py:262
  212.0 36.5 %collective-permute-start.31 = (bf16[3,128,2048]{2,1,0:T(8,128)(2,1)S(1)}, bf16[3,128,2048]{2,1,0:T(8,128)(2,1)S(1)}, u32[]{:S(2)}, u32[]{:S(2)}) collective-permute-start(bf16[3,128,2048]{2,1,0:T(8,128)(2,1)S(1)} %collective-permute-done.30), channel_id=1, source_target_pairs={{0,8},{4,12},{8,24},{12,28},{24,16},{28,20},{16,0},{20,4},{1,9},{5... | collective-permute-start | bytes 4718600 | tf_op jit(solution)/shard_map/ppermute | solution.py:256
  212.3 3.8 %collective-permute-start.20 = (bf16[3,128,2048]{2,1,0:T(8,128)(2,1)}, bf16[3,128,2048]{2,1,0:T(8,128)(2,1)}, u32[]{:S(2)}, u32[]{:S(2)}) collective-permute-start(bf16[3,128,2048]{2,1,0:T(8,128)(2,1)} %get-tuple-element.204.refs_0_.refs_4_), channel_id=1, source_target_pairs={{0,4},{4,0},{8,12},{12,8},{16,20},{20,16},{24,28},{28,24},{1,5},{5... | collective-permute-start | bytes 4718600 | tf_op jit(solution)/shard_map/cond/branch_1_fun/ppermute | solution.py:259
  216.1 14.0 %copy-start.5 = (bf16[1024,2048]{1,0:T(8,128)(2,1)S(1)}, bf16[1024,2048]{1,0:T(8,128)(2,1)}, u32[]{:S(2)}) copy-start(bf16[1024,2048]{1,0:T(8,128)(2,1)} %get-tuple-element.219.refs_8_) | copy-start | bytes 12582916 | tf_op jit(solution)/shard_map/cond
  216.1 14.0 %copy-start.6 = (bf16[1024,2048]{1,0:T(8,128)(2,1)S(1)}, bf16[1024,2048]{1,0:T(8,128)(2,1)}, u32[]{:S(2)}) copy-start(bf16[1024,2048]{1,0:T(8,128)(2,1)} %get-tuple-element.218.refs_7_) | copy-start | bytes 12582916 | tf_op jit(solution)/shard_map/cond
  216.1 14.0 %copy-start.7 = (bf16[1024,2048]{1,0:T(8,128)(2,1)S(1)}, bf16[1024,2048]{1,0:T(8,128)(2,1)}, u32[]{:S(2)}) copy-start(bf16[1024,2048]{1,0:T(8,128)(2,1)} %get-tuple-element.217.refs_6_) | copy-start | bytes 12582916 | tf_op jit(solution)/shard_map/cond
  226.5 13.1 %collective-permute-start.21 = (bf16[64,1024]{1,0:T(8,128)(2,1)S(1)}, bf16[64,1024]{1,0:T(8,128)(2,1)S(1)}, u32[]{:S(2)}, u32[]{:S(2)}) collective-permute-start(bf16[64,1024]{1,0:T(8,128)(2,1)S(1)} %get-tuple-element.210), channel_id=1, source_target_pairs={{0,1},{1,0},{2,3},{3,2},{4,5},{5,4},{6,7},{7,6},{8,9},{9,8},{10,11... | collective-permute-start | bytes 393224 | tf_op jit(solution)/shard_map/cond/branch_1_fun/ppermute | solution.py:262
  228.0 11.5 %collective-permute-start.22 = (bf16[64,1024]{1,0:T(8,128)(2,1)S(1)}, bf16[64,1024]{1,0:T(8,128)(2,1)S(1)}, u32[]{:S(2)}, u32[]{:S(2)}) collective-permute-start(bf16[64,1024]{1,0:T(8,128)(2,1)S(1)} %get-tuple-element.211), channel_id=1, source_target_pairs={{0,2},{1,3},{2,0},{3,1},{4,6},{5,7},{6,4},{7,5},{8,10},{9,11},{10,... | collective-permute-start | bytes 393224 | tf_op jit(solution)/shard_map/cond/branch_1_fun/ppermute | solution.py:262
  229.6 10.0 %collective-permute-start.23 = (bf16[64,1024]{1,0:T(8,128)(2,1)S(1)}, bf16[64,1024]{1,0:T(8,128)(2,1)}, u32[]{:S(2)}, u32[]{:S(2)}) collective-permute-start(bf16[64,1024]{1,0:T(8,128)(2,1)S(1)} %get-tuple-element.212), channel_id=1, source_target_pairs={{0,3},{1,2},{2,1},{3,0},{4,7},{5,6},{6,5},{7,4},{8,11},{9,10},{10,... | collective-permute-start | bytes 393224 | tf_op jit(solution)/shard_map/cond/branch_1_fun/ppermute | solution.py:262
  230.0 11.1 %collective-permute-start.25 = (bf16[64,1024]{1,0:T(8,128)(2,1)}, bf16[64,1024]{1,0:T(8,128)(2,1)}, u32[]{:S(2)}, u32[]{:S(2)}) collective-permute-start(bf16[64,1024]{1,0:T(8,128)(2,1)} %pad_maximum_fusion.6), channel_id=1, source_target_pairs={{0,4},{4,0},{8,12},{12,8},{16,20},{20,16},{24,28},{28,24},{1,5},{5... | collective-permute-start | bytes 393224 | tf_op jit(solution)/shard_map/cond/branch_1_fun/ppermute | solution.py:259
  240.6 2.2 collective-permute-start.24
  248.5 3.4 %collective-permute-start.34 = (bf16[3,128,2048]{2,1,0:T(8,128)(2,1)S(1)}, bf16[3,128,2048]{2,1,0:T(8,128)(2,1)S(1)}, u32[]{:S(2)}, u32[]{:S(2)}) collective-permute-start(bf16[3,128,2048]{2,1,0:T(8,128)(2,1)S(1)} %collective-permute-done.31.refs_0_.refs_4_), channel_id=1, source_target_pairs={{0,4},{4,0},{8,12},{12,8},{16,20},{20,16},{24,28},{28,24},{1,5},{5... | collective-permute-start | bytes 4718600 | tf_op jit(solution)/shard_map/ppermute | solution.py:259
  248.5 31.1 %copy-start.9 = (bf16[2,64,1024]{2,1,0:T(8,128)(2,1)S(1)}, bf16[2,64,1024]{2,1,0:T(8,128)(2,1)}, u32[]{:S(2)}) copy-start(bf16[2,64,1024]{2,1,0:T(8,128)(2,1)} %copy-done.8) | copy-start | bytes 786436
  248.5 36.2 %copy-start.11 = (f32[16,1,128]{2,1,0:T(1,128)S(1)}, f32[16,1,128]{2,1,0:T(1,128)}, u32[]{:S(2)}) copy-start(f32[16,1,128]{2,1,0:T(1,128)} %get-tuple-element.358) | copy-start | bytes 24580
  248.5 14.6 %collective-permute-start.32 = (bf16[2,64,1024]{2,1,0:T(8,128)(2,1)}, bf16[2,64,1024]{2,1,0:T(8,128)(2,1)S(1)}, u32[]{:S(2)}, u32[]{:S(2)}) collective-permute-start(bf16[2,64,1024]{2,1,0:T(8,128)(2,1)} %copy-done.10), channel_id=1, source_target_pairs={{0,16},{4,20},{8,0},{12,4},{24,8},{28,12},{16,24},{20,28},{1,17},{... | collective-permute-start | bytes 786440 | tf_op jit(solution)/shard_map/ppermute | solution.py:359
  249.5 14.9 %collective-permute-start.33 = (bf16[2,64,1024]{2,1,0:T(8,128)(2,1)}, bf16[2,64,1024]{2,1,0:T(8,128)(2,1)S(1)}, u32[]{:S(2)}, u32[]{:S(2)}) collective-permute-start(bf16[2,64,1024]{2,1,0:T(8,128)(2,1)} %get-tuple-element.334), channel_id=1, source_target_pairs={{0,24},{4,28},{8,16},{12,20},{24,0},{28,4},{16,8},{20,12},{1,25},{... | collective-permute-start | bytes 786440 | tf_op jit(solution)/shard_map/ppermute | solution.py:359
  259.5 6.3 %collective-permute-start.35 = (bf16[64,1024]{1,0:T(8,128)(2,1)S(1)}, bf16[64,1024]{1,0:T(8,128)(2,1)S(1)}, u32[]{:S(2)}, u32[]{:S(2)}) collective-permute-start(bf16[64,1024]{1,0:T(8,128)(2,1)S(1)} %get-tuple-element.337), channel_id=1, source_target_pairs={{0,1},{1,0},{2,3},{3,2},{4,5},{5,4},{6,7},{7,6},{8,9},{9,8},{10,11... | collective-permute-start | bytes 393224 | tf_op jit(solution)/shard_map/ppermute | solution.py:262
  260.9 8.0 %collective-permute-start.36 = (bf16[64,1024]{1,0:T(8,128)(2,1)S(1)}, bf16[64,1024]{1,0:T(8,128)(2,1)S(1)}, u32[]{:S(2)}, u32[]{:S(2)}) collective-permute-start(bf16[64,1024]{1,0:T(8,128)(2,1)S(1)} %get-tuple-element.338), channel_id=1, source_target_pairs={{0,2},{1,3},{2,0},{3,1},{4,6},{5,7},{6,4},{7,5},{8,10},{9,11},{10,... | collective-permute-start | bytes 393224 | tf_op jit(solution)/shard_map/ppermute | solution.py:262
  262.4 6.5 %collective-permute-start.37 = (bf16[64,1024]{1,0:T(8,128)(2,1)S(1)}, bf16[64,1024]{1,0:T(8,128)(2,1)S(1)}, u32[]{:S(2)}, u32[]{:S(2)}) collective-permute-start(bf16[64,1024]{1,0:T(8,128)(2,1)S(1)} %get-tuple-element.339), channel_id=1, source_target_pairs={{0,3},{1,2},{2,1},{3,0},{4,7},{5,6},{6,5},{7,4},{8,11},{9,10},{10,... | collective-permute-start | bytes 393224 | tf_op jit(solution)/shard_map/ppermute | solution.py:262
  269.0 1.3 collective-permute-start.38
  270.3 9.3 %collective-permute-start.39 = (bf16[2,64,1024]{2,1,0:T(8,128)(2,1)S(1)}, bf16[2,64,1024]{2,1,0:T(8,128)(2,1)S(1)}, u32[]{:S(2)}, u32[]{:S(2)}) collective-permute-start(bf16[2,64,1024]{2,1,0:T(8,128)(2,1)S(1)} %maximum_maximum_fusion), channel_id=1, source_target_pairs={{0,8},{4,12},{8,24},{12,28},{24,16},{28,20},{16,0},{20,4},{1,9},{5... | collective-permute-start | bytes 786440 | tf_op jit(solution)/shard_map/ppermute | solution.py:359
  281.2 20.1 %collective-permute-start.40 = (bf16[2,64,1024]{2,1,0:T(8,128)(2,1)}, bf16[2,64,1024]{2,1,0:T(8,128)(2,1)}, u32[]{:S(2)}, u32[]{:S(2)}) collective-permute-start(bf16[2,64,1024]{2,1,0:T(8,128)(2,1)} %get-tuple-element.345), channel_id=1, source_target_pairs={{0,1},{1,0},{2,3},{3,2},{4,5},{5,4},{6,7},{7,6},{8,9},{9,8},{10,11... | collective-permute-start | bytes 786440 | tf_op jit(solution)/shard_map/ppermute | solution.py:262
  282.4 18.8 %collective-permute-start.41 = (bf16[2,64,1024]{2,1,0:T(8,128)(2,1)}, bf16[2,64,1024]{2,1,0:T(8,128)(2,1)}, u32[]{:S(2)}, u32[]{:S(2)}) collective-permute-start(bf16[2,64,1024]{2,1,0:T(8,128)(2,1)} %get-tuple-element.346), channel_id=1, source_target_pairs={{0,2},{1,3},{2,0},{3,1},{4,6},{5,7},{6,4},{7,5},{8,10},{9,11},{10,... | collective-permute-start | bytes 786440 | tf_op jit(solution)/shard_map/ppermute | solution.py:262
  283.2 18.0 %collective-permute-start.42 = (bf16[2,64,1024]{2,1,0:T(8,128)(2,1)}, bf16[2,64,1024]{2,1,0:T(8,128)(2,1)}, u32[]{:S(2)}, u32[]{:S(2)}) collective-permute-start(bf16[2,64,1024]{2,1,0:T(8,128)(2,1)} %get-tuple-element.347), channel_id=1, source_target_pairs={{0,3},{1,2},{2,1},{3,0},{4,7},{5,6},{6,5},{7,4},{8,11},{9,10},{10,... | collective-permute-start | bytes 786440 | tf_op jit(solution)/shard_map/ppermute | solution.py:262
  285.5 15.2 %all-to-all-start.2 = ((f32[8,1,16]{2,1,0:T(1,128)}), f32[8,1,16]{2,1,0:T(1,128)S(1)}, u32[]{:S(2)}, u32[]{:S(2)}) async-start(f32[8,1,16]{2,1,0:T(1,128)} %bitcast.24), calls=%async_computation.2 | async-start | bytes 8192 | tf_op jit(solution)/shard_map/all_to_all | solution.py:237

commit v4 on v3

--- a/solution.py
+++ b/solution.py
@@ -52,7 +52,7 @@
     length, width = queries.shape
     heads = key_bias.shape[0]
     head_dim = width // heads
-    heads_step = 2 if heads % 2 == 0 else 1
+    heads_step = math.gcd(heads, 4)
     block = pl.BlockSpec((length, heads_step * head_dim), lambda h: (0, h))
     outs = pl.pallas_call(
         functools.partial(attention_body, sizes, head_dim, heads_step),
@@ -205,6 +205,40 @@
     )(place, *parts)
 
 
+def assemble_body(count, sizes, place_ref, *refs):
+    part_refs, out_ref = refs[:count], refs[count]
+    me = place_ref[place_ref.shape[0] - 1]
+    spread, _, rows_in = part_refs[0].shape
+    begin = at = 0
+    for whole in sizes:
+        size = whole // count
+        for d, ref in enumerate(part_refs):
+            rows = pl.ds(pl.multiple_of(begin + (me ^ d) * size, 16), size)
+            for n in range(spread):
+                out_ref[rows, n * rows_in:(n + 1) * rows_in] = ref[n, at:at + size, :]
+        begin += whole
+        at += size
+
+
+def assemble(place, parts, sizes):
+    spread, tokens, rows_in = parts[0].shape
+    return pl.pallas_call(
+        functools.partial(assemble_body, len(parts), sizes),
+        grid_spec=pltpu.PrefetchScalarGridSpec(
+            num_scalar_prefetch=1,
+            grid=(1,),
+            in_specs=[pl.BlockSpec(part.shape, lambda n, place: (0, 0, 0)) for part in parts],
+            out_specs=pl.BlockSpec((sum(sizes), spread * rows_in), lambda n, place: (0, 0)),
+        ),
+        out_shape=jax.ShapeDtypeStruct((sum(sizes), spread * rows_in), jnp.bfloat16),
+        compiler_params=pltpu.CompilerParams(vmem_limit_bytes=24 * MIB),
+        cost_estimate=pl.CostEstimate(
+            flops=0, bytes_accessed=4 * len(parts) * spread * tokens * rows_in, transcendentals=0
+        ),
+        name="assemble",
+    )(place, *parts)
+
+
 def ring_order(chips):
     return [0] + list(range(1, chips, 2)) + list(range(chips - 2 + chips % 2, 0, -2))
 
@@ -362,21 +396,22 @@
     others[final][last] = other(landed)
     sums, sooner = after((sums, sooner), landed)
     at_home = [homeward(sums[step], step) for step in range(final)]
-    total = summed(partial_of([(landed, others[final][last])], others[final][0]), at_home)
-    at_home.append(homeward(jnp.concatenate([sooner, shared(total, sizes[last:])], axis=1), final))
+    partial = partial_of([(landed, others[final][last])], others[final][0])
+
+    def folded(bias, bit, ahead):
+        bias = after(bias, ahead)
+        return bias + lax.ppermute(bias, "row", [(n, n ^ 1 << bit) for n in range(row_count)])
+
+    bias_grad = folded(bias_part, 0, landed)
+    total = summed(partial, (at_home, bias_grad))
+    sooner = homeward(jnp.concatenate([sooner, shared(total, sizes[last:])], axis=1), final)
+    weight_grads = weight_part(after(x, total), [(final, last)], [both(final, last)], weight_grads)
+    at_home.append(after(sooner, weight_grads[0]))
     mine = sort_home(place, at_home, col_count, spread)
     got = [across(mine[d], d) if d else mine[d] for d in range(col_count)]
-    weight_grads = weight_part(after(x, mine), [(final, last)], [both(final, last)], weight_grads)
-    got = jnp.take(jnp.stack(got), my_col ^ jnp.arange(col_count), axis=0)
-    home = []
-    at = 0
-    for chunk in sizes:
-        size = chunk // col_count
-        home.append(jnp.transpose(got[:, :, at:at + size], (0, 2, 1, 3)).reshape(chunk, spread * rows_in))
-        at += size
-    layer_grad = jnp.concatenate(home, axis=0)
-    bias_all = a2a(after(jnp.broadcast_to(bias_part[None], (row_count,) + bias_part.shape), mine[0]), "row")
-    bias_grad = jnp.sum(after(bias_all, weight_grads[0]), axis=0)
+    for bit in range(1, row_count.bit_length() - 1):
+        bias_grad = folded(bias_grad, bit, mine[0])
+    layer_grad = assemble(place, after(got, bias_grad), sizes)
     return (layer_grad, *weight_grads, bias_grad)
 
 

time: 306 us -> 301 us (0.984)
    ppermute x3, waiting for transfers between devices: 8.95 us -> 0.01 us  [homeward(): return lax.ppermute(mine, 'row', route) if step else mine]
    all_to_all x3 -> x2, starting transfers between devices: 13.2 us -> 8.61 us  [a2a(): return lax.all_to_all(array, axis, split_axis=0, concat_axis=0, tiled=True)]
    ppermute x0 -> x3, waiting for transfers between devices: none -> 4.34 us  [folded(): lax.ppermute(bias, 'row', [(n, n ^ 1 << bit) for n in range(row_count)])]
    ppermute x21, waiting for transfers between devices: 50.5 us -> 54.8 us  [across(): return lax.ppermute(mine, 'col', [(n, n ^ apart) for n in range(col_count)])]
    ppermute x0 -> x3, starting transfers between devices: none -> 4.09 us  [folded(): lax.ppermute(bias, 'row', [(n, n ^ 1 << bit) for n in range(row_count)])]
    all_to_all x3 -> x2, waiting for transfers between devices: 15.1 us -> 15.2 us  [a2a(): return lax.all_to_all(array, axis, split_axis=0, concat_axis=0, tiled=True)]
  transfers between devices with their start and end apart: 46 -> 48, of which waited for: 22 -> 23; matrix products, arithmetic and copies ran while one was open for 3% -> 3% of each run, Pallas kernels for 35% -> 36%
where the time goes in v4:
time: 301 us
  Pallas kernels  122 us (41%)
  waiting for transfers between devices  114 us (38%)
  starting transfers between devices  53.7 us (18%)
  other arithmetic  5.84 us (2%)
  local copies, waits for them, and re-layouts  4.05 us (1%)
    pallas_call x5, Pallas kernels, input_grad(): pl.pallas_call(functools.partial(input_grad_body, len(grads)), grid_spec=...  56.8 us
    ppermute x21, waiting for transfers between devices, across(): return lax.ppermute(mine, 'col', [(n, n ^ apart) for n in range(col_count)])  54.8 us
    pallas_call x4, Pallas kernels, weight_grad(): pl.pallas_call(functools.partial(weight_grad_body, len(x), tuple(units),...  50.4 us
    ppermute x6, waiting for transfers between devices, hop(): return lax.ppermute(mine, 'row', ring)  27.8 us
    ppermute x21, starting transfers between devices, across(): return lax.ppermute(mine, 'col', [(n, n ^ apart) for n in range(col_count)])  26.8 us
    all_to_all x2, waiting for transfers between devices, a2a(): return lax.all_to_all(array, axis, split_axis=0, concat_axis=0, tiled=True)  15.2 us
    ppermute x13, waiting for transfers between devices, other(): return lax.ppermute(mine, 'row', swap)  11.7 us
    pallas_call x1, Pallas kernels, attention(): pl.pallas_call(functools.partial(attention_body, sizes, head_dim, heads_s...  11.2 us
  transfers between devices with their start and end apart: 48, of which 23 were waited for; matrix products, arithmetic and copies ran while one was open for 3% of the time, Pallas kernels for 36%

profile of v4, /device:TPU:0, one launch (start us, length us, event | category | flops | bytes accessed | tf_op | source)
XLA Modules:
  0.0 300.7 jit_solution(7521915544725777700)
XLA Ops:
  0.6 11.2 %attention_back.1 = (bf16[3,128,2048]{2,1,0:T(8,128)(2,1)}, bf16[3,128,2048]{2,1,0:T(8,128)(2,1)}, f32[16,1,128]{2,1,0:T(1,128)}) custom-call(f32[16]{0:T(128)} %bias_ref.1, s32[1,256]{1,0:T(1,128)} %flag_ref.1, bf16[256,2048]{1,0:T(8,128)(2,1)} %bitcast.24, bf16[256,2048]{1,0:T(8,128)(2,1)} %bitcast.25, bf16[256,2048]{1,0:T(8,128)(2,1)} %bitcast.26, ...), custom_call_target="tpu_custom_call" | custom-call | flops 67108864 | bytes 367001 | tf_op jit(solution)/shard_map/attention_back/pallas_call | solution.py:57
  11.8 3.0 %collective-permute-start.26 = (bf16[3,128,2048]{2,1,0:T(8,128)(2,1)}, bf16[3,128,2048]{2,1,0:T(8,128)(2,1)}, u32[]{:S(2)}, u32[]{:S(2)}) collective-permute-start(bf16[3,128,2048]{2,1,0:T(8,128)(2,1)} %get-tuple-element.303), channel_id=1, source_target_pairs={{0,8},{4,12},{8,24},{12,28},{24,16},{28,20},{16,0},{20,4},{1,9},{5... | collective-permute-start | bytes 4718600 | tf_op jit(solution)/shard_map/ppermute | solution.py:290
  16.8 56.3 %conditional.6 = (bf16[3,128,2048]{2,1,0:T(8,128)(2,1)}, bf16[3,128,2048]{2,1,0:T(8,128)(2,1)S(1)}, bf16[2,64,1024]{2,1,0:T(8,128)(2,1)S(1)}, bf16[8,256,256]{2,1,0:T(8,128)(2,1)}) conditional(s32[]{:T(128)} %convert_element_type.83, () %tuple.76, (bf16[3,128,2048]{2,1,0:T(8,128)(2,1)}, bf16[3,128,2048]{2,1,0:T(8,128)(2,1)}, s32[17]{0:T(128)S(1)}, ...), branch_computations={%region_1.0_spmd, %region_2.0_spmd} | conditional | flops 323826496 | bytes 43149296 | solution.py:284
  17.4 1.8 reshape.14
  19.3 1.2 copy.20
  20.4 4.2 %all-to-all-start = ((bf16[4,2,256,256]{3,2,1,0:T(8,128)(2,1)}), bf16[4,2,256,256]{3,2,1,0:T(8,128)(2,1)}, u32[]{:S(2)}, u32[]{:S(2)}) async-start(bf16[4,2,256,256]{3,2,1,0:T(8,128)(2,1)} %bitcast.23), calls=%async_computation | async-start | bytes 2097152 | tf_op jit(solution)/shard_map/cond/branch_1_fun/all_to_all | solution.py:271
  24.7 11.8 %input_grad.5 = (bf16[128,1024]{1,0:T(8,128)(2,1)S(1)}, bf16[128,1024]{1,0:T(8,128)(2,1)S(1)}, bf16[128,1024]{1,0:T(8,128)(2,1)S(1)}, bf16[128,1024]{1,0:T(8,128)(2,1)S(1)}) custom-call(s32[17]{0:T(128)S(1)} %get-tuple-element.126.place_ref, bf16[3,128,2048]{2,1,0:T(8,128)(2,1)} %get-tuple-element.124.refs_0_, ...), custom_call_target="tpu_custom_call" | custom-call | flops 322122560 | bytes 943718 | tf_op jit(solution)/shard_map/cond/branch_1_fun/input_grad/pallas_call | solution.py:104
  36.5 2.4 all-to-all-done
  38.9 4.4 %all-to-all-start.1 = ((bf16[8,256,256]{2,1,0:T(8,128)(2,1)}), bf16[8,256,256]{2,1,0:T(8,128)(2,1)}, u32[]{:S(2)}, u32[]{:S(2)}) async-start(bf16[8,256,256]{2,1,0:T(8,128)(2,1)} %bitcast.3), calls=%async_computation.1 | async-start | bytes 2097152 | tf_op jit(solution)/shard_map/cond/branch_1_fun/all_to_all | solution.py:271
  43.3 1.5 collective-permute-start.11
  45.3 1.5 collective-permute-start.13
  46.8 5.6 %collective-permute-done.11 = bf16[128,1024]{1,0:T(8,128)(2,1)S(1)} collective-permute-done((bf16[128,1024]{1,0:T(8,128)(2,1)S(1)}, bf16[128,1024]{1,0:T(8,128)(2,1)S(1)}, u32[]{:S(2)}, u32[]{:S(2)}) %collective-permute-start.11) | collective-permute-done | bytes 262176 | tf_op jit(solution)/shard_map/cond/branch_1_fun/ppermute | solution.py:296
  52.5 6.2 %collective-permute-done.12 = bf16[128,1024]{1,0:T(8,128)(2,1)S(1)} collective-permute-done((bf16[128,1024]{1,0:T(8,128)(2,1)S(1)}, bf16[128,1024]{1,0:T(8,128)(2,1)S(1)}, u32[]{:S(2)}, u32[]{:S(2)}) %collective-permute-start.12) | collective-permute-done | bytes 262176 | tf_op jit(solution)/shard_map/cond/branch_1_fun/ppermute | solution.py:296
  58.9 1.3 collective-permute-done.14
  60.3 12.8 %all-to-all-done.1 = bf16[8,256,256]{2,1,0:T(8,128)(2,1)} async-done(((bf16[8,256,256]{2,1,0:T(8,128)(2,1)}), bf16[8,256,256]{2,1,0:T(8,128)(2,1)}, u32[]{:S(2)}, u32[]{:S(2)}) %all-to-all-start.1) | async-done | bytes 1048608 | tf_op jit(solution)/shard_map/cond/branch_1_fun/all_to_all | solution.py:271
  73.9 27.1 %conditional.7 = (bf16[3,128,2048]{2,1,0:T(8,128)(2,1)}, bf16[8,256,256]{2,1,0:T(8,128)(2,1)}, bf16[8,256,256]{2,1,0:T(8,128)(2,1)}) conditional(s32[]{:T(128)} %convert_element_type.83, () %tuple.79, (bf16[3,128,2048]{2,1,0:T(8,128)(2,1)}, bf16[8,256,256]{2,1,0:T(8,128)(2,1)}) %tuple.80), branch_computations={%region_3.0_spmd, %region_4.0_spmd} | conditional | bytes 14680208 | solution.py:284
  73.9 1.5 collective-permute-start.2
  75.4 1.5 collective-permute-start.1
  76.9 22.9 %collective-permute-done.2 = bf16[8,256,256]{2,1,0:T(8,128)(2,1)} collective-permute-done((bf16[8,256,256]{2,1,0:T(8,128)(2,1)}, bf16[8,256,256]{2,1,0:T(8,128)(2,1)}, u32[]{:S(2)}, u32[]{:S(2)}) %collective-permute-start.2) | collective-permute-done | bytes 1048608 | tf_op jit(solution)/shard_map/cond/branch_1_fun/ppermute | solution.py:296
  99.8 1.2 collective-permute-done.1
  101.0 3.4 %collective-permute-start.27 = (bf16[3,128,2048]{2,1,0:T(8,128)(2,1)}, bf16[3,128,2048]{2,1,0:T(8,128)(2,1)}, u32[]{:S(2)}, u32[]{:S(2)}) collective-permute-start(bf16[3,128,2048]{2,1,0:T(8,128)(2,1)} %collective-permute-done.26), channel_id=1, source_target_pairs={{0,8},{4,12},{8,24},{12,28},{24,16},{28,20},{16,0},{20,4},{1,9},{5... | collective-permute-start | bytes 4718600 | tf_op jit(solution)/shard_map/ppermute | solution.py:290
  104.4 7.2 %collective-permute-done.28 = bf16[3,128,2048]{2,1,0:T(8,128)(2,1)} collective-permute-done((bf16[3,128,2048]{2,1,0:T(8,128)(2,1)}, bf16[3,128,2048]{2,1,0:T(8,128)(2,1)}, u32[]{:S(2)}, u32[]{:S(2)}) %collective-permute-start.28) | collective-permute-done | bytes 1572896 | tf_op jit(solution)/shard_map/ppermute | solution.py:290
  111.6 26.8 %conditional.8 = (bf16[3,128,2048]{2,1,0:T(8,128)(2,1)}, bf16[128,1024]{1,0:T(8,128)(2,1)S(1)}, bf16[128,1024]{1,0:T(8,128)(2,1)}, bf16[128,1024]{1,0:T(8,128)(2...) conditional(s32[]{:T(128)} %convert_element_type.83, () %tuple.82, (bf16[3,128,2048]{2,1,0:T(8,128)(2,1)}, ...), branch_computations={%region_5.0_spmd, %region_6.0_spmd} | conditional | flops 322122560 | bytes 11429606 | solution.py:284
  111.6 2.5 collective-permute-start.4
  114.1 1.2 collective-permute-done.3.refs_3_.refs_7_
  115.4 12.9 %input_grad.6 = (bf16[128,1024]{1,0:T(8,128)(2,1)S(1)}, bf16[128,1024]{1,0:T(8,128)(2,1)}, bf16[128,1024]{1,0:T(8,128)(2,1)}, bf16[128,1024]{1,0:T(8,128)(2,1)}) custom-call(s32[17]{0:T(128)S(1)} %get-tuple-element.143.place_ref, bf16[3,128,2048]{2,1,0:T(8,128)(2,1)} %get-tuple-element.144.refs_0_, bf16[3,128,2048]{2,1,0:T(8,128)(2,1)} %get-tuple-element.145.refs_1_, ...), custom_call_target="tpu_custom_call" | custom-call | flops 322122560 | bytes 943718 | tf_op jit(solution)/shard_map/cond/branch_1_fun/input_grad/pallas_call | solution.py:104
  128.2 10.2 %collective-permute-done.4 = bf16[8,256,256]{2,1,0:T(8,128)(2,1)} collective-permute-done((bf16[8,256,256]{2,1,0:T(8,128)(2,1)}, bf16[8,256,256]{2,1,0:T(8,128)(2,1)}, u32[]{:S(2)}, u32[]{:S(2)}) %collective-permute-start.4) | collective-permute-done | bytes 1048608 | tf_op jit(solution)/shard_map/cond/branch_1_fun/ppermute | solution.py:296
  139.2 5.9 %collective-permute-done.27 = bf16[3,128,2048]{2,1,0:T(8,128)(2,1)} collective-permute-done((bf16[3,128,2048]{2,1,0:T(8,128)(2,1)}, bf16[3,128,2048]{2,1,0:T(8,128)(2,1)}, u32[]{:S(2)}, u32[]{:S(2)}) %collective-permute-start.27) | collective-permute-done | bytes 1572896 | tf_op jit(solution)/shard_map/ppermute | solution.py:290
  145.1 24.3 %conditional.9 = (bf16[3,128,2048]{2,1,0:T(8,128)(2,1)}, bf16[2,64,1024]{2,1,0:T(8,128)(2,1)S(1)}, bf16[1024,2048]{1,0:T(8,128)(2,1)}, bf16[1024,2048]{1,0:T(8,128)(2,1)}, bf16[1024,2048]{1,0:T(8,128)(2,1)}) conditional(s32[]{:T(128)} %convert_element_type.83, () %tuple.78, (bf16[3,128,2048]{2,1,0:T(8,128)(2,1)}, bf16[128,1024]{1,0:T(8,128)(2,1)}, ...), branch_computations={%region_7.0_spmd, %region_8.0_spmd} | conditional | flops 645949056 | bytes 14417970 | solution.py:284
  146.0 1.5 collective-permute-start.17
  148.6 19.1 %weight_grad.4 = (bf16[1024,2048]{1,0:T(8,128)(2,1)}, bf16[1024,2048]{1,0:T(8,128)(2,1)}, bf16[1024,2048]{1,0:T(8,128)(2,1)}) custom-call(s32[17]{0:T(128)S(1)} %get-tuple-element.159.place_ref, bf16[8,256,256]{2,1,0:T(8,128)(2,1)} %get-tuple-element.160.refs_0_, bf16[8,256,256]{2,1,0:T(8,128)(2,1)} %get-tuple-element.161.refs_1_, ...), custom_call_target="tpu_custom_call" | custom-call | flops 644245120 | bytes 1258291 | tf_op jit(solution)/shard_map/cond/branch_1_fun/weight_grad/pallas_call | solution.py:158
  168.1 1.3 collective-permute-done.19
  169.7 9.0 %collective-permute-done.30 = bf16[3,128,2048]{2,1,0:T(8,128)(2,1)S(1)} collective-permute-done((bf16[3,128,2048]{2,1,0:T(8,128)(2,1)}, bf16[3,128,2048]{2,1,0:T(8,128)(2,1)S(1)}, u32[]{:S(2)}, u32[]{:S(2)}) %collective-permute-start.30) | collective-permute-done | bytes 1572896 | tf_op jit(solution)/shard_map/ppermute | solution.py:290
  178.7 32.2 %conditional.10 = (bf16[3,128,2048]{2,1,0:T(8,128)(2,1)}, bf16[128,1024]{1,0:T(8,128)(2,1)S(1)}, bf16[1024,2048]{1,0:T(8,128)(2,1)}, bf16[1024,2048]{1,0:T(8,128)(2,1)}, bf16[1024,2048]{1,0:T(8,128)(2,1)}) conditional(s32[]{:T(128)} %convert_element_type.83, () %tuple.88, (bf16[3,128,2048]{2,1,0:T(8,128)(2,1)S(1)}, s32[17]{0:T(128)S(1)}, ...), branch_computations={%region_9.0_spmd, %region_10.0_spmd} | conditional | flops 645293696 | bytes 63596420 | solution.py:284
  178.7 3.5 %collective-permute-done.5.refs_3_.refs_7_ = bf16[3,128,2048]{2,1,0:T(8,128)(2,1)} collective-permute-done((bf16[3,128,2048]{2,1,0:T(8,128)(2,1)S(1)}, bf16[3,128,2048]{2,1,0:T(8,128)(2,1)}, u32[]{:S(2)}, u32[]{:S(2)}) %collective-permute-start.5) | collective-permute-done | bytes 1572896 | tf_op jit(solution)/shard_map/cond/branch_1_fun/ppermute | solution.py:293
  182.3 12.5 %input_grad.7 = (bf16[128,1024]{1,0:T(8,128)(2,1)S(1)}, bf16[128,1024]{1,0:T(8,128)(2,1)S(1)}, bf16[128,1024]{1,0:T(8,128)(2,1)S(1)}, bf16[128,1024]{1,0:T(8,128)(2,1)S(1)}) custom-call(s32[17]{0:T(128)S(1)} %get-tuple-element.180.place_ref, bf16[3,128,2048]{2,1,0:T(8,128)(2,1)} %get-tuple-element.181.refs_0_.refs_4_, ...), custom_call_target="tpu_custom_call" | custom-call | flops 322122560 | bytes 943718 | tf_op jit(solution)/shard_map/cond/branch_1_fun/input_grad/pallas_call | solution.py:104
  195.8 1.5 collective-permute-start.7
  198.4 12.4 %weight_grad.5 = (bf16[1024,2048]{1,0:T(8,128)(2,1)}, bf16[1024,2048]{1,0:T(8,128)(2,1)}, bf16[1024,2048]{1,0:T(8,128)(2,1)}) custom-call(s32[17]{0:T(128)S(1)} %get-tuple-element.180.place_ref, bf16[8,256,256]{2,1,0:T(8,128)(2,1)} %get-tuple-element.190.refs_0_, bf16[8,256,256]{2,1,0:T(8,128)(2,1)} %get-tuple-element.191.refs_1_, ...), custom_call_target="tpu_custom_call" | custom-call | flops 322122560 | bytes 1572864 | tf_op jit(solution)/shard_map/cond/branch_1_fun/weight_grad/pallas_call | solution.py:158
  211.3 30.5 %conditional.11 = (bf16[3,128,2048]{2,1,0:T(8,128)(2,1)}, bf16[2,32,1024]{2,1,0:T(8,128)(2,1)S(1)}, bf16[1024,2048]{1,0:T(8,128)(2,1)}, bf16[1024,2048]{1,0:T(8,...) conditional(s32[]{:T(128)} %convert_element_type.83, () %tuple.86, ...), branch_computations={%region_11.0_spmd, %region_12.0_spmd} | conditional | flops 323367744 | bytes 63937292 | solution.py:284
  212.1 3.0 %collective-permute-done.20.refs_1_.refs_5_ = bf16[3,128,2048]{2,1,0:T(8,128)(2,1)} collective-permute-done((bf16[3,128,2048]{2,1,0:T(8,128)(2,1)}, bf16[3,128,2048]{2,1,0:T(8,128)(2,1)}, u32[]{:S(2)}, u32[]{:S(2)}) %collective-permute-start.20) | collective-permute-done | bytes 1572896 | tf_op jit(solution)/shard_map/cond/branch_1_fun/ppermute | solution.py:293
  215.1 10.4 %input_grad.8 = (bf16[64,1024]{1,0:T(8,128)(2,1)S(1)}, bf16[64,1024]{1,0:T(8,128)(2,1)S(1)}, bf16[64,1024]{1,0:T(8,128)(2,1)S(1)}, bf16[64,1024]{1,0:T(8,128)(2,1)S(1)}) custom-call(s32[17]{0:T(128)S(1)} %get-tuple-element.205.place_ref, bf16[3,128,2048]{2,1,0:T(8,128)(2,1)} %get-tuple-element.204.refs_0_.refs_4_, ...), custom_call_target="tpu_custom_call" | custom-call | flops 161061280 | bytes 786432 | tf_op jit(solution)/shard_map/cond/branch_1_fun/input_grad/pallas_call | solution.py:104
  225.5 1.5 collective-permute-start.21
  227.0 1.5 collective-permute-start.22
  229.1 9.4 %weight_grad.6 = (bf16[1024,2048]{1,0:T(8,128)(2,1)}, bf16[1024,2048]{1,0:T(8,128)(2,1)}, bf16[1024,2048]{1,0:T(8,128)(2,1)}) custom-call(s32[17]{0:T(128)S(1)} %get-tuple-element.205.place_ref, bf16[8,256,256]{2,1,0:T(8,128)(2,1)} %get-tuple-element.213.refs_0_, bf16[8,256,256]{2,1,0:T(8,128)(2,1)} %get-tuple-element.214.refs_1_, ...), custom_call_target="tpu_custom_call" | custom-call | flops 161061280 | bytes 1415577 | tf_op jit(solution)/shard_map/cond/branch_1_fun/weight_grad/pallas_call | solution.py:158
  240.2 1.6 pad_maximum_fusion.4
  241.8 5.7 %collective-permute-done.31.refs_0_.refs_4_ = bf16[3,128,2048]{2,1,0:T(8,128)(2,1)S(1)} collective-permute-done((bf16[3,128,2048]{2,1,0:T(8,128)(2,1)S(1)}, bf16[3,128,2048]{2,1,0:T(8,128)(2,1)S(1)}, u32[]{:S(2)}, u32[]{:S(2)}) %collective-permute-start.31) | collective-permute-done | bytes 1572896 | tf_op jit(solution)/shard_map/ppermute | solution.py:290
  248.5 2.1 collective-permute-start.33
  251.0 9.2 %input_grad.9 = (bf16[64,1024]{1,0:T(8,128)(2,1)S(1)}, bf16[64,1024]{1,0:T(8,128)(2,1)S(1)}, bf16[64,1024]{1,0:T(8,128)(2,1)S(1)}, bf16[64,1024]{1,0:T(8,128)(2,1)S(1)}) custom-call(s32[17]{0:T(128)S(1)} %dynamic-slice_bitcast_fusion.place_ref, bf16[3,128,2048]{2,1,0:T(8,128)(2,1)S(1)} %collective-permute-done.31.refs_0_.refs_4_, ...), custom_call_target="tpu_custom_call" | custom-call | flops 161061280 | bytes 786432 | tf_op jit(solution)/shard_map/input_grad/pallas_call | solution.py:104
  260.3 1.6 collective-permute-start.35
  261.8 1.5 collective-permute-start.36
  263.8 2.5 collective-permute-done.35
  266.4 3.7 %collective-permute-done.36 = bf16[64,1024]{1,0:T(8,128)(2,1)S(1)} collective-permute-done((bf16[64,1024]{1,0:T(8,128)(2,1)S(1)}, bf16[64,1024]{1,0:T(8,128)(2,1)S(1)}, u32[]{:S(2)}, u32[]{:S(2)}) %collective-permute-start.36) | collective-permute-done | bytes 131104 | tf_op jit(solution)/shard_map/ppermute | solution.py:296
  270.2 1.2 collective-permute-done.39
  272.2 1.1 collective-permute-start.40
  273.3 9.4 %weight_grad.7 = (bf16[1024,2048]{1,0:T(8,128)(2,1)}, bf16[1024,2048]{1,0:T(8,128)(2,1)}, bf16[1024,2048]{1,0:T(8,128)(2,1)}) custom-call(s32[17]{0:T(128)S(1)} %dynamic-slice_bitcast_fusion.place_ref, bf16[8,256,256]{2,1,0:T(8,128)(2,1)} %get-tuple-element.352.refs_0_, bf16[8,256,256]{2,1,0:T(8,128)(2,1)} %get-tuple-element.353.refs_1_, ...), custom_call_target="tpu_custom_call" | custom-call | flops 161061280 | bytes 1415577 | tf_op jit(solution)/shard_map/weight_grad/pallas_call | solution.py:158
  282.7 1.6 sort_home.1
  284.3 1.3 collective-permute-start.41
  286.5 1.4 collective-permute-start.43
  287.9 2.2 collective-permute-start.44
  290.1 1.5 collective-permute-done.44
  291.6 1.6 collective-permute-start.45
  293.2 2.8 collective-permute-done.45
  297.4 1.6 collective-permute-done.43.refs_3_
  299.1 1.6 assemble.1
  (109 shorter events, 17.4 us)
Async XLA Ops:
  0.6 14.9 %copy-start.14 = (s32[1,256]{1,0:T(1,128)S(1)}, s32[1,256]{1,0:T(1,128)}, u32[]{:S(2)}) copy-start(s32[1,256]{1,0:T(1,128)} %flag_ref.1) | copy-start | bytes 3076
  11.8 62.1 %collective-permute-start.26 = (bf16[3,128,2048]{2,1,0:T(8,128)(2,1)}, bf16[3,128,2048]{2,1,0:T(8,128)(2,1)}, u32[]{:S(2)}, u32[]{:S(2)}) collective-permute-start(bf16[3,128,2048]{2,1,0:T(8,128)(2,1)} %get-tuple-element.303), channel_id=1, source_target_pairs={{0,8},{4,12},{8,24},{12,28},{24,16},{28,20},{16,0},{20,4},{1,9},{5... | collective-permute-start | bytes 4718600 | tf_op jit(solution)/shard_map/ppermute | solution.py:290
  16.8 7.8 %collective-permute-start.9 = (bf16[3,128,2048]{2,1,0:T(8,128)(2,1)}, bf16[3,128,2048]{2,1,0:T(8,128)(2,1)}, u32[]{:S(2)}, u32[]{:S(2)}) collective-permute-start(bf16[3,128,2048]{2,1,0:T(8,128)(2,1)} %get-tuple-element.124.refs_0_), channel_id=1, source_target_pairs={{0,4},{4,0},{8,12},{12,8},{16,20},{20,16},{24,28},{28,24},{1,5},{5... | collective-permute-start | bytes 4718600 | tf_op jit(solution)/shard_map/cond/branch_1_fun/ppermute | solution.py:293
  16.9 7.8 %collective-permute-start.10 = (bf16[3,128,2048]{2,1,0:T(8,128)(2,1)}, bf16[3,128,2048]{2,1,0:T(8,128)(2,1)S(1)}, u32[]{:S(2)}, u32[]{:S(2)}) collective-permute-start(bf16[3,128,2048]{2,1,0:T(8,128)(2,1)} %get-tuple-element.125.refs_2_), channel_id=1, source_target_pairs={{0,4},{4,0},{8,12},{12,8},{16,20},{20,16},{24,28},{28,24},{1,5},{5... | collective-permute-start | bytes 4718600 | tf_op jit(solution)/shard_map/cond/branch_1_fun/ppermute | solution.py:293
  20.4 18.5 %all-to-all-start = ((bf16[4,2,256,256]{3,2,1,0:T(8,128)(2,1)}), bf16[4,2,256,256]{3,2,1,0:T(8,128)(2,1)}, u32[]{:S(2)}, u32[]{:S(2)}) async-start(bf16[4,2,256,256]{3,2,1,0:T(8,128)(2,1)} %bitcast.23), calls=%async_computation | async-start | bytes 2097152 | tf_op jit(solution)/shard_map/cond/branch_1_fun/all_to_all | solution.py:271
  24.7 11.8 %copy-start = (bf16[3,128,2048]{2,1,0:T(8,128)(2,1)}, bf16[3,128,2048]{2,1,0:T(8,128)(2,1)S(1)}, u32[]{:S(2)}) copy-start(bf16[3,128,2048]{2,1,0:T(8,128)(2,1)S(1)} %collective-permute-done.10.refs_3_.refs_7_) | copy-start | bytes 4718596 | tf_op jit(solution)/shard_map/cond
  38.9 34.2 %copy-start.1 = (bf16[3,128,2048]{2,1,0:T(8,128)(2,1)S(1)}, bf16[3,128,2048]{2,1,0:T(8,128)(2,1)}, u32[]{:S(2)}) copy-start(bf16[3,128,2048]{2,1,0:T(8,128)(2,1)} %copy-done) | copy-start | bytes 4718596 | tf_op jit(solution)/shard_map/cond
  38.9 34.2 %all-to-all-start.1 = ((bf16[8,256,256]{2,1,0:T(8,128)(2,1)}), bf16[8,256,256]{2,1,0:T(8,128)(2,1)}, u32[]{:S(2)}, u32[]{:S(2)}) async-start(bf16[8,256,256]{2,1,0:T(8,128)(2,1)} %bitcast.3), calls=%async_computation.1 | async-start | bytes 2097152 | tf_op jit(solution)/shard_map/cond/branch_1_fun/all_to_all | solution.py:271
  43.3 9.2 %collective-permute-start.11 = (bf16[128,1024]{1,0:T(8,128)(2,1)S(1)}, bf16[128,1024]{1,0:T(8,128)(2,1)S(1)}, u32[]{:S(2)}, u32[]{:S(2)}) collective-permute-start(bf16[128,1024]{1,0:T(8,128)(2,1)S(1)} %get-tuple-element.131), channel_id=1, source_target_pairs={{0,1},{1,0},{2,3},{3,2},{4,5},{5,4},{6,7},{7,6},{8,9},{9,8},{10,11... | collective-permute-start | bytes 786440 | tf_op jit(solution)/shard_map/cond/branch_1_fun/ppermute | solution.py:296
  44.8 13.9 %collective-permute-start.12 = (bf16[128,1024]{1,0:T(8,128)(2,1)S(1)}, bf16[128,1024]{1,0:T(8,128)(2,1)S(1)}, u32[]{:S(2)}, u32[]{:S(2)}) collective-permute-start(bf16[128,1024]{1,0:T(8,128)(2,1)S(1)} %get-tuple-element.132), channel_id=1, source_target_pairs={{0,2},{1,3},{2,0},{3,1},{4,6},{5,7},{6,4},{7,5},{8,10},{9,11},{10,... | collective-permute-start | bytes 786440 | tf_op jit(solution)/shard_map/cond/branch_1_fun/ppermute | solution.py:296
  45.3 13.3 %collective-permute-start.13 = (bf16[128,1024]{1,0:T(8,128)(2,1)S(1)}, bf16[128,1024]{1,0:T(8,128)(2,1)S(1)}, u32[]{:S(2)}, u32[]{:S(2)}) collective-permute-start(bf16[128,1024]{1,0:T(8,128)(2,1)S(1)} %get-tuple-element.133), channel_id=1, source_target_pairs={{0,3},{1,2},{2,1},{3,0},{4,7},{5,6},{6,5},{7,4},{8,11},{9,10},{10,... | collective-permute-start | bytes 786440 | tf_op jit(solution)/shard_map/cond/branch_1_fun/ppermute | solution.py:296
  58.8 1.4 collective-permute-start.14
  73.1 38.6 %copy-start.11 = (bf16[2,64,1024]{2,1,0:T(8,128)(2,1)}, bf16[2,64,1024]{2,1,0:T(8,128)(2,1)S(1)}, u32[]{:S(2)}) copy-start(bf16[2,64,1024]{2,1,0:T(8,128)(2,1)S(1)} %get-tuple-element.338.refs_0_) | copy-start | bytes 786436
  73.1 38.5 %collective-permute-start.28 = (bf16[3,128,2048]{2,1,0:T(8,128)(2,1)}, bf16[3,128,2048]{2,1,0:T(8,128)(2,1)}, u32[]{:S(2)}, u32[]{:S(2)}) collective-permute-start(bf16[3,128,2048]{2,1,0:T(8,128)(2,1)} %get-tuple-element.310), channel_id=1, source_target_pairs={{0,8},{4,12},{8,24},{12,28},{24,16},{28,20},{16,0},{20,4},{1,9},{5... | collective-permute-start | bytes 4718600 | tf_op jit(solution)/shard_map/ppermute | solution.py:290
  73.9 27.1 %collective-permute-start = (bf16[3,128,2048]{2,1,0:T(8,128)(2,1)}, bf16[3,128,2048]{2,1,0:T(8,128)(2,1)}, u32[]{:S(2)}, u32[]{:S(2)}) collective-permute-start(bf16[3,128,2048]{2,1,0:T(8,128)(2,1)} %get-tuple-element.140), channel_id=1, source_target_pairs={{0,4},{4,0},{8,12},{12,8},{16,20},{20,16},{24,28},{28,24},{1,5},{5... | collective-permute-start | bytes 4718600 | tf_op jit(solution)/shard_map/cond/branch_1_fun/ppermute | solution.py:293
  73.9 25.9 %collective-permute-start.2 = (bf16[8,256,256]{2,1,0:T(8,128)(2,1)}, bf16[8,256,256]{2,1,0:T(8,128)(2,1)}, u32[]{:S(2)}, u32[]{:S(2)}) collective-permute-start(bf16[8,256,256]{2,1,0:T(8,128)(2,1)} %get-tuple-element.141), channel_id=1, source_target_pairs={{0,2},{1,3},{2,0},{3,1},{4,6},{5,7},{6,4},{7,5},{8,10},{9,11},{10,... | collective-permute-start | bytes 3145736 | tf_op jit(solution)/shard_map/cond/branch_1_fun/ppermute | solution.py:296
  75.4 25.6 %collective-permute-start.1 = (bf16[8,256,256]{2,1,0:T(8,128)(2,1)}, bf16[8,256,256]{2,1,0:T(8,128)(2,1)}, u32[]{:S(2)}, u32[]{:S(2)}) collective-permute-start(bf16[8,256,256]{2,1,0:T(8,128)(2,1)} %get-tuple-element.141), channel_id=1, source_target_pairs={{0,1},{1,0},{2,3},{3,2},{4,5},{5,4},{6,7},{7,6},{8,9},{9,8},{10,11... | collective-permute-start | bytes 3145736 | tf_op jit(solution)/shard_map/cond/branch_1_fun/ppermute | solution.py:296
  101.0 44.1 %collective-permute-start.27 = (bf16[3,128,2048]{2,1,0:T(8,128)(2,1)}, bf16[3,128,2048]{2,1,0:T(8,128)(2,1)}, u32[]{:S(2)}, u32[]{:S(2)}) collective-permute-start(bf16[3,128,2048]{2,1,0:T(8,128)(2,1)} %collective-permute-done.26), channel_id=1, source_target_pairs={{0,8},{4,12},{8,24},{12,28},{24,16},{28,20},{16,0},{20,4},{1,9},{5... | collective-permute-start | bytes 4718600 | tf_op jit(solution)/shard_map/ppermute | solution.py:290
  111.6 3.8 %collective-permute-start.3 = (bf16[3,128,2048]{2,1,0:T(8,128)(2,1)}, bf16[3,128,2048]{2,1,0:T(8,128)(2,1)}, u32[]{:S(2)}, u32[]{:S(2)}) collective-permute-start(bf16[3,128,2048]{2,1,0:T(8,128)(2,1)} %get-tuple-element.142.refs_2_), channel_id=1, source_target_pairs={{0,4},{4,0},{8,12},{12,8},{16,20},{20,16},{24,28},{28,24},{1,5},{5... | collective-permute-start | bytes 4718600 | tf_op jit(solution)/shard_map/cond/branch_1_fun/ppermute | solution.py:293
  111.6 26.8 %collective-permute-start.4 = (bf16[8,256,256]{2,1,0:T(8,128)(2,1)}, bf16[8,256,256]{2,1,0:T(8,128)(2,1)}, u32[]{:S(2)}, u32[]{:S(2)}) collective-permute-start(bf16[8,256,256]{2,1,0:T(8,128)(2,1)} %get-tuple-element.153), channel_id=1, source_target_pairs={{0,3},{1,2},{2,1},{3,0},{4,7},{5,6},{6,5},{7,4},{8,11},{9,10},{10,... | collective-permute-start | bytes 3145736 | tf_op jit(solution)/shard_map/cond/branch_1_fun/ppermute | solution.py:296
  138.4 40.3 %collective-permute-start.30 = (bf16[3,128,2048]{2,1,0:T(8,128)(2,1)}, bf16[3,128,2048]{2,1,0:T(8,128)(2,1)S(1)}, u32[]{:S(2)}, u32[]{:S(2)}) collective-permute-start(bf16[3,128,2048]{2,1,0:T(8,128)(2,1)} %collective-permute-done.28), channel_id=1, source_target_pairs={{0,8},{4,12},{8,24},{12,28},{24,16},{28,20},{16,0},{20,4},{1,9},{5... | collective-permute-start | bytes 4718600 | tf_op jit(solution)/shard_map/ppermute | solution.py:290
  145.1 24.3 %collective-permute-start.15 = (bf16[3,128,2048]{2,1,0:T(8,128)(2,1)}, bf16[3,128,2048]{2,1,0:T(8,128)(2,1)}, u32[]{:S(2)}, u32[]{:S(2)}) collective-permute-start(bf16[3,128,2048]{2,1,0:T(8,128)(2,1)} %get-tuple-element.154), channel_id=1, source_target_pairs={{0,4},{4,0},{8,12},{12,8},{16,20},{20,16},{24,28},{28,24},{1,5},{5... | collective-permute-start | bytes 4718600 | tf_op jit(solution)/shard_map/cond/branch_1_fun/ppermute | solution.py:293
  145.1 22.6 %collective-permute-start.16 = (bf16[128,1024]{1,0:T(8,128)(2,1)}, bf16[128,1024]{1,0:T(8,128)(2,1)S(1)}, u32[]{:S(2)}, u32[]{:S(2)}) collective-permute-start(bf16[128,1024]{1,0:T(8,128)(2,1)} %get-tuple-element.156), channel_id=1, source_target_pairs={{0,1},{1,0},{2,3},{3,2},{4,5},{5,4},{6,7},{7,6},{8,9},{9,8},{10,11... | collective-permute-start | bytes 786440 | tf_op jit(solution)/shard_map/cond/branch_1_fun/ppermute | solution.py:296
  146.0 21.7 %collective-permute-start.17 = (bf16[128,1024]{1,0:T(8,128)(2,1)}, bf16[128,1024]{1,0:T(8,128)(2,1)S(1)}, u32[]{:S(2)}, u32[]{:S(2)}) collective-permute-start(bf16[128,1024]{1,0:T(8,128)(2,1)} %get-tuple-element.157), channel_id=1, source_target_pairs={{0,2},{1,3},{2,0},{3,1},{4,6},{5,7},{6,4},{7,5},{8,10},{9,11},{10,... | collective-permute-start | bytes 786440 | tf_op jit(solution)/shard_map/cond/branch_1_fun/ppermute | solution.py:296
  147.6 20.2 %collective-permute-start.18 = (bf16[128,1024]{1,0:T(8,128)(2,1)}, bf16[128,1024]{1,0:T(8,128)(2,1)S(1)}, u32[]{:S(2)}, u32[]{:S(2)}) collective-permute-start(bf16[128,1024]{1,0:T(8,128)(2,1)} %get-tuple-element.158), channel_id=1, source_target_pairs={{0,3},{1,2},{2,1},{3,0},{4,7},{5,6},{6,5},{7,4},{8,11},{9,10},{10,... | collective-permute-start | bytes 786440 | tf_op jit(solution)/shard_map/cond/branch_1_fun/ppermute | solution.py:296
  168.0 1.4 collective-permute-start.19
  169.5 9.3 %copy-start.12 = (bf16[2,64,1024]{2,1,0:T(8,128)(2,1)}, bf16[2,64,1024]{2,1,0:T(8,128)(2,1)S(1)}, u32[]{:S(2)}) copy-start(bf16[2,64,1024]{2,1,0:T(8,128)(2,1)S(1)} %get-tuple-element.339) | copy-start | bytes 786436
  169.5 41.8 %collective-permute-start.29 = (bf16[3,128,2048]{2,1,0:T(8,128)(2,1)}, bf16[3,128,2048]{2,1,0:T(8,128)(2,1)}, u32[]{:S(2)}, u32[]{:S(2)}) collective-permute-start(bf16[3,128,2048]{2,1,0:T(8,128)(2,1)} %collective-permute-done.27), channel_id=1, source_target_pairs={{0,8},{4,12},{8,24},{12,28},{24,16},{28,20},{16,0},{20,4},{1,9},{5... | collective-permute-start | bytes 4718600 | tf_op jit(solution)/shard_map/ppermute | solution.py:290
  178.7 3.5 %collective-permute-start.5 = (bf16[3,128,2048]{2,1,0:T(8,128)(2,1)S(1)}, bf16[3,128,2048]{2,1,0:T(8,128)(2,1)}, u32[]{:S(2)}, u32[]{:S(2)}) collective-permute-start(bf16[3,128,2048]{2,1,0:T(8,128)(2,1)S(1)} %get-tuple-element.179.refs_2_.refs_6_), channel_id=1, source_target_pairs={{0,4},{4,0},{8,12},{12,8},{16,20},{20,16},{24,28},{28,24},{1,5},{5... | collective-permute-start | bytes 4718600 | tf_op jit(solution)/shard_map/cond/branch_1_fun/ppermute | solution.py:293
  182.3 16.1 %copy-start.2 = (bf16[1024,2048]{1,0:T(8,128)(2,1)S(1)}, bf16[1024,2048]{1,0:T(8,128)(2,1)}, u32[]{:S(2)}) copy-start(bf16[1024,2048]{1,0:T(8,128)(2,1)} %get-tuple-element.196.refs_10_) | copy-start | bytes 12582916 | tf_op jit(solution)/shard_map/cond
  182.3 16.1 %copy-start.3 = (bf16[1024,2048]{1,0:T(8,128)(2,1)S(1)}, bf16[1024,2048]{1,0:T(8,128)(2,1)}, u32[]{:S(2)}) copy-start(bf16[1024,2048]{1,0:T(8,128)(2,1)} %get-tuple-element.195.refs_9_) | copy-start | bytes 12582916 | tf_op jit(solution)/shard_map/cond
  182.3 16.1 %copy-start.4 = (bf16[1024,2048]{1,0:T(8,128)(2,1)S(1)}, bf16[1024,2048]{1,0:T(8,128)(2,1)}, u32[]{:S(2)}) copy-start(bf16[1024,2048]{1,0:T(8,128)(2,1)} %get-tuple-element.194.refs_8_) | copy-start | bytes 12582916 | tf_op jit(solution)/shard_map/cond
  194.8 16.0 %collective-permute-start.6 = (bf16[128,1024]{1,0:T(8,128)(2,1)S(1)}, bf16[128,1024]{1,0:T(8,128)(2,1)S(1)}, u32[]{:S(2)}, u32[]{:S(2)}) collective-permute-start(bf16[128,1024]{1,0:T(8,128)(2,1)S(1)} %get-tuple-element.187), channel_id=1, source_target_pairs={{0,1},{1,0},{2,3},{3,2},{4,5},{5,4},{6,7},{7,6},{8,9},{9,8},{10,11... | collective-permute-start | bytes 786440 | tf_op jit(solution)/shard_map/cond/branch_1_fun/ppermute | solution.py:296
  195.8 15.0 %collective-permute-start.7 = (bf16[128,1024]{1,0:T(8,128)(2,1)S(1)}, bf16[128,1024]{1,0:T(8,128)(2,1)S(1)}, u32[]{:S(2)}, u32[]{:S(2)}) collective-permute-start(bf16[128,1024]{1,0:T(8,128)(2,1)S(1)} %get-tuple-element.188), channel_id=1, source_target_pairs={{0,2},{1,3},{2,0},{3,1},{4,6},{5,7},{6,4},{7,5},{8,10},{9,11},{10,... | collective-permute-start | bytes 786440 | tf_op jit(solution)/shard_map/cond/branch_1_fun/ppermute | solution.py:296
  197.3 13.5 %collective-permute-start.8 = (bf16[128,1024]{1,0:T(8,128)(2,1)S(1)}, bf16[128,1024]{1,0:T(8,128)(2,1)S(1)}, u32[]{:S(2)}, u32[]{:S(2)}) collective-permute-start(bf16[128,1024]{1,0:T(8,128)(2,1)S(1)} %get-tuple-element.189), channel_id=1, source_target_pairs={{0,3},{1,2},{2,1},{3,0},{4,7},{5,6},{6,5},{7,4},{8,11},{9,10},{10,... | collective-permute-start | bytes 786440 | tf_op jit(solution)/shard_map/cond/branch_1_fun/ppermute | solution.py:296
  211.0 36.5 %collective-permute-start.31 = (bf16[3,128,2048]{2,1,0:T(8,128)(2,1)S(1)}, bf16[3,128,2048]{2,1,0:T(8,128)(2,1)S(1)}, u32[]{:S(2)}, u32[]{:S(2)}) collective-permute-start(bf16[3,128,2048]{2,1,0:T(8,128)(2,1)S(1)} %collective-permute-done.30), channel_id=1, source_target_pairs={{0,8},{4,12},{8,24},{12,28},{24,16},{28,20},{16,0},{20,4},{1,9},{5... | collective-permute-start | bytes 4718600 | tf_op jit(solution)/shard_map/ppermute | solution.py:290
  211.3 39.2 %copy-start.13 = (f32[16,1,128]{2,1,0:T(1,128)S(1)}, f32[16,1,128]{2,1,0:T(1,128)}, u32[]{:S(2)}) copy-start(f32[16,1,128]{2,1,0:T(1,128)} %get-tuple-element.346) | copy-start | bytes 24580
  211.3 3.8 %collective-permute-start.20 = (bf16[3,128,2048]{2,1,0:T(8,128)(2,1)}, bf16[3,128,2048]{2,1,0:T(8,128)(2,1)}, u32[]{:S(2)}, u32[]{:S(2)}) collective-permute-start(bf16[3,128,2048]{2,1,0:T(8,128)(2,1)} %get-tuple-element.204.refs_0_.refs_4_), channel_id=1, source_target_pairs={{0,4},{4,0},{8,12},{12,8},{16,20},{20,16},{24,28},{28,24},{1,5},{5... | collective-permute-start | bytes 4718600 | tf_op jit(solution)/shard_map/cond/branch_1_fun/ppermute | solution.py:293
  215.1 14.0 %copy-start.8 = (bf16[1024,2048]{1,0:T(8,128)(2,1)S(1)}, bf16[1024,2048]{1,0:T(8,128)(2,1)}, u32[]{:S(2)}) copy-start(bf16[1024,2048]{1,0:T(8,128)(2,1)} %get-tuple-element.219.refs_8_) | copy-start | bytes 12582916 | tf_op jit(solution)/shard_map/cond
  215.1 14.0 %copy-start.9 = (bf16[1024,2048]{1,0:T(8,128)(2,1)S(1)}, bf16[1024,2048]{1,0:T(8,128)(2,1)}, u32[]{:S(2)}) copy-start(bf16[1024,2048]{1,0:T(8,128)(2,1)} %get-tuple-element.218.refs_7_) | copy-start | bytes 12582916 | tf_op jit(solution)/shard_map/cond
  215.1 14.0 %copy-start.10 = (bf16[1024,2048]{1,0:T(8,128)(2,1)S(1)}, bf16[1024,2048]{1,0:T(8,128)(2,1)}, u32[]{:S(2)}) copy-start(bf16[1024,2048]{1,0:T(8,128)(2,1)} %get-tuple-element.217.refs_6_) | copy-start | bytes 12582916 | tf_op jit(solution)/shard_map/cond
  225.5 13.1 %collective-permute-start.21 = (bf16[64,1024]{1,0:T(8,128)(2,1)S(1)}, bf16[64,1024]{1,0:T(8,128)(2,1)S(1)}, u32[]{:S(2)}, u32[]{:S(2)}) collective-permute-start(bf16[64,1024]{1,0:T(8,128)(2,1)S(1)} %get-tuple-element.210), channel_id=1, source_target_pairs={{0,1},{1,0},{2,3},{3,2},{4,5},{5,4},{6,7},{7,6},{8,9},{9,8},{10,11... | collective-permute-start | bytes 393224 | tf_op jit(solution)/shard_map/cond/branch_1_fun/ppermute | solution.py:296
  227.0 11.5 %collective-permute-start.22 = (bf16[64,1024]{1,0:T(8,128)(2,1)S(1)}, bf16[64,1024]{1,0:T(8,128)(2,1)S(1)}, u32[]{:S(2)}, u32[]{:S(2)}) collective-permute-start(bf16[64,1024]{1,0:T(8,128)(2,1)S(1)} %get-tuple-element.211), channel_id=1, source_target_pairs={{0,2},{1,3},{2,0},{3,1},{4,6},{5,7},{6,4},{7,5},{8,10},{9,11},{10,... | collective-permute-start | bytes 393224 | tf_op jit(solution)/shard_map/cond/branch_1_fun/ppermute | solution.py:296
  228.6 10.0 %collective-permute-start.23 = (bf16[64,1024]{1,0:T(8,128)(2,1)S(1)}, bf16[64,1024]{1,0:T(8,128)(2,1)}, u32[]{:S(2)}, u32[]{:S(2)}) collective-permute-start(bf16[64,1024]{1,0:T(8,128)(2,1)S(1)} %get-tuple-element.212), channel_id=1, source_target_pairs={{0,3},{1,2},{2,1},{3,0},{4,7},{5,6},{6,5},{7,4},{8,11},{9,10},{10,... | collective-permute-start | bytes 393224 | tf_op jit(solution)/shard_map/cond/branch_1_fun/ppermute | solution.py:296
  229.1 11.1 %collective-permute-start.25 = (bf16[64,1024]{1,0:T(8,128)(2,1)}, bf16[64,1024]{1,0:T(8,128)(2,1)}, u32[]{:S(2)}, u32[]{:S(2)}) collective-permute-start(bf16[64,1024]{1,0:T(8,128)(2,1)} %pad_maximum_fusion.6), channel_id=1, source_target_pairs={{0,4},{4,0},{8,12},{12,8},{16,20},{20,16},{24,28},{28,24},{1,5},{5... | collective-permute-start | bytes 393224 | tf_op jit(solution)/shard_map/cond/branch_1_fun/ppermute | solution.py:293
  239.6 2.2 collective-permute-start.24
  247.5 3.5 %collective-permute-start.34 = (bf16[3,128,2048]{2,1,0:T(8,128)(2,1)S(1)}, bf16[3,128,2048]{2,1,0:T(8,128)(2,1)S(1)}, u32[]{:S(2)}, u32[]{:S(2)}) collective-permute-start(bf16[3,128,2048]{2,1,0:T(8,128)(2,1)S(1)} %collective-permute-done.31.refs_0_.refs_4_), channel_id=1, source_target_pairs={{0,4},{4,0},{8,12},{12,8},{16,20},{20,16},{24,28},{28,24},{1,5},{5... | collective-permute-start | bytes 4718600 | tf_op jit(solution)/shard_map/ppermute | solution.py:293
  247.5 16.3 %collective-permute-start.32 = (bf16[2,64,1024]{2,1,0:T(8,128)(2,1)}, bf16[2,64,1024]{2,1,0:T(8,128)(2,1)S(1)}, u32[]{:S(2)}, u32[]{:S(2)}) collective-permute-start(bf16[2,64,1024]{2,1,0:T(8,128)(2,1)} %copy-done.12), channel_id=1, source_target_pairs={{0,16},{4,20},{8,0},{12,4},{24,8},{28,12},{16,24},{20,28},{1,17},{... | collective-permute-start | bytes 786440 | tf_op jit(solution)/shard_map/ppermute | solution.py:393
  248.5 15.4 %collective-permute-start.33 = (bf16[2,64,1024]{2,1,0:T(8,128)(2,1)}, bf16[2,64,1024]{2,1,0:T(8,128)(2,1)S(1)}, u32[]{:S(2)}, u32[]{:S(2)}) collective-permute-start(bf16[2,64,1024]{2,1,0:T(8,128)(2,1)} %get-tuple-element.340), channel_id=1, source_target_pairs={{0,24},{4,28},{8,16},{12,20},{24,0},{28,4},{16,8},{20,12},{1,25},{... | collective-permute-start | bytes 786440 | tf_op jit(solution)/shard_map/ppermute | solution.py:393
  250.7 12.6 %collective-permute-start.38 = (f32[16]{0:T(128)S(1)}, f32[16]{0:T(128)S(1)}, u32[]{:S(2)}, u32[]{:S(2)}) collective-permute-start(f32[16]{0:T(128)S(1)} %slice_reduce_fusion), channel_id=1, source_target_pairs={{0,4},{4,0},{8,12},{12,8},{16,20},{20,16},{24,28},{28,24},{1,5},{5... | collective-permute-start | bytes 200 | tf_op jit(solution)/shard_map/ppermute | solution.py:403
  251.0 22.3 %copy-start.5 = (bf16[1024,2048]{1,0:T(8,128)(2,1)S(1)}, bf16[1024,2048]{1,0:T(8,128)(2,1)}, u32[]{:S(2)}) copy-start(bf16[1024,2048]{1,0:T(8,128)(2,1)} %get-tuple-element.358.refs_8_) | copy-start | bytes 12582916
  251.0 22.3 %copy-start.6 = (bf16[1024,2048]{1,0:T(8,128)(2,1)S(1)}, bf16[1024,2048]{1,0:T(8,128)(2,1)}, u32[]{:S(2)}) copy-start(bf16[1024,2048]{1,0:T(8,128)(2,1)} %get-tuple-element.357.refs_7_) | copy-start | bytes 12582916
  251.0 22.3 %copy-start.7 = (bf16[1024,2048]{1,0:T(8,128)(2,1)S(1)}, bf16[1024,2048]{1,0:T(8,128)(2,1)}, u32[]{:S(2)}) copy-start(bf16[1024,2048]{1,0:T(8,128)(2,1)} %get-tuple-element.356.refs_6_) | copy-start | bytes 12582916
  260.3 6.1 %collective-permute-start.35 = (bf16[64,1024]{1,0:T(8,128)(2,1)S(1)}, bf16[64,1024]{1,0:T(8,128)(2,1)S(1)}, u32[]{:S(2)}, u32[]{:S(2)}) collective-permute-start(bf16[64,1024]{1,0:T(8,128)(2,1)S(1)} %get-tuple-element.343), channel_id=1, source_target_pairs={{0,1},{1,0},{2,3},{3,2},{4,5},{5,4},{6,7},{7,6},{8,9},{9,8},{10,11... | collective-permute-start | bytes 393224 | tf_op jit(solution)/shard_map/ppermute | solution.py:296
  261.8 8.2 %collective-permute-start.36 = (bf16[64,1024]{1,0:T(8,128)(2,1)S(1)}, bf16[64,1024]{1,0:T(8,128)(2,1)S(1)}, u32[]{:S(2)}, u32[]{:S(2)}) collective-permute-start(bf16[64,1024]{1,0:T(8,128)(2,1)S(1)} %get-tuple-element.344), channel_id=1, source_target_pairs={{0,2},{1,3},{2,0},{3,1},{4,6},{5,7},{6,4},{7,5},{8,10},{9,11},{10,... | collective-permute-start | bytes 393224 | tf_op jit(solution)/shard_map/ppermute | solution.py:296
  263.4 6.7 %collective-permute-start.37 = (bf16[64,1024]{1,0:T(8,128)(2,1)S(1)}, bf16[64,1024]{1,0:T(8,128)(2,1)S(1)}, u32[]{:S(2)}, u32[]{:S(2)}) collective-permute-start(bf16[64,1024]{1,0:T(8,128)(2,1)S(1)} %get-tuple-element.345), channel_id=1, source_target_pairs={{0,3},{1,2},{2,1},{3,0},{4,7},{5,6},{6,5},{7,4},{8,11},{9,10},{10,... | collective-permute-start | bytes 393224 | tf_op jit(solution)/shard_map/ppermute | solution.py:296
  270.1 1.3 collective-permute-start.39
  272.2 10.5 %collective-permute-start.40 = (bf16[2,64,1024]{2,1,0:T(8,128)(2,1)}, bf16[2,64,1024]{2,1,0:T(8,128)(2,1)S(1)}, u32[]{:S(2)}, u32[]{:S(2)}) collective-permute-start(bf16[2,64,1024]{2,1,0:T(8,128)(2,1)} %maximum_maximum_fusion), channel_id=1, source_target_pairs={{0,8},{4,12},{8,24},{12,28},{24,16},{28,20},{16,0},{20,4},{1,9},{5... | collective-permute-start | bytes 786440 | tf_op jit(solution)/shard_map/ppermute | solution.py:393
  284.3 12.2 %collective-permute-start.41 = (bf16[2,64,1024]{2,1,0:T(8,128)(2,1)S(1)}, bf16[2,64,1024]{2,1,0:T(8,128)(2,1)S(1)}, u32[]{:S(2)}, u32[]{:S(2)}) collective-permute-start(bf16[2,64,1024]{2,1,0:T(8,128)(2,1)S(1)} %get-tuple-element.362), channel_id=1, source_target_pairs={{0,1},{1,0},{2,3},{3,2},{4,5},{5,4},{6,7},{7,6},{8,9},{9,8},{10,11... | collective-permute-start | bytes 786440 | tf_op jit(solution)/shard_map/ppermute | solution.py:296
  285.6 11.8 %collective-permute-start.42 = (bf16[2,64,1024]{2,1,0:T(8,128)(2,1)S(1)}, bf16[2,64,1024]{2,1,0:T(8,128)(2,1)S(1)}, u32[]{:S(2)}, u32[]{:S(2)}) collective-permute-start(bf16[2,64,1024]{2,1,0:T(8,128)(2,1)S(1)} %get-tuple-element.363), channel_id=1, source_target_pairs={{0,2},{1,3},{2,0},{3,1},{4,6},{5,7},{6,4},{7,5},{8,10},{9,11},{10,... | collective-permute-start | bytes 786440 | tf_op jit(solution)/shard_map/ppermute | solution.py:296
  286.5 12.6 %collective-permute-start.43 = (bf16[2,64,1024]{2,1,0:T(8,128)(2,1)S(1)}, bf16[2,64,1024]{2,1,0:T(8,128)(2,1)S(1)}, u32[]{:S(2)}, u32[]{:S(2)}) collective-permute-start(bf16[2,64,1024]{2,1,0:T(8,128)(2,1)S(1)} %get-tuple-element.364), channel_id=1, source_target_pairs={{0,3},{1,2},{2,1},{3,0},{4,7},{5,6},{6,5},{7,4},{8,11},{9,10},{10,... | collective-permute-start | bytes 786440 | tf_op jit(solution)/shard_map/ppermute | solution.py:296
  287.9 3.7 %collective-permute-start.44 = (f32[16]{0:T(128)S(1)}, f32[16]{0:T(128)S(1)}, u32[]{:S(2)}, u32[]{:S(2)}) collective-permute-start(f32[16]{0:T(128)S(1)} %add.62), channel_id=1, source_target_pairs={{0,8},{4,12},{8,0},{12,4},{16,24},{20,28},{24,16},{28,20},{1,9},{5... | collective-permute-start | bytes 200 | tf_op jit(solution)/shard_map/ppermute | solution.py:403
  291.6 4.4 %collective-permute-start.45 = (f32[16]{0:T(128)S(1)}, f32[16]{0:T(128)S(1)}, u32[]{:S(2)}, u32[]{:S(2)}) collective-permute-start(f32[16]{0:T(128)S(1)} %add.66), channel_id=1, source_target_pairs={{0,16},{4,20},{8,24},{12,28},{16,0},{20,4},{24,8},{28,12},{1,17},{... | collective-permute-start | bytes 200 | tf_op jit(solution)/shard_map/ppermute | solution.py:403

commit v5 on v4

--- a/solution.py
+++ b/solution.py
@@ -405,13 +405,13 @@
     bias_grad = folded(bias_part, 0, landed)
     total = summed(partial, (at_home, bias_grad))
     sooner = homeward(jnp.concatenate([sooner, shared(total, sizes[last:])], axis=1), final)
-    weight_grads = weight_part(after(x, total), [(final, last)], [both(final, last)], weight_grads)
-    at_home.append(after(sooner, weight_grads[0]))
+    for bit in range(1, row_count.bit_length() - 1):
+        bias_grad = folded(bias_grad, bit, total)
+    at_home.append(after(sooner, bias_grad))
     mine = sort_home(place, at_home, col_count, spread)
     got = [across(mine[d], d) if d else mine[d] for d in range(col_count)]
-    for bit in range(1, row_count.bit_length() - 1):
-        bias_grad = folded(bias_grad, bit, mine[0])
-    layer_grad = assemble(place, after(got, bias_grad), sizes)
+    weight_grads = weight_part(after(x, mine), [(final, last)], [both(final, last)], weight_grads)
+    layer_grad = assemble(place, after(got, weight_grads[0]), sizes)
     return (layer_grad, *weight_grads, bias_grad)
 
 

time: 301 us -> 299 us (level)
  no operation moved by 1% of the time
where the time goes in v5:
time: 299 us
  Pallas kernels  120 us (40%)
  waiting for transfers between devices  113 us (38%)
  starting transfers between devices  55.1 us (18%)
  other arithmetic  5.15 us (2%)
  local copies, waits for them, and re-layouts  4.05 us (1%)
    pallas_call x5, Pallas kernels, input_grad(): pl.pallas_call(functools.partial(input_grad_body, len(grads)), grid_spec=...  55.9 us
    ppermute x21, waiting for transfers between devices, across(): return lax.ppermute(mine, 'col', [(n, n ^ apart) for n in range(col_count)])  52.1 us
    pallas_call x4, Pallas kernels, weight_grad(): pl.pallas_call(functools.partial(weight_grad_body, len(x), tuple(units),...  50.6 us
    ppermute x6, waiting for transfers between devices, hop(): return lax.ppermute(mine, 'row', ring)  27.8 us
    ppermute x21, starting transfers between devices, across(): return lax.ppermute(mine, 'col', [(n, n ^ apart) for n in range(col_count)])  26.8 us
    all_to_all x2, waiting for transfers between devices, a2a(): return lax.all_to_all(array, axis, split_axis=0, concat_axis=0, tiled=True)  15.2 us
    ppermute x13, waiting for transfers between devices, other(): return lax.ppermute(mine, 'row', swap)  11.7 us
    pallas_call x1, Pallas kernels, attention(): pl.pallas_call(functools.partial(attention_body, sizes, head_dim, heads_s...  11.2 us
  transfers between devices with their start and end apart: 48, of which 23 were waited for; matrix products, arithmetic and copies ran while one was open for 3% of the time, Pallas kernels for 36%

profile of v5, /device:TPU:0, one launch (start us, length us, event | category | flops | bytes accessed | tf_op | source)
XLA Modules:
  0.0 298.5 jit_solution(16529332261955505491)
XLA Ops:
  0.6 11.2 %attention_back.1 = (bf16[3,128,2048]{2,1,0:T(8,128)(2,1)}, bf16[3,128,2048]{2,1,0:T(8,128)(2,1)}, f32[16,1,128]{2,1,0:T(1,128)}) custom-call(f32[16]{0:T(128)} %bias_ref.1, s32[1,256]{1,0:T(1,128)} %flag_ref.1, bf16[256,2048]{1,0:T(8,128)(2,1)} %bitcast.24, bf16[256,2048]{1,0:T(8,128)(2,1)} %bitcast.25, bf16[256,2048]{1,0:T(8,128)(2,1)} %bitcast.26, ...), custom_call_target="tpu_custom_call" | custom-call | flops 67108864 | bytes 367001 | tf_op jit(solution)/shard_map/attention_back/pallas_call | solution.py:57
  11.8 3.0 %collective-permute-start.26 = (bf16[3,128,2048]{2,1,0:T(8,128)(2,1)}, bf16[3,128,2048]{2,1,0:T(8,128)(2,1)}, u32[]{:S(2)}, u32[]{:S(2)}) collective-permute-start(bf16[3,128,2048]{2,1,0:T(8,128)(2,1)} %get-tuple-element.303), channel_id=1, source_target_pairs={{0,8},{4,12},{8,24},{12,28},{24,16},{28,20},{16,0},{20,4},{1,9},{5... | collective-permute-start | bytes 4718600 | tf_op jit(solution)/shard_map/ppermute | solution.py:290
  16.9 56.3 %conditional.6 = (bf16[3,128,2048]{2,1,0:T(8,128)(2,1)}, bf16[3,128,2048]{2,1,0:T(8,128)(2,1)S(1)}, bf16[2,64,1024]{2,1,0:T(8,128)(2,1)S(1)}, bf16[8,256,256]{2,1,0:T(8,128)(2,1)}) conditional(s32[]{:T(128)} %convert_element_type.83, () %tuple.76, (bf16[3,128,2048]{2,1,0:T(8,128)(2,1)}, bf16[3,128,2048]{2,1,0:T(8,128)(2,1)}, s32[17]{0:T(128)S(1)}, ...), branch_computations={%region_1.0_spmd, %region_2.0_spmd} | conditional | flops 323826496 | bytes 43149296 | solution.py:284
  17.4 1.8 reshape.14
  19.3 1.2 copy.20
  20.5 4.2 %all-to-all-start = ((bf16[4,2,256,256]{3,2,1,0:T(8,128)(2,1)}), bf16[4,2,256,256]{3,2,1,0:T(8,128)(2,1)}, u32[]{:S(2)}, u32[]{:S(2)}) async-start(bf16[4,2,256,256]{3,2,1,0:T(8,128)(2,1)} %bitcast.23), calls=%async_computation | async-start | bytes 2097152 | tf_op jit(solution)/shard_map/cond/branch_1_fun/all_to_all | solution.py:271
  24.8 11.8 %input_grad.5 = (bf16[128,1024]{1,0:T(8,128)(2,1)S(1)}, bf16[128,1024]{1,0:T(8,128)(2,1)S(1)}, bf16[128,1024]{1,0:T(8,128)(2,1)S(1)}, bf16[128,1024]{1,0:T(8,128)(2,1)S(1)}) custom-call(s32[17]{0:T(128)S(1)} %get-tuple-element.126.place_ref, bf16[3,128,2048]{2,1,0:T(8,128)(2,1)} %get-tuple-element.124.refs_0_, ...), custom_call_target="tpu_custom_call" | custom-call | flops 322122560 | bytes 943718 | tf_op jit(solution)/shard_map/cond/branch_1_fun/input_grad/pallas_call | solution.py:104
  36.5 2.4 all-to-all-done
  38.9 4.4 %all-to-all-start.1 = ((bf16[8,256,256]{2,1,0:T(8,128)(2,1)}), bf16[8,256,256]{2,1,0:T(8,128)(2,1)}, u32[]{:S(2)}, u32[]{:S(2)}) async-start(bf16[8,256,256]{2,1,0:T(8,128)(2,1)} %bitcast.3), calls=%async_computation.1 | async-start | bytes 2097152 | tf_op jit(solution)/shard_map/cond/branch_1_fun/all_to_all | solution.py:271
  43.3 1.5 collective-permute-start.11
  45.4 1.5 collective-permute-start.13
  46.9 5.6 %collective-permute-done.11 = bf16[128,1024]{1,0:T(8,128)(2,1)S(1)} collective-permute-done((bf16[128,1024]{1,0:T(8,128)(2,1)S(1)}, bf16[128,1024]{1,0:T(8,128)(2,1)S(1)}, u32[]{:S(2)}, u32[]{:S(2)}) %collective-permute-start.11) | collective-permute-done | bytes 262176 | tf_op jit(solution)/shard_map/cond/branch_1_fun/ppermute | solution.py:296
  52.5 6.2 %collective-permute-done.12 = bf16[128,1024]{1,0:T(8,128)(2,1)S(1)} collective-permute-done((bf16[128,1024]{1,0:T(8,128)(2,1)S(1)}, bf16[128,1024]{1,0:T(8,128)(2,1)S(1)}, u32[]{:S(2)}, u32[]{:S(2)}) %collective-permute-start.12) | collective-permute-done | bytes 262176 | tf_op jit(solution)/shard_map/cond/branch_1_fun/ppermute | solution.py:296
  59.0 1.3 collective-permute-done.14
  60.3 12.8 %all-to-all-done.1 = bf16[8,256,256]{2,1,0:T(8,128)(2,1)} async-done(((bf16[8,256,256]{2,1,0:T(8,128)(2,1)}), bf16[8,256,256]{2,1,0:T(8,128)(2,1)}, u32[]{:S(2)}, u32[]{:S(2)}) %all-to-all-start.1) | async-done | bytes 1048608 | tf_op jit(solution)/shard_map/cond/branch_1_fun/all_to_all | solution.py:271
  74.0 27.1 %conditional.7 = (bf16[3,128,2048]{2,1,0:T(8,128)(2,1)}, bf16[8,256,256]{2,1,0:T(8,128)(2,1)}, bf16[8,256,256]{2,1,0:T(8,128)(2,1)}) conditional(s32[]{:T(128)} %convert_element_type.83, () %tuple.79, (bf16[3,128,2048]{2,1,0:T(8,128)(2,1)}, bf16[8,256,256]{2,1,0:T(8,128)(2,1)}) %tuple.80), branch_computations={%region_3.0_spmd, %region_4.0_spmd} | conditional | bytes 14680208 | solution.py:284
  74.0 1.5 collective-permute-start.2
  75.5 1.5 collective-permute-start.1
  77.0 22.9 %collective-permute-done.2 = bf16[8,256,256]{2,1,0:T(8,128)(2,1)} collective-permute-done((bf16[8,256,256]{2,1,0:T(8,128)(2,1)}, bf16[8,256,256]{2,1,0:T(8,128)(2,1)}, u32[]{:S(2)}, u32[]{:S(2)}) %collective-permute-start.2) | collective-permute-done | bytes 1048608 | tf_op jit(solution)/shard_map/cond/branch_1_fun/ppermute | solution.py:296
  99.8 1.2 collective-permute-done.1
  101.1 3.4 %collective-permute-start.27 = (bf16[3,128,2048]{2,1,0:T(8,128)(2,1)}, bf16[3,128,2048]{2,1,0:T(8,128)(2,1)}, u32[]{:S(2)}, u32[]{:S(2)}) collective-permute-start(bf16[3,128,2048]{2,1,0:T(8,128)(2,1)} %collective-permute-done.26), channel_id=1, source_target_pairs={{0,8},{4,12},{8,24},{12,28},{24,16},{28,20},{16,0},{20,4},{1,9},{5... | collective-permute-start | bytes 4718600 | tf_op jit(solution)/shard_map/ppermute | solution.py:290
  104.5 7.2 %collective-permute-done.28 = bf16[3,128,2048]{2,1,0:T(8,128)(2,1)} collective-permute-done((bf16[3,128,2048]{2,1,0:T(8,128)(2,1)}, bf16[3,128,2048]{2,1,0:T(8,128)(2,1)}, u32[]{:S(2)}, u32[]{:S(2)}) %collective-permute-start.28) | collective-permute-done | bytes 1572896 | tf_op jit(solution)/shard_map/ppermute | solution.py:290
  111.7 26.8 %conditional.8 = (bf16[3,128,2048]{2,1,0:T(8,128)(2,1)}, bf16[128,1024]{1,0:T(8,128)(2,1)S(1)}, bf16[128,1024]{1,0:T(8,128)(2,1)}, bf16[128,1024]{1,0:T(8,128)(2...) conditional(s32[]{:T(128)} %convert_element_type.83, () %tuple.82, (bf16[3,128,2048]{2,1,0:T(8,128)(2,1)}, ...), branch_computations={%region_5.0_spmd, %region_6.0_spmd} | conditional | flops 322122560 | bytes 11429606 | solution.py:284
  111.7 2.5 collective-permute-start.4
  114.2 1.2 collective-permute-done.3.refs_3_.refs_7_
  115.4 12.9 %input_grad.6 = (bf16[128,1024]{1,0:T(8,128)(2,1)S(1)}, bf16[128,1024]{1,0:T(8,128)(2,1)}, bf16[128,1024]{1,0:T(8,128)(2,1)}, bf16[128,1024]{1,0:T(8,128)(2,1)}) custom-call(s32[17]{0:T(128)S(1)} %get-tuple-element.143.place_ref, bf16[3,128,2048]{2,1,0:T(8,128)(2,1)} %get-tuple-element.144.refs_0_, bf16[3,128,2048]{2,1,0:T(8,128)(2,1)} %get-tuple-element.145.refs_1_, ...), custom_call_target="tpu_custom_call" | custom-call | flops 322122560 | bytes 943718 | tf_op jit(solution)/shard_map/cond/branch_1_fun/input_grad/pallas_call | solution.py:104
  128.3 10.2 %collective-permute-done.4 = bf16[8,256,256]{2,1,0:T(8,128)(2,1)} collective-permute-done((bf16[8,256,256]{2,1,0:T(8,128)(2,1)}, bf16[8,256,256]{2,1,0:T(8,128)(2,1)}, u32[]{:S(2)}, u32[]{:S(2)}) %collective-permute-start.4) | collective-permute-done | bytes 1048608 | tf_op jit(solution)/shard_map/cond/branch_1_fun/ppermute | solution.py:296
  139.3 5.9 %collective-permute-done.27 = bf16[3,128,2048]{2,1,0:T(8,128)(2,1)} collective-permute-done((bf16[3,128,2048]{2,1,0:T(8,128)(2,1)}, bf16[3,128,2048]{2,1,0:T(8,128)(2,1)}, u32[]{:S(2)}, u32[]{:S(2)}) %collective-permute-start.27) | collective-permute-done | bytes 1572896 | tf_op jit(solution)/shard_map/ppermute | solution.py:290
  145.2 24.3 %conditional.9 = (bf16[3,128,2048]{2,1,0:T(8,128)(2,1)}, bf16[2,64,1024]{2,1,0:T(8,128)(2,1)S(1)}, bf16[1024,2048]{1,0:T(8,128)(2,1)}, bf16[1024,2048]{1,0:T(8,128)(2,1)}, bf16[1024,2048]{1,0:T(8,128)(2,1)}) conditional(s32[]{:T(128)} %convert_element_type.83, () %tuple.78, (bf16[3,128,2048]{2,1,0:T(8,128)(2,1)}, bf16[128,1024]{1,0:T(8,128)(2,1)}, ...), branch_computations={%region_7.0_spmd, %region_8.0_spmd} | conditional | flops 645949056 | bytes 14417970 | solution.py:284
  146.1 1.5 collective-permute-start.17
  147.6 1.1 collective-permute-start.18
  148.7 19.1 %weight_grad.4 = (bf16[1024,2048]{1,0:T(8,128)(2,1)}, bf16[1024,2048]{1,0:T(8,128)(2,1)}, bf16[1024,2048]{1,0:T(8,128)(2,1)}) custom-call(s32[17]{0:T(128)S(1)} %get-tuple-element.159.place_ref, bf16[8,256,256]{2,1,0:T(8,128)(2,1)} %get-tuple-element.160.refs_0_, bf16[8,256,256]{2,1,0:T(8,128)(2,1)} %get-tuple-element.161.refs_1_, ...), custom_call_target="tpu_custom_call" | custom-call | flops 644245120 | bytes 1258291 | tf_op jit(solution)/shard_map/cond/branch_1_fun/weight_grad/pallas_call | solution.py:158
  168.2 1.3 collective-permute-done.19
  169.8 9.0 %collective-permute-done.30 = bf16[3,128,2048]{2,1,0:T(8,128)(2,1)S(1)} collective-permute-done((bf16[3,128,2048]{2,1,0:T(8,128)(2,1)}, bf16[3,128,2048]{2,1,0:T(8,128)(2,1)S(1)}, u32[]{:S(2)}, u32[]{:S(2)}) %collective-permute-start.30) | collective-permute-done | bytes 1572896 | tf_op jit(solution)/shard_map/ppermute | solution.py:290
  178.8 32.2 %conditional.10 = (bf16[3,128,2048]{2,1,0:T(8,128)(2,1)}, bf16[128,1024]{1,0:T(8,128)(2,1)S(1)}, bf16[1024,2048]{1,0:T(8,128)(2,1)}, bf16[1024,2048]{1,0:T(8,128)(2,1)}, bf16[1024,2048]{1,0:T(8,128)(2,1)}) conditional(s32[]{:T(128)} %convert_element_type.83, () %tuple.88, (bf16[3,128,2048]{2,1,0:T(8,128)(2,1)S(1)}, s32[17]{0:T(128)S(1)}, ...), branch_computations={%region_9.0_spmd, %region_10.0_spmd} | conditional | flops 645293696 | bytes 63596420 | solution.py:284
  178.8 3.5 %collective-permute-done.5.refs_3_.refs_7_ = bf16[3,128,2048]{2,1,0:T(8,128)(2,1)} collective-permute-done((bf16[3,128,2048]{2,1,0:T(8,128)(2,1)S(1)}, bf16[3,128,2048]{2,1,0:T(8,128)(2,1)}, u32[]{:S(2)}, u32[]{:S(2)}) %collective-permute-start.5) | collective-permute-done | bytes 1572896 | tf_op jit(solution)/shard_map/cond/branch_1_fun/ppermute | solution.py:293
  182.3 12.5 %input_grad.7 = (bf16[128,1024]{1,0:T(8,128)(2,1)S(1)}, bf16[128,1024]{1,0:T(8,128)(2,1)S(1)}, bf16[128,1024]{1,0:T(8,128)(2,1)S(1)}, bf16[128,1024]{1,0:T(8,128)(2,1)S(1)}) custom-call(s32[17]{0:T(128)S(1)} %get-tuple-element.180.place_ref, bf16[3,128,2048]{2,1,0:T(8,128)(2,1)} %get-tuple-element.181.refs_0_.refs_4_, ...), custom_call_target="tpu_custom_call" | custom-call | flops 322122560 | bytes 943718 | tf_op jit(solution)/shard_map/cond/branch_1_fun/input_grad/pallas_call | solution.py:104
  195.8 1.5 collective-permute-start.7
  197.3 1.1 collective-permute-start.8
  198.4 12.4 %weight_grad.5 = (bf16[1024,2048]{1,0:T(8,128)(2,1)}, bf16[1024,2048]{1,0:T(8,128)(2,1)}, bf16[1024,2048]{1,0:T(8,128)(2,1)}) custom-call(s32[17]{0:T(128)S(1)} %get-tuple-element.180.place_ref, bf16[8,256,256]{2,1,0:T(8,128)(2,1)} %get-tuple-element.190.refs_0_, bf16[8,256,256]{2,1,0:T(8,128)(2,1)} %get-tuple-element.191.refs_1_, ...), custom_call_target="tpu_custom_call" | custom-call | flops 322122560 | bytes 1572864 | tf_op jit(solution)/shard_map/cond/branch_1_fun/weight_grad/pallas_call | solution.py:158
  211.4 30.5 %conditional.11 = (bf16[3,128,2048]{2,1,0:T(8,128)(2,1)}, bf16[2,32,1024]{2,1,0:T(8,128)(2,1)S(1)}, bf16[1024,2048]{1,0:T(8,128)(2,1)}, bf16[1024,2048]{1,0:T(8,...) conditional(s32[]{:T(128)} %convert_element_type.83, () %tuple.86, ...), branch_computations={%region_11.0_spmd, %region_12.0_spmd} | conditional | flops 323367744 | bytes 63937292 | solution.py:284
  212.1 3.0 %collective-permute-done.20.refs_1_.refs_5_ = bf16[3,128,2048]{2,1,0:T(8,128)(2,1)} collective-permute-done((bf16[3,128,2048]{2,1,0:T(8,128)(2,1)}, bf16[3,128,2048]{2,1,0:T(8,128)(2,1)}, u32[]{:S(2)}, u32[]{:S(2)}) %collective-permute-start.20) | collective-permute-done | bytes 1572896 | tf_op jit(solution)/shard_map/cond/branch_1_fun/ppermute | solution.py:293
  215.2 10.4 %input_grad.8 = (bf16[64,1024]{1,0:T(8,128)(2,1)S(1)}, bf16[64,1024]{1,0:T(8,128)(2,1)S(1)}, bf16[64,1024]{1,0:T(8,128)(2,1)S(1)}, bf16[64,1024]{1,0:T(8,128)(2,1)S(1)}) custom-call(s32[17]{0:T(128)S(1)} %get-tuple-element.205.place_ref, bf16[3,128,2048]{2,1,0:T(8,128)(2,1)} %get-tuple-element.204.refs_0_.refs_4_, ...), custom_call_target="tpu_custom_call" | custom-call | flops 161061280 | bytes 786432 | tf_op jit(solution)/shard_map/cond/branch_1_fun/input_grad/pallas_call | solution.py:104
  225.6 1.5 collective-permute-start.21
  227.1 1.5 collective-permute-start.22
  229.2 9.5 %weight_grad.6 = (bf16[1024,2048]{1,0:T(8,128)(2,1)}, bf16[1024,2048]{1,0:T(8,128)(2,1)}, bf16[1024,2048]{1,0:T(8,128)(2,1)}) custom-call(s32[17]{0:T(128)S(1)} %get-tuple-element.205.place_ref, bf16[8,256,256]{2,1,0:T(8,128)(2,1)} %get-tuple-element.213.refs_0_, bf16[8,256,256]{2,1,0:T(8,128)(2,1)} %get-tuple-element.214.refs_1_, ...), custom_call_target="tpu_custom_call" | custom-call | flops 161061280 | bytes 1415577 | tf_op jit(solution)/shard_map/cond/branch_1_fun/weight_grad/pallas_call | solution.py:158
  240.2 1.6 pad_maximum_fusion.4
  241.9 5.7 %collective-permute-done.31.refs_0_.refs_4_ = bf16[3,128,2048]{2,1,0:T(8,128)(2,1)S(1)} collective-permute-done((bf16[3,128,2048]{2,1,0:T(8,128)(2,1)S(1)}, bf16[3,128,2048]{2,1,0:T(8,128)(2,1)S(1)}, u32[]{:S(2)}, u32[]{:S(2)}) %collective-permute-start.31) | collective-permute-done | bytes 1572896 | tf_op jit(solution)/shard_map/ppermute | solution.py:290
  248.5 2.1 collective-permute-start.33
  251.1 8.3 %input_grad.9 = (bf16[64,1024]{1,0:T(8,128)(2,1)S(1)}, bf16[64,1024]{1,0:T(8,128)(2,1)S(1)}, bf16[64,1024]{1,0:T(8,128)(2,1)S(1)}, bf16[64,1024]{1,0:T(8,128)(2,1)S(1)}) custom-call(s32[17]{0:T(128)S(1)} %dynamic-slice_bitcast_fusion.place_ref, bf16[3,128,2048]{2,1,0:T(8,128)(2,1)S(1)} %collective-permute-done.31.refs_0_.refs_4_, ...), custom_call_target="tpu_custom_call" | custom-call | flops 161061280 | bytes 786432 | tf_op jit(solution)/shard_map/input_grad/pallas_call | solution.py:104
  259.4 1.6 collective-permute-start.35
  260.9 1.5 collective-permute-start.36
  263.5 2.0 collective-permute-done.35
  265.5 3.7 %collective-permute-done.36 = bf16[64,1024]{1,0:T(8,128)(2,1)S(1)} collective-permute-done((bf16[64,1024]{1,0:T(8,128)(2,1)S(1)}, bf16[64,1024]{1,0:T(8,128)(2,1)S(1)}, u32[]{:S(2)}, u32[]{:S(2)}) %collective-permute-start.36) | collective-permute-done | bytes 131104 | tf_op jit(solution)/shard_map/ppermute | solution.py:296
  269.3 1.2 collective-permute-done.39
  270.6 1.2 collective-permute-start.40
  271.8 2.2 collective-permute-start.41
  274.0 3.7 %collective-permute-done.41 = f32[16]{0:T(128)S(1)} collective-permute-done((f32[16]{0:T(128)S(1)}, f32[16]{0:T(128)S(1)}, u32[]{:S(2)}, u32[]{:S(2)}) %collective-permute-start.41) | collective-permute-done | bytes 96 | tf_op jit(solution)/shard_map/ppermute | solution.py:403
  277.7 3.0 collective-permute-start.42
  280.7 1.5 collective-permute-done.42
  283.4 1.3 collective-permute-start.43
  285.7 1.2 collective-permute-start.45
  287.0 9.6 %weight_grad.7 = (bf16[1024,2048]{1,0:T(8,128)(2,1)}, bf16[1024,2048]{1,0:T(8,128)(2,1)}, bf16[1024,2048]{1,0:T(8,128)(2,1)}) custom-call(s32[17]{0:T(128)S(1)} %dynamic-slice_bitcast_fusion.place_ref, bf16[8,256,256]{2,1,0:T(8,128)(2,1)} %get-tuple-element.359.refs_0_, bf16[8,256,256]{2,1,0:T(8,128)(2,1)} %get-tuple-element.360.refs_1_, ...), custom_call_target="tpu_custom_call" | custom-call | flops 161061280 | bytes 1415577 | tf_op jit(solution)/shard_map/weight_grad/pallas_call | solution.py:158
  297.0 1.6 assemble.1
  (109 shorter events, 15.5 us)
Async XLA Ops:
  0.6 14.9 %copy-start.14 = (s32[1,256]{1,0:T(1,128)S(1)}, s32[1,256]{1,0:T(1,128)}, u32[]{:S(2)}) copy-start(s32[1,256]{1,0:T(1,128)} %flag_ref.1) | copy-start | bytes 3076
  11.8 62.1 %collective-permute-start.26 = (bf16[3,128,2048]{2,1,0:T(8,128)(2,1)}, bf16[3,128,2048]{2,1,0:T(8,128)(2,1)}, u32[]{:S(2)}, u32[]{:S(2)}) collective-permute-start(bf16[3,128,2048]{2,1,0:T(8,128)(2,1)} %get-tuple-element.303), channel_id=1, source_target_pairs={{0,8},{4,12},{8,24},{12,28},{24,16},{28,20},{16,0},{20,4},{1,9},{5... | collective-permute-start | bytes 4718600 | tf_op jit(solution)/shard_map/ppermute | solution.py:290
  16.9 7.8 %collective-permute-start.9 = (bf16[3,128,2048]{2,1,0:T(8,128)(2,1)}, bf16[3,128,2048]{2,1,0:T(8,128)(2,1)}, u32[]{:S(2)}, u32[]{:S(2)}) collective-permute-start(bf16[3,128,2048]{2,1,0:T(8,128)(2,1)} %get-tuple-element.124.refs_0_), channel_id=1, source_target_pairs={{0,4},{4,0},{8,12},{12,8},{16,20},{20,16},{24,28},{28,24},{1,5},{5... | collective-permute-start | bytes 4718600 | tf_op jit(solution)/shard_map/cond/branch_1_fun/ppermute | solution.py:293
  17.0 7.8 %collective-permute-start.10 = (bf16[3,128,2048]{2,1,0:T(8,128)(2,1)}, bf16[3,128,2048]{2,1,0:T(8,128)(2,1)S(1)}, u32[]{:S(2)}, u32[]{:S(2)}) collective-permute-start(bf16[3,128,2048]{2,1,0:T(8,128)(2,1)} %get-tuple-element.125.refs_2_), channel_id=1, source_target_pairs={{0,4},{4,0},{8,12},{12,8},{16,20},{20,16},{24,28},{28,24},{1,5},{5... | collective-permute-start | bytes 4718600 | tf_op jit(solution)/shard_map/cond/branch_1_fun/ppermute | solution.py:293
  20.5 18.5 %all-to-all-start = ((bf16[4,2,256,256]{3,2,1,0:T(8,128)(2,1)}), bf16[4,2,256,256]{3,2,1,0:T(8,128)(2,1)}, u32[]{:S(2)}, u32[]{:S(2)}) async-start(bf16[4,2,256,256]{3,2,1,0:T(8,128)(2,1)} %bitcast.23), calls=%async_computation | async-start | bytes 2097152 | tf_op jit(solution)/shard_map/cond/branch_1_fun/all_to_all | solution.py:271
  24.7 11.8 %copy-start = (bf16[3,128,2048]{2,1,0:T(8,128)(2,1)}, bf16[3,128,2048]{2,1,0:T(8,128)(2,1)S(1)}, u32[]{:S(2)}) copy-start(bf16[3,128,2048]{2,1,0:T(8,128)(2,1)S(1)} %collective-permute-done.10.refs_3_.refs_7_) | copy-start | bytes 4718596 | tf_op jit(solution)/shard_map/cond
  38.9 34.2 %copy-start.1 = (bf16[3,128,2048]{2,1,0:T(8,128)(2,1)S(1)}, bf16[3,128,2048]{2,1,0:T(8,128)(2,1)}, u32[]{:S(2)}) copy-start(bf16[3,128,2048]{2,1,0:T(8,128)(2,1)} %copy-done) | copy-start | bytes 4718596 | tf_op jit(solution)/shard_map/cond
  38.9 34.2 %all-to-all-start.1 = ((bf16[8,256,256]{2,1,0:T(8,128)(2,1)}), bf16[8,256,256]{2,1,0:T(8,128)(2,1)}, u32[]{:S(2)}, u32[]{:S(2)}) async-start(bf16[8,256,256]{2,1,0:T(8,128)(2,1)} %bitcast.3), calls=%async_computation.1 | async-start | bytes 2097152 | tf_op jit(solution)/shard_map/cond/branch_1_fun/all_to_all | solution.py:271
  43.3 9.2 %collective-permute-start.11 = (bf16[128,1024]{1,0:T(8,128)(2,1)S(1)}, bf16[128,1024]{1,0:T(8,128)(2,1)S(1)}, u32[]{:S(2)}, u32[]{:S(2)}) collective-permute-start(bf16[128,1024]{1,0:T(8,128)(2,1)S(1)} %get-tuple-element.131), channel_id=1, source_target_pairs={{0,1},{1,0},{2,3},{3,2},{4,5},{5,4},{6,7},{7,6},{8,9},{9,8},{10,11... | collective-permute-start | bytes 786440 | tf_op jit(solution)/shard_map/cond/branch_1_fun/ppermute | solution.py:296
  44.8 13.9 %collective-permute-start.12 = (bf16[128,1024]{1,0:T(8,128)(2,1)S(1)}, bf16[128,1024]{1,0:T(8,128)(2,1)S(1)}, u32[]{:S(2)}, u32[]{:S(2)}) collective-permute-start(bf16[128,1024]{1,0:T(8,128)(2,1)S(1)} %get-tuple-element.132), channel_id=1, source_target_pairs={{0,2},{1,3},{2,0},{3,1},{4,6},{5,7},{6,4},{7,5},{8,10},{9,11},{10,... | collective-permute-start | bytes 786440 | tf_op jit(solution)/shard_map/cond/branch_1_fun/ppermute | solution.py:296
  45.4 13.3 %collective-permute-start.13 = (bf16[128,1024]{1,0:T(8,128)(2,1)S(1)}, bf16[128,1024]{1,0:T(8,128)(2,1)S(1)}, u32[]{:S(2)}, u32[]{:S(2)}) collective-permute-start(bf16[128,1024]{1,0:T(8,128)(2,1)S(1)} %get-tuple-element.133), channel_id=1, source_target_pairs={{0,3},{1,2},{2,1},{3,0},{4,7},{5,6},{6,5},{7,4},{8,11},{9,10},{10,... | collective-permute-start | bytes 786440 | tf_op jit(solution)/shard_map/cond/branch_1_fun/ppermute | solution.py:296
  58.9 1.4 collective-permute-start.14
  73.1 38.6 %copy-start.10 = (bf16[2,64,1024]{2,1,0:T(8,128)(2,1)}, bf16[2,64,1024]{2,1,0:T(8,128)(2,1)S(1)}, u32[]{:S(2)}) copy-start(bf16[2,64,1024]{2,1,0:T(8,128)(2,1)S(1)} %get-tuple-element.338.refs_0_) | copy-start | bytes 786436
  73.1 38.5 %collective-permute-start.28 = (bf16[3,128,2048]{2,1,0:T(8,128)(2,1)}, bf16[3,128,2048]{2,1,0:T(8,128)(2,1)}, u32[]{:S(2)}, u32[]{:S(2)}) collective-permute-start(bf16[3,128,2048]{2,1,0:T(8,128)(2,1)} %get-tuple-element.310), channel_id=1, source_target_pairs={{0,8},{4,12},{8,24},{12,28},{24,16},{28,20},{16,0},{20,4},{1,9},{5... | collective-permute-start | bytes 4718600 | tf_op jit(solution)/shard_map/ppermute | solution.py:290
  74.0 27.1 %collective-permute-start = (bf16[3,128,2048]{2,1,0:T(8,128)(2,1)}, bf16[3,128,2048]{2,1,0:T(8,128)(2,1)}, u32[]{:S(2)}, u32[]{:S(2)}) collective-permute-start(bf16[3,128,2048]{2,1,0:T(8,128)(2,1)} %get-tuple-element.140), channel_id=1, source_target_pairs={{0,4},{4,0},{8,12},{12,8},{16,20},{20,16},{24,28},{28,24},{1,5},{5... | collective-permute-start | bytes 4718600 | tf_op jit(solution)/shard_map/cond/branch_1_fun/ppermute | solution.py:293
  74.0 25.9 %collective-permute-start.2 = (bf16[8,256,256]{2,1,0:T(8,128)(2,1)}, bf16[8,256,256]{2,1,0:T(8,128)(2,1)}, u32[]{:S(2)}, u32[]{:S(2)}) collective-permute-start(bf16[8,256,256]{2,1,0:T(8,128)(2,1)} %get-tuple-element.141), channel_id=1, source_target_pairs={{0,2},{1,3},{2,0},{3,1},{4,6},{5,7},{6,4},{7,5},{8,10},{9,11},{10,... | collective-permute-start | bytes 3145736 | tf_op jit(solution)/shard_map/cond/branch_1_fun/ppermute | solution.py:296
  75.5 25.6 %collective-permute-start.1 = (bf16[8,256,256]{2,1,0:T(8,128)(2,1)}, bf16[8,256,256]{2,1,0:T(8,128)(2,1)}, u32[]{:S(2)}, u32[]{:S(2)}) collective-permute-start(bf16[8,256,256]{2,1,0:T(8,128)(2,1)} %get-tuple-element.141), channel_id=1, source_target_pairs={{0,1},{1,0},{2,3},{3,2},{4,5},{5,4},{6,7},{7,6},{8,9},{9,8},{10,11... | collective-permute-start | bytes 3145736 | tf_op jit(solution)/shard_map/cond/branch_1_fun/ppermute | solution.py:296
  101.1 44.1 %collective-permute-start.27 = (bf16[3,128,2048]{2,1,0:T(8,128)(2,1)}, bf16[3,128,2048]{2,1,0:T(8,128)(2,1)}, u32[]{:S(2)}, u32[]{:S(2)}) collective-permute-start(bf16[3,128,2048]{2,1,0:T(8,128)(2,1)} %collective-permute-done.26), channel_id=1, source_target_pairs={{0,8},{4,12},{8,24},{12,28},{24,16},{28,20},{16,0},{20,4},{1,9},{5... | collective-permute-start | bytes 4718600 | tf_op jit(solution)/shard_map/ppermute | solution.py:290
  111.7 3.8 %collective-permute-start.3 = (bf16[3,128,2048]{2,1,0:T(8,128)(2,1)}, bf16[3,128,2048]{2,1,0:T(8,128)(2,1)}, u32[]{:S(2)}, u32[]{:S(2)}) collective-permute-start(bf16[3,128,2048]{2,1,0:T(8,128)(2,1)} %get-tuple-element.142.refs_2_), channel_id=1, source_target_pairs={{0,4},{4,0},{8,12},{12,8},{16,20},{20,16},{24,28},{28,24},{1,5},{5... | collective-permute-start | bytes 4718600 | tf_op jit(solution)/shard_map/cond/branch_1_fun/ppermute | solution.py:293
  111.7 26.8 %collective-permute-start.4 = (bf16[8,256,256]{2,1,0:T(8,128)(2,1)}, bf16[8,256,256]{2,1,0:T(8,128)(2,1)}, u32[]{:S(2)}, u32[]{:S(2)}) collective-permute-start(bf16[8,256,256]{2,1,0:T(8,128)(2,1)} %get-tuple-element.153), channel_id=1, source_target_pairs={{0,3},{1,2},{2,1},{3,0},{4,7},{5,6},{6,5},{7,4},{8,11},{9,10},{10,... | collective-permute-start | bytes 3145736 | tf_op jit(solution)/shard_map/cond/branch_1_fun/ppermute | solution.py:296
  138.5 40.3 %collective-permute-start.30 = (bf16[3,128,2048]{2,1,0:T(8,128)(2,1)}, bf16[3,128,2048]{2,1,0:T(8,128)(2,1)S(1)}, u32[]{:S(2)}, u32[]{:S(2)}) collective-permute-start(bf16[3,128,2048]{2,1,0:T(8,128)(2,1)} %collective-permute-done.28), channel_id=1, source_target_pairs={{0,8},{4,12},{8,24},{12,28},{24,16},{28,20},{16,0},{20,4},{1,9},{5... | collective-permute-start | bytes 4718600 | tf_op jit(solution)/shard_map/ppermute | solution.py:290
  145.2 24.3 %collective-permute-start.15 = (bf16[3,128,2048]{2,1,0:T(8,128)(2,1)}, bf16[3,128,2048]{2,1,0:T(8,128)(2,1)}, u32[]{:S(2)}, u32[]{:S(2)}) collective-permute-start(bf16[3,128,2048]{2,1,0:T(8,128)(2,1)} %get-tuple-element.154), channel_id=1, source_target_pairs={{0,4},{4,0},{8,12},{12,8},{16,20},{20,16},{24,28},{28,24},{1,5},{5... | collective-permute-start | bytes 4718600 | tf_op jit(solution)/shard_map/cond/branch_1_fun/ppermute | solution.py:293
  145.2 22.6 %collective-permute-start.16 = (bf16[128,1024]{1,0:T(8,128)(2,1)}, bf16[128,1024]{1,0:T(8,128)(2,1)S(1)}, u32[]{:S(2)}, u32[]{:S(2)}) collective-permute-start(bf16[128,1024]{1,0:T(8,128)(2,1)} %get-tuple-element.156), channel_id=1, source_target_pairs={{0,1},{1,0},{2,3},{3,2},{4,5},{5,4},{6,7},{7,6},{8,9},{9,8},{10,11... | collective-permute-start | bytes 786440 | tf_op jit(solution)/shard_map/cond/branch_1_fun/ppermute | solution.py:296
  146.1 21.7 %collective-permute-start.17 = (bf16[128,1024]{1,0:T(8,128)(2,1)}, bf16[128,1024]{1,0:T(8,128)(2,1)S(1)}, u32[]{:S(2)}, u32[]{:S(2)}) collective-permute-start(bf16[128,1024]{1,0:T(8,128)(2,1)} %get-tuple-element.157), channel_id=1, source_target_pairs={{0,2},{1,3},{2,0},{3,1},{4,6},{5,7},{6,4},{7,5},{8,10},{9,11},{10,... | collective-permute-start | bytes 786440 | tf_op jit(solution)/shard_map/cond/branch_1_fun/ppermute | solution.py:296
  147.6 20.2 %collective-permute-start.18 = (bf16[128,1024]{1,0:T(8,128)(2,1)}, bf16[128,1024]{1,0:T(8,128)(2,1)S(1)}, u32[]{:S(2)}, u32[]{:S(2)}) collective-permute-start(bf16[128,1024]{1,0:T(8,128)(2,1)} %get-tuple-element.158), channel_id=1, source_target_pairs={{0,3},{1,2},{2,1},{3,0},{4,7},{5,6},{6,5},{7,4},{8,11},{9,10},{10,... | collective-permute-start | bytes 786440 | tf_op jit(solution)/shard_map/cond/branch_1_fun/ppermute | solution.py:296
  168.1 1.4 collective-permute-start.19
  169.5 9.3 %copy-start.12 = (bf16[2,64,1024]{2,1,0:T(8,128)(2,1)}, bf16[2,64,1024]{2,1,0:T(8,128)(2,1)S(1)}, u32[]{:S(2)}) copy-start(bf16[2,64,1024]{2,1,0:T(8,128)(2,1)S(1)} %get-tuple-element.339) | copy-start | bytes 786436
  169.5 41.8 %collective-permute-start.29 = (bf16[3,128,2048]{2,1,0:T(8,128)(2,1)}, bf16[3,128,2048]{2,1,0:T(8,128)(2,1)}, u32[]{:S(2)}, u32[]{:S(2)}) collective-permute-start(bf16[3,128,2048]{2,1,0:T(8,128)(2,1)} %collective-permute-done.27), channel_id=1, source_target_pairs={{0,8},{4,12},{8,24},{12,28},{24,16},{28,20},{16,0},{20,4},{1,9},{5... | collective-permute-start | bytes 4718600 | tf_op jit(solution)/shard_map/ppermute | solution.py:290
  178.8 3.5 %collective-permute-start.5 = (bf16[3,128,2048]{2,1,0:T(8,128)(2,1)S(1)}, bf16[3,128,2048]{2,1,0:T(8,128)(2,1)}, u32[]{:S(2)}, u32[]{:S(2)}) collective-permute-start(bf16[3,128,2048]{2,1,0:T(8,128)(2,1)S(1)} %get-tuple-element.179.refs_2_.refs_6_), channel_id=1, source_target_pairs={{0,4},{4,0},{8,12},{12,8},{16,20},{20,16},{24,28},{28,24},{1,5},{5... | collective-permute-start | bytes 4718600 | tf_op jit(solution)/shard_map/cond/branch_1_fun/ppermute | solution.py:293
  182.3 16.1 %copy-start.2 = (bf16[1024,2048]{1,0:T(8,128)(2,1)S(1)}, bf16[1024,2048]{1,0:T(8,128)(2,1)}, u32[]{:S(2)}) copy-start(bf16[1024,2048]{1,0:T(8,128)(2,1)} %get-tuple-element.196.refs_10_) | copy-start | bytes 12582916 | tf_op jit(solution)/shard_map/cond
  182.3 16.1 %copy-start.3 = (bf16[1024,2048]{1,0:T(8,128)(2,1)S(1)}, bf16[1024,2048]{1,0:T(8,128)(2,1)}, u32[]{:S(2)}) copy-start(bf16[1024,2048]{1,0:T(8,128)(2,1)} %get-tuple-element.195.refs_9_) | copy-start | bytes 12582916 | tf_op jit(solution)/shard_map/cond
  182.3 16.1 %copy-start.4 = (bf16[1024,2048]{1,0:T(8,128)(2,1)S(1)}, bf16[1024,2048]{1,0:T(8,128)(2,1)}, u32[]{:S(2)}) copy-start(bf16[1024,2048]{1,0:T(8,128)(2,1)} %get-tuple-element.194.refs_8_) | copy-start | bytes 12582916 | tf_op jit(solution)/shard_map/cond
  194.9 16.0 %collective-permute-start.6 = (bf16[128,1024]{1,0:T(8,128)(2,1)S(1)}, bf16[128,1024]{1,0:T(8,128)(2,1)S(1)}, u32[]{:S(2)}, u32[]{:S(2)}) collective-permute-start(bf16[128,1024]{1,0:T(8,128)(2,1)S(1)} %get-tuple-element.187), channel_id=1, source_target_pairs={{0,1},{1,0},{2,3},{3,2},{4,5},{5,4},{6,7},{7,6},{8,9},{9,8},{10,11... | collective-permute-start | bytes 786440 | tf_op jit(solution)/shard_map/cond/branch_1_fun/ppermute | solution.py:296
  195.8 15.0 %collective-permute-start.7 = (bf16[128,1024]{1,0:T(8,128)(2,1)S(1)}, bf16[128,1024]{1,0:T(8,128)(2,1)S(1)}, u32[]{:S(2)}, u32[]{:S(2)}) collective-permute-start(bf16[128,1024]{1,0:T(8,128)(2,1)S(1)} %get-tuple-element.188), channel_id=1, source_target_pairs={{0,2},{1,3},{2,0},{3,1},{4,6},{5,7},{6,4},{7,5},{8,10},{9,11},{10,... | collective-permute-start | bytes 786440 | tf_op jit(solution)/shard_map/cond/branch_1_fun/ppermute | solution.py:296
  197.3 13.5 %collective-permute-start.8 = (bf16[128,1024]{1,0:T(8,128)(2,1)S(1)}, bf16[128,1024]{1,0:T(8,128)(2,1)S(1)}, u32[]{:S(2)}, u32[]{:S(2)}) collective-permute-start(bf16[128,1024]{1,0:T(8,128)(2,1)S(1)} %get-tuple-element.189), channel_id=1, source_target_pairs={{0,3},{1,2},{2,1},{3,0},{4,7},{5,6},{6,5},{7,4},{8,11},{9,10},{10,... | collective-permute-start | bytes 786440 | tf_op jit(solution)/shard_map/cond/branch_1_fun/ppermute | solution.py:296
  211.0 36.5 %collective-permute-start.31 = (bf16[3,128,2048]{2,1,0:T(8,128)(2,1)S(1)}, bf16[3,128,2048]{2,1,0:T(8,128)(2,1)S(1)}, u32[]{:S(2)}, u32[]{:S(2)}) collective-permute-start(bf16[3,128,2048]{2,1,0:T(8,128)(2,1)S(1)} %collective-permute-done.30), channel_id=1, source_target_pairs={{0,8},{4,12},{8,24},{12,28},{24,16},{28,20},{16,0},{20,4},{1,9},{5... | collective-permute-start | bytes 4718600 | tf_op jit(solution)/shard_map/ppermute | solution.py:290
  211.4 39.2 %copy-start.13 = (f32[16,1,128]{2,1,0:T(1,128)S(1)}, f32[16,1,128]{2,1,0:T(1,128)}, u32[]{:S(2)}) copy-start(f32[16,1,128]{2,1,0:T(1,128)} %get-tuple-element.346) | copy-start | bytes 24580
  211.4 3.8 %collective-permute-start.20 = (bf16[3,128,2048]{2,1,0:T(8,128)(2,1)}, bf16[3,128,2048]{2,1,0:T(8,128)(2,1)}, u32[]{:S(2)}, u32[]{:S(2)}) collective-permute-start(bf16[3,128,2048]{2,1,0:T(8,128)(2,1)} %get-tuple-element.204.refs_0_.refs_4_), channel_id=1, source_target_pairs={{0,4},{4,0},{8,12},{12,8},{16,20},{20,16},{24,28},{28,24},{1,5},{5... | collective-permute-start | bytes 4718600 | tf_op jit(solution)/shard_map/cond/branch_1_fun/ppermute | solution.py:293
  215.2 14.0 %copy-start.7 = (bf16[1024,2048]{1,0:T(8,128)(2,1)S(1)}, bf16[1024,2048]{1,0:T(8,128)(2,1)}, u32[]{:S(2)}) copy-start(bf16[1024,2048]{1,0:T(8,128)(2,1)} %get-tuple-element.219.refs_8_) | copy-start | bytes 12582916 | tf_op jit(solution)/shard_map/cond
  215.2 14.0 %copy-start.8 = (bf16[1024,2048]{1,0:T(8,128)(2,1)S(1)}, bf16[1024,2048]{1,0:T(8,128)(2,1)}, u32[]{:S(2)}) copy-start(bf16[1024,2048]{1,0:T(8,128)(2,1)} %get-tuple-element.218.refs_7_) | copy-start | bytes 12582916 | tf_op jit(solution)/shard_map/cond
  215.2 14.0 %copy-start.9 = (bf16[1024,2048]{1,0:T(8,128)(2,1)S(1)}, bf16[1024,2048]{1,0:T(8,128)(2,1)}, u32[]{:S(2)}) copy-start(bf16[1024,2048]{1,0:T(8,128)(2,1)} %get-tuple-element.217.refs_6_) | copy-start | bytes 12582916 | tf_op jit(solution)/shard_map/cond
  225.6 13.1 %collective-permute-start.21 = (bf16[64,1024]{1,0:T(8,128)(2,1)S(1)}, bf16[64,1024]{1,0:T(8,128)(2,1)S(1)}, u32[]{:S(2)}, u32[]{:S(2)}) collective-permute-start(bf16[64,1024]{1,0:T(8,128)(2,1)S(1)} %get-tuple-element.210), channel_id=1, source_target_pairs={{0,1},{1,0},{2,3},{3,2},{4,5},{5,4},{6,7},{7,6},{8,9},{9,8},{10,11... | collective-permute-start | bytes 393224 | tf_op jit(solution)/shard_map/cond/branch_1_fun/ppermute | solution.py:296
  227.1 11.5 %collective-permute-start.22 = (bf16[64,1024]{1,0:T(8,128)(2,1)S(1)}, bf16[64,1024]{1,0:T(8,128)(2,1)S(1)}, u32[]{:S(2)}, u32[]{:S(2)}) collective-permute-start(bf16[64,1024]{1,0:T(8,128)(2,1)S(1)} %get-tuple-element.211), channel_id=1, source_target_pairs={{0,2},{1,3},{2,0},{3,1},{4,6},{5,7},{6,4},{7,5},{8,10},{9,11},{10,... | collective-permute-start | bytes 393224 | tf_op jit(solution)/shard_map/cond/branch_1_fun/ppermute | solution.py:296
  228.6 10.0 %collective-permute-start.23 = (bf16[64,1024]{1,0:T(8,128)(2,1)S(1)}, bf16[64,1024]{1,0:T(8,128)(2,1)}, u32[]{:S(2)}, u32[]{:S(2)}) collective-permute-start(bf16[64,1024]{1,0:T(8,128)(2,1)S(1)} %get-tuple-element.212), channel_id=1, source_target_pairs={{0,3},{1,2},{2,1},{3,0},{4,7},{5,6},{6,5},{7,4},{8,11},{9,10},{10,... | collective-permute-start | bytes 393224 | tf_op jit(solution)/shard_map/cond/branch_1_fun/ppermute | solution.py:296
  229.1 11.1 %collective-permute-start.25 = (bf16[64,1024]{1,0:T(8,128)(2,1)}, bf16[64,1024]{1,0:T(8,128)(2,1)}, u32[]{:S(2)}, u32[]{:S(2)}) collective-permute-start(bf16[64,1024]{1,0:T(8,128)(2,1)} %pad_maximum_fusion.6), channel_id=1, source_target_pairs={{0,4},{4,0},{8,12},{12,8},{16,20},{20,16},{24,28},{28,24},{1,5},{5... | collective-permute-start | bytes 393224 | tf_op jit(solution)/shard_map/cond/branch_1_fun/ppermute | solution.py:293
  239.6 2.2 collective-permute-start.24
  247.6 3.5 %collective-permute-start.34 = (bf16[3,128,2048]{2,1,0:T(8,128)(2,1)S(1)}, bf16[3,128,2048]{2,1,0:T(8,128)(2,1)S(1)}, u32[]{:S(2)}, u32[]{:S(2)}) collective-permute-start(bf16[3,128,2048]{2,1,0:T(8,128)(2,1)S(1)} %collective-permute-done.31.refs_0_.refs_4_), channel_id=1, source_target_pairs={{0,4},{4,0},{8,12},{12,8},{16,20},{20,16},{24,28},{28,24},{1,5},{5... | collective-permute-start | bytes 4718600 | tf_op jit(solution)/shard_map/ppermute | solution.py:293
  247.6 15.4 %collective-permute-start.32 = (bf16[2,64,1024]{2,1,0:T(8,128)(2,1)}, bf16[2,64,1024]{2,1,0:T(8,128)(2,1)S(1)}, u32[]{:S(2)}, u32[]{:S(2)}) collective-permute-start(bf16[2,64,1024]{2,1,0:T(8,128)(2,1)} %copy-done.12), channel_id=1, source_target_pairs={{0,16},{4,20},{8,0},{12,4},{24,8},{28,12},{16,24},{20,28},{1,17},{... | collective-permute-start | bytes 786440 | tf_op jit(solution)/shard_map/ppermute | solution.py:393
  248.5 15.0 %collective-permute-start.33 = (bf16[2,64,1024]{2,1,0:T(8,128)(2,1)}, bf16[2,64,1024]{2,1,0:T(8,128)(2,1)S(1)}, u32[]{:S(2)}, u32[]{:S(2)}) collective-permute-start(bf16[2,64,1024]{2,1,0:T(8,128)(2,1)} %get-tuple-element.340), channel_id=1, source_target_pairs={{0,24},{4,28},{8,16},{12,20},{24,0},{28,4},{16,8},{20,12},{1,25},{... | collective-permute-start | bytes 786440 | tf_op jit(solution)/shard_map/ppermute | solution.py:393
  250.8 31.9 %copy-start.11 = (bf16[2,64,1024]{2,1,0:T(8,128)(2,1)S(1)}, bf16[2,64,1024]{2,1,0:T(8,128)(2,1)}, u32[]{:S(2)}) copy-start(bf16[2,64,1024]{2,1,0:T(8,128)(2,1)} %copy-done.10) | copy-start | bytes 786436
  250.8 11.7 %collective-permute-start.38 = (f32[16]{0:T(128)S(1)}, f32[16]{0:T(128)S(1)}, u32[]{:S(2)}, u32[]{:S(2)}) collective-permute-start(f32[16]{0:T(128)S(1)} %slice_reduce_fusion), channel_id=1, source_target_pairs={{0,4},{4,0},{8,12},{12,8},{16,20},{20,16},{24,28},{28,24},{1,5},{5... | collective-permute-start | bytes 200 | tf_op jit(solution)/shard_map/ppermute | solution.py:403
  251.1 35.9 %copy-start.5 = (bf16[1024,2048]{1,0:T(8,128)(2,1)S(1)}, bf16[1024,2048]{1,0:T(8,128)(2,1)}, u32[]{:S(2)}) copy-start(bf16[1024,2048]{1,0:T(8,128)(2,1)} %get-tuple-element.365.refs_8_) | copy-start | bytes 12582916
  251.1 35.9 %copy-start.6 = (bf16[1024,2048]{1,0:T(8,128)(2,1)S(1)}, bf16[1024,2048]{1,0:T(8,128)(2,1)}, u32[]{:S(2)}) copy-start(bf16[1024,2048]{1,0:T(8,128)(2,1)} %get-tuple-element.364.refs_7_) | copy-start | bytes 12582916
  259.4 6.1 %collective-permute-start.35 = (bf16[64,1024]{1,0:T(8,128)(2,1)S(1)}, bf16[64,1024]{1,0:T(8,128)(2,1)S(1)}, u32[]{:S(2)}, u32[]{:S(2)}) collective-permute-start(bf16[64,1024]{1,0:T(8,128)(2,1)S(1)} %get-tuple-element.343), channel_id=1, source_target_pairs={{0,1},{1,0},{2,3},{3,2},{4,5},{5,4},{6,7},{7,6},{8,9},{9,8},{10,11... | collective-permute-start | bytes 393224 | tf_op jit(solution)/shard_map/ppermute | solution.py:296
  260.9 8.2 %collective-permute-start.36 = (bf16[64,1024]{1,0:T(8,128)(2,1)S(1)}, bf16[64,1024]{1,0:T(8,128)(2,1)S(1)}, u32[]{:S(2)}, u32[]{:S(2)}) collective-permute-start(bf16[64,1024]{1,0:T(8,128)(2,1)S(1)} %get-tuple-element.344), channel_id=1, source_target_pairs={{0,2},{1,3},{2,0},{3,1},{4,6},{5,7},{6,4},{7,5},{8,10},{9,11},{10,... | collective-permute-start | bytes 393224 | tf_op jit(solution)/shard_map/ppermute | solution.py:296
  262.5 6.7 %collective-permute-start.37 = (bf16[64,1024]{1,0:T(8,128)(2,1)S(1)}, bf16[64,1024]{1,0:T(8,128)(2,1)S(1)}, u32[]{:S(2)}, u32[]{:S(2)}) collective-permute-start(bf16[64,1024]{1,0:T(8,128)(2,1)S(1)} %get-tuple-element.345), channel_id=1, source_target_pairs={{0,3},{1,2},{2,1},{3,0},{4,7},{5,6},{6,5},{7,4},{8,11},{9,10},{10,... | collective-permute-start | bytes 393224 | tf_op jit(solution)/shard_map/ppermute | solution.py:296
  269.3 1.3 collective-permute-start.39
  270.6 12.1 %collective-permute-start.40 = (bf16[2,64,1024]{2,1,0:T(8,128)(2,1)S(1)}, bf16[2,64,1024]{2,1,0:T(8,128)(2,1)S(1)}, u32[]{:S(2)}, u32[]{:S(2)}) collective-permute-start(bf16[2,64,1024]{2,1,0:T(8,128)(2,1)S(1)} %maximum_maximum_fusion), channel_id=1, source_target_pairs={{0,8},{4,12},{8,24},{12,28},{24,16},{28,20},{16,0},{20,4},{1,9},{5... | collective-permute-start | bytes 786440 | tf_op jit(solution)/shard_map/ppermute | solution.py:393
  271.8 5.9 %collective-permute-start.41 = (f32[16]{0:T(128)S(1)}, f32[16]{0:T(128)S(1)}, u32[]{:S(2)}, u32[]{:S(2)}) collective-permute-start(f32[16]{0:T(128)S(1)} %add.62), channel_id=1, source_target_pairs={{0,8},{4,12},{8,0},{12,4},{16,24},{20,28},{24,16},{28,20},{1,9},{5... | collective-permute-start | bytes 200 | tf_op jit(solution)/shard_map/ppermute | solution.py:403
  277.7 4.5 %collective-permute-start.42 = (f32[16]{0:T(128)S(1)}, f32[16]{0:T(128)S(1)}, u32[]{:S(2)}, u32[]{:S(2)}) collective-permute-start(f32[16]{0:T(128)S(1)} %add.66), channel_id=1, source_target_pairs={{0,16},{4,20},{8,24},{12,28},{16,0},{20,4},{24,8},{28,12},{1,17},{... | collective-permute-start | bytes 200 | tf_op jit(solution)/shard_map/ppermute | solution.py:403
  283.4 13.2 %collective-permute-start.43 = (bf16[2,64,1024]{2,1,0:T(8,128)(2,1)S(1)}, bf16[2,64,1024]{2,1,0:T(8,128)(2,1)S(1)}, u32[]{:S(2)}, u32[]{:S(2)}) collective-permute-start(bf16[2,64,1024]{2,1,0:T(8,128)(2,1)S(1)} %get-tuple-element.356), channel_id=1, source_target_pairs={{0,1},{1,0},{2,3},{3,2},{4,5},{5,4},{6,7},{7,6},{8,9},{9,8},{10,11... | collective-permute-start | bytes 786440 | tf_op jit(solution)/shard_map/ppermute | solution.py:296
  284.7 11.9 %collective-permute-start.44 = (bf16[2,64,1024]{2,1,0:T(8,128)(2,1)S(1)}, bf16[2,64,1024]{2,1,0:T(8,128)(2,1)S(1)}, u32[]{:S(2)}, u32[]{:S(2)}) collective-permute-start(bf16[2,64,1024]{2,1,0:T(8,128)(2,1)S(1)} %get-tuple-element.357), channel_id=1, source_target_pairs={{0,2},{1,3},{2,0},{3,1},{4,6},{5,7},{6,4},{7,5},{8,10},{9,11},{10,... | collective-permute-start | bytes 786440 | tf_op jit(solution)/shard_map/ppermute | solution.py:296
  285.7 11.2 %collective-permute-start.45 = (bf16[2,64,1024]{2,1,0:T(8,128)(2,1)S(1)}, bf16[2,64,1024]{2,1,0:T(8,128)(2,1)S(1)}, u32[]{:S(2)}, u32[]{:S(2)}) collective-permute-start(bf16[2,64,1024]{2,1,0:T(8,128)(2,1)S(1)} %get-tuple-element.358), channel_id=1, source_target_pairs={{0,3},{1,2},{2,1},{3,0},{4,7},{5,6},{6,5},{7,4},{8,11},{9,10},{10,... | collective-permute-start | bytes 786440 | tf_op jit(solution)/shard_map/ppermute | solution.py:296

commit v6 on v5

--- a/solution.py
+++ b/solution.py
@@ -100,7 +100,7 @@
 def input_grad(place, grads, weights, pieces, ahead):
     rows_in, width = weights[0].shape
     tokens = sum(grad.shape[1] for grad in grads)
-    step = 256
+    step = min(rows_in, 512 if len(grads) <= 2 else 256)
     return pl.pallas_call(
         functools.partial(input_grad_body, len(grads)),
         grid_spec=pltpu.PrefetchScalarGridSpec(

time: 299 us -> 298 us (level)
  transfers between devices with their start and end apart: 48 -> 48, of which waited for: 23 -> 23; matrix products, arithmetic and copies ran while one was open for 3% -> 3% of each run, Pallas kernels for 36% -> 35%
where the time goes in v6:
time: 298 us
  Pallas kernels  118 us (40%)
  waiting for transfers between devices  114 us (38%)
  starting transfers between devices  55 us (18%)
  other arithmetic  5.15 us (2%)
  local copies, waits for them, and re-layouts  4.05 us (1%)
    pallas_call x5, Pallas kernels, input_grad(): pl.pallas_call(functools.partial(input_grad_body, len(grads)), grid_spec=...  53.5 us
    ppermute x21, waiting for transfers between devices, across(): return lax.ppermute(mine, 'col', [(n, n ^ apart) for n in range(col_count)])  51.2 us
    pallas_call x4, Pallas kernels, weight_grad(): pl.pallas_call(functools.partial(weight_grad_body, len(x), tuple(units),...  50.6 us
    ppermute x6, waiting for transfers between devices, hop(): return lax.ppermute(mine, 'row', ring)  29.2 us
    ppermute x21, starting transfers between devices, across(): return lax.ppermute(mine, 'col', [(n, n ^ apart) for n in range(col_count)])  26.8 us
    all_to_all x2, waiting for transfers between devices, a2a(): return lax.all_to_all(array, axis, split_axis=0, concat_axis=0, tiled=True)  15.2 us
    ppermute x13, waiting for transfers between devices, other(): return lax.ppermute(mine, 'row', swap)  11.7 us
    pallas_call x1, Pallas kernels, attention(): pl.pallas_call(functools.partial(attention_body, sizes, head_dim, heads_s...  11.2 us
  transfers between devices with their start and end apart: 48, of which 23 were waited for; matrix products, arithmetic and copies ran while one was open for 3% of the time, Pallas kernels for 35%

profile of v6, /device:TPU:0, one launch (start us, length us, event | category | flops | bytes accessed | tf_op | source)
XLA Modules:
  0.0 297.8 jit_solution(12823192807998063648)
XLA Ops:
  0.6 11.2 %attention_back.1 = (bf16[3,128,2048]{2,1,0:T(8,128)(2,1)}, bf16[3,128,2048]{2,1,0:T(8,128)(2,1)}, f32[16,1,128]{2,1,0:T(1,128)}) custom-call(f32[16]{0:T(128)} %bias_ref.1, s32[1,256]{1,0:T(1,128)} %flag_ref.1, bf16[256,2048]{1,0:T(8,128)(2,1)} %bitcast.24, bf16[256,2048]{1,0:T(8,128)(2,1)} %bitcast.25, bf16[256,2048]{1,0:T(8,128)(2,1)} %bitcast.26, ...), custom_call_target="tpu_custom_call" | custom-call | flops 67108864 | bytes 367001 | tf_op jit(solution)/shard_map/attention_back/pallas_call | solution.py:57
  11.8 3.0 %collective-permute-start.26 = (bf16[3,128,2048]{2,1,0:T(8,128)(2,1)}, bf16[3,128,2048]{2,1,0:T(8,128)(2,1)}, u32[]{:S(2)}, u32[]{:S(2)}) collective-permute-start(bf16[3,128,2048]{2,1,0:T(8,128)(2,1)} %get-tuple-element.303), channel_id=1, source_target_pairs={{0,8},{4,12},{8,24},{12,28},{24,16},{28,20},{16,0},{20,4},{1,9},{5... | collective-permute-start | bytes 4718600 | tf_op jit(solution)/shard_map/ppermute | solution.py:290
  16.9 56.3 %conditional.6 = (bf16[3,128,2048]{2,1,0:T(8,128)(2,1)}, bf16[3,128,2048]{2,1,0:T(8,128)(2,1)S(1)}, bf16[2,64,1024]{2,1,0:T(8,128)(2,1)S(1)}, bf16[8,256,256]{2,1,0:T(8,128)(2,1)}) conditional(s32[]{:T(128)} %convert_element_type.83, () %tuple.76, (bf16[3,128,2048]{2,1,0:T(8,128)(2,1)}, bf16[3,128,2048]{2,1,0:T(8,128)(2,1)}, s32[17]{0:T(128)S(1)}, ...), branch_computations={%region_1.0_spmd, %region_2.0_spmd} | conditional | flops 323826496 | bytes 43149296 | solution.py:284
  17.4 1.8 reshape.14
  19.3 1.2 copy.20
  20.5 4.2 %all-to-all-start = ((bf16[4,2,256,256]{3,2,1,0:T(8,128)(2,1)}), bf16[4,2,256,256]{3,2,1,0:T(8,128)(2,1)}, u32[]{:S(2)}, u32[]{:S(2)}) async-start(bf16[4,2,256,256]{3,2,1,0:T(8,128)(2,1)} %bitcast.23), calls=%async_computation | async-start | bytes 2097152 | tf_op jit(solution)/shard_map/cond/branch_1_fun/all_to_all | solution.py:271
  24.8 11.8 %input_grad.5 = (bf16[128,1024]{1,0:T(8,128)(2,1)S(1)}, bf16[128,1024]{1,0:T(8,128)(2,1)S(1)}, bf16[128,1024]{1,0:T(8,128)(2,1)S(1)}, bf16[128,1024]{1,0:T(8,128)(2,1)S(1)}) custom-call(s32[17]{0:T(128)S(1)} %get-tuple-element.126.place_ref, bf16[3,128,2048]{2,1,0:T(8,128)(2,1)} %get-tuple-element.124.refs_0_, ...), custom_call_target="tpu_custom_call" | custom-call | flops 322122560 | bytes 943718 | tf_op jit(solution)/shard_map/cond/branch_1_fun/input_grad/pallas_call | solution.py:104
  36.5 2.4 all-to-all-done
  38.9 4.4 %all-to-all-start.1 = ((bf16[8,256,256]{2,1,0:T(8,128)(2,1)}), bf16[8,256,256]{2,1,0:T(8,128)(2,1)}, u32[]{:S(2)}, u32[]{:S(2)}) async-start(bf16[8,256,256]{2,1,0:T(8,128)(2,1)} %bitcast.3), calls=%async_computation.1 | async-start | bytes 2097152 | tf_op jit(solution)/shard_map/cond/branch_1_fun/all_to_all | solution.py:271
  43.3 1.5 collective-permute-start.11
  45.4 1.5 collective-permute-start.13
  46.9 5.6 %collective-permute-done.11 = bf16[128,1024]{1,0:T(8,128)(2,1)S(1)} collective-permute-done((bf16[128,1024]{1,0:T(8,128)(2,1)S(1)}, bf16[128,1024]{1,0:T(8,128)(2,1)S(1)}, u32[]{:S(2)}, u32[]{:S(2)}) %collective-permute-start.11) | collective-permute-done | bytes 262176 | tf_op jit(solution)/shard_map/cond/branch_1_fun/ppermute | solution.py:296
  52.5 6.2 %collective-permute-done.12 = bf16[128,1024]{1,0:T(8,128)(2,1)S(1)} collective-permute-done((bf16[128,1024]{1,0:T(8,128)(2,1)S(1)}, bf16[128,1024]{1,0:T(8,128)(2,1)S(1)}, u32[]{:S(2)}, u32[]{:S(2)}) %collective-permute-start.12) | collective-permute-done | bytes 262176 | tf_op jit(solution)/shard_map/cond/branch_1_fun/ppermute | solution.py:296
  59.0 1.3 collective-permute-done.14
  60.3 12.8 %all-to-all-done.1 = bf16[8,256,256]{2,1,0:T(8,128)(2,1)} async-done(((bf16[8,256,256]{2,1,0:T(8,128)(2,1)}), bf16[8,256,256]{2,1,0:T(8,128)(2,1)}, u32[]{:S(2)}, u32[]{:S(2)}) %all-to-all-start.1) | async-done | bytes 1048608 | tf_op jit(solution)/shard_map/cond/branch_1_fun/all_to_all | solution.py:271
  74.0 27.1 %conditional.7 = (bf16[3,128,2048]{2,1,0:T(8,128)(2,1)}, bf16[8,256,256]{2,1,0:T(8,128)(2,1)}, bf16[8,256,256]{2,1,0:T(8,128)(2,1)}) conditional(s32[]{:T(128)} %convert_element_type.83, () %tuple.79, (bf16[3,128,2048]{2,1,0:T(8,128)(2,1)}, bf16[8,256,256]{2,1,0:T(8,128)(2,1)}) %tuple.80), branch_computations={%region_3.0_spmd, %region_4.0_spmd} | conditional | bytes 14680208 | solution.py:284
  74.0 1.5 collective-permute-start.2
  75.5 1.5 collective-permute-start.1
  77.0 22.9 %collective-permute-done.2 = bf16[8,256,256]{2,1,0:T(8,128)(2,1)} collective-permute-done((bf16[8,256,256]{2,1,0:T(8,128)(2,1)}, bf16[8,256,256]{2,1,0:T(8,128)(2,1)}, u32[]{:S(2)}, u32[]{:S(2)}) %collective-permute-start.2) | collective-permute-done | bytes 1048608 | tf_op jit(solution)/shard_map/cond/branch_1_fun/ppermute | solution.py:296
  99.8 1.2 collective-permute-done.1
  101.1 3.4 %collective-permute-start.27 = (bf16[3,128,2048]{2,1,0:T(8,128)(2,1)}, bf16[3,128,2048]{2,1,0:T(8,128)(2,1)}, u32[]{:S(2)}, u32[]{:S(2)}) collective-permute-start(bf16[3,128,2048]{2,1,0:T(8,128)(2,1)} %collective-permute-done.26), channel_id=1, source_target_pairs={{0,8},{4,12},{8,24},{12,28},{24,16},{28,20},{16,0},{20,4},{1,9},{5... | collective-permute-start | bytes 4718600 | tf_op jit(solution)/shard_map/ppermute | solution.py:290
  104.5 7.2 %collective-permute-done.28 = bf16[3,128,2048]{2,1,0:T(8,128)(2,1)} collective-permute-done((bf16[3,128,2048]{2,1,0:T(8,128)(2,1)}, bf16[3,128,2048]{2,1,0:T(8,128)(2,1)}, u32[]{:S(2)}, u32[]{:S(2)}) %collective-permute-start.28) | collective-permute-done | bytes 1572896 | tf_op jit(solution)/shard_map/ppermute | solution.py:290
  111.7 26.8 %conditional.8 = (bf16[3,128,2048]{2,1,0:T(8,128)(2,1)}, bf16[128,1024]{1,0:T(8,128)(2,1)S(1)}, bf16[128,1024]{1,0:T(8,128)(2,1)}, bf16[128,1024]{1,0:T(8,128)(2...) conditional(s32[]{:T(128)} %convert_element_type.83, () %tuple.82, (bf16[3,128,2048]{2,1,0:T(8,128)(2,1)}, ...), branch_computations={%region_5.0_spmd, %region_6.0_spmd} | conditional | flops 322122560 | bytes 11429606 | solution.py:284
  111.7 2.5 collective-permute-start.4
  114.2 1.2 collective-permute-done.3.refs_3_.refs_7_
  115.4 12.9 %input_grad.6 = (bf16[128,1024]{1,0:T(8,128)(2,1)S(1)}, bf16[128,1024]{1,0:T(8,128)(2,1)}, bf16[128,1024]{1,0:T(8,128)(2,1)}, bf16[128,1024]{1,0:T(8,128)(2,1)}) custom-call(s32[17]{0:T(128)S(1)} %get-tuple-element.143.place_ref, bf16[3,128,2048]{2,1,0:T(8,128)(2,1)} %get-tuple-element.144.refs_0_, bf16[3,128,2048]{2,1,0:T(8,128)(2,1)} %get-tuple-element.145.refs_1_, ...), custom_call_target="tpu_custom_call" | custom-call | flops 322122560 | bytes 943718 | tf_op jit(solution)/shard_map/cond/branch_1_fun/input_grad/pallas_call | solution.py:104
  128.3 10.2 %collective-permute-done.4 = bf16[8,256,256]{2,1,0:T(8,128)(2,1)} collective-permute-done((bf16[8,256,256]{2,1,0:T(8,128)(2,1)}, bf16[8,256,256]{2,1,0:T(8,128)(2,1)}, u32[]{:S(2)}, u32[]{:S(2)}) %collective-permute-start.4) | collective-permute-done | bytes 1048608 | tf_op jit(solution)/shard_map/cond/branch_1_fun/ppermute | solution.py:296
  139.3 5.9 %collective-permute-done.27 = bf16[3,128,2048]{2,1,0:T(8,128)(2,1)} collective-permute-done((bf16[3,128,2048]{2,1,0:T(8,128)(2,1)}, bf16[3,128,2048]{2,1,0:T(8,128)(2,1)}, u32[]{:S(2)}, u32[]{:S(2)}) %collective-permute-start.27) | collective-permute-done | bytes 1572896 | tf_op jit(solution)/shard_map/ppermute | solution.py:290
  145.2 24.3 %conditional.9 = (bf16[3,128,2048]{2,1,0:T(8,128)(2,1)}, bf16[2,64,1024]{2,1,0:T(8,128)(2,1)S(1)}, bf16[1024,2048]{1,0:T(8,128)(2,1)}, bf16[1024,2048]{1,0:T(8,128)(2,1)}, bf16[1024,2048]{1,0:T(8,128)(2,1)}) conditional(s32[]{:T(128)} %convert_element_type.83, () %tuple.78, (bf16[3,128,2048]{2,1,0:T(8,128)(2,1)}, bf16[128,1024]{1,0:T(8,128)(2,1)}, ...), branch_computations={%region_7.0_spmd, %region_8.0_spmd} | conditional | flops 645949056 | bytes 14417970 | solution.py:284
  146.1 1.5 collective-permute-start.17
  148.7 19.1 %weight_grad.4 = (bf16[1024,2048]{1,0:T(8,128)(2,1)}, bf16[1024,2048]{1,0:T(8,128)(2,1)}, bf16[1024,2048]{1,0:T(8,128)(2,1)}) custom-call(s32[17]{0:T(128)S(1)} %get-tuple-element.159.place_ref, bf16[8,256,256]{2,1,0:T(8,128)(2,1)} %get-tuple-element.160.refs_0_, bf16[8,256,256]{2,1,0:T(8,128)(2,1)} %get-tuple-element.161.refs_1_, ...), custom_call_target="tpu_custom_call" | custom-call | flops 644245120 | bytes 1258291 | tf_op jit(solution)/shard_map/cond/branch_1_fun/weight_grad/pallas_call | solution.py:158
  168.2 1.3 collective-permute-done.19
  169.8 9.0 %collective-permute-done.30 = bf16[3,128,2048]{2,1,0:T(8,128)(2,1)S(1)} collective-permute-done((bf16[3,128,2048]{2,1,0:T(8,128)(2,1)}, bf16[3,128,2048]{2,1,0:T(8,128)(2,1)S(1)}, u32[]{:S(2)}, u32[]{:S(2)}) %collective-permute-start.30) | collective-permute-done | bytes 1572896 | tf_op jit(solution)/shard_map/ppermute | solution.py:290
  178.8 32.2 %conditional.10 = (bf16[3,128,2048]{2,1,0:T(8,128)(2,1)}, bf16[128,1024]{1,0:T(8,128)(2,1)S(1)}, bf16[1024,2048]{1,0:T(8,128)(2,1)}, bf16[1024,2048]{1,0:T(8,128)(2,1)}, bf16[1024,2048]{1,0:T(8,128)(2,1)}) conditional(s32[]{:T(128)} %convert_element_type.83, () %tuple.88, (bf16[3,128,2048]{2,1,0:T(8,128)(2,1)S(1)}, s32[17]{0:T(128)S(1)}, ...), branch_computations={%region_9.0_spmd, %region_10.0_spmd} | conditional | flops 645293696 | bytes 63596420 | solution.py:284
  178.8 3.5 %collective-permute-done.5.refs_3_.refs_7_ = bf16[3,128,2048]{2,1,0:T(8,128)(2,1)} collective-permute-done((bf16[3,128,2048]{2,1,0:T(8,128)(2,1)S(1)}, bf16[3,128,2048]{2,1,0:T(8,128)(2,1)}, u32[]{:S(2)}, u32[]{:S(2)}) %collective-permute-start.5) | collective-permute-done | bytes 1572896 | tf_op jit(solution)/shard_map/cond/branch_1_fun/ppermute | solution.py:293
  182.3 12.5 %input_grad.7 = (bf16[128,1024]{1,0:T(8,128)(2,1)S(1)}, bf16[128,1024]{1,0:T(8,128)(2,1)S(1)}, bf16[128,1024]{1,0:T(8,128)(2,1)S(1)}, bf16[128,1024]{1,0:T(8,128)(2,1)S(1)}) custom-call(s32[17]{0:T(128)S(1)} %get-tuple-element.180.place_ref, bf16[3,128,2048]{2,1,0:T(8,128)(2,1)} %get-tuple-element.181.refs_0_.refs_4_, ...), custom_call_target="tpu_custom_call" | custom-call | flops 322122560 | bytes 943718 | tf_op jit(solution)/shard_map/cond/branch_1_fun/input_grad/pallas_call | solution.py:104
  195.8 1.5 collective-permute-start.7
  197.3 1.1 collective-permute-start.8
  198.4 12.4 %weight_grad.5 = (bf16[1024,2048]{1,0:T(8,128)(2,1)}, bf16[1024,2048]{1,0:T(8,128)(2,1)}, bf16[1024,2048]{1,0:T(8,128)(2,1)}) custom-call(s32[17]{0:T(128)S(1)} %get-tuple-element.180.place_ref, bf16[8,256,256]{2,1,0:T(8,128)(2,1)} %get-tuple-element.190.refs_0_, bf16[8,256,256]{2,1,0:T(8,128)(2,1)} %get-tuple-element.191.refs_1_, ...), custom_call_target="tpu_custom_call" | custom-call | flops 322122560 | bytes 1572864 | tf_op jit(solution)/shard_map/cond/branch_1_fun/weight_grad/pallas_call | solution.py:158
  211.4 29.0 %conditional.11 = (bf16[3,128,2048]{2,1,0:T(8,128)(2,1)}, bf16[2,32,1024]{2,1,0:T(8,128)(2,1)S(1)}, bf16[1024,2048]{1,0:T(8,128)(2,1)}, bf16[1024,2048]{1,0:T(8,...) conditional(s32[]{:T(128)} %convert_element_type.83, () %tuple.86, ...), branch_computations={%region_11.0_spmd, %region_12.0_spmd} | conditional | flops 323367744 | bytes 63937292 | solution.py:284
  212.1 3.0 %collective-permute-done.20.refs_1_.refs_5_ = bf16[3,128,2048]{2,1,0:T(8,128)(2,1)} collective-permute-done((bf16[3,128,2048]{2,1,0:T(8,128)(2,1)}, bf16[3,128,2048]{2,1,0:T(8,128)(2,1)}, u32[]{:S(2)}, u32[]{:S(2)}) %collective-permute-start.20) | collective-permute-done | bytes 1572896 | tf_op jit(solution)/shard_map/cond/branch_1_fun/ppermute | solution.py:293
  215.2 8.9 %input_grad.8 = (bf16[64,1024]{1,0:T(8,128)(2,1)S(1)}, bf16[64,1024]{1,0:T(8,128)(2,1)S(1)}, bf16[64,1024]{1,0:T(8,128)(2,1)S(1)}, bf16[64,1024]{1,0:T(8,128)(2,1)S(1)}) custom-call(s32[17]{0:T(128)S(1)} %get-tuple-element.205.place_ref, bf16[3,128,2048]{2,1,0:T(8,128)(2,1)} %get-tuple-element.204.refs_0_.refs_4_, ...), custom_call_target="tpu_custom_call" | custom-call | flops 161061280 | bytes 786432 | tf_op jit(solution)/shard_map/cond/branch_1_fun/input_grad/pallas_call | solution.py:104
  224.1 1.5 collective-permute-start.21
  225.6 1.5 collective-permute-start.22
  227.7 9.4 %weight_grad.6 = (bf16[1024,2048]{1,0:T(8,128)(2,1)}, bf16[1024,2048]{1,0:T(8,128)(2,1)}, bf16[1024,2048]{1,0:T(8,128)(2,1)}) custom-call(s32[17]{0:T(128)S(1)} %get-tuple-element.205.place_ref, bf16[8,256,256]{2,1,0:T(8,128)(2,1)} %get-tuple-element.213.refs_0_, bf16[8,256,256]{2,1,0:T(8,128)(2,1)} %get-tuple-element.214.refs_1_, ...), custom_call_target="tpu_custom_call" | custom-call | flops 161061280 | bytes 1415577 | tf_op jit(solution)/shard_map/cond/branch_1_fun/weight_grad/pallas_call | solution.py:158
  238.7 1.6 pad_maximum_fusion.4
  240.4 7.2 %collective-permute-done.31.refs_0_.refs_4_ = bf16[3,128,2048]{2,1,0:T(8,128)(2,1)S(1)} collective-permute-done((bf16[3,128,2048]{2,1,0:T(8,128)(2,1)S(1)}, bf16[3,128,2048]{2,1,0:T(8,128)(2,1)S(1)}, u32[]{:S(2)}, u32[]{:S(2)}) %collective-permute-start.31) | collective-permute-done | bytes 1572896 | tf_op jit(solution)/shard_map/ppermute | solution.py:290
  248.5 2.1 collective-permute-start.33
  251.1 7.4 %input_grad.9 = (bf16[64,1024]{1,0:T(8,128)(2,1)S(1)}, bf16[64,1024]{1,0:T(8,128)(2,1)S(1)}, bf16[64,1024]{1,0:T(8,128)(2,1)S(1)}, bf16[64,1024]{1,0:T(8,128)(2,1)S(1)}) custom-call(s32[17]{0:T(128)S(1)} %dynamic-slice_bitcast_fusion.place_ref, bf16[3,128,2048]{2,1,0:T(8,128)(2,1)S(1)} %collective-permute-done.31.refs_0_.refs_4_, ...), custom_call_target="tpu_custom_call" | custom-call | flops 161061280 | bytes 786432 | tf_op jit(solution)/shard_map/input_grad/pallas_call | solution.py:104
  258.5 1.6 collective-permute-start.35
  260.1 1.5 collective-permute-start.36
  262.1 1.4 collective-permute-done.33.refs_2_
  263.5 1.1 collective-permute-done.35
  264.6 3.7 %collective-permute-done.36 = bf16[64,1024]{1,0:T(8,128)(2,1)S(1)} collective-permute-done((bf16[64,1024]{1,0:T(8,128)(2,1)S(1)}, bf16[64,1024]{1,0:T(8,128)(2,1)S(1)}, u32[]{:S(2)}, u32[]{:S(2)}) %collective-permute-start.36) | collective-permute-done | bytes 131104 | tf_op jit(solution)/shard_map/ppermute | solution.py:296
  268.5 1.2 collective-permute-done.39
  269.7 1.3 collective-permute-start.40
  271.1 2.0 collective-permute-start.41
  273.1 3.9 %collective-permute-done.41 = f32[16]{0:T(128)S(1)} collective-permute-done((f32[16]{0:T(128)S(1)}, f32[16]{0:T(128)S(1)}, u32[]{:S(2)}, u32[]{:S(2)}) %collective-permute-start.41) | collective-permute-done | bytes 96 | tf_op jit(solution)/shard_map/ppermute | solution.py:403
  277.0 2.8 collective-permute-start.42
  279.8 1.6 collective-permute-done.42
  282.6 1.6 collective-permute-start.43
  284.2 1.5 collective-permute-start.44
  286.2 9.6 %weight_grad.7 = (bf16[1024,2048]{1,0:T(8,128)(2,1)}, bf16[1024,2048]{1,0:T(8,128)(2,1)}, bf16[1024,2048]{1,0:T(8,128)(2,1)}) custom-call(s32[17]{0:T(128)S(1)} %dynamic-slice_bitcast_fusion.place_ref, bf16[8,256,256]{2,1,0:T(8,128)(2,1)} %get-tuple-element.359.refs_0_, bf16[8,256,256]{2,1,0:T(8,128)(2,1)} %get-tuple-element.360.refs_1_, ...), custom_call_target="tpu_custom_call" | custom-call | flops 161061280 | bytes 1415577 | tf_op jit(solution)/shard_map/weight_grad/pallas_call | solution.py:158
  296.2 1.6 assemble.1
  (109 shorter events, 15.5 us)
Async XLA Ops:
  0.6 14.9 %copy-start.14 = (s32[1,256]{1,0:T(1,128)S(1)}, s32[1,256]{1,0:T(1,128)}, u32[]{:S(2)}) copy-start(s32[1,256]{1,0:T(1,128)} %flag_ref.1) | copy-start | bytes 3076
  11.8 62.1 %collective-permute-start.26 = (bf16[3,128,2048]{2,1,0:T(8,128)(2,1)}, bf16[3,128,2048]{2,1,0:T(8,128)(2,1)}, u32[]{:S(2)}, u32[]{:S(2)}) collective-permute-start(bf16[3,128,2048]{2,1,0:T(8,128)(2,1)} %get-tuple-element.303), channel_id=1, source_target_pairs={{0,8},{4,12},{8,24},{12,28},{24,16},{28,20},{16,0},{20,4},{1,9},{5... | collective-permute-start | bytes 4718600 | tf_op jit(solution)/shard_map/ppermute | solution.py:290
  16.9 7.8 %collective-permute-start.9 = (bf16[3,128,2048]{2,1,0:T(8,128)(2,1)}, bf16[3,128,2048]{2,1,0:T(8,128)(2,1)}, u32[]{:S(2)}, u32[]{:S(2)}) collective-permute-start(bf16[3,128,2048]{2,1,0:T(8,128)(2,1)} %get-tuple-element.124.refs_0_), channel_id=1, source_target_pairs={{0,4},{4,0},{8,12},{12,8},{16,20},{20,16},{24,28},{28,24},{1,5},{5... | collective-permute-start | bytes 4718600 | tf_op jit(solution)/shard_map/cond/branch_1_fun/ppermute | solution.py:293
  17.0 7.8 %collective-permute-start.10 = (bf16[3,128,2048]{2,1,0:T(8,128)(2,1)}, bf16[3,128,2048]{2,1,0:T(8,128)(2,1)S(1)}, u32[]{:S(2)}, u32[]{:S(2)}) collective-permute-start(bf16[3,128,2048]{2,1,0:T(8,128)(2,1)} %get-tuple-element.125.refs_2_), channel_id=1, source_target_pairs={{0,4},{4,0},{8,12},{12,8},{16,20},{20,16},{24,28},{28,24},{1,5},{5... | collective-permute-start | bytes 4718600 | tf_op jit(solution)/shard_map/cond/branch_1_fun/ppermute | solution.py:293
  20.5 18.5 %all-to-all-start = ((bf16[4,2,256,256]{3,2,1,0:T(8,128)(2,1)}), bf16[4,2,256,256]{3,2,1,0:T(8,128)(2,1)}, u32[]{:S(2)}, u32[]{:S(2)}) async-start(bf16[4,2,256,256]{3,2,1,0:T(8,128)(2,1)} %bitcast.23), calls=%async_computation | async-start | bytes 2097152 | tf_op jit(solution)/shard_map/cond/branch_1_fun/all_to_all | solution.py:271
  24.7 11.8 %copy-start = (bf16[3,128,2048]{2,1,0:T(8,128)(2,1)}, bf16[3,128,2048]{2,1,0:T(8,128)(2,1)S(1)}, u32[]{:S(2)}) copy-start(bf16[3,128,2048]{2,1,0:T(8,128)(2,1)S(1)} %collective-permute-done.10.refs_3_.refs_7_) | copy-start | bytes 4718596 | tf_op jit(solution)/shard_map/cond
  38.9 34.2 %copy-start.1 = (bf16[3,128,2048]{2,1,0:T(8,128)(2,1)S(1)}, bf16[3,128,2048]{2,1,0:T(8,128)(2,1)}, u32[]{:S(2)}) copy-start(bf16[3,128,2048]{2,1,0:T(8,128)(2,1)} %copy-done) | copy-start | bytes 4718596 | tf_op jit(solution)/shard_map/cond
  38.9 34.2 %all-to-all-start.1 = ((bf16[8,256,256]{2,1,0:T(8,128)(2,1)}), bf16[8,256,256]{2,1,0:T(8,128)(2,1)}, u32[]{:S(2)}, u32[]{:S(2)}) async-start(bf16[8,256,256]{2,1,0:T(8,128)(2,1)} %bitcast.3), calls=%async_computation.1 | async-start | bytes 2097152 | tf_op jit(solution)/shard_map/cond/branch_1_fun/all_to_all | solution.py:271
  43.3 9.2 %collective-permute-start.11 = (bf16[128,1024]{1,0:T(8,128)(2,1)S(1)}, bf16[128,1024]{1,0:T(8,128)(2,1)S(1)}, u32[]{:S(2)}, u32[]{:S(2)}) collective-permute-start(bf16[128,1024]{1,0:T(8,128)(2,1)S(1)} %get-tuple-element.131), channel_id=1, source_target_pairs={{0,1},{1,0},{2,3},{3,2},{4,5},{5,4},{6,7},{7,6},{8,9},{9,8},{10,11... | collective-permute-start | bytes 786440 | tf_op jit(solution)/shard_map/cond/branch_1_fun/ppermute | solution.py:296
  44.8 13.9 %collective-permute-start.12 = (bf16[128,1024]{1,0:T(8,128)(2,1)S(1)}, bf16[128,1024]{1,0:T(8,128)(2,1)S(1)}, u32[]{:S(2)}, u32[]{:S(2)}) collective-permute-start(bf16[128,1024]{1,0:T(8,128)(2,1)S(1)} %get-tuple-element.132), channel_id=1, source_target_pairs={{0,2},{1,3},{2,0},{3,1},{4,6},{5,7},{6,4},{7,5},{8,10},{9,11},{10,... | collective-permute-start | bytes 786440 | tf_op jit(solution)/shard_map/cond/branch_1_fun/ppermute | solution.py:296
  45.4 13.3 %collective-permute-start.13 = (bf16[128,1024]{1,0:T(8,128)(2,1)S(1)}, bf16[128,1024]{1,0:T(8,128)(2,1)S(1)}, u32[]{:S(2)}, u32[]{:S(2)}) collective-permute-start(bf16[128,1024]{1,0:T(8,128)(2,1)S(1)} %get-tuple-element.133), channel_id=1, source_target_pairs={{0,3},{1,2},{2,1},{3,0},{4,7},{5,6},{6,5},{7,4},{8,11},{9,10},{10,... | collective-permute-start | bytes 786440 | tf_op jit(solution)/shard_map/cond/branch_1_fun/ppermute | solution.py:296
  58.9 1.4 collective-permute-start.14
  73.1 38.6 %copy-start.10 = (bf16[2,64,1024]{2,1,0:T(8,128)(2,1)}, bf16[2,64,1024]{2,1,0:T(8,128)(2,1)S(1)}, u32[]{:S(2)}) copy-start(bf16[2,64,1024]{2,1,0:T(8,128)(2,1)S(1)} %get-tuple-element.338.refs_0_) | copy-start | bytes 786436
  73.1 38.5 %collective-permute-start.28 = (bf16[3,128,2048]{2,1,0:T(8,128)(2,1)}, bf16[3,128,2048]{2,1,0:T(8,128)(2,1)}, u32[]{:S(2)}, u32[]{:S(2)}) collective-permute-start(bf16[3,128,2048]{2,1,0:T(8,128)(2,1)} %get-tuple-element.310), channel_id=1, source_target_pairs={{0,8},{4,12},{8,24},{12,28},{24,16},{28,20},{16,0},{20,4},{1,9},{5... | collective-permute-start | bytes 4718600 | tf_op jit(solution)/shard_map/ppermute | solution.py:290
  74.0 27.1 %collective-permute-start = (bf16[3,128,2048]{2,1,0:T(8,128)(2,1)}, bf16[3,128,2048]{2,1,0:T(8,128)(2,1)}, u32[]{:S(2)}, u32[]{:S(2)}) collective-permute-start(bf16[3,128,2048]{2,1,0:T(8,128)(2,1)} %get-tuple-element.140), channel_id=1, source_target_pairs={{0,4},{4,0},{8,12},{12,8},{16,20},{20,16},{24,28},{28,24},{1,5},{5... | collective-permute-start | bytes 4718600 | tf_op jit(solution)/shard_map/cond/branch_1_fun/ppermute | solution.py:293
  74.0 25.9 %collective-permute-start.2 = (bf16[8,256,256]{2,1,0:T(8,128)(2,1)}, bf16[8,256,256]{2,1,0:T(8,128)(2,1)}, u32[]{:S(2)}, u32[]{:S(2)}) collective-permute-start(bf16[8,256,256]{2,1,0:T(8,128)(2,1)} %get-tuple-element.141), channel_id=1, source_target_pairs={{0,2},{1,3},{2,0},{3,1},{4,6},{5,7},{6,4},{7,5},{8,10},{9,11},{10,... | collective-permute-start | bytes 3145736 | tf_op jit(solution)/shard_map/cond/branch_1_fun/ppermute | solution.py:296
  75.5 25.6 %collective-permute-start.1 = (bf16[8,256,256]{2,1,0:T(8,128)(2,1)}, bf16[8,256,256]{2,1,0:T(8,128)(2,1)}, u32[]{:S(2)}, u32[]{:S(2)}) collective-permute-start(bf16[8,256,256]{2,1,0:T(8,128)(2,1)} %get-tuple-element.141), channel_id=1, source_target_pairs={{0,1},{1,0},{2,3},{3,2},{4,5},{5,4},{6,7},{7,6},{8,9},{9,8},{10,11... | collective-permute-start | bytes 3145736 | tf_op jit(solution)/shard_map/cond/branch_1_fun/ppermute | solution.py:296
  101.1 44.1 %collective-permute-start.27 = (bf16[3,128,2048]{2,1,0:T(8,128)(2,1)}, bf16[3,128,2048]{2,1,0:T(8,128)(2,1)}, u32[]{:S(2)}, u32[]{:S(2)}) collective-permute-start(bf16[3,128,2048]{2,1,0:T(8,128)(2,1)} %collective-permute-done.26), channel_id=1, source_target_pairs={{0,8},{4,12},{8,24},{12,28},{24,16},{28,20},{16,0},{20,4},{1,9},{5... | collective-permute-start | bytes 4718600 | tf_op jit(solution)/shard_map/ppermute | solution.py:290
  111.7 3.8 %collective-permute-start.3 = (bf16[3,128,2048]{2,1,0:T(8,128)(2,1)}, bf16[3,128,2048]{2,1,0:T(8,128)(2,1)}, u32[]{:S(2)}, u32[]{:S(2)}) collective-permute-start(bf16[3,128,2048]{2,1,0:T(8,128)(2,1)} %get-tuple-element.142.refs_2_), channel_id=1, source_target_pairs={{0,4},{4,0},{8,12},{12,8},{16,20},{20,16},{24,28},{28,24},{1,5},{5... | collective-permute-start | bytes 4718600 | tf_op jit(solution)/shard_map/cond/branch_1_fun/ppermute | solution.py:293
  111.7 26.8 %collective-permute-start.4 = (bf16[8,256,256]{2,1,0:T(8,128)(2,1)}, bf16[8,256,256]{2,1,0:T(8,128)(2,1)}, u32[]{:S(2)}, u32[]{:S(2)}) collective-permute-start(bf16[8,256,256]{2,1,0:T(8,128)(2,1)} %get-tuple-element.153), channel_id=1, source_target_pairs={{0,3},{1,2},{2,1},{3,0},{4,7},{5,6},{6,5},{7,4},{8,11},{9,10},{10,... | collective-permute-start | bytes 3145736 | tf_op jit(solution)/shard_map/cond/branch_1_fun/ppermute | solution.py:296
  138.5 40.3 %collective-permute-start.30 = (bf16[3,128,2048]{2,1,0:T(8,128)(2,1)}, bf16[3,128,2048]{2,1,0:T(8,128)(2,1)S(1)}, u32[]{:S(2)}, u32[]{:S(2)}) collective-permute-start(bf16[3,128,2048]{2,1,0:T(8,128)(2,1)} %collective-permute-done.28), channel_id=1, source_target_pairs={{0,8},{4,12},{8,24},{12,28},{24,16},{28,20},{16,0},{20,4},{1,9},{5... | collective-permute-start | bytes 4718600 | tf_op jit(solution)/shard_map/ppermute | solution.py:290
  145.2 24.3 %collective-permute-start.15 = (bf16[3,128,2048]{2,1,0:T(8,128)(2,1)}, bf16[3,128,2048]{2,1,0:T(8,128)(2,1)}, u32[]{:S(2)}, u32[]{:S(2)}) collective-permute-start(bf16[3,128,2048]{2,1,0:T(8,128)(2,1)} %get-tuple-element.154), channel_id=1, source_target_pairs={{0,4},{4,0},{8,12},{12,8},{16,20},{20,16},{24,28},{28,24},{1,5},{5... | collective-permute-start | bytes 4718600 | tf_op jit(solution)/shard_map/cond/branch_1_fun/ppermute | solution.py:293
  145.2 22.6 %collective-permute-start.16 = (bf16[128,1024]{1,0:T(8,128)(2,1)}, bf16[128,1024]{1,0:T(8,128)(2,1)S(1)}, u32[]{:S(2)}, u32[]{:S(2)}) collective-permute-start(bf16[128,1024]{1,0:T(8,128)(2,1)} %get-tuple-element.156), channel_id=1, source_target_pairs={{0,1},{1,0},{2,3},{3,2},{4,5},{5,4},{6,7},{7,6},{8,9},{9,8},{10,11... | collective-permute-start | bytes 786440 | tf_op jit(solution)/shard_map/cond/branch_1_fun/ppermute | solution.py:296
  146.1 21.7 %collective-permute-start.17 = (bf16[128,1024]{1,0:T(8,128)(2,1)}, bf16[128,1024]{1,0:T(8,128)(2,1)S(1)}, u32[]{:S(2)}, u32[]{:S(2)}) collective-permute-start(bf16[128,1024]{1,0:T(8,128)(2,1)} %get-tuple-element.157), channel_id=1, source_target_pairs={{0,2},{1,3},{2,0},{3,1},{4,6},{5,7},{6,4},{7,5},{8,10},{9,11},{10,... | collective-permute-start | bytes 786440 | tf_op jit(solution)/shard_map/cond/branch_1_fun/ppermute | solution.py:296
  147.6 20.2 %collective-permute-start.18 = (bf16[128,1024]{1,0:T(8,128)(2,1)}, bf16[128,1024]{1,0:T(8,128)(2,1)S(1)}, u32[]{:S(2)}, u32[]{:S(2)}) collective-permute-start(bf16[128,1024]{1,0:T(8,128)(2,1)} %get-tuple-element.158), channel_id=1, source_target_pairs={{0,3},{1,2},{2,1},{3,0},{4,7},{5,6},{6,5},{7,4},{8,11},{9,10},{10,... | collective-permute-start | bytes 786440 | tf_op jit(solution)/shard_map/cond/branch_1_fun/ppermute | solution.py:296
  168.1 1.4 collective-permute-start.19
  169.5 9.3 %copy-start.12 = (bf16[2,64,1024]{2,1,0:T(8,128)(2,1)}, bf16[2,64,1024]{2,1,0:T(8,128)(2,1)S(1)}, u32[]{:S(2)}) copy-start(bf16[2,64,1024]{2,1,0:T(8,128)(2,1)S(1)} %get-tuple-element.339) | copy-start | bytes 786436
  169.5 41.8 %collective-permute-start.29 = (bf16[3,128,2048]{2,1,0:T(8,128)(2,1)}, bf16[3,128,2048]{2,1,0:T(8,128)(2,1)}, u32[]{:S(2)}, u32[]{:S(2)}) collective-permute-start(bf16[3,128,2048]{2,1,0:T(8,128)(2,1)} %collective-permute-done.27), channel_id=1, source_target_pairs={{0,8},{4,12},{8,24},{12,28},{24,16},{28,20},{16,0},{20,4},{1,9},{5... | collective-permute-start | bytes 4718600 | tf_op jit(solution)/shard_map/ppermute | solution.py:290
  178.8 3.5 %collective-permute-start.5 = (bf16[3,128,2048]{2,1,0:T(8,128)(2,1)S(1)}, bf16[3,128,2048]{2,1,0:T(8,128)(2,1)}, u32[]{:S(2)}, u32[]{:S(2)}) collective-permute-start(bf16[3,128,2048]{2,1,0:T(8,128)(2,1)S(1)} %get-tuple-element.179.refs_2_.refs_6_), channel_id=1, source_target_pairs={{0,4},{4,0},{8,12},{12,8},{16,20},{20,16},{24,28},{28,24},{1,5},{5... | collective-permute-start | bytes 4718600 | tf_op jit(solution)/shard_map/cond/branch_1_fun/ppermute | solution.py:293
  182.3 16.1 %copy-start.2 = (bf16[1024,2048]{1,0:T(8,128)(2,1)S(1)}, bf16[1024,2048]{1,0:T(8,128)(2,1)}, u32[]{:S(2)}) copy-start(bf16[1024,2048]{1,0:T(8,128)(2,1)} %get-tuple-element.196.refs_10_) | copy-start | bytes 12582916 | tf_op jit(solution)/shard_map/cond
  182.3 16.1 %copy-start.3 = (bf16[1024,2048]{1,0:T(8,128)(2,1)S(1)}, bf16[1024,2048]{1,0:T(8,128)(2,1)}, u32[]{:S(2)}) copy-start(bf16[1024,2048]{1,0:T(8,128)(2,1)} %get-tuple-element.195.refs_9_) | copy-start | bytes 12582916 | tf_op jit(solution)/shard_map/cond
  182.3 16.1 %copy-start.4 = (bf16[1024,2048]{1,0:T(8,128)(2,1)S(1)}, bf16[1024,2048]{1,0:T(8,128)(2,1)}, u32[]{:S(2)}) copy-start(bf16[1024,2048]{1,0:T(8,128)(2,1)} %get-tuple-element.194.refs_8_) | copy-start | bytes 12582916 | tf_op jit(solution)/shard_map/cond
  194.9 16.0 %collective-permute-start.6 = (bf16[128,1024]{1,0:T(8,128)(2,1)S(1)}, bf16[128,1024]{1,0:T(8,128)(2,1)S(1)}, u32[]{:S(2)}, u32[]{:S(2)}) collective-permute-start(bf16[128,1024]{1,0:T(8,128)(2,1)S(1)} %get-tuple-element.187), channel_id=1, source_target_pairs={{0,1},{1,0},{2,3},{3,2},{4,5},{5,4},{6,7},{7,6},{8,9},{9,8},{10,11... | collective-permute-start | bytes 786440 | tf_op jit(solution)/shard_map/cond/branch_1_fun/ppermute | solution.py:296
  195.8 15.0 %collective-permute-start.7 = (bf16[128,1024]{1,0:T(8,128)(2,1)S(1)}, bf16[128,1024]{1,0:T(8,128)(2,1)S(1)}, u32[]{:S(2)}, u32[]{:S(2)}) collective-permute-start(bf16[128,1024]{1,0:T(8,128)(2,1)S(1)} %get-tuple-element.188), channel_id=1, source_target_pairs={{0,2},{1,3},{2,0},{3,1},{4,6},{5,7},{6,4},{7,5},{8,10},{9,11},{10,... | collective-permute-start | bytes 786440 | tf_op jit(solution)/shard_map/cond/branch_1_fun/ppermute | solution.py:296
  197.3 13.5 %collective-permute-start.8 = (bf16[128,1024]{1,0:T(8,128)(2,1)S(1)}, bf16[128,1024]{1,0:T(8,128)(2,1)S(1)}, u32[]{:S(2)}, u32[]{:S(2)}) collective-permute-start(bf16[128,1024]{1,0:T(8,128)(2,1)S(1)} %get-tuple-element.189), channel_id=1, source_target_pairs={{0,3},{1,2},{2,1},{3,0},{4,7},{5,6},{6,5},{7,4},{8,11},{9,10},{10,... | collective-permute-start | bytes 786440 | tf_op jit(solution)/shard_map/cond/branch_1_fun/ppermute | solution.py:296
  211.0 36.5 %collective-permute-start.31 = (bf16[3,128,2048]{2,1,0:T(8,128)(2,1)S(1)}, bf16[3,128,2048]{2,1,0:T(8,128)(2,1)S(1)}, u32[]{:S(2)}, u32[]{:S(2)}) collective-permute-start(bf16[3,128,2048]{2,1,0:T(8,128)(2,1)S(1)} %collective-permute-done.30), channel_id=1, source_target_pairs={{0,8},{4,12},{8,24},{12,28},{24,16},{28,20},{16,0},{20,4},{1,9},{5... | collective-permute-start | bytes 4718600 | tf_op jit(solution)/shard_map/ppermute | solution.py:290
  211.4 39.2 %copy-start.13 = (f32[16,1,128]{2,1,0:T(1,128)S(1)}, f32[16,1,128]{2,1,0:T(1,128)}, u32[]{:S(2)}) copy-start(f32[16,1,128]{2,1,0:T(1,128)} %get-tuple-element.346) | copy-start | bytes 24580
  211.4 3.8 %collective-permute-start.20 = (bf16[3,128,2048]{2,1,0:T(8,128)(2,1)}, bf16[3,128,2048]{2,1,0:T(8,128)(2,1)}, u32[]{:S(2)}, u32[]{:S(2)}) collective-permute-start(bf16[3,128,2048]{2,1,0:T(8,128)(2,1)} %get-tuple-element.204.refs_0_.refs_4_), channel_id=1, source_target_pairs={{0,4},{4,0},{8,12},{12,8},{16,20},{20,16},{24,28},{28,24},{1,5},{5... | collective-permute-start | bytes 4718600 | tf_op jit(solution)/shard_map/cond/branch_1_fun/ppermute | solution.py:293
  215.2 12.5 %copy-start.7 = (bf16[1024,2048]{1,0:T(8,128)(2,1)S(1)}, bf16[1024,2048]{1,0:T(8,128)(2,1)}, u32[]{:S(2)}) copy-start(bf16[1024,2048]{1,0:T(8,128)(2,1)} %get-tuple-element.219.refs_8_) | copy-start | bytes 12582916 | tf_op jit(solution)/shard_map/cond
  215.2 12.5 %copy-start.8 = (bf16[1024,2048]{1,0:T(8,128)(2,1)S(1)}, bf16[1024,2048]{1,0:T(8,128)(2,1)}, u32[]{:S(2)}) copy-start(bf16[1024,2048]{1,0:T(8,128)(2,1)} %get-tuple-element.218.refs_7_) | copy-start | bytes 12582916 | tf_op jit(solution)/shard_map/cond
  215.2 12.5 %copy-start.9 = (bf16[1024,2048]{1,0:T(8,128)(2,1)S(1)}, bf16[1024,2048]{1,0:T(8,128)(2,1)}, u32[]{:S(2)}) copy-start(bf16[1024,2048]{1,0:T(8,128)(2,1)} %get-tuple-element.217.refs_6_) | copy-start | bytes 12582916 | tf_op jit(solution)/shard_map/cond
  224.1 13.0 %collective-permute-start.21 = (bf16[64,1024]{1,0:T(8,128)(2,1)S(1)}, bf16[64,1024]{1,0:T(8,128)(2,1)S(1)}, u32[]{:S(2)}, u32[]{:S(2)}) collective-permute-start(bf16[64,1024]{1,0:T(8,128)(2,1)S(1)} %get-tuple-element.210), channel_id=1, source_target_pairs={{0,1},{1,0},{2,3},{3,2},{4,5},{5,4},{6,7},{7,6},{8,9},{9,8},{10,11... | collective-permute-start | bytes 393224 | tf_op jit(solution)/shard_map/cond/branch_1_fun/ppermute | solution.py:296
  225.6 11.5 %collective-permute-start.22 = (bf16[64,1024]{1,0:T(8,128)(2,1)S(1)}, bf16[64,1024]{1,0:T(8,128)(2,1)S(1)}, u32[]{:S(2)}, u32[]{:S(2)}) collective-permute-start(bf16[64,1024]{1,0:T(8,128)(2,1)S(1)} %get-tuple-element.211), channel_id=1, source_target_pairs={{0,2},{1,3},{2,0},{3,1},{4,6},{5,7},{6,4},{7,5},{8,10},{9,11},{10,... | collective-permute-start | bytes 393224 | tf_op jit(solution)/shard_map/cond/branch_1_fun/ppermute | solution.py:296
  227.1 10.0 %collective-permute-start.23 = (bf16[64,1024]{1,0:T(8,128)(2,1)S(1)}, bf16[64,1024]{1,0:T(8,128)(2,1)}, u32[]{:S(2)}, u32[]{:S(2)}) collective-permute-start(bf16[64,1024]{1,0:T(8,128)(2,1)S(1)} %get-tuple-element.212), channel_id=1, source_target_pairs={{0,3},{1,2},{2,1},{3,0},{4,7},{5,6},{6,5},{7,4},{8,11},{9,10},{10,... | collective-permute-start | bytes 393224 | tf_op jit(solution)/shard_map/cond/branch_1_fun/ppermute | solution.py:296
  227.7 11.1 %collective-permute-start.25 = (bf16[64,1024]{1,0:T(8,128)(2,1)}, bf16[64,1024]{1,0:T(8,128)(2,1)}, u32[]{:S(2)}, u32[]{:S(2)}) collective-permute-start(bf16[64,1024]{1,0:T(8,128)(2,1)} %pad_maximum_fusion.6), channel_id=1, source_target_pairs={{0,4},{4,0},{8,12},{12,8},{16,20},{20,16},{24,28},{28,24},{1,5},{5... | collective-permute-start | bytes 393224 | tf_op jit(solution)/shard_map/cond/branch_1_fun/ppermute | solution.py:293
  238.2 2.2 collective-permute-start.24
  247.6 3.5 %collective-permute-start.34 = (bf16[3,128,2048]{2,1,0:T(8,128)(2,1)S(1)}, bf16[3,128,2048]{2,1,0:T(8,128)(2,1)S(1)}, u32[]{:S(2)}, u32[]{:S(2)}) collective-permute-start(bf16[3,128,2048]{2,1,0:T(8,128)(2,1)S(1)} %collective-permute-done.31.refs_0_.refs_4_), channel_id=1, source_target_pairs={{0,4},{4,0},{8,12},{12,8},{16,20},{20,16},{24,28},{28,24},{1,5},{5... | collective-permute-start | bytes 4718600 | tf_op jit(solution)/shard_map/ppermute | solution.py:293
  247.6 14.5 %collective-permute-start.32 = (bf16[2,64,1024]{2,1,0:T(8,128)(2,1)}, bf16[2,64,1024]{2,1,0:T(8,128)(2,1)S(1)}, u32[]{:S(2)}, u32[]{:S(2)}) collective-permute-start(bf16[2,64,1024]{2,1,0:T(8,128)(2,1)} %copy-done.12), channel_id=1, source_target_pairs={{0,16},{4,20},{8,0},{12,4},{24,8},{28,12},{16,24},{20,28},{1,17},{... | collective-permute-start | bytes 786440 | tf_op jit(solution)/shard_map/ppermute | solution.py:393
  248.5 15.0 %collective-permute-start.33 = (bf16[2,64,1024]{2,1,0:T(8,128)(2,1)}, bf16[2,64,1024]{2,1,0:T(8,128)(2,1)S(1)}, u32[]{:S(2)}, u32[]{:S(2)}) collective-permute-start(bf16[2,64,1024]{2,1,0:T(8,128)(2,1)} %get-tuple-element.340), channel_id=1, source_target_pairs={{0,24},{4,28},{8,16},{12,20},{24,0},{28,4},{16,8},{20,12},{1,25},{... | collective-permute-start | bytes 786440 | tf_op jit(solution)/shard_map/ppermute | solution.py:393
  250.8 31.2 %copy-start.11 = (bf16[2,64,1024]{2,1,0:T(8,128)(2,1)S(1)}, bf16[2,64,1024]{2,1,0:T(8,128)(2,1)}, u32[]{:S(2)}) copy-start(bf16[2,64,1024]{2,1,0:T(8,128)(2,1)} %copy-done.10) | copy-start | bytes 786436
  250.8 10.8 %collective-permute-start.38 = (f32[16]{0:T(128)S(1)}, f32[16]{0:T(128)S(1)}, u32[]{:S(2)}, u32[]{:S(2)}) collective-permute-start(f32[16]{0:T(128)S(1)} %slice_reduce_fusion), channel_id=1, source_target_pairs={{0,4},{4,0},{8,12},{12,8},{16,20},{20,16},{24,28},{28,24},{1,5},{5... | collective-permute-start | bytes 200 | tf_op jit(solution)/shard_map/ppermute | solution.py:403
  251.1 35.1 %copy-start.5 = (bf16[1024,2048]{1,0:T(8,128)(2,1)S(1)}, bf16[1024,2048]{1,0:T(8,128)(2,1)}, u32[]{:S(2)}) copy-start(bf16[1024,2048]{1,0:T(8,128)(2,1)} %get-tuple-element.365.refs_8_) | copy-start | bytes 12582916
  251.1 35.1 %copy-start.6 = (bf16[1024,2048]{1,0:T(8,128)(2,1)S(1)}, bf16[1024,2048]{1,0:T(8,128)(2,1)}, u32[]{:S(2)}) copy-start(bf16[1024,2048]{1,0:T(8,128)(2,1)} %get-tuple-element.364.refs_7_) | copy-start | bytes 12582916
  258.5 6.1 %collective-permute-start.35 = (bf16[64,1024]{1,0:T(8,128)(2,1)S(1)}, bf16[64,1024]{1,0:T(8,128)(2,1)S(1)}, u32[]{:S(2)}, u32[]{:S(2)}) collective-permute-start(bf16[64,1024]{1,0:T(8,128)(2,1)S(1)} %get-tuple-element.343), channel_id=1, source_target_pairs={{0,1},{1,0},{2,3},{3,2},{4,5},{5,4},{6,7},{7,6},{8,9},{9,8},{10,11... | collective-permute-start | bytes 393224 | tf_op jit(solution)/shard_map/ppermute | solution.py:296
  260.1 8.2 %collective-permute-start.36 = (bf16[64,1024]{1,0:T(8,128)(2,1)S(1)}, bf16[64,1024]{1,0:T(8,128)(2,1)S(1)}, u32[]{:S(2)}, u32[]{:S(2)}) collective-permute-start(bf16[64,1024]{1,0:T(8,128)(2,1)S(1)} %get-tuple-element.344), channel_id=1, source_target_pairs={{0,2},{1,3},{2,0},{3,1},{4,6},{5,7},{6,4},{7,5},{8,10},{9,11},{10,... | collective-permute-start | bytes 393224 | tf_op jit(solution)/shard_map/ppermute | solution.py:296
  261.6 6.7 %collective-permute-start.37 = (bf16[64,1024]{1,0:T(8,128)(2,1)S(1)}, bf16[64,1024]{1,0:T(8,128)(2,1)S(1)}, u32[]{:S(2)}, u32[]{:S(2)}) collective-permute-start(bf16[64,1024]{1,0:T(8,128)(2,1)S(1)} %get-tuple-element.345), channel_id=1, source_target_pairs={{0,3},{1,2},{2,1},{3,0},{4,7},{5,6},{6,5},{7,4},{8,11},{9,10},{10,... | collective-permute-start | bytes 393224 | tf_op jit(solution)/shard_map/ppermute | solution.py:296
  268.4 1.3 collective-permute-start.39
  269.7 12.2 %collective-permute-start.40 = (bf16[2,64,1024]{2,1,0:T(8,128)(2,1)S(1)}, bf16[2,64,1024]{2,1,0:T(8,128)(2,1)S(1)}, u32[]{:S(2)}, u32[]{:S(2)}) collective-permute-start(bf16[2,64,1024]{2,1,0:T(8,128)(2,1)S(1)} %maximum_maximum_fusion), channel_id=1, source_target_pairs={{0,8},{4,12},{8,24},{12,28},{24,16},{28,20},{16,0},{20,4},{1,9},{5... | collective-permute-start | bytes 786440 | tf_op jit(solution)/shard_map/ppermute | solution.py:393
  271.1 5.9 %collective-permute-start.41 = (f32[16]{0:T(128)S(1)}, f32[16]{0:T(128)S(1)}, u32[]{:S(2)}, u32[]{:S(2)}) collective-permute-start(f32[16]{0:T(128)S(1)} %add.62), channel_id=1, source_target_pairs={{0,8},{4,12},{8,0},{12,4},{16,24},{20,28},{24,16},{28,20},{1,9},{5... | collective-permute-start | bytes 200 | tf_op jit(solution)/shard_map/ppermute | solution.py:403
  277.0 4.4 %collective-permute-start.42 = (f32[16]{0:T(128)S(1)}, f32[16]{0:T(128)S(1)}, u32[]{:S(2)}, u32[]{:S(2)}) collective-permute-start(f32[16]{0:T(128)S(1)} %add.66), channel_id=1, source_target_pairs={{0,16},{4,20},{8,24},{12,28},{16,0},{20,4},{24,8},{28,12},{1,17},{... | collective-permute-start | bytes 200 | tf_op jit(solution)/shard_map/ppermute | solution.py:403
  282.6 13.2 %collective-permute-start.43 = (bf16[2,64,1024]{2,1,0:T(8,128)(2,1)S(1)}, bf16[2,64,1024]{2,1,0:T(8,128)(2,1)S(1)}, u32[]{:S(2)}, u32[]{:S(2)}) collective-permute-start(bf16[2,64,1024]{2,1,0:T(8,128)(2,1)S(1)} %get-tuple-element.356), channel_id=1, source_target_pairs={{0,1},{1,0},{2,3},{3,2},{4,5},{5,4},{6,7},{7,6},{8,9},{9,8},{10,11... | collective-permute-start | bytes 786440 | tf_op jit(solution)/shard_map/ppermute | solution.py:296
  284.2 11.7 %collective-permute-start.44 = (bf16[2,64,1024]{2,1,0:T(8,128)(2,1)S(1)}, bf16[2,64,1024]{2,1,0:T(8,128)(2,1)S(1)}, u32[]{:S(2)}, u32[]{:S(2)}) collective-permute-start(bf16[2,64,1024]{2,1,0:T(8,128)(2,1)S(1)} %get-tuple-element.357), channel_id=1, source_target_pairs={{0,2},{1,3},{2,0},{3,1},{4,6},{5,7},{6,4},{7,5},{8,10},{9,11},{10,... | collective-permute-start | bytes 786440 | tf_op jit(solution)/shard_map/ppermute | solution.py:296
  285.7 10.5 %collective-permute-start.45 = (bf16[2,64,1024]{2,1,0:T(8,128)(2,1)S(1)}, bf16[2,64,1024]{2,1,0:T(8,128)(2,1)S(1)}, u32[]{:S(2)}, u32[]{:S(2)}) collective-permute-start(bf16[2,64,1024]{2,1,0:T(8,128)(2,1)S(1)} %get-tuple-element.358), channel_id=1, source_target_pairs={{0,3},{1,2},{2,1},{3,0},{4,7},{5,6},{6,5},{7,4},{8,11},{9,10},{10,... | collective-permute-start | bytes 786440 | tf_op jit(solution)/shard_map/ppermute | solution.py:296
